TPU v7x, 128 devices: a whole 4x4x4 slice. The times are simulated.
128 devices in a mesh: adapter: 8 (over z, core), tensor: 16 (over y, x).
Axes of the slice: x: 4, y: 4, z: 4, core: 2. Of those that a mesh axis runs over, the one named last changes fastest.
Arguments:
- normed_input: bfloat16 [8192, 8192], P('adapter', 'tensor'), may hold values from -6 to 6
- query_matrix: bfloat16 [8192, 8192], P(None, 'tensor'), may hold values from -0.0625 to 0.0625
- key_value_matrix: bfloat16 [8192, 2048], P(None, 'tensor'), may hold values from -0.0625 to 0.0625
- output_matrix: bfloat16 [8192, 8192], P('tensor'), may hold values from -0.09375 to 0.09375
- adapter_down_qkv: bfloat16 [64, 8192, 192], P('adapter', 'tensor'), may hold values from -0.0625 to 0.0625
- adapter_up_query: bfloat16 [64, 64, 8192], P('adapter', None, 'tensor'), may hold values from -0.75 to 0.75
- adapter_up_key_value: bfloat16 [64, 64, 2048], P('adapter', None, 'tensor'), may hold values from -0.75 to 0.75
- adapter_down_output: bfloat16 [64, 8192, 64], P('adapter', 'tensor'), may hold values from -0.0625 to 0.0625
- adapter_up_output: bfloat16 [64, 64, 8192], P('adapter', None, 'tensor'), may hold values from -0.75 to 0.75
- adapter_choice: int32 [8, 4], replicated, may hold values from 0 to 63, as said below
- request_block_count: int32 [8, 4], P('adapter'), may hold values from 1 to 3, 8 in all within a row
- last_block_tokens: int32 [8, 4], P('adapter'), may hold values from 1 to 128
Outputs:
- attention_out: float32 [8192, 8192], P('adapter', 'tensor')
Inputs may be any that keep to these rules, and one draw needn't show every extreme that they name: `adapter_choice`: the owner of adapter j is j // 8. In each group at most 1 request use adapters of one owner, and in every group some owner has exactly 1. `request_block_count`: each row sums to 8.
All inputs are finite; a program needn't handle non-finite values.
Results may differ from a plain program's by a relative error of at most 0.01.
Values may be sent and summed in bfloat16 or wider, within the bound.
No kernel may reach another device: no remote copies, remote signals or barrier semaphores. Data moves between devices by JAX's collectives and lax.ppermute only.
A program may use at most 192 MiB of HBM per device.

v0:
```python
import math

import jax
import jax.numpy as jnp
from jax import lax
from jax.sharding import PartitionSpec as P

HEAD_SIZE = 128
BLOCK = 128


rope_base = 500000.0


def partner_2(block, axis, distance):
    count = lax.axis_size(axis)
    route = []
    for low in range(count):
        high = low | 1 << distance
        if high != low and high < count:
            route += [(low, high), (high, low)]
    return lax.ppermute(block, axis, route)


def small_lookup(table, index):
    entries = jnp.arange(table.shape[0], dtype=jnp.int32)
    return jnp.sum(jnp.where(index[:, None] == entries[None, :], table[None, :], 0), axis=1)


def request_layout(counts, tails, token_rows, block):
    block_total = token_rows // block
    starts = jnp.cumsum(counts) - counts
    blocks = jnp.arange(block_total, dtype=jnp.int32)
    block_req = jnp.sum((starts[None, :] <= blocks[:, None]).astype(jnp.int32), axis=1) - 1
    first_tok = small_lookup(starts, block_req) * block
    used = (small_lookup(counts, block_req) - 1) * block + small_lookup(tails, block_req)
    offset = jnp.arange(block, dtype=jnp.int32)
    token_position = (blocks[:, None] * block + offset[None, :] - first_tok[:, None]).reshape(
        token_rows
    )
    token_req = jnp.broadcast_to(block_req[:, None], (block_total, block)).reshape(token_rows)
    limit = jnp.broadcast_to(used[:, None], (block_total, block)).reshape(token_rows)
    return (block_req, token_req, token_position, token_position < limit)


def rotary_heads(values, token_position):
    width = values.shape[-1]
    half = width // 2
    freq = jnp.exp(-(2.0 * jnp.arange(half, dtype=jnp.float32) / width) * math.log(rope_base))
    angle = token_position.astype(jnp.float32)[:, None] * freq[None, :]
    cosine = jnp.cos(angle)[:, None, :]
    sine = jnp.sin(angle)[:, None, :]
    first = values[..., :half]
    second = values[..., half:]
    return jnp.concatenate(
        [first * cosine - second * sine, second * cosine + first * sine], axis=-1
    )


def attend(query, keys, values, token_req, token_position, valid_mask, rows):
    token_rows = query.shape[0]
    heads = query.shape[1]
    width = query.shape[2]

    def one_block(index):
        start = index * rows
        q_rows = lax.dynamic_slice_in_dim(query, start, rows, 0)
        r_rows = lax.dynamic_slice_in_dim(token_req, start, rows, 0)
        p_rows = lax.dynamic_slice_in_dim(token_position, start, rows, 0)
        scores = jnp.einsum(
            "qhd,kd->hqk", q_rows, keys, preferred_element_type=jnp.float32
        ) / math.sqrt(width)
        allowed = (
            (r_rows[:, None] == token_req[None, :])
            & (token_position[None, :] <= p_rows[:, None])
            & valid_mask[None, :]
        )
        weights = jnp.where(allowed[None], jnp.exp(scores), 0.0)
        weights = (weights / jnp.sum(weights, axis=2, keepdims=True)).astype(jnp.bfloat16)
        mixed = jnp.einsum("hqk,kd->qhd", weights, values, preferred_element_type=jnp.float32)
        return mixed.astype(jnp.bfloat16).reshape(rows, heads * width)

    parts = lax.map(one_block, jnp.arange(token_rows // rows, dtype=jnp.int32))
    return parts.reshape(token_rows, heads * width)


def join_halves(mine, partner, my_column, bit_number, along):
    lower_side = my_column // 2**bit_number % 2 == 0
    return jnp.where(
        lower_side,
        jnp.concatenate([mine, partner], axis=along),
        jnp.concatenate([partner, mine], axis=along),
    )


def key_value_pieces(kv_base, shrunk_tiles, b_blocks, first_piece, token_position, rank_span_width):
    token_rows = kv_base.shape[0]
    piece_total = kv_base.shape[1] // HEAD_SIZE
    key_rank = shrunk_tiles[..., rank_span_width : 2 * rank_span_width]
    value_rank = shrunk_tiles[..., 2 * rank_span_width :]
    outputs = []
    for piece in range(piece_total):
        is_key = (first_piece + piece) % 2 == 0
        rank_in = jnp.where(is_key, key_rank, value_rank)
        extra = jnp.einsum(
            "fnw,fwv->fnv",
            rank_in,
            b_blocks[:, :, piece * HEAD_SIZE : (piece + 1) * HEAD_SIZE],
            preferred_element_type=jnp.float32,
        )
        summed = kv_base[:, piece * HEAD_SIZE : (piece + 1) * HEAD_SIZE] + extra.reshape(
            token_rows, HEAD_SIZE
        )
        turned = rotary_heads(summed.reshape(token_rows, 1, HEAD_SIZE), token_position).reshape(
            token_rows, HEAD_SIZE
        )
        outputs.append(jnp.where(is_key, turned, summed).astype(jnp.bfloat16))
    return jnp.concatenate(outputs, axis=1)


def on_device(
    normed_input,
    query_matrix,
    key_value_matrix,
    output_matrix,
    adapter_down_qkv,
    adapter_up_query,
    adapter_up_key_value,
    adapter_down_output,
    adapter_up_output,
    adapter_choice,
    request_block_count,
    last_block_tokens,
):
    group_total = lax.axis_size("adapter")
    my_group = lax.axis_index("adapter")
    my_column = lax.axis_index("tensor")
    each_holder = adapter_down_qkv.shape[0]
    group_reqs = adapter_choice.shape[1]
    capacity = (group_reqs + group_total - 1) // group_total
    token_rows = normed_input.shape[0]
    local_width = normed_input.shape[1]
    rank_span_width = adapter_up_query.shape[1]
    block_total = token_rows // BLOCK
    kv_cols = key_value_matrix.shape[1]
    owners = adapter_choice // each_holder
    slot_in = adapter_choice % each_holder
    mine = owners == my_group
    order = jnp.cumsum(mine.astype(jnp.int32), axis=1) - 1
    slot_ids = jnp.arange(capacity, dtype=jnp.int32)
    entries = jnp.arange(each_holder, dtype=jnp.int32)
    chosen = (
        mine[:, None, :, None]
        & (order[:, None, :, None] == slot_ids[None, :, None, None])
        & (slot_in[:, None, :, None] == entries[None, None, None, :])
    )
    picker = (
        jnp.any(chosen, axis=2).astype(jnp.bfloat16).reshape(group_total * capacity, each_holder)
    )

    def selector_mask(store):
        flat = jnp.dot(picker, store.reshape(each_holder, -1), preferred_element_type=jnp.float32)
        return flat.astype(jnp.bfloat16).reshape((group_total, capacity) + store.shape[1:])

    output_departing = (
        selector_mask(adapter_down_qkv),
        selector_mask(adapter_up_query),
        selector_mask(adapter_up_key_value),
        selector_mask(adapter_down_output),
        selector_mask(adapter_up_output),
    )
    arrived = (
        lax.all_to_all(output_departing[0], "adapter", split_axis=0, concat_axis=0, tiled=True),
        lax.all_to_all(output_departing[1], "adapter", split_axis=0, concat_axis=0, tiled=True),
        lax.all_to_all(output_departing[2], "adapter", split_axis=0, concat_axis=0, tiled=True),
        lax.all_to_all(output_departing[3], "adapter", split_axis=0, concat_axis=0, tiled=True),
        lax.all_to_all(output_departing[4], "adapter", split_axis=0, concat_axis=0, tiled=True),
    )
    own_ids = lax.dynamic_index_in_dim(adapter_choice, my_group, 0, keepdims=False)
    own_owner = own_ids // each_holder
    req_index = jnp.arange(group_reqs, dtype=jnp.int32)
    earlier = (own_owner[:, None] == own_owner[None, :]) & (req_index[None, :] < req_index[:, None])
    req_slot = own_owner * capacity + jnp.sum(earlier.astype(jnp.int32), axis=1)
    block_req, token_req, token_position, valid_mask = request_layout(
        request_block_count[0], last_block_tokens[0], token_rows, BLOCK
    )
    block_slot = small_lookup(req_slot, block_req)

    def per_block(received):
        flat = received.reshape((group_total * capacity,) + received.shape[2:])
        return jnp.take(flat, block_slot, axis=0)

    down_block_rows = per_block(arrived[0])
    query_up_blocks = per_block(arrived[1])
    key_value_up_blocks = per_block(arrived[2])
    output_down_blocks = per_block(arrived[3])
    output_up_blocks = per_block(arrived[4])
    token_tiles = normed_input.reshape(block_total, BLOCK, local_width)
    partial_rank = jnp.einsum(
        "btd,bdr->btr", token_tiles, down_block_rows, preferred_element_type=jnp.float32
    ).reshape(token_rows, 3 * rank_span_width)
    reduced_rows = lax.psum(partial_rank, "tensor").astype(jnp.bfloat16)
    shrunk_tiles = reduced_rows.reshape(block_total, BLOCK, 3 * rank_span_width)
    kv_cols_full = key_value_matrix
    kv_b_full = key_value_up_blocks
    other_cols, other_b = partner_2((kv_cols_full, kv_b_full), "tensor", 0)
    kv_cols_full = join_halves(kv_cols_full, other_cols, my_column, 0, 1)
    kv_b_full = join_halves(kv_b_full, other_b, my_column, 0, 2)
    first_piece = my_column * kv_cols // HEAD_SIZE // 2 * 2
    piece = lax.all_gather(normed_input, "tensor", axis=1, tiled=True)
    query_plain = jnp.dot(piece, query_matrix, preferred_element_type=jnp.float32)
    kv_base = jnp.dot(piece, kv_cols_full, preferred_element_type=jnp.float32)
    key_value = key_value_pieces(
        kv_base, shrunk_tiles, kv_b_full, first_piece, token_position, rank_span_width
    )
    keys = key_value[:, :HEAD_SIZE]
    values = key_value[:, HEAD_SIZE:]
    query_adapter_delta = jnp.einsum(
        "fnw,fwv->fnv",
        shrunk_tiles[..., :rank_span_width],
        query_up_blocks,
        preferred_element_type=jnp.float32,
    ).reshape(token_rows, -1)
    heads_here = query_matrix.shape[1] // HEAD_SIZE
    query_rows_all = rotary_heads(
        (query_plain + query_adapter_delta).reshape(token_rows, heads_here, HEAD_SIZE),
        token_position,
    ).astype(jnp.bfloat16)
    attended = attend(
        query_rows_all, keys, values, token_req, token_position, valid_mask, min(512, token_rows)
    )
    projected_rows = lax.psum_scatter(
        lax.dot_general(
            output_matrix, attended, (((0,), (1,)), ((), ())), preferred_element_type=jnp.float32
        ),
        "tensor",
        scatter_dimension=0,
        tiled=True,
    ).T
    att_tiles = attended.reshape(block_total, BLOCK, -1)
    partial_head = jnp.einsum(
        "btq,bqr->btr", att_tiles, output_down_blocks, preferred_element_type=jnp.float32
    ).reshape(token_rows, rank_span_width)
    head_rank_index = lax.psum(partial_head, "tensor").astype(jnp.bfloat16)
    output_adapter_delta = jnp.einsum(
        "fps,fsq->fpq",
        head_rank_index.reshape(block_total, BLOCK, rank_span_width),
        output_up_blocks,
        preferred_element_type=jnp.float32,
    ).reshape(token_rows, local_width)
    return jnp.where(valid_mask[:, None], projected_rows + output_adapter_delta, 0.0)


def solution(mesh):
    placed = (
        P("adapter", "tensor"),
        P(None, "tensor"),
        P(None, "tensor"),
        P("tensor", None),
        P("adapter", "tensor", None),
        P("adapter", None, "tensor"),
        P("adapter", None, "tensor"),
        P("adapter", "tensor", None),
        P("adapter", None, "tensor"),
        P(),
        P("adapter", None),
        P("adapter", None),
    )
    return jax.shard_map(
        on_device, mesh=mesh, in_specs=placed, out_specs=P("adapter", "tensor"), check_vma=False
    )
```

profile of v0, /device:TPU:0, one launch (start us, length us, event | category | flops | bytes accessed | tf_op | source)
XLA Modules:
  0.0 483.7 jit_solution(10750574076216280560)
XLA Ops:
  10.6 5.4 %all-to-all-start.2 = ((bf16[8,1,64,128]{3,2,1,0:T(8,128)(2,1)}), bf16[8,1,64,128]{3,2,1,0:T(8,128)(2,1)S(1)}, u32[]{:S(2)}, u32[]{:S(2)}) async-start(bf16[8,1,64,128]{3,2,1,0:T(8,128)(2,1)} %copy.79), calls=%async_computation.2 | async-start | bytes 262144 | tf_op jit(solution)/shard_map/all_to_all | solution.py:175
  19.1 2.8 copy.71
  21.9 3.7 reshape.497
  25.6 2.1 reshape.414
  30.3 4.8 all-to-all-start.1
  37.0 3.1 reshape.500
  40.1 2.3 copy.72
  43.0 2.6 all-to-all-done.1
  45.6 3.6 all-to-all-start
  49.3 3.1 multiply_cosine_fusion
  53.7 42.0 %collective-permute-done.1 = bf16[8,64,128]{2,1,0:T(8,128)(2,1)S(1)} collective-permute-done((bf16[8,64,128]{2,1,0:T(8,128)(2,1)S(1)}, bf16[8,64,128]{2,1,0:T(8,128)(2,1)S(1)}, u32[]{:S(2)}, u32[]{:S(2)}) %collective-permute-start.1) | collective-permute-done | bytes 131104 | tf_op jit(solution)/shard_map/ppermute | solution.py:22
  95.8 2.4 gather_fusion.3
  98.9 1.9 fusion.31
  100.9 96.0 %all-reduce.2 = bf16[1024,192]{0,1:T(8,128)(2,1)S(1)} all-reduce(f32[1024,192]{0,1:T(8,128)S(1)} %bitcast.179), channel_id=1, replica_groups=mesh['adapter'=8,'tensor'=16] {'tensor'}, use_global_device_ids=true, to_apply=%region_9.10 | all-reduce | flops 196608 | bytes 1179648 | tf_op jit(solution)/shard_map/psum | solution.py:202
  201.4 10.7 %fusion.30 = f32[1024,256]{0,1:T(8,128)S(1)} fusion(bf16[1024,8192]{1,0:T(8,128)(2,1)} %all-gather.2.cloned.1.call-done, bf16[8192,128]{1,0:T(8,128)(2,1)} %collective-permute-done, bf16[8192,128]{1,0:T(8,128)(2,1)} %param.18, pred[]{:T(512)S(6)} %eq.131), kind=kOutput, calls=%fused_computation.48 | convolution fusion | flops 4313841664 | bytes 22020096 | tf_op jit(solution)/shard_map/dot_general | solution.py:212
  215.8 15.8 %convolution_add_fusion = f32[1024,512]{0,1:T(8,128)} fusion(f32[1024,512]{0,1:T(8,128)S(1)} %copy-done, bf16[1024,8192]{1,0:T(8,128)(2,1)} %all-gather.2.cloned.1.call-done, bf16[8192,512]{1,0:T(8,128)(2,1)} %param.17), kind=kOutput, calls=%fused_computation.44 | convolution fusion | flops 8590458880 | bytes 29360128 | tf_op jit(solution)/shard_map/dot_general | solution.py:211
  231.6 2.7 fusion.92
  236.2 1.9 copy.99
  238.1 2.4 subtract_convert_fusion
  241.5 16.4 %while.12 = (s32[]{:T(128)}, bf16[2,512,512]{2,1,0:T(8,128)(2,1)}, s32[2]{0:T(128)S(1)}, s32[1024]{0:T(1024)S(1)}, s32[1024]{0:T(1024)S(1)}, /*index=5*/bf16[102...) while((s32[]{:T(128)}, bf16[2,512,512]{2,1,0:T(8,128)(2,1)}, ...), condition=%wide.region_12.14_spmd.clone.clone, body=%wide.region_10.13_spmd.clone.clone.sunk | while | flops 1090784256 | bytes 22068124 | solution.py:83
  243.8 2.5 bitcast_reduce_fusion.2
  246.3 2.5 fusion.116
  251.9 2.5 bitcast_reduce_fusion.2
  254.4 2.5 fusion.116
  257.9 17.8 %convolution_bitcast_fusion = f32[8192,1024]{0,1:T(8,128)} fusion(bf16[1024,512]{1,0:T(8,128)(2,1)} %bitcast.198, bf16[512,8192]{1,0:T(8,128)(2,1)} %param.19), kind=kOutput, calls=%fused_computation.30 | convolution fusion | flops 8589934592 | bytes 42991616 | tf_op jit(solution)/shard_map/dot_general | solution.py:233
  280.7 4.7 all-to-all-start.3
  286.9 8.8 %all-to-all-done.3 = bf16[8,1,512,64]{2,3,1,0:T(8,128)(2,1)S(1)} async-done(((bf16[8,1,512,64]{2,3,1,0:T(8,128)(2,1)}), bf16[8,1,512,64]{2,3,1,0:T(8,128)(2,1)S(1)}, u32[]{:S(2)}, u32[]{:S(2)}) %all-to-all-start.3) | async-done | bytes 524320 | tf_op jit(solution)/shard_map/all_to_all | solution.py:176
  295.7 3.5 all-to-all-start.4
  300.0 9.5 %all-to-all-done.4 = bf16[8,1,64,512]{3,2,1,0:T(8,128)(2,1)S(1)} async-done(((bf16[8,1,64,512]{3,2,1,0:T(8,128)(2,1)}), bf16[8,1,64,512]{3,2,1,0:T(8,128)(2,1)S(1)}, u32[]{:S(2)}, u32[]{:S(2)}) %all-to-all-start.4) | async-done | bytes 524320 | tf_op jit(solution)/shard_map/all_to_all | solution.py:177
  312.0 78.8 %all-reduce.3 = bf16[1024,64]{0,1:T(8,128)(2,1)S(1)} all-reduce(f32[1024,64]{0,1:T(8,128)S(1)} %bitcast.191), channel_id=1, replica_groups=mesh['adapter'=8,'tensor'=16] {'tensor'}, use_global_device_ids=true, to_apply=%region_14.16 | all-reduce | flops 65536 | bytes 393216 | tf_op jit(solution)/shard_map/psum | solution.py:244
  391.2 82.2 %reduce-scatter.2.cloned.1.call-done = f32[512,1024]{0,1:T(8,128)} async-done(((f32[8192,1024]{0,1:T(8,128)}), f32[512,1024]{0,1:T(8,128)}) %reduce-scatter.2.cloned.1.call-update) | async-done | bytes 2097168 | tf_op jit(solution)/shard_map/reduce_scatter | solution.py:232
  473.4 3.5 fusion.26
  (136 shorter events, 40.5 us)
Async XLA Ops:
  6.5 194.8 %all-gather.2.cloned.1.call-start = ((), (), s32[]{:S(2)}) async-start(), calls=%async_computation.6 | async-start | bytes 17825792 | tf_op jit(solution)/shard_map/all_gather | solution.py:210
  8.8 20.0 %copy-start.6 = (pred[8,8]{1,0:T(8,128)(4,1)}, pred[8,8]{1,0:T(8,128)(4,1)S(1)}, u32[]{:S(2)}) copy-start(pred[8,8]{1,0:T(8,128)(4,1)S(1)} %fusion.77) | copy-start | bytes 196
  10.6 19.8 %all-to-all-start.2 = ((bf16[8,1,64,128]{3,2,1,0:T(8,128)(2,1)}), bf16[8,1,64,128]{3,2,1,0:T(8,128)(2,1)S(1)}, u32[]{:S(2)}, u32[]{:S(2)}) async-start(bf16[8,1,64,128]{3,2,1,0:T(8,128)(2,1)} %copy.79), calls=%async_computation.2 | async-start | bytes 262144 | tf_op jit(solution)/shard_map/all_to_all | solution.py:175
  16.0 185.4 %collective-permute-start = (bf16[8192,128]{1,0:T(8,128)(2,1)}, bf16[8192,128]{1,0:T(8,128)(2,1)}, u32[]{:S(2)}, u32[]{:S(2)}) collective-permute-start(bf16[8192,128]{1,0:T(8,128)(2,1)} %param.18), channel_id=1, source_target_pairs={{0,1},{1,0},{2,3},{3,2},{4,5},{5,4},{6,7},{7,6},{8,9},{9,8},{10,11... | collective-permute-start | bytes 6291464 | tf_op jit(solution)/shard_map/ppermute | solution.py:22
  25.6 2.2 copy-start.2
  25.6 2.5 copy-start.19
  25.6 2.8 copy-start.20
  28.4 14.6 %copy-start.11 = (s32[8]{0:T(128)}, s32[8]{0:T(128)S(1)}, u32[]{:S(2)}) copy-start(s32[8]{0:T(128)S(1)} %broadcast_add_fusion) | copy-start | bytes 100
  30.3 67.9 %copy-start.13 = (s32[1024]{0:T(1024)}, s32[1024]{0:T(1024)S(1)}, u32[]{:S(2)}) copy-start(s32[1024]{0:T(1024)S(1)} %pad_clamp_fusion.1) | copy-start | bytes 12292
  30.3 15.3 %all-to-all-start.1 = ((bf16[8,1,64,512]{3,2,1,0:T(8,128)(2,1)}), bf16[8,1,64,512]{3,2,1,0:T(8,128)(2,1)}, u32[]{:S(2)}, u32[]{:S(2)}) async-start(bf16[8,1,64,512]{3,2,1,0:T(8,128)(2,1)} %copy.75), calls=%async_computation.1 | async-start | bytes 1048576 | tf_op jit(solution)/shard_map/all_to_all | solution.py:174
  35.2 14.2 %copy-start.17 = (f32[64]{0:T(128)}, f32[64]{0:T(128)S(1)}, u32[]{:S(2)}) copy-start(f32[64]{0:T(128)S(1)} %multiply_exponential_fusion) | copy-start | bytes 772
  45.6 52.6 %all-to-all-start = ((bf16[8,1,512,192]{2,3,1,0:T(8,128)(2,1)}), bf16[8,1,512,192]{2,3,1,0:T(8,128)(2,1)S(1)}, u32[]{:S(2)}, u32[]{:S(2)}) async-start(bf16[8,1,512,192]{2,3,1,0:T(8,128)(2,1)} %copy.72), calls=%async_computation | async-start | bytes 3145728 | tf_op jit(solution)/shard_map/all_to_all | solution.py:173
  49.2 424.3 %reduce-scatter.2.cloned.1.call-start = ((), (), s32[]{:S(2)}) async-start(), calls=%async_computation.7 | async-start | bytes 35651584 | tf_op jit(solution)/shard_map/reduce_scatter | solution.py:232
  49.3 49.7 %copy-start.15 = (pred[8]{0:T(512)(128)(4,1)}, pred[8]{0:T(512)(128)(4,1)S(1)}, u32[]{:S(2)}) copy-start(pred[8]{0:T(512)(128)(4,1)S(1)} %compare_and_fusion) | copy-start | bytes 28
  49.3 4.4 copy-start.8
  53.1 42.6 %collective-permute-start.1 = (bf16[8,64,128]{2,1,0:T(8,128)(2,1)S(1)}, bf16[8,64,128]{2,1,0:T(8,128)(2,1)S(1)}, u32[]{:S(2)}, u32[]{:S(2)}) collective-permute-start(bf16[8,64,128]{2,1,0:T(8,128)(2,1)S(1)} %broadcast_select_fusion), channel_id=1, source_target_pairs={{0,1},{1,0},{2,3},{3,2},{4,5},{5,4},{6,7},{7,6},{8,9},{9,8},{10,11... | collective-permute-start | bytes 393224 | tf_op jit(solution)/shard_map/ppermute | solution.py:22
  53.7 45.2 %copy-start.14 = (s32[1024]{0:T(1024)}, s32[1024]{0:T(1024)S(1)}, u32[]{:S(2)}) copy-start(s32[1024]{0:T(1024)S(1)} %pad_clamp_fusion) | copy-start | bytes 12292
  212.1 0.7 copy-start.9
  212.1 0.7 copy-start.18
  214.0 1.8 copy-start
  240.5 1.0 copy-start.4
  240.5 1.0 copy-start.5
  240.5 1.0 copy-start.10
  240.5 1.0 copy-start.12
  275.7 1.0 copy-start.1
  276.7 1.3 copy-start.7
  278.3 7.0 %copy-start.3 = (bf16[8,64,512]{2,1,0:T(8,128)(2,1)S(1)}, bf16[8,64,512]{2,1,0:T(8,128)(2,1)}, u32[]{:S(2)}) copy-start(bf16[8,64,512]{2,1,0:T(8,128)(2,1)} %param.24) | copy-start | bytes 1572868
  280.7 15.0 %all-to-all-start.3 = ((bf16[8,1,512,64]{2,3,1,0:T(8,128)(2,1)}), bf16[8,1,512,64]{2,3,1,0:T(8,128)(2,1)S(1)}, u32[]{:S(2)}, u32[]{:S(2)}) async-start(bf16[8,1,512,64]{2,3,1,0:T(8,128)(2,1)} %copy.88), calls=%async_computation.4 | async-start | bytes 1048576 | tf_op jit(solution)/shard_map/all_to_all | solution.py:176
  286.9 23.3 %copy-start.16 = (pred[8]{0:T(512)(128)(4,1)S(1)}, pred[8]{0:T(512)(128)(4,1)}, u32[]{:S(2)}) copy-start(pred[8]{0:T(512)(128)(4,1)} %copy-done.15) | copy-start | bytes 28
  295.7 13.8 %all-to-all-start.4 = ((bf16[8,1,64,512]{3,2,1,0:T(8,128)(2,1)}), bf16[8,1,64,512]{3,2,1,0:T(8,128)(2,1)S(1)}, u32[]{:S(2)}, u32[]{:S(2)}) async-start(bf16[8,1,64,512]{3,2,1,0:T(8,128)(2,1)} %copy.90), calls=%async_computation.5 | async-start | bytes 1048576 | tf_op jit(solution)/shard_map/all_to_all | solution.py:177
Sparse Core Ops, SparseCore 0:
  9.5 158.3 all-gather.1
  275.8 197.5 reduce-scatter.1
where the time goes:
time: 485 us; the launch traced here: 484 us
  blocking collectives  175 us (36%)
  waiting for transfers between devices  146 us (30%)
  matrix products  62.9 us (13%)
  local copies, waits for them, and re-layouts  43.8 us (9%)
  starting transfers between devices  24.1 us (5%)
  other arithmetic  16.9 us (3%)
  between operations  13.9 us (3%)
    psum x1, blocking collectives, on_device(): reduced_rows = lax.psum(partial_rank, 'tensor').astype(jnp.bfloat16)  96 us
    reduce_scatter x1, waiting for transfers between devices, on_device(): lax.psum_scatter(lax.dot_general(output_matrix, attended, (((0,), (1,)),...  82.2 us
    psum x1, blocking collectives, on_device(): head_rank_index = lax.psum(partial_head, 'tensor').astype(jnp.bfloat16)  78.8 us
    ppermute x2, waiting for transfers between devices, partner_2(): return lax.ppermute(block, axis, route)  42 us
    unnamed x54, local copies, waits for them, and re-layouts  19.2 us
    dot_general x1, matrix products, on_device(): lax.dot_general(output_matrix, attended, (((0,), (1,)), ((), ())), prefer...  17.8 us
    dot_general x1, matrix products, on_device(): jnp.dot(piece, query_matrix, preferred_element_type=jnp.float32)  15.8 us
    dot_general x1, matrix products, on_device(): kv_base = jnp.dot(piece, kv_cols_full, preferred_element_type=jnp.float32)  10.7 us
  transfers between devices with their start and end apart: 9, of which 5 were waited for; matrix products, arithmetic and copies ran while one was open for 10% of the time, Pallas kernels for 0%

commit v1 on v0

v1 whole, which is shorter than its diff:
```python
import math

import jax
import jax.numpy as jnp
from jax import lax
from jax.experimental import pallas as pl
from jax.experimental.pallas import tpu as pltpu
from jax.sharding import Mesh, PartitionSpec as P

HEAD = 128
BLOCK = 128
SIDE = 4
CORES = 2
ADAPTER_AXES = ("z", "c")
TENSOR_AXES = ("y", "x")
ROPE_BASE = 500000.0
VMEM = 56 * 1024 * 1024
bf16 = jnp.bfloat16
f32 = jnp.float32
i32 = jnp.int32


def params():
    return pltpu.CompilerParams(vmem_limit_bytes=VMEM)


def cost(flops, moved, exps=0):
    return pl.CostEstimate(flops=flops, bytes_accessed=moved, transcendentals=exps)


def shift(block, axis, step):
    return lax.ppermute(block, axis, [(i, (i + step) % SIDE) for i in range(SIDE)])


def ring_gather(block, axis):
    half = block.shape[1] // 2
    behind = shift(block, axis, 1)
    ahead = shift(block, axis, -1)
    far_low = shift(behind[:, :half], axis, 1)
    far_high = shift(ahead[:, half:], axis, -1)
    return block, behind, ahead, far_low, far_high


def ring_order(index):
    return [index, (index + SIDE - 1) % SIDE, (index + 1) % SIDE, (index + 2) % SIDE]


def pick_adapters(pick, down_qkv, up_q, up_kv, down_o, up_o):
    groups = pick.shape[0]
    depth, rank3 = down_qkv.shape[1:]
    rank, wide = up_q.shape[1:]
    narrow = up_kv.shape[2]

    def body(pick_ref, dq, uq, ukv, do, uo, down, up):
        down[0, :, :rank3] = dq[0]
        down[0, :, rank3:] = do[0]
        up[0, :, :wide] = uq[0]
        up[0, :, wide : 2 * wide] = uo[0]
        up[0, :, 2 * wide :] = ukv[0]

    def chosen(a):
        return pl.BlockSpec((1,) + a.shape[1:], lambda i, p: (p[i], 0, 0))

    down_shape = (groups, depth, rank3 + rank)
    up_shape = (groups, rank, 2 * wide + narrow)
    return pl.pallas_call(
        body,
        out_shape=(
            jax.ShapeDtypeStruct(down_shape, bf16),
            jax.ShapeDtypeStruct(up_shape, bf16),
        ),
        grid_spec=pltpu.PrefetchScalarGridSpec(
            num_scalar_prefetch=1,
            grid=(groups,),
            in_specs=[chosen(a) for a in (down_qkv, up_q, up_kv, down_o, up_o)],
            out_specs=[
                pl.BlockSpec((1,) + s[1:], lambda i, p: (i, 0, 0)) for s in (down_shape, up_shape)
            ],
        ),
        compiler_params=params(),
        cost_estimate=cost(0, 2 * 2 * (math.prod(down_shape) + math.prod(up_shape))),
    )(pick, down_qkv, up_q, up_kv, down_o, up_o)


def rank_partial(slot, x, down, rank3):
    tokens, depth = x.shape

    def body(slot_ref, x_ref, d_ref, out):
        out[...] = jnp.dot(x_ref[...], d_ref[0], preferred_element_type=f32)[:, :rank3]

    return pl.pallas_call(
        body,
        out_shape=jax.ShapeDtypeStruct((tokens, rank3), f32),
        grid_spec=pltpu.PrefetchScalarGridSpec(
            num_scalar_prefetch=1,
            grid=(tokens // BLOCK,),
            in_specs=[
                pl.BlockSpec((BLOCK, depth), lambda i, s: (i, 0)),
                pl.BlockSpec((1,) + down.shape[1:], lambda i, s: (s[i], 0, 0)),
            ],
            out_specs=pl.BlockSpec((BLOCK, rank3), lambda i, s: (i, 0)),
        ),
        compiler_params=params(),
        cost_estimate=cost(2 * tokens * depth * rank3, 2 * tokens * depth + 8 * tokens * rank3),
    )(slot, x, down)


def sum_over_tensor(partial):
    tokens, rank = partial.shape
    ways = SIDE * SIDE
    pieces = lax.all_to_all(
        partial.reshape(ways, tokens // ways, rank), TENSOR_AXES, 0, 0, tiled=True
    )
    mine = jnp.sum(pieces, axis=0).astype(bf16)
    copies = jnp.broadcast_to(mine[None], (ways,) + mine.shape)
    return lax.all_to_all(copies, TENSOR_AXES, 0, 0, tiled=True).reshape(tokens, rank)


def project(index, total, blocks, wq, wkv, rows=256):
    tokens = blocks[0].shape[0]
    wide, narrow = wq.shape[1], wkv.shape[1]
    tile = 256
    counts = [b.shape[1] // rows for b in blocks]
    pieces = sum(counts)
    first = total is None

    def body(index_ref, *refs):
        x_refs = refs[: len(blocks)]
        q_refs = refs[len(blocks) : len(blocks) + pieces]
        kv_refs = refs[len(blocks) + pieces : len(blocks) + 2 * pieces]
        rest = refs[len(blocks) + 2 * pieces :]
        q_out, kv_out = rest[-2:]
        q = kv = None
        at = 0
        for x_ref, n in zip(x_refs, counts):
            x = x_ref[...]
            wq_rows = jnp.concatenate([r[...] for r in q_refs[at : at + n]], axis=0)
            wkv_rows = jnp.concatenate([r[...] for r in kv_refs[at : at + n]], axis=0)
            q_add = jnp.dot(x, wq_rows, preferred_element_type=f32)
            kv_add = jnp.dot(x, wkv_rows, preferred_element_type=f32)
            q = q_add if q is None else q + q_add
            kv = kv_add if kv is None else kv + kv_add
            at += n
        if not first:
            q = q + rest[0][...]
            kv = kv + rest[1][...]
        q_out[...] = q
        kv_out[...] = kv

    def weight(k, width):
        return pl.BlockSpec((rows, width), lambda i, p, k=k: (p[k], 0))

    row_spec = [
        pl.BlockSpec((tile, wide), lambda i, p: (i, 0)),
        pl.BlockSpec((tile, narrow), lambda i, p: (i, 0)),
    ]
    in_specs = (
        [pl.BlockSpec((tile, b.shape[1]), lambda i, p: (i, 0)) for b in blocks]
        + [weight(k, wide) for k in range(pieces)]
        + [weight(k, narrow) for k in range(pieces)]
        + ([] if first else row_spec)
    )
    operands = list(blocks) + [wq] * pieces + [wkv] * pieces + ([] if first else list(total))
    aliases = {} if first else {len(operands) - 1: 0, len(operands): 1}
    depth = pieces * rows
    return pl.pallas_call(
        body,
        out_shape=(
            jax.ShapeDtypeStruct((tokens, wide), f32),
            jax.ShapeDtypeStruct((tokens, narrow), f32),
        ),
        grid_spec=pltpu.PrefetchScalarGridSpec(
            num_scalar_prefetch=1,
            grid=(tokens // tile,),
            in_specs=in_specs,
            out_specs=row_spec,
        ),
        input_output_aliases=aliases,
        compiler_params=params(),
        cost_estimate=cost(
            2 * tokens * depth * (wide + narrow),
            2 * depth * (tokens + wide + narrow) + 8 * tokens * (wide + narrow),
        ),
    )(index, *operands)


def finish_key_value(meta, kv, shrunk, up, cosine, sine, wide):
    tokens, narrow = kv.shape
    rank = shrunk.shape[1] // 3

    def body(meta_ref, kv_ref, s_ref, up_ref, c_ref, n_ref, out):
        is_key = meta_ref[3, 0] == 1
        s = s_ref[...].astype(f32)
        rank_in = jnp.where(is_key, s[:, rank : 2 * rank], s[:, 2 * rank :]).astype(bf16)
        u = kv_ref[...] + jnp.dot(rank_in, up_ref[0], preferred_element_type=f32)
        turned = u * c_ref[0] + pltpu.roll(u, HEAD // 2, 1) * n_ref[0]
        out[...] = jnp.where(is_key, turned, u).astype(bf16)

    table = pl.BlockSpec((1, BLOCK, HEAD), lambda i, m: (m[1, i], 0, 0))
    return pl.pallas_call(
        body,
        out_shape=jax.ShapeDtypeStruct((tokens, narrow), bf16),
        grid_spec=pltpu.PrefetchScalarGridSpec(
            num_scalar_prefetch=1,
            grid=(tokens // BLOCK,),
            in_specs=[
                pl.BlockSpec((BLOCK, narrow), lambda i, m: (i, 0)),
                pl.BlockSpec((BLOCK, 3 * rank), lambda i, m: (i, 0)),
                pl.BlockSpec((1, rank, narrow), lambda i, m: (m[0, i], 0, 2 * wide // narrow)),
                table,
                table,
            ],
            out_specs=pl.BlockSpec((BLOCK, narrow), lambda i, m: (i, 0)),
        ),
        compiler_params=params(),
        cost_estimate=cost(2 * tokens * rank * narrow, 6 * tokens * narrow + 6 * tokens * rank),
    )(meta, kv, shrunk, up, cosine, sine)


def attention(meta, q, shrunk, up, down, mine, other, cosine, sine):
    tokens, wide = q.shape
    rank = shrunk.shape[1] // 3
    heads = wide // HEAD
    window = min(3 * BLOCK, tokens)
    scale = 1.0 / math.sqrt(HEAD)

    def body(meta_ref, q_ref, s_ref, up_ref, d_ref, m_ref, o_ref, c_ref, n_ref, att, head):
        i = pl.program_id(0)
        is_key = meta_ref[3, 0] == 1
        first = meta_ref[2, i]
        limit = meta_ref[4, i]
        u = q_ref[...] + jnp.dot(
            s_ref[...][:, :rank], up_ref[0], preferred_element_type=f32
        )
        start = pl.multiple_of(jnp.maximum(i - 2, 0) * BLOCK, BLOCK)
        own = m_ref[pl.ds(start, window), :]
        far = o_ref[pl.ds(start, window), :]
        keys = jnp.where(is_key, own, far)
        values = jnp.where(is_key, far, own)
        row = i * BLOCK + lax.broadcasted_iota(i32, (BLOCK, window), 0)
        col = start + lax.broadcasted_iota(i32, (BLOCK, window), 1)
        allowed = (col >= first) & (col <= row) & (col < limit)
        for h in range(heads):
            at = slice(h * HEAD, (h + 1) * HEAD)
            part = u[:, at]
            turned = part * c_ref[0] + pltpu.roll(part, HEAD // 2, 1) * n_ref[0]
            scores = lax.dot_general(
                turned.astype(bf16), keys, (((1,), (1,)), ((), ())), preferred_element_type=f32
            )
            weights = jnp.where(allowed, jnp.exp(scores * scale), 0.0)
            weights = weights / jnp.sum(weights, axis=1, keepdims=True)
            mixed = jnp.dot(weights.astype(bf16), values, preferred_element_type=f32)
            att[:, at] = mixed.astype(bf16)
        head[...] = jnp.dot(att[...], d_ref[0], preferred_element_type=f32)[:, 3 * rank :]

    table = pl.BlockSpec((1, BLOCK, HEAD), lambda i, m: (m[1, i], 0, 0))
    whole = pl.BlockSpec((tokens, HEAD), lambda i, m: (0, 0))
    return pl.pallas_call(
        body,
        out_shape=(
            jax.ShapeDtypeStruct((tokens, wide), bf16),
            jax.ShapeDtypeStruct((tokens, rank), f32),
        ),
        grid_spec=pltpu.PrefetchScalarGridSpec(
            num_scalar_prefetch=1,
            grid=(tokens // BLOCK,),
            in_specs=[
                pl.BlockSpec((BLOCK, wide), lambda i, m: (i, 0)),
                pl.BlockSpec((BLOCK, 3 * rank), lambda i, m: (i, 0)),
                pl.BlockSpec((1, rank, wide), lambda i, m: (m[0, i], 0, 0)),
                pl.BlockSpec((1,) + down.shape[1:], lambda i, m: (m[0, i], 0, 0)),
                whole,
                whole,
                table,
                table,
            ],
            out_specs=[
                pl.BlockSpec((BLOCK, wide), lambda i, m: (i, 0)),
                pl.BlockSpec((BLOCK, rank), lambda i, m: (i, 0)),
            ],
        ),
        compiler_params=params(),
        cost_estimate=cost(
            4 * tokens * window * wide, 8 * tokens * wide, heads * tokens * window
        ),
    )(meta, q, shrunk, up, down, mine, other, cosine, sine)


def pick_columns(index, matrix, width):
    depth = matrix.shape[0]
    count = index.shape[0]

    def body(index_ref, m_ref, out):
        out[0] = m_ref[...]

    return pl.pallas_call(
        body,
        out_shape=jax.ShapeDtypeStruct((count, depth, width), bf16),
        grid_spec=pltpu.PrefetchScalarGridSpec(
            num_scalar_prefetch=1,
            grid=(count,),
            in_specs=[pl.BlockSpec((depth, width), lambda i, p: (0, p[i]))],
            out_specs=pl.BlockSpec((1, depth, width), lambda i, p: (i, 0, 0)),
        ),
        compiler_params=params(),
        cost_estimate=cost(0, 4 * count * depth * width),
    )(index, matrix)


def output_partial(index, pieces, weights, dtype):
    tokens = pieces[0].shape[0]
    shards, depth, width = weights.shape
    per = shards // SIDE
    unit = depth // SIDE

    def body(index_ref, *refs):
        x_refs, w_ref, out = refs[:-2], refs[-2], refs[-1]
        total = None
        for k, (x_ref, (place, offset)) in enumerate(zip(x_refs, places)):
            size = x_ref.shape[1]
            start = pl.multiple_of(index_ref[1 + place] * unit + offset, 128)
            rows = w_ref[0, pl.ds(start, size), :]
            add = jnp.dot(x_ref[...], rows, preferred_element_type=f32)
            total = add if total is None else total + add
        out[...] = total.astype(dtype)

    places = [(0, 0), (1, 0), (2, 0), (3, 0), (3, unit // 2)]
    return pl.pallas_call(
        body,
        out_shape=jax.ShapeDtypeStruct((tokens, per * width), dtype),
        grid_spec=pltpu.PrefetchScalarGridSpec(
            num_scalar_prefetch=1,
            grid=(per,),
            in_specs=[pl.BlockSpec(p.shape, lambda j, d: (0, 0)) for p in pieces]
            + [pl.BlockSpec((1, depth, width), lambda j, d: (d[0] * per + j, 0, 0))],
            out_specs=pl.BlockSpec((tokens, width), lambda j, d: (0, j)),
        ),
        compiler_params=params(),
        cost_estimate=cost(
            2 * tokens * depth * per * width, 2 * depth * (tokens + per * width)
        ),
    )(index, *pieces, weights)


def finish(meta, parts_a, parts_b, head_rank, up, wide):
    half, width = parts_a[0].shape
    tokens = 2 * half
    steps = half // BLOCK
    rank = head_rank.shape[1]
    count = len(parts_a)

    def body(meta_ref, *refs):
        a_refs, b_refs = refs[:count], refs[count : 2 * count]
        h_ref, up_ref, out = refs[2 * count :]
        i = pl.program_id(0)
        extra = jnp.dot(h_ref[...], up_ref[0], preferred_element_type=f32)
        row = i * BLOCK + lax.broadcasted_iota(i32, (BLOCK, width), 0)
        valid = row < meta_ref[4, i]

        def put(group):
            total = extra
            for ref in group:
                total = total + ref[...].astype(f32)
            out[...] = jnp.where(valid, total, 0.0)

        @pl.when(i < steps)
        def _():
            put(a_refs)

        @pl.when(i >= steps)
        def _():
            put(b_refs)

    spec_a = pl.BlockSpec((BLOCK, width), lambda i, m: (jnp.minimum(i, steps - 1), 0))
    spec_b = pl.BlockSpec((BLOCK, width), lambda i, m: (jnp.maximum(i - steps, 0), 0))
    return pl.pallas_call(
        body,
        out_shape=jax.ShapeDtypeStruct((tokens, width), f32),
        grid_spec=pltpu.PrefetchScalarGridSpec(
            num_scalar_prefetch=1,
            grid=(2 * steps,),
            in_specs=[spec_a] * count
            + [spec_b] * count
            + [
                pl.BlockSpec((BLOCK, rank), lambda i, m: (i, 0)),
                pl.BlockSpec((1, rank, wide), lambda i, m: (m[0, i], 0, 1)),
            ],
            out_specs=pl.BlockSpec((BLOCK, width), lambda i, m: (i, 0)),
        ),
        compiler_params=params(),
        cost_estimate=cost(2 * tokens * rank * width, 14 * tokens * width),
    )(meta, *parts_a, *parts_b, head_rank, up)


def output_ring(pieces, weights, axis, places):
    me, behind, ahead, far = ring_order(lax.axis_index(axis))

    def partial(dest, dtype=bf16):
        return output_partial(jnp.stack([dest] + places).astype(i32), pieces, weights, dtype)

    away = partial(far)
    half = away.shape[1] // 2
    via_ahead = shift(away[:, :half], axis, 1)
    via_behind = shift(away[:, half:], axis, -1)
    to_ahead = partial(ahead)
    to_behind = partial(behind)
    mine = partial(me, f32)
    to_ahead = jnp.concatenate([to_ahead[:, :half] + via_ahead, to_ahead[:, half:]], axis=1)
    to_behind = jnp.concatenate([to_behind[:, :half], to_behind[:, half:] + via_behind], axis=1)
    return mine, shift(to_ahead, axis, 1), shift(to_behind, axis, -1)


def on_device(x, wq, wkv, wo, down_qkv, up_q, up_kv, down_o, up_o, choice, counts, tails):
    z, c, y, xi = (lax.axis_index(n) for n in ADAPTER_AXES + TENSOR_AXES)
    group = z * CORES + c
    tokens, local = x.shape
    holders = down_qkv.shape[0]
    requests = choice.shape[1]
    wide = wq.shape[1]
    rank = up_q.shape[1]
    blocks = tokens // BLOCK

    owners = choice // holders
    pick = jnp.sum(jnp.where(owners == group, choice % holders, 0), axis=1).astype(i32)
    own_owner = lax.dynamic_index_in_dim(owners, group, 0, keepdims=False)
    req = jnp.arange(requests, dtype=i32)
    starts = jnp.sum(jnp.where(req[None, :] < req[:, None], counts[0][None, :], 0), axis=1)
    block = jnp.arange(blocks, dtype=i32)
    of_block = (starts[None, :] <= block[:, None]) & (
        block[:, None] < (starts + counts[0])[None, :]
    )

    def lookup(values):
        return jnp.sum(jnp.where(of_block, values[None, :], 0), axis=1).astype(i32)

    slot = lookup(own_owner)
    first = lookup(starts)
    limit = (first + lookup(counts[0]) - 1) * BLOCK + lookup(tails[0])
    is_key = jnp.broadcast_to(1 - xi % 2, (blocks,)).astype(i32)
    meta = jnp.stack([slot, block - first, first * BLOCK, is_key, limit]).astype(i32)

    freq = jnp.exp(-(2.0 * jnp.arange(HEAD // 2, dtype=f32) / HEAD) * math.log(ROPE_BASE))
    angle = jnp.arange(3 * BLOCK, dtype=f32)[:, None] * freq[None, :]
    cosine = jnp.tile(jnp.cos(angle), (1, 2)).reshape(3, BLOCK, HEAD)
    sine = jnp.concatenate([-jnp.sin(angle), jnp.sin(angle)], axis=1).reshape(3, BLOCK, HEAD)

    half = local // 2
    ys, xs = ring_order(y), ring_order(xi)
    flat_a = jnp.concatenate(ring_gather(x[:, :half], "x"), axis=1)
    flat_b = jnp.concatenate(ring_gather(x[:, half:], "y"), axis=1)

    def rows_a(k, cols):
        return [(ys[k] * SIDE + xs[j]) * 2 for j in cols]

    def rows_b(k, cols):
        return [(ys[j] * SIDE + xs[k]) * 2 + 1 for j in cols]

    def index_of(rows):
        return jnp.stack(rows).astype(i32)

    every = range(SIDE)
    a0, a1, a2, a3, a4 = ring_gather(flat_a, "y")
    b0, b1, b2, b3, b4 = ring_gather(flat_b, "x")

    down_out, up_out = pick_adapters(pick, down_qkv, up_q, up_kv, down_o, up_o)
    down = lax.all_to_all(down_out, ADAPTER_AXES, 0, 0, tiled=True)
    up = lax.all_to_all(up_out, ADAPTER_AXES, 0, 0, tiled=True)
    shrunk = sum_over_tensor(rank_partial(slot, x, down, 3 * rank))

    unit = wo.shape[1] // (SIDE * SIDE * 2)
    four = jnp.arange(SIDE, dtype=i32)
    wo, _ = lax.optimization_barrier((wo, down))
    send_a = pick_columns(four * (2 * SIDE) + group, wo, unit)
    send_b = pick_columns((group // 2) * (2 * SIDE) + four * 2 + group % 2, wo, unit)
    got_a = lax.all_to_all(send_a, "y", 0, 0, tiled=True).reshape(-1, unit)
    got_b = lax.all_to_all(send_b, "x", 0, 0, tiled=True).reshape(-1, unit)
    wo_a = lax.all_gather(got_a, ADAPTER_AXES, axis=0)
    wo_b = lax.all_gather(got_b, ADAPTER_AXES, axis=0)

    total = project(index_of(rows_a(0, every) + rows_b(0, every)), None, [a0, b0], wq, wkv)
    total = project(
        index_of(rows_a(1, every) + rows_a(2, every) + rows_b(1, every) + rows_b(2, every)),
        total,
        [a1, a2, b1, b2],
        wq,
        wkv,
    )
    q, kv = project(
        index_of(rows_a(3, every) + rows_b(3, every)), total, [a3, a4, b3, b4], wq, wkv
    )

    mine = finish_key_value(meta, kv, shrunk, up, cosine, sine, wide)
    other = lax.ppermute(mine, "x", [(i, i ^ 1) for i in range(SIDE)])
    attended, head_partial = attention(meta, q, shrunk, up, down, mine, other, cosine, sine)

    cut = tokens // 2
    pieces_a = ring_gather(attended[:cut], "y")
    pieces_b = ring_gather(attended[cut:], "x")
    head_rank = sum_over_tensor(head_partial)
    parts_a = output_ring(pieces_a, wo_a, "x", ys)
    parts_b = output_ring(pieces_b, wo_b, "y", xs)
    return finish(meta, parts_a, parts_b, head_rank, up, wide)


def solution(mesh):
    fine = Mesh(mesh.devices.reshape(SIDE, CORES, SIDE, SIDE), ADAPTER_AXES + TENSOR_AXES)
    placed = (
        P(ADAPTER_AXES, TENSOR_AXES),
        P(None, TENSOR_AXES),
        P(None, TENSOR_AXES),
        P(TENSOR_AXES, None),
        P(ADAPTER_AXES, TENSOR_AXES, None),
        P(ADAPTER_AXES, None, TENSOR_AXES),
        P(ADAPTER_AXES, None, TENSOR_AXES),
        P(ADAPTER_AXES, TENSOR_AXES, None),
        P(ADAPTER_AXES, None, TENSOR_AXES),
        P(),
        P(ADAPTER_AXES, None),
        P(ADAPTER_AXES, None),
    )
    return jax.shard_map(
        on_device,
        mesh=fine,
        in_specs=placed,
        out_specs=P(ADAPTER_AXES, TENSOR_AXES),
        check_vma=False,
    )
```

time: 485 us -> 406 us (0.84)
  blocking collectives: 175 us -> 38.1 us
  Pallas kernels: 0 us -> 121 us
  matrix products: 62.9 us -> 0 us
  starting transfers between devices: 24.1 us -> 80 us
  waiting for transfers between devices: 146 us -> 92.2 us
  other arithmetic: 16.9 us -> 10.1 us
    psum x2 -> x0, blocking collectives: 175 us -> none  [the longest x1 96 us: on_device(): reduced_rows = lax.psum(partial_rank, 'tensor').astype(jnp.bfloat16)]
    pallas_call x0 -> x18, Pallas kernels: none -> 121 us  [the longest x8 37.8 us: output_partial(): pl.pallas_call(body, out_shape=jax.ShapeDtypeStruct((tokens, per * width)...]
    reduce_scatter x1 -> x0, waiting for transfers between devices: 82.2 us -> none  [on_device(): lax.psum_scatter(lax.dot_general(output_matrix, attended, (((0,), (1,)),...]
    dot_general x18 -> x0, matrix products: 62.9 us -> none  [the longest x1 17.8 us: on_device(): lax.dot_general(output_matrix, attended, (((0,), (1,)), ((), ())), prefer...]
    all_to_all x5 -> x6, waiting for transfers between devices: 20.9 us -> 73.3 us  [the longest x2 40 us: sum_over_tensor(): lax.all_to_all(partial.reshape(ways, tokens // ways, rank), TENSOR_AXES,...]
    ppermute x2 -> x33, starting transfers between devices: 2.11 us -> 52.1 us  [the longest x32 50.4 us: shift(): lax.ppermute(block, axis, [(i, (i + step) % SIDE) for i in range(SIDE)])]
    all_to_all x0 -> x2, blocking collectives: none -> 38.1 us  [the longest x1 19.5 us: on_device(): got_b = lax.all_to_all(send_b, 'x', 0, 0, tiled=True).reshape(-1, unit)]
    ppermute x2 -> x33, waiting for transfers between devices: 42 us -> 18.9 us  [the longest x32 12.9 us: shift(): lax.ppermute(block, axis, [(i, (i + step) % SIDE) for i in range(SIDE)])]
  transfers between devices with their start and end apart: 9 -> 41, of which waited for: 5 -> 7; matrix products, arithmetic and copies ran while one was open for 10% -> 12% of each run, Pallas kernels for 0% -> 25%
where the time goes in v1:
time: 406 us; the launch traced here: 404 us
  Pallas kernels  121 us (30%)
  waiting for transfers between devices  92.2 us (23%)
  starting transfers between devices  80 us (20%)
  local copies, waits for them, and re-layouts  48.3 us (12%)
  blocking collectives  38.1 us (9%)
  between operations  14 us (3%)
  other arithmetic  10.1 us (2%)
    ppermute x32, starting transfers between devices, shift(): lax.ppermute(block, axis, [(i, (i + step) % SIDE) for i in range(SIDE)])  50.4 us
    all_to_all x2, waiting for transfers between devices, sum_over_tensor(): lax.all_to_all(partial.reshape(ways, tokens // ways, rank), TENSOR_AXES,...  40 us
    pallas_call x8, Pallas kernels, output_partial(): pl.pallas_call(body, out_shape=jax.ShapeDtypeStruct((tokens, per * width)...  37.8 us
    pallas_call x3, Pallas kernels, project(): pl.pallas_call(body, out_shape=(jax.ShapeDtypeStruct((tokens, wide), f32)...  29.7 us
    all_to_all x1, waiting for transfers between devices, on_device(): down = lax.all_to_all(down_out, ADAPTER_AXES, 0, 0, tiled=True)  26.6 us
    all_to_all x1, blocking collectives, on_device(): got_b = lax.all_to_all(send_b, 'x', 0, 0, tiled=True).reshape(-1, unit)  19.5 us
    unnamed x70, local copies, waits for them, and re-layouts  19.2 us
    all_to_all x1, blocking collectives, on_device(): got_a = lax.all_to_all(send_a, 'y', 0, 0, tiled=True).reshape(-1, unit)  18.6 us
  transfers between devices with their start and end apart: 41, of which 7 were waited for; matrix products, arithmetic and copies ran while one was open for 12% of the time, Pallas kernels for 25%

profile of v1, /device:TPU:0, one launch (start us, length us, event | category | flops | bytes accessed | tf_op | source)
XLA Modules:
  0.0 403.8 jit_solution(4606607944619637971)
XLA Ops:
  6.5 3.8 copy.27.dq
  12.2 6.9 %shard_map.121 = (bf16[8,512,256]{2,1,0:T(8,128)(2,1)}, bf16[8,64,1152]{2,1,0:T(8,128)(2,1)}) custom-call(s32[8]{0:T(128)} %get-tuple-element.31.pick_ref, bf16[8,512,192]{2,1,0:T(8,128)(2,1)} %copy.27.dq, bf16[8,64,512]{2,1,0:T(8,128)(2,1)} %uq.1, bf16[8,64,128]{2,1,0:T(8,128)(2,1)} %ukv.1, bf16[8,512,64]{2,1,0:T(8,128)(2,1)} %copy.28.do, ...), custom_call_target="tpu_custom_call" | custom-call | bytes 6553600 | tf_op jit(solution)/shard_map/pallas_call | solution.py:66
  19.1 5.4 %all-to-all-start = ((bf16[8,512,256]{2,1,0:T(8,128)(2,1)}), bf16[8,512,256]{2,1,0:T(8,128)(2,1)S(1)}, u32[]{:S(2)}, u32[]{:S(2)}) async-start(bf16[8,512,256]{2,1,0:T(8,128)(2,1)} %get-tuple-element.21), calls=%async_computation | async-start | bytes 4194304 | tf_op jit(solution)/shard_map/all_to_all | solution.py:466
  25.1 26.6 %all-to-all-done.d_ref = bf16[8,512,256]{2,1,0:T(8,128)(2,1)S(1)} async-done(((bf16[8,512,256]{2,1,0:T(8,128)(2,1)}), bf16[8,512,256]{2,1,0:T(8,128)(2,1)S(1)}, u32[]{:S(2)}, u32[]{:S(2)}) %all-to-all-start) | async-done | bytes 2097184 | tf_op jit(solution)/shard_map/all_to_all | solution.py:466
  51.7 4.1 %shard_map.130 = bf16[4,512,256]{2,1,0:T(8,128)(2,1)} custom-call(s32[4]{0:T(128)} %add_add_fusion.index_ref, bf16[512,8192]{1,0:T(8,128)(2,1)} %m_ref.1), custom_call_target="tpu_custom_call" | custom-call | bytes 2097152 | tf_op jit(solution)/shard_map/pallas_call | solution.py:296
  55.8 19.5 %all_to_all.40 = bf16[4,512,256]{2,1,0:T(8,128)(2,1)} all-to-all(bf16[4,512,256]{2,1,0:T(8,128)(2,1)} %shard_map.130), channel_id=1, replica_groups=mesh['z'=4,'c'=2,'y'=4,'x'=4] {'x'}, dimensions={0} | all-to-all | bytes 2097152 | tf_op jit(solution)/shard_map/all_to_all | solution.py:476
  75.9 4.0 shard_map.125
  79.9 18.6 %all_to_all.41 = bf16[4,512,256]{2,1,0:T(8,128)(2,1)} all-to-all(bf16[4,512,256]{2,1,0:T(8,128)(2,1)} %shard_map.125), channel_id=1, replica_groups=mesh['z'=4,'c'=2,'y'=4,'x'=4] {'y'}, dimensions={0} | all-to-all | bytes 2097152 | tf_op jit(solution)/shard_map/all_to_all | solution.py:475
  106.1 5.7 %collective-permute-done.8 = bf16[1024,256]{1,0:T(8,128)(2,1)S(1)} collective-permute-done((bf16[1024,256]{1,0:T(8,128)(2,1)S(1)}, bf16[1024,256]{1,0:T(8,128)(2,1)S(1)}, u32[]{:S(2)}, u32[]{:S(2)}) %collective-permute-start.8) | collective-permute-done | bytes 524320 | tf_op jit(solution)/shard_map/ppermute | solution.py:32
  132.5 7.0 %shard_map.122 = f32[1024,192]{1,0:T(8,128)} custom-call(s32[8]{0:T(128)} %get-tuple-element.30.slot_ref, bf16[1024,512]{1,0:T(8,128)(2,1)} %x_ref.1, bf16[8,512,256]{2,1,0:T(8,128)(2,1)} %copy-done), custom_call_target="tpu_custom_call" | custom-call | flops 201326592 | bytes 2621440 | tf_op jit(solution)/shard_map/pallas_call | solution.py:91
  139.5 3.7 all-to-all-start.1
  143.2 40.0 %all-to-all-done.1 = f32[16,64,192]{2,1,0:T(8,128)S(1)} async-done(((f32[16,64,192]{2,1,0:T(8,128)}), f32[16,64,192]{2,1,0:T(8,128)S(1)}, u32[]{:S(2)}, u32[]{:S(2)}) %all-to-all-start.1) | async-done | bytes 786464 | tf_op jit(solution)/shard_map/all_to_all | solution.py:111
  210.1 8.0 %shard_map.118 = (f32[1024,512]{1,0:T(8,128)}, f32[1024,128]{1,0:T(8,128)}) custom-call(s32[8]{0:T(128)} %stack.236.index_ref, bf16[1024,1024]{1,0:T(8,128)(2,1)} %constant_dynamic-update-slice_fusion.refs_0_, bf16[1024,1024]{1,0:T(8,128)(2,1)} %constant_dynamic-update-slice_fusion.5.refs_1_, bf16[8192,512]{1,0:T(8,128)(2,1)} %refs_11_.5, ...), custom_call_target="tpu_custom_call" | custom-call | flops 2684354560 | bytes 12058624 | tf_op jit(solution)/shard_map/pallas_call | solution.py:166
  219.1 3.8 all-to-all-start.2
  222.8 13.1 %shard_map.119 = (f32[1024,512]{1,0:T(8,128)}, f32[1024,128]{1,0:T(8,128)}) custom-call(s32[16]{0:T(128)} %stack.227.index_ref, bf16[1024,1024]{1,0:T(8,128)(2,1)} %collective-permute-done.4.refs_0_, bf16[1024,1024]{1,0:T(8,128)(2,1)} %collective-permute-done.6.refs_1_, ...), custom_call_target="tpu_custom_call", output_to_operand_aliasing={{0}: (37, {}), {1}: (38, {})} | custom-call | flops 5368709120 | bytes 18874368 | tf_op jit(solution)/shard_map/pallas_call | solution.py:166
  237.0 8.6 %shard_map.120 = (f32[1024,512]{1,0:T(8,128)}, f32[1024,128]{1,0:T(8,128)}) custom-call(s32[8]{0:T(128)} %stack.210.index_ref, bf16[1024,512]{1,0:T(8,128)(2,1)} %copy-done.18, bf16[1024,512]{1,0:T(8,128)(2,1)} %collective-permute-done.7.refs_1_, bf16[1024,512]{1,0:T(8,128)(2,1)} %collective-permute-done.13.refs_2_, ...), custom_call_target="tpu_custom_call", output_to_operand_aliasing={{0}: (21, {}), {1}: (22, {})} | custom-call | flops 2684354560 | bytes 12058624 | tf_op jit(solution)/shard_map/pallas_call | solution.py:166
  246.4 7.2 %shard_map.123.m_ref = bf16[1024,128]{1,0:T(8,128)(2,1)} custom-call(s32[5,8]{1,0:T(8,128)} %stack.195.meta_ref, f32[1024,128]{1,0:T(8,128)} %get-tuple-element.23.kv_ref, bf16[1024,192]{1,0:T(8,128)(2,1)} %bitcast.71, bf16[8,64,1152]{2,1,0:T(8,128)(2,1)} %copy-done.1, f32[3,128,128]{2,1,0:T(8,128)} %copy.29.c_ref, f32[3,128,128]{2,1,0:T(8,128)} %pad_maximum_fusion.4.n_ref), custom_call_target="tpu_custom_call" | custom-call | flops 16777216 | bytes 1179648 | tf_op jit(solution)/shard_map/pallas_call | solution.py:200
  255.4 6.0 %collective-permute-done.16.o_ref = bf16[1024,128]{1,0:T(8,128)(2,1)S(1)} collective-permute-done((bf16[1024,128]{1,0:T(8,128)(2,1)}, bf16[1024,128]{1,0:T(8,128)(2,1)S(1)}, u32[]{:S(2)}, u32[]{:S(2)}) %collective-permute-start.16) | collective-permute-done | bytes 262176 | tf_op jit(solution)/shard_map/ppermute | solution.py:493
  262.1 16.5 %shard_map.124 = (bf16[1024,512]{1,0:T(8,128)(2,1)}, f32[1024,64]{1,0:T(8,128)}) custom-call(s32[5,8]{1,0:T(8,128)} %stack.195.meta_ref, f32[1024,512]{1,0:T(8,128)} %get-tuple-element.20.q_ref, bf16[1024,192]{1,0:T(8,128)(2,1)} %bitcast.72, bf16[8,64,1152]{2,1,0:T(8,128)(2,1)} %copy-done.1, bf16[8,512,256]{2,1,0:T(8,128)(2,1)} %copy-done, ...), custom_call_target="tpu_custom_call" | custom-call | flops 805306368 | bytes 4194304 | tf_op jit(solution)/shard_map/pallas_call | solution.py:258
  286.4 6.9 %collective-permute-done.25.refs_1_ = bf16[512,512]{1,0:T(8,128)(2,1)S(1)} collective-permute-done((bf16[512,512]{1,0:T(8,128)(2,1)S(1)}, bf16[512,512]{1,0:T(8,128)(2,1)S(1)}, u32[]{:S(2)}, u32[]{:S(2)}) %collective-permute-start.25) | collective-permute-done | bytes 524320 | tf_op jit(solution)/shard_map/ppermute | solution.py:32
  304.0 4.2 %all-to-all-start.6 = ((f32[16,1,4096]{2,1,0:T(1,128)}), f32[16,1,4096]{2,1,0:T(1,128)}, u32[]{:S(2)}, u32[]{:S(2)}) async-start(f32[16,1,4096]{2,1,0:T(1,128)} %reshape.123), calls=%async_computation.6 | async-start | bytes 524288 | tf_op jit(solution)/shard_map/all_to_all | solution.py:111
  313.7 4.7 %shard_map.133 = bf16[512,512]{1,0:T(8,128)(2,1)} custom-call(s32[5]{0:T(128)} %stack.245.index_ref, bf16[512,512]{1,0:T(8,128)(2,1)} %copy-done.3, bf16[512,512]{1,0:T(8,128)(2,1)} %copy-done.4, bf16[512,512]{1,0:T(8,128)(2,1)} %copy-done.6, bf16[512,256]{1,0:T(8,128)(2,1)} %copy-done.11, bf16[512,256]{1,0:T(8,128)(2,1)} %collective-permute-done.28.refs_4_, ...), custom_call_target="tpu_custom_call" | custom-call | flops 1073741824 | bytes 4194304 | tf_op jit(solution)/shard_map/pallas_call | solution.py:328
  321.5 4.7 %shard_map.128 = bf16[512,512]{1,0:T(8,128)(2,1)} custom-call(s32[5]{0:T(128)} %stack.240.index_ref, bf16[512,512]{1,0:T(8,128)(2,1)} %copy-done.2, bf16[512,512]{1,0:T(8,128)(2,1)} %copy-done.5, bf16[512,512]{1,0:T(8,128)(2,1)} %copy-done.7, bf16[512,256]{1,0:T(8,128)(2,1)} %collective-permute-done.19.refs_3_, ...), custom_call_target="tpu_custom_call" | custom-call | flops 1073741824 | bytes 4194304 | tf_op jit(solution)/shard_map/pallas_call | solution.py:328
  330.4 4.7 %shard_map.134 = bf16[512,512]{1,0:T(8,128)(2,1)} custom-call(s32[5]{0:T(128)} %stack.246.index_ref, bf16[512,512]{1,0:T(8,128)(2,1)} %copy-done.3, bf16[512,512]{1,0:T(8,128)(2,1)} %copy-done.4, bf16[512,512]{1,0:T(8,128)(2,1)} %copy-done.6, bf16[512,256]{1,0:T(8,128)(2,1)} %copy-done.11, bf16[512,256]{1,0:T(8,128)(2,1)} %collective-permute-done.28.refs_4_, ...), custom_call_target="tpu_custom_call" | custom-call | flops 1073741824 | bytes 4194304 | tf_op jit(solution)/shard_map/pallas_call | solution.py:328
  335.1 4.7 %shard_map.132 = bf16[512,512]{1,0:T(8,128)(2,1)} custom-call(s32[5]{0:T(128)} %stack.244.index_ref, bf16[512,512]{1,0:T(8,128)(2,1)} %copy-done.3, bf16[512,512]{1,0:T(8,128)(2,1)} %copy-done.4, bf16[512,512]{1,0:T(8,128)(2,1)} %copy-done.6, bf16[512,256]{1,0:T(8,128)(2,1)} %copy-done.11, bf16[512,256]{1,0:T(8,128)(2,1)} %collective-permute-done.28.refs_4_, ...), custom_call_target="tpu_custom_call" | custom-call | flops 1073741824 | bytes 4194304 | tf_op jit(solution)/shard_map/pallas_call | solution.py:328
  339.8 4.7 %shard_map.129 = bf16[512,512]{1,0:T(8,128)(2,1)} custom-call(s32[5]{0:T(128)} %stack.242.index_ref, bf16[512,512]{1,0:T(8,128)(2,1)} %copy-done.2, bf16[512,512]{1,0:T(8,128)(2,1)} %copy-done.5, bf16[512,512]{1,0:T(8,128)(2,1)} %copy-done.7, bf16[512,256]{1,0:T(8,128)(2,1)} %collective-permute-done.19.refs_3_, ...), custom_call_target="tpu_custom_call" | custom-call | flops 1073741824 | bytes 4194304 | tf_op jit(solution)/shard_map/pallas_call | solution.py:328
  344.5 4.8 %shard_map.127 = bf16[512,512]{1,0:T(8,128)(2,1)} custom-call(s32[5]{0:T(128)} %stack.238.index_ref, bf16[512,512]{1,0:T(8,128)(2,1)} %copy-done.2, bf16[512,512]{1,0:T(8,128)(2,1)} %copy-done.5, bf16[512,512]{1,0:T(8,128)(2,1)} %copy-done.7, bf16[512,256]{1,0:T(8,128)(2,1)} %collective-permute-done.19.refs_3_, ...), custom_call_target="tpu_custom_call" | custom-call | flops 1073741824 | bytes 4194304 | tf_op jit(solution)/shard_map/pallas_call | solution.py:328
  362.2 7.3 %all-to-all-start.7 = ((bf16[16,2,2048]{2,1,0:T(2,128)(2,1)}), bf16[16,2,2048]{2,1,0:T(2,128)(2,1)S(1)}, u32[]{:S(2)}, u32[]{:S(2)}) async-start(bf16[16,2,2048]{2,1,0:T(2,128)(2,1)} %reshape.125), calls=%async_computation.7 | async-start | bytes 262144 | tf_op jit(solution)/shard_map/all_to_all | solution.py:116
  370.7 6.7 %all-to-all-done.7 = bf16[16,2,2048]{2,1,0:T(2,128)(2,1)S(1)} async-done(((bf16[16,2,2048]{2,1,0:T(2,128)(2,1)}), bf16[16,2,2048]{2,1,0:T(2,128)(2,1)S(1)}, u32[]{:S(2)}, u32[]{:S(2)}) %all-to-all-start.7) | async-done | bytes 131104 | tf_op jit(solution)/shard_map/all_to_all | solution.py:116
  378.3 4.8 %shard_map.131.refs_3_ = f32[512,512]{1,0:T(8,128)} custom-call(s32[5]{0:T(128)} %stack.243.index_ref, bf16[512,512]{1,0:T(8,128)(2,1)} %copy-done.3, bf16[512,512]{1,0:T(8,128)(2,1)} %copy-done.4, bf16[512,512]{1,0:T(8,128)(2,1)} %copy-done.6, bf16[512,256]{1,0:T(8,128)(2,1)} %copy-done.11, bf16[512,256]{1,0:T(8,128)(2,1)} %collective-permute-done.28.refs_4_, ...), custom_call_target="tpu_custom_call" | custom-call | flops 1073741824 | bytes 4194304 | tf_op jit(solution)/shard_map/pallas_call | solution.py:328
  383.2 4.8 %shard_map.126.refs_0_ = f32[512,512]{1,0:T(8,128)} custom-call(s32[5]{0:T(128)} %stack.201.index_ref, bf16[512,512]{1,0:T(8,128)(2,1)} %copy-done.2, bf16[512,512]{1,0:T(8,128)(2,1)} %copy-done.5, bf16[512,512]{1,0:T(8,128)(2,1)} %copy-done.7, bf16[512,256]{1,0:T(8,128)(2,1)} %collective-permute-done.19.refs_3_, ...), custom_call_target="tpu_custom_call" | custom-call | flops 1073741824 | bytes 4194304 | tf_op jit(solution)/shard_map/pallas_call | solution.py:328
  389.2 7.7 %shard_map.135 = f32[1024,512]{1,0:T(8,128)} custom-call(s32[5,8]{1,0:T(8,128)} %stack.195.meta_ref, f32[512,512]{1,0:T(8,128)} %shard_map.126.refs_0_, bf16[512,512]{1,0:T(8,128)(2,1)} %copy-done.23, bf16[512,512]{1,0:T(8,128)(2,1)} %copy-done.22, f32[512,512]{1,0:T(8,128)} %shard_map.131.refs_3_, bf16[512,512]{1,0:T(8,128)(2,1)} %copy-done.21, ...), custom_call_target="tpu_custom_call" | custom-call | flops 67108864 | bytes 7340032 | tf_op jit(solution)/shard_map/pallas_call | solution.py:376
  (203 shorter events, 110.8 us)
Async XLA Ops:
  19.1 32.6 %all-to-all-start = ((bf16[8,512,256]{2,1,0:T(8,128)(2,1)}), bf16[8,512,256]{2,1,0:T(8,128)(2,1)S(1)}, u32[]{:S(2)}, u32[]{:S(2)}) async-start(bf16[8,512,256]{2,1,0:T(8,128)(2,1)} %get-tuple-element.21), calls=%async_computation | async-start | bytes 4194304 | tf_op jit(solution)/shard_map/all_to_all | solution.py:466
  24.5 288.5 %all-gather.5.cloned.1.call-start = ((), (), s32[]{:S(2)}) async-start(), calls=%async_computation.9 | async-start | bytes 9437184 | tf_op jit(solution)/shard_map/all_gather | solution.py:478
  75.3 246.2 %all-gather.3.cloned.1.call-start = ((), (), s32[]{:S(2)}) async-start(), calls=%async_computation.8 | async-start | bytes 9437184 | tf_op jit(solution)/shard_map/all_gather | solution.py:477
  103.4 12.5 %collective-permute-start.1 = (bf16[1024,256]{1,0:T(8,128)(2,1)S(1)}, bf16[1024,256]{1,0:T(8,128)(2,1)S(1)}, u32[]{:S(2)}, u32[]{:S(2)}) collective-permute-start(bf16[1024,256]{1,0:T(8,128)(2,1)S(1)} %get-tuple-element.38), channel_id=1, source_target_pairs={{0,3},{1,0},{2,1},{3,2},{4,7},{5,4},{6,5},{7,6},{8,11},{9,8},{10,9... | collective-permute-start | bytes 1572872 | tf_op jit(solution)/shard_map/ppermute | solution.py:32
  123.6 70.3 %collective-permute-start.12 = (bf16[1024,1024]{1,0:T(8,128)(2,1)}, bf16[1024,1024]{1,0:T(8,128)(2,1)S(1)}, u32[]{:S(2)}, u32[]{:S(2)}) collective-permute-start(bf16[1024,1024]{1,0:T(8,128)(2,1)} %constant_dynamic-update-slice_fusion.5.refs_1_), channel_id=1, source_target_pairs={{0,1},{1,2},{2,3},{3,0},{4,5},{5,6},{6,7},{7,4},{8,9},{9,10},{10,1... | collective-permute-start | bytes 6291464 | tf_op jit(solution)/shard_map/ppermute | solution.py:32
  123.6 71.6 %collective-permute-start.14 = (bf16[1024,1024]{1,0:T(8,128)(2,1)}, bf16[1024,1024]{1,0:T(8,128)(2,1)}, u32[]{:S(2)}, u32[]{:S(2)}) collective-permute-start(bf16[1024,1024]{1,0:T(8,128)(2,1)} %constant_dynamic-update-slice_fusion.5.refs_1_), channel_id=1, source_target_pairs={{0,3},{1,0},{2,1},{3,2},{4,7},{5,4},{6,5},{7,6},{8,11},{9,8},{10,9... | collective-permute-start | bytes 6291464 | tf_op jit(solution)/shard_map/ppermute | solution.py:32
  128.3 72.4 %collective-permute-start.4 = (bf16[1024,1024]{1,0:T(8,128)(2,1)}, bf16[1024,1024]{1,0:T(8,128)(2,1)}, u32[]{:S(2)}, u32[]{:S(2)}) collective-permute-start(bf16[1024,1024]{1,0:T(8,128)(2,1)} %constant_dynamic-update-slice_fusion.refs_0_), channel_id=1, source_target_pairs={{0,4},{4,8},{8,12},{12,0},{1,5},{5,9},{9,13},{13,1},{2,6},{6,10},{... | collective-permute-start | bytes 6291464 | tf_op jit(solution)/shard_map/ppermute | solution.py:32
  128.3 74.9 %collective-permute-start.6 = (bf16[1024,1024]{1,0:T(8,128)(2,1)}, bf16[1024,1024]{1,0:T(8,128)(2,1)}, u32[]{:S(2)}, u32[]{:S(2)}) collective-permute-start(bf16[1024,1024]{1,0:T(8,128)(2,1)} %constant_dynamic-update-slice_fusion.refs_0_), channel_id=1, source_target_pairs={{0,12},{4,0},{8,4},{12,8},{1,13},{5,1},{9,5},{13,9},{2,14},{6,2},{... | collective-permute-start | bytes 6291464 | tf_op jit(solution)/shard_map/ppermute | solution.py:32
  139.5 43.7 %all-to-all-start.1 = ((f32[16,64,192]{2,1,0:T(8,128)}), f32[16,64,192]{2,1,0:T(8,128)S(1)}, u32[]{:S(2)}, u32[]{:S(2)}) async-start(f32[16,64,192]{2,1,0:T(8,128)} %bitcast.73), calls=%async_computation.1 | async-start | bytes 2097152 | tf_op jit(solution)/shard_map/all_to_all | solution.py:111
  184.1 34.0 %all-to-all-start.3 = ((bf16[8,64,1152]{2,1,0:T(8,128)(2,1)}), bf16[8,64,1152]{2,1,0:T(8,128)(2,1)S(1)}, u32[]{:S(2)}, u32[]{:S(2)}) async-start(bf16[8,64,1152]{2,1,0:T(8,128)(2,1)} %get-tuple-element.22), calls=%async_computation.3 | async-start | bytes 2359296 | tf_op jit(solution)/shard_map/all_to_all | solution.py:467
  195.2 40.8 %collective-permute-start.13 = (bf16[1024,512]{1,0:T(8,128)(2,1)}, bf16[1024,512]{1,0:T(8,128)(2,1)}, u32[]{:S(2)}, u32[]{:S(2)}) collective-permute-start(bf16[1024,512]{1,0:T(8,128)(2,1)} %slice.118), channel_id=1, source_target_pairs={{0,1},{1,2},{2,3},{3,0},{4,5},{5,6},{6,7},{7,4},{8,9},{9,10},{10,1... | collective-permute-start | bytes 3145736 | tf_op jit(solution)/shard_map/ppermute | solution.py:32
  197.5 38.5 %collective-permute-start.15 = (bf16[1024,512]{1,0:T(8,128)(2,1)}, bf16[1024,512]{1,0:T(8,128)(2,1)}, u32[]{:S(2)}, u32[]{:S(2)}) collective-permute-start(bf16[1024,512]{1,0:T(8,128)(2,1)} %slice.119), channel_id=1, source_target_pairs={{0,3},{1,0},{2,1},{3,2},{4,7},{5,4},{6,5},{7,6},{8,11},{9,8},{10,9... | collective-permute-start | bytes 3145736 | tf_op jit(solution)/shard_map/ppermute | solution.py:32
  203.0 33.1 %collective-permute-start.5 = (bf16[1024,512]{1,0:T(8,128)(2,1)}, bf16[1024,512]{1,0:T(8,128)(2,1)S(1)}, u32[]{:S(2)}, u32[]{:S(2)}) collective-permute-start(bf16[1024,512]{1,0:T(8,128)(2,1)} %slice.114), channel_id=1, source_target_pairs={{0,4},{4,8},{8,12},{12,0},{1,5},{5,9},{9,13},{13,1},{2,6},{6,10},{... | collective-permute-start | bytes 3145736 | tf_op jit(solution)/shard_map/ppermute | solution.py:32
  205.5 30.8 %collective-permute-start.7 = (bf16[1024,512]{1,0:T(8,128)(2,1)}, bf16[1024,512]{1,0:T(8,128)(2,1)}, u32[]{:S(2)}, u32[]{:S(2)}) collective-permute-start(bf16[1024,512]{1,0:T(8,128)(2,1)} %slice.115), channel_id=1, source_target_pairs={{0,12},{4,0},{8,4},{12,8},{1,13},{5,1},{9,5},{13,9},{2,14},{6,2},{... | collective-permute-start | bytes 3145736 | tf_op jit(solution)/shard_map/ppermute | solution.py:32
  219.1 26.5 %all-to-all-start.2 = ((bf16[16,64,192]{2,1,0:T(8,128)(2,1)}), bf16[16,64,192]{2,1,0:T(8,128)(2,1)S(1)}, u32[]{:S(2)}, u32[]{:S(2)}) async-start(bf16[16,64,192]{2,1,0:T(8,128)(2,1)} %broadcast_in_dim.76), calls=%async_computation.2 | async-start | bytes 1048576 | tf_op jit(solution)/shard_map/all_to_all | solution.py:116
  279.9 13.4 %collective-permute-start.25 = (bf16[512,512]{1,0:T(8,128)(2,1)S(1)}, bf16[512,512]{1,0:T(8,128)(2,1)S(1)}, u32[]{:S(2)}, u32[]{:S(2)}) collective-permute-start(bf16[512,512]{1,0:T(8,128)(2,1)S(1)} %get-tuple-element.33.refs_0_), channel_id=1, source_target_pairs={{0,1},{1,2},{2,3},{3,0},{4,5},{5,6},{6,7},{7,4},{8,9},{9,10},{10,1... | collective-permute-start | bytes 1572872 | tf_op jit(solution)/shard_map/ppermute | solution.py:32
  281.4 12.7 %collective-permute-start.26 = (bf16[512,512]{1,0:T(8,128)(2,1)S(1)}, bf16[512,512]{1,0:T(8,128)(2,1)S(1)}, u32[]{:S(2)}, u32[]{:S(2)}) collective-permute-start(bf16[512,512]{1,0:T(8,128)(2,1)S(1)} %get-tuple-element.33.refs_0_), channel_id=1, source_target_pairs={{0,3},{1,0},{2,1},{3,2},{4,7},{5,4},{6,5},{7,6},{8,11},{9,8},{10,9... | collective-permute-start | bytes 1572872 | tf_op jit(solution)/shard_map/ppermute | solution.py:32
  283.2 25.0 %collective-permute-start.17 = (bf16[512,512]{1,0:T(8,128)(2,1)S(1)}, bf16[512,512]{1,0:T(8,128)(2,1)S(1)}, u32[]{:S(2)}, u32[]{:S(2)}) collective-permute-start(bf16[512,512]{1,0:T(8,128)(2,1)S(1)} %get-tuple-element.34.refs_0_), channel_id=1, source_target_pairs={{0,4},{4,8},{8,12},{12,0},{1,5},{5,9},{9,13},{13,1},{2,6},{6,10},{... | collective-permute-start | bytes 1572872 | tf_op jit(solution)/shard_map/ppermute | solution.py:32
  284.7 26.1 %collective-permute-start.18 = (bf16[512,512]{1,0:T(8,128)(2,1)S(1)}, bf16[512,512]{1,0:T(8,128)(2,1)S(1)}, u32[]{:S(2)}, u32[]{:S(2)}) collective-permute-start(bf16[512,512]{1,0:T(8,128)(2,1)S(1)} %get-tuple-element.34.refs_0_), channel_id=1, source_target_pairs={{0,12},{4,0},{8,4},{12,8},{1,13},{5,1},{9,5},{13,9},{2,14},{6,2},{... | collective-permute-start | bytes 1572872 | tf_op jit(solution)/shard_map/ppermute | solution.py:32
  294.0 18.9 %collective-permute-start.27 = (bf16[512,256]{1,0:T(8,128)(2,1)}, bf16[512,256]{1,0:T(8,128)(2,1)S(1)}, u32[]{:S(2)}, u32[]{:S(2)}) collective-permute-start(bf16[512,256]{1,0:T(8,128)(2,1)} %slice.128), channel_id=1, source_target_pairs={{0,1},{1,2},{2,3},{3,0},{4,5},{5,6},{6,7},{7,4},{8,9},{9,10},{10,1... | collective-permute-start | bytes 786440 | tf_op jit(solution)/shard_map/ppermute | solution.py:32
  294.8 18.1 %collective-permute-start.28 = (bf16[512,256]{1,0:T(8,128)(2,1)}, bf16[512,256]{1,0:T(8,128)(2,1)}, u32[]{:S(2)}, u32[]{:S(2)}) collective-permute-start(bf16[512,256]{1,0:T(8,128)(2,1)} %slice.129), channel_id=1, source_target_pairs={{0,3},{1,0},{2,1},{3,2},{4,7},{5,4},{6,5},{7,6},{8,11},{9,8},{10,9... | collective-permute-start | bytes 786440 | tf_op jit(solution)/shard_map/ppermute | solution.py:32
  304.0 54.1 %all-to-all-start.6 = ((f32[16,1,4096]{2,1,0:T(1,128)}), f32[16,1,4096]{2,1,0:T(1,128)}, u32[]{:S(2)}, u32[]{:S(2)}) async-start(f32[16,1,4096]{2,1,0:T(1,128)} %reshape.123), calls=%async_computation.6 | async-start | bytes 524288 | tf_op jit(solution)/shard_map/all_to_all | solution.py:111
  308.9 12.6 %collective-permute-start.19 = (bf16[512,256]{1,0:T(8,128)(2,1)}, bf16[512,256]{1,0:T(8,128)(2,1)}, u32[]{:S(2)}, u32[]{:S(2)}) collective-permute-start(bf16[512,256]{1,0:T(8,128)(2,1)} %slice.120), channel_id=1, source_target_pairs={{0,4},{4,8},{8,12},{12,0},{1,5},{5,9},{9,13},{13,1},{2,6},{6,10},{... | collective-permute-start | bytes 786440 | tf_op jit(solution)/shard_map/ppermute | solution.py:32
  319.4 29.9 %collective-permute-start.31 = (bf16[512,256]{1,0:T(8,128)(2,1)S(1)}, bf16[512,256]{1,0:T(8,128)(2,1)S(1)}, u32[]{:S(2)}, u32[]{:S(2)}) collective-permute-start(bf16[512,256]{1,0:T(8,128)(2,1)S(1)} %get-tuple-element.41), channel_id=1, source_target_pairs={{0,12},{4,0},{8,4},{12,8},{1,13},{5,1},{9,5},{13,9},{2,14},{6,2},{... | collective-permute-start | bytes 786440 | tf_op jit(solution)/shard_map/ppermute | solution.py:32
  321.3 30.8 %collective-permute-start.29 = (bf16[512,256]{1,0:T(8,128)(2,1)S(1)}, bf16[512,256]{1,0:T(8,128)(2,1)S(1)}, u32[]{:S(2)}, u32[]{:S(2)}) collective-permute-start(bf16[512,256]{1,0:T(8,128)(2,1)S(1)} %get-tuple-element.42), channel_id=1, source_target_pairs={{0,4},{4,8},{8,12},{12,0},{1,5},{5,9},{9,13},{13,1},{2,6},{6,10},{... | collective-permute-start | bytes 786440 | tf_op jit(solution)/shard_map/ppermute | solution.py:32
  327.3 25.8 %collective-permute-start.23 = (bf16[512,256]{1,0:T(8,128)(2,1)S(1)}, bf16[512,256]{1,0:T(8,128)(2,1)S(1)}, u32[]{:S(2)}, u32[]{:S(2)}) collective-permute-start(bf16[512,256]{1,0:T(8,128)(2,1)S(1)} %get-tuple-element.47), channel_id=1, source_target_pairs={{0,3},{1,0},{2,1},{3,2},{4,7},{5,4},{6,5},{7,6},{8,11},{9,8},{10,9... | collective-permute-start | bytes 786440 | tf_op jit(solution)/shard_map/ppermute | solution.py:32
  330.4 26.8 %collective-permute-start.21 = (bf16[512,256]{1,0:T(8,128)(2,1)S(1)}, bf16[512,256]{1,0:T(8,128)(2,1)S(1)}, u32[]{:S(2)}, u32[]{:S(2)}) collective-permute-start(bf16[512,256]{1,0:T(8,128)(2,1)S(1)} %get-tuple-element.48), channel_id=1, source_target_pairs={{0,1},{1,2},{2,3},{3,0},{4,5},{5,6},{6,7},{7,4},{8,9},{9,10},{10,1... | collective-permute-start | bytes 786440 | tf_op jit(solution)/shard_map/ppermute | solution.py:32
  349.4 38.5 %collective-permute-start.32 = (bf16[512,512]{1,0:T(8,128)(2,1)S(1)}, bf16[512,512]{1,0:T(8,128)(2,1)S(1)}, u32[]{:S(2)}, u32[]{:S(2)}) collective-permute-start(bf16[512,512]{1,0:T(8,128)(2,1)S(1)} %pad_maximum_fusion.3), channel_id=1, source_target_pairs={{0,12},{4,0},{8,4},{12,8},{1,13},{5,1},{9,5},{13,9},{2,14},{6,2},{... | collective-permute-start | bytes 1572872 | tf_op jit(solution)/shard_map/ppermute | solution.py:32
  353.0 34.9 %collective-permute-start.30 = (bf16[512,512]{1,0:T(8,128)(2,1)}, bf16[512,512]{1,0:T(8,128)(2,1)S(1)}, u32[]{:S(2)}, u32[]{:S(2)}) collective-permute-start(bf16[512,512]{1,0:T(8,128)(2,1)} %pad_maximum_fusion.2), channel_id=1, source_target_pairs={{0,4},{4,8},{8,12},{12,0},{1,5},{5,9},{9,13},{13,1},{2,6},{6,10},{... | collective-permute-start | bytes 1572872 | tf_op jit(solution)/shard_map/ppermute | solution.py:32
  353.9 34.0 %collective-permute-start.24 = (bf16[512,512]{1,0:T(8,128)(2,1)}, bf16[512,512]{1,0:T(8,128)(2,1)S(1)}, u32[]{:S(2)}, u32[]{:S(2)}) collective-permute-start(bf16[512,512]{1,0:T(8,128)(2,1)} %pad_maximum_fusion.1), channel_id=1, source_target_pairs={{0,3},{1,0},{2,1},{3,2},{4,7},{5,4},{6,5},{7,6},{8,11},{9,8},{10,9... | collective-permute-start | bytes 1572872 | tf_op jit(solution)/shard_map/ppermute | solution.py:32
  358.1 29.9 %collective-permute-start.22 = (bf16[512,512]{1,0:T(8,128)(2,1)}, bf16[512,512]{1,0:T(8,128)(2,1)S(1)}, u32[]{:S(2)}, u32[]{:S(2)}) collective-permute-start(bf16[512,512]{1,0:T(8,128)(2,1)} %pad_maximum_fusion), channel_id=1, source_target_pairs={{0,1},{1,2},{2,3},{3,0},{4,5},{5,6},{6,7},{7,4},{8,9},{9,10},{10,1... | collective-permute-start | bytes 1572872 | tf_op jit(solution)/shard_map/ppermute | solution.py:32
  362.2 15.3 %all-to-all-start.7 = ((bf16[16,2,2048]{2,1,0:T(2,128)(2,1)}), bf16[16,2,2048]{2,1,0:T(2,128)(2,1)S(1)}, u32[]{:S(2)}, u32[]{:S(2)}) async-start(bf16[16,2,2048]{2,1,0:T(2,128)(2,1)} %reshape.125), calls=%async_computation.7 | async-start | bytes 262144 | tf_op jit(solution)/shard_map/all_to_all | solution.py:116
  (38 other events, 385.7 us)
Sparse Core Ops, SparseCore 0:
  75.4 47.5 all-gather.4
  124.7 49.9 all-gather.2

commit v2 on v1

v2 whole, which is shorter than its diff:
```python
import math

import jax
import jax.numpy as jnp
from jax import lax
from jax.experimental import pallas as pl
from jax.experimental.pallas import tpu as pltpu
from jax.sharding import Mesh, PartitionSpec as P

HEAD = 128
BLOCK = 128
SIDE = 4
CORES = 2
ADAPTER_AXES = ("z", "c")
TENSOR_AXES = ("y", "x")
ROPE_BASE = 500000.0
VMEM = 56 * 1024 * 1024
bf16 = jnp.bfloat16
f32 = jnp.float32
i32 = jnp.int32


def params():
    return pltpu.CompilerParams(vmem_limit_bytes=VMEM)


def cost(flops, moved, exps=0):
    return pl.CostEstimate(flops=flops, bytes_accessed=moved, transcendentals=exps)


def shift(block, axis, step):
    return lax.ppermute(block, axis, [(i, (i + step) % SIDE) for i in range(SIDE)])


def ring_gather(block, axis):
    half = block.shape[1] // 2
    behind = shift(block, axis, 1)
    ahead = shift(block, axis, -1)
    far_low = shift(behind[:, :half], axis, 1)
    far_high = shift(ahead[:, half:], axis, -1)
    return block, behind, ahead, far_low, far_high


def ring_order(index):
    return [index, (index + SIDE - 1) % SIDE, (index + 1) % SIDE, (index + 2) % SIDE]


def pick_adapters(pick, down_qkv, up_q, up_kv, down_o, up_o):
    groups = pick.shape[0]
    rank3, depth = down_qkv.shape[1:]
    rank, wide = up_q.shape[1:]
    narrow = up_kv.shape[2]

    def body(pick_ref, dq, uq, ukv, do, uo, down, up):
        down[0, :rank3, :] = dq[0]
        down[0, rank3:, :] = do[0]
        up[0, :, :wide] = uq[0]
        up[0, :, wide : 2 * wide] = uo[0]
        up[0, :, 2 * wide :] = ukv[0]

    def chosen(a):
        return pl.BlockSpec((1,) + a.shape[1:], lambda i, p: (p[i], 0, 0))

    down_shape = (groups, rank3 + rank, depth)
    up_shape = (groups, rank, 2 * wide + narrow)
    return pl.pallas_call(
        body,
        out_shape=(
            jax.ShapeDtypeStruct(down_shape, bf16),
            jax.ShapeDtypeStruct(up_shape, bf16),
        ),
        grid_spec=pltpu.PrefetchScalarGridSpec(
            num_scalar_prefetch=1,
            grid=(groups,),
            in_specs=[chosen(a) for a in (down_qkv, up_q, up_kv, down_o, up_o)],
            out_specs=[
                pl.BlockSpec((1,) + s[1:], lambda i, p: (i, 0, 0)) for s in (down_shape, up_shape)
            ],
        ),
        compiler_params=params(),
        cost_estimate=cost(0, 2 * 2 * (math.prod(down_shape) + math.prod(up_shape))),
    )(pick, down_qkv, up_q, up_kv, down_o, up_o)


def rank_partial(meta, x, down, rank3):
    tokens, depth = x.shape
    per = 2
    rows = per * BLOCK

    def body(meta_ref, x_ref, *rest):
        d_refs, out = rest[:-1], rest[-1]
        for k in range(per):
            at = slice(k * BLOCK, (k + 1) * BLOCK)
            out[at, :] = lax.dot_general(
                x_ref[at, :], d_refs[k][0], (((1,), (1,)), ((), ())), preferred_element_type=f32
            )

    def chosen(k):
        return pl.BlockSpec((1, rank3, depth), lambda i, m: (m[0, i * per + k], 0, 0))

    return pl.pallas_call(
        body,
        out_shape=jax.ShapeDtypeStruct((tokens, rank3), f32),
        grid_spec=pltpu.PrefetchScalarGridSpec(
            num_scalar_prefetch=1,
            grid=(tokens // rows,),
            in_specs=[pl.BlockSpec((rows, depth), lambda i, m: (i, 0))]
            + [chosen(k) for k in range(per)],
            out_specs=pl.BlockSpec((rows, rank3), lambda i, m: (i, 0)),
        ),
        compiler_params=params(),
        cost_estimate=cost(2 * tokens * depth * rank3, 2 * tokens * depth + 8 * tokens * rank3),
    )(meta, x, *[down] * per)


def sum_over_tensor(partial):
    rows, rank = partial.shape
    ways = SIDE * SIDE
    pieces = lax.all_to_all(
        partial.reshape(ways, rows // ways, rank), TENSOR_AXES, 0, 0, tiled=True
    )
    mine = jnp.sum(pieces, axis=0).astype(bf16)
    copies = jnp.broadcast_to(mine[None], (ways,) + mine.shape)
    return lax.all_to_all(copies, TENSOR_AXES, 0, 0, tiled=True).reshape(rows, rank)


def project(index, total, blocks, weights, tile, last=None, rows=256):
    tokens = blocks[0].shape[0]
    counts = [b.shape[1] // rows for b in blocks]
    pieces = sum(counts)
    kinds = len(weights)
    first = total is None
    tail, tail_operands, tail_specs, dtype = last or (None, [], [], f32)

    def body(index_ref, meta_ref, *refs):
        x_refs = refs[: len(blocks)]
        w_refs = refs[len(blocks) : len(blocks) + kinds * pieces]
        rest = refs[len(blocks) + kinds * pieces :]
        outs = rest[len(rest) - kinds :]
        for kind in range(kinds):
            mine = w_refs[kind * pieces : (kind + 1) * pieces]
            acc = None if first else rest[kind][...]
            at = 0
            for x_ref, n in zip(x_refs, counts):
                w = jnp.concatenate([r[...] for r in mine[at : at + n]], axis=0)
                add = jnp.dot(x_ref[...], w, preferred_element_type=f32)
                acc = add if acc is None else acc + add
                at += n
            if tail is not None:
                acc = tail(meta_ref, acc, rest[kinds : len(rest) - kinds])
            outs[kind][...] = acc

    def weight(k, width):
        return pl.BlockSpec((rows, width), lambda i, p, m: (p[k], 0))

    widths = [w.shape[1] for w in weights]
    row_specs = [pl.BlockSpec((tile, w), lambda i, p, m: (i, 0)) for w in widths]
    in_specs = [pl.BlockSpec((tile, b.shape[1]), lambda i, p, m: (i, 0)) for b in blocks]
    operands = list(blocks)
    for w in weights:
        in_specs += [weight(k, w.shape[1]) for k in range(pieces)]
        operands += [w] * pieces
    aliases = {}
    if not first:
        if tail is None:
            aliases = {2 + len(operands) + k: k for k in range(kinds)}
        in_specs += row_specs
        operands += list(total)
    index, meta = index
    depth = pieces * rows
    return pl.pallas_call(
        body,
        out_shape=tuple(jax.ShapeDtypeStruct((tokens, w), dtype) for w in widths),
        grid_spec=pltpu.PrefetchScalarGridSpec(
            num_scalar_prefetch=2,
            grid=(tokens // tile,),
            in_specs=in_specs + tail_specs,
            out_specs=row_specs,
        ),
        input_output_aliases=aliases,
        compiler_params=params(),
        cost_estimate=cost(
            2 * tokens * depth * sum(widths),
            2 * depth * (tokens + sum(widths)) + 8 * tokens * sum(widths),
        ),
    )(index, meta, *operands, *tail_operands)


def key_value_tail(shrunk, up, cosine, sine, wide, narrow, tile):
    rank = shrunk.shape[1] // 3
    per = tile // BLOCK

    def tail(meta_ref, acc, refs):
        s_ref, up_ref, c_ref, n_ref = refs
        i = pl.program_id(0)
        is_key = meta_ref[3, 0] == 1
        done = []
        for k in range(per):
            at = slice(k * BLOCK, (k + 1) * BLOCK)
            s = s_ref[at, :].astype(f32)
            rank_in = jnp.where(is_key, s[:, rank : 2 * rank], s[:, 2 * rank :]).astype(bf16)
            u = acc[at, :] + jnp.dot(
                rank_in, up_ref[meta_ref[0, i * per + k]], preferred_element_type=f32
            )
            place = meta_ref[1, i * per + k]
            turned = u * c_ref[place] + pltpu.roll(u, HEAD // 2, 1) * n_ref[place]
            done.append(jnp.where(is_key, turned, u).astype(bf16))
        return jnp.concatenate(done, axis=0)

    specs = [
        pl.BlockSpec((tile, 3 * rank), lambda i, p, m: (i, 0)),
        pl.BlockSpec((up.shape[0], rank, narrow), lambda i, p, m: (0, 0, 2 * wide // narrow)),
        pl.BlockSpec(cosine.shape, lambda i, p, m: (0, 0, 0)),
        pl.BlockSpec(sine.shape, lambda i, p, m: (0, 0, 0)),
    ]
    return tail, [shrunk, up, cosine, sine], specs, bf16


def attention(meta, q, shrunk, up, down, mine, other, cosine, sine, begin, count):
    tokens, wide = q.shape
    rank = shrunk.shape[1] // 3
    heads = wide // HEAD
    window = min(3 * BLOCK, tokens)
    scale = 1.0 / math.sqrt(HEAD)

    def body(meta_ref, q_ref, s_ref, up_ref, d_ref, m_ref, o_ref, c_ref, n_ref, att, head):
        i = begin + pl.program_id(0)
        is_key = meta_ref[3, 0] == 1
        first = meta_ref[2, i]
        limit = meta_ref[4, i]
        u = q_ref[...] + jnp.dot(
            s_ref[...][:, :rank], up_ref[0], preferred_element_type=f32
        )
        start = pl.multiple_of(jnp.maximum(i - 2, 0) * BLOCK, BLOCK)
        own = m_ref[pl.ds(start, window), :]
        far = o_ref[pl.ds(start, window), :]
        keys = jnp.where(is_key, own, far)
        values = jnp.where(is_key, far, own)
        row = i * BLOCK + lax.broadcasted_iota(i32, (BLOCK, window), 0)
        col = start + lax.broadcasted_iota(i32, (BLOCK, window), 1)
        allowed = (col >= first) & (col <= row) & (col < limit)
        cosines = c_ref[0]
        sines = n_ref[0]
        turned = []
        for h in range(heads):
            part = u[:, h * HEAD : (h + 1) * HEAD]
            turned.append(
                (part * cosines + pltpu.roll(part, HEAD // 2, 1) * sines).astype(bf16)
            )
        scores = lax.dot_general(
            jnp.concatenate(turned, axis=0),
            keys,
            (((1,), (1,)), ((), ())),
            preferred_element_type=f32,
        )
        for h in range(heads):
            at = slice(h * HEAD, (h + 1) * HEAD)
            weights = jnp.where(allowed, jnp.exp(scores[at, :] * scale), 0.0)
            weights = weights * (1.0 / jnp.sum(weights, axis=1, keepdims=True))
            mixed = jnp.dot(weights.astype(bf16), values, preferred_element_type=f32)
            att[:, at] = mixed.astype(bf16)
        head[...] = lax.dot_general(
            att[...], d_ref[0], (((1,), (1,)), ((), ())), preferred_element_type=f32
        )

    table = pl.BlockSpec((1, BLOCK, HEAD), lambda i, m: (m[1, i + begin], 0, 0))
    whole = pl.BlockSpec((tokens, HEAD), lambda i, m: (0, 0))
    return pl.pallas_call(
        body,
        out_shape=(
            jax.ShapeDtypeStruct((count * BLOCK, wide), bf16),
            jax.ShapeDtypeStruct((count * BLOCK, rank), f32),
        ),
        grid_spec=pltpu.PrefetchScalarGridSpec(
            num_scalar_prefetch=1,
            grid=(count,),
            in_specs=[
                pl.BlockSpec((BLOCK, wide), lambda i, m: (i + begin, 0)),
                pl.BlockSpec((BLOCK, 3 * rank), lambda i, m: (i + begin, 0)),
                pl.BlockSpec((1, rank, wide), lambda i, m: (m[0, i + begin], 0, 0)),
                pl.BlockSpec((1, rank, down.shape[2]), lambda i, m: (m[0, i + begin], 3, 0)),
                whole,
                whole,
                table,
                table,
            ],
            out_specs=[
                pl.BlockSpec((BLOCK, wide), lambda i, m: (i, 0)),
                pl.BlockSpec((BLOCK, rank), lambda i, m: (i, 0)),
            ],
        ),
        compiler_params=params(),
        cost_estimate=cost(
            4 * count * BLOCK * window * wide, 8 * count * BLOCK * wide, heads * count * BLOCK * window
        ),
    )(meta, q, shrunk, up, down, mine, other, cosine, sine)


def pick_columns(index, matrix, width):
    depth = matrix.shape[0]
    count = index.shape[0]

    def body(index_ref, m_ref, out):
        out[0] = m_ref[...]

    return pl.pallas_call(
        body,
        out_shape=jax.ShapeDtypeStruct((count, depth, width), bf16),
        grid_spec=pltpu.PrefetchScalarGridSpec(
            num_scalar_prefetch=1,
            grid=(count,),
            in_specs=[pl.BlockSpec((depth, width), lambda i, p: (0, p[i]))],
            out_specs=pl.BlockSpec((1, depth, width), lambda i, p: (i, 0, 0)),
        ),
        compiler_params=params(),
        cost_estimate=cost(0, 4 * count * depth * width),
    )(index, matrix)


def output_partial(index, pieces, weights, dtypes):
    tokens = pieces[0].shape[0]
    depth, width = weights.shape[1:]
    unit = depth // SIDE
    count = len(dtypes)
    places = [(0, 0), (1, 0), (2, 0), (3, 0), (3, unit // 2)]

    def body(index_ref, *refs):
        x_refs, w_ref, outs = refs[: len(pieces)], refs[len(pieces)], refs[len(pieces) + 1 :]
        total = None
        for x_ref, (place, offset) in zip(x_refs, places):
            start = pl.multiple_of(index_ref[place] * unit + offset, 128)
            rows = w_ref[0, pl.ds(start, x_ref.shape[1]), :]
            add = jnp.dot(x_ref[...], rows, preferred_element_type=f32)
            total = add if total is None else total + add
        for k, out in enumerate(outs):

            @pl.when(pl.program_id(0) == k)
            def _():
                out[...] = total.astype(out.dtype)

    return pl.pallas_call(
        body,
        out_shape=tuple(jax.ShapeDtypeStruct((tokens, width), d) for d in dtypes),
        grid_spec=pltpu.PrefetchScalarGridSpec(
            num_scalar_prefetch=1,
            grid=(count,),
            in_specs=[pl.BlockSpec(p.shape, lambda j, d: (0, 0)) for p in pieces]
            + [pl.BlockSpec((1, depth, width), lambda j, d: (d[SIDE + j], 0, 0))],
            out_specs=[pl.BlockSpec((tokens, width), lambda j, d: (0, 0))] * count,
        ),
        compiler_params=params(),
        cost_estimate=cost(
            2 * tokens * depth * count * width, 2 * depth * (tokens + count * width)
        ),
    )(index, *pieces, weights)


def output_ring(pieces, weights, axis, places):
    me, behind, ahead, far = ring_order(lax.axis_index(axis))

    def partial(shards, dtypes):
        return output_partial(jnp.stack(places + shards).astype(i32), pieces, weights, dtypes)

    far_low, far_high = partial([2 * far, 2 * far + 1], [bf16] * 2)
    via_behind = shift(far_low, axis, 1)
    via_ahead = shift(far_high, axis, -1)
    ahead_high, behind_low, ahead_low, behind_high, low, high = partial(
        [2 * ahead + 1, 2 * behind, 2 * ahead, 2 * behind + 1, 2 * me, 2 * me + 1],
        [bf16] * 4 + [f32] * 2,
    )
    return (
        (low, shift(behind_low, axis, -1), shift(ahead_low + via_behind, axis, 1)),
        (high, shift(ahead_high, axis, 1), shift(behind_high + via_ahead, axis, -1)),
    )


def finish(meta, parts, head_rank, up, wide):
    cuts = len(parts)
    rows, width = parts[0][0][0].shape
    per = 2
    steps = rows // (per * BLOCK)
    rank = head_rank.shape[1] // cuts
    terms = [t for cut in parts for side in cut for t in side]
    each = len(parts[0][0])

    def body(meta_ref, *refs):
        h_ref, up_ref, out = refs[len(terms) :]
        i = pl.program_id(0)

        def put(cut):
            for k in range(per):
                at = slice(k * BLOCK, (k + 1) * BLOCK)
                block = i * per + k
                extra = jnp.dot(
                    h_ref[at, cut * rank : (cut + 1) * rank],
                    up_ref[meta_ref[0, block]],
                    preferred_element_type=f32,
                )
                row = block * BLOCK + lax.broadcasted_iota(i32, (BLOCK, width), 0)
                valid = row < meta_ref[4, block]
                for side in range(2):
                    cols = slice(side * width, (side + 1) * width)
                    total = extra[:, cols]
                    begin = (cut * 2 + side) * each
                    for ref in refs[begin : begin + each]:
                        total = total + ref[at, :].astype(f32)
                    out[at, cols] = jnp.where(valid, total, 0.0)

        for cut in range(cuts):

            @pl.when(i // steps == cut)
            def _():
                put(cut)

    def term_spec(cut):
        return pl.BlockSpec(
            (per * BLOCK, width), lambda i, m: (jnp.clip(i - cut * steps, 0, steps - 1), 0)
        )

    return pl.pallas_call(
        body,
        out_shape=jax.ShapeDtypeStruct((cuts * rows, 2 * width), f32),
        grid_spec=pltpu.PrefetchScalarGridSpec(
            num_scalar_prefetch=1,
            grid=(cuts * steps,),
            in_specs=[term_spec(cut) for cut in range(cuts) for _ in range(2 * each)]
            + [
                pl.BlockSpec((per * BLOCK, cuts * rank), lambda i, m: (lax.rem(i, steps), 0)),
                pl.BlockSpec((up.shape[0], rank, wide), lambda i, m: (0, 0, 1)),
            ],
            out_specs=pl.BlockSpec((per * BLOCK, 2 * width), lambda i, m: (i, 0)),
        ),
        compiler_params=params(),
        cost_estimate=cost(4 * cuts * rows * rank * width, 28 * cuts * rows * width),
    )(meta, *terms, head_rank, up)


def on_device(x, wq, wkv, wo, down_qkv, up_q, up_kv, down_o, up_o, choice, counts, tails):
    z, c, y, xi = (lax.axis_index(n) for n in ADAPTER_AXES + TENSOR_AXES)
    group = z * CORES + c
    tokens, local = x.shape
    holders = down_qkv.shape[0]
    requests = choice.shape[1]
    wide = wq.shape[1]
    rank = up_q.shape[1]
    blocks = tokens // BLOCK

    owners = choice // holders
    pick = jnp.sum(jnp.where(owners == group, choice % holders, 0), axis=1).astype(i32)
    own_owner = lax.dynamic_index_in_dim(owners, group, 0, keepdims=False)
    req = jnp.arange(requests, dtype=i32)
    starts = jnp.sum(jnp.where(req[None, :] < req[:, None], counts[0][None, :], 0), axis=1)
    block = jnp.arange(blocks, dtype=i32)
    of_block = (starts[None, :] <= block[:, None]) & (
        block[:, None] < (starts + counts[0])[None, :]
    )

    def lookup(values):
        return jnp.sum(jnp.where(of_block, values[None, :], 0), axis=1).astype(i32)

    slot = lookup(own_owner)
    first = lookup(starts)
    limit = (first + lookup(counts[0]) - 1) * BLOCK + lookup(tails[0])
    is_key = jnp.broadcast_to(1 - xi % 2, (blocks,)).astype(i32)
    meta = jnp.stack([slot, block - first, first * BLOCK, is_key, limit]).astype(i32)

    freq = jnp.exp(-(2.0 * jnp.arange(HEAD // 2, dtype=f32) / HEAD) * math.log(ROPE_BASE))
    angle = jnp.arange(3 * BLOCK, dtype=f32)[:, None] * freq[None, :]
    cosine = jnp.tile(jnp.cos(angle), (1, 2)).reshape(3, BLOCK, HEAD)
    sine = jnp.concatenate([-jnp.sin(angle), jnp.sin(angle)], axis=1).reshape(3, BLOCK, HEAD)

    half = local // 2
    ys, xs = ring_order(y), ring_order(xi)
    flat_first = ring_gather(x[:, :half], "x")
    flat_a = jnp.concatenate(flat_first, axis=1)
    flat_b = jnp.concatenate(ring_gather(x[:, half:], "y"), axis=1)

    def rows_a(k, cols):
        return [(ys[k] * SIDE + xs[j]) * 2 for j in cols]

    def rows_b(k, cols):
        return [(ys[j] * SIDE + xs[k]) * 2 + 1 for j in cols]

    def index_of(rows):
        return jnp.stack(rows).astype(i32)

    every = range(SIDE)
    a0, a1, a2, a3, a4 = ring_gather(flat_a, "y")
    b0, b1, b2, b3, b4 = ring_gather(flat_b, "x")

    stores = (jnp.swapaxes(down_qkv, 1, 2), up_q, up_kv, jnp.swapaxes(down_o, 1, 2), up_o)
    stores, _ = lax.optimization_barrier((stores, flat_first[1]))
    down_out, up_out = pick_adapters(pick, *stores)
    down = lax.all_to_all(down_out, ADAPTER_AXES, 0, 0, tiled=True)
    up = lax.all_to_all(up_out, ADAPTER_AXES, 0, 0, tiled=True)
    shrunk = sum_over_tensor(rank_partial(meta, x, down, 3 * rank))

    unit = wo.shape[1] // (SIDE * SIDE * 2)
    tied, _ = lax.optimization_barrier((wo, down))
    order = ring_order(y)
    sent = pick_columns(jnp.stack(order).astype(i32) * (2 * SIDE) + group, tied, unit)
    got = [sent[0], shift(sent[2], "y", 1), shift(sent[1], "y", -1), shift(sent[3], "y", 2)]
    wo_all = lax.all_gather(jnp.concatenate(got, axis=0), ADAPTER_AXES, axis=0)

    total = project(
        (index_of(rows_a(0, every) + rows_b(0, every)), meta), None, [a0, b0], [wq, wkv], 512
    )
    total = project(
        (index_of(rows_a(1, every) + rows_a(2, every) + rows_b(1, every) + rows_b(2, every)), meta),
        total,
        [a1, a2, b1, b2],
        [wq, wkv],
        512,
    )
    final = (index_of(rows_a(3, every) + rows_b(3, every)), meta)
    far = [a3, a4, b3, b4]
    tail = key_value_tail(shrunk, up, cosine, sine, wide, wkv.shape[1], 512)
    (mine,) = project(final, total[1:], far, [wkv], 512, tail)
    other = lax.ppermute(mine, "x", [(i, i ^ 1) for i in range(SIDE)])
    (q,) = project(final, total[:1], far, [wq], 512)

    cuts = 2
    parts, ranks = [], []
    for cut in range(cuts):
        attended, head = attention(
            meta, q, shrunk, up, down, mine, other, cosine, sine, cut * blocks // cuts, blocks // cuts
        )
        ranks.append(head)
        parts.append(output_ring(ring_gather(attended, "y"), wo_all, "x", [jnp.int32(k) for k in range(SIDE)]))
    head_rank = sum_over_tensor(jnp.concatenate(ranks, axis=1))
    return finish(meta, parts, head_rank, up, wide)


def solution(mesh):
    fine = Mesh(mesh.devices.reshape(SIDE, CORES, SIDE, SIDE), ADAPTER_AXES + TENSOR_AXES)
    placed = (
        P(ADAPTER_AXES, TENSOR_AXES),
        P(None, TENSOR_AXES),
        P(None, TENSOR_AXES),
        P(TENSOR_AXES, None),
        P(ADAPTER_AXES, TENSOR_AXES, None),
        P(ADAPTER_AXES, None, TENSOR_AXES),
        P(ADAPTER_AXES, None, TENSOR_AXES),
        P(ADAPTER_AXES, TENSOR_AXES, None),
        P(ADAPTER_AXES, None, TENSOR_AXES),
        P(),
        P(ADAPTER_AXES, None),
        P(ADAPTER_AXES, None),
    )
    return jax.shard_map(
        on_device,
        mesh=fine,
        in_specs=placed,
        out_specs=P(ADAPTER_AXES, TENSOR_AXES),
        check_vma=False,
    )
```

time: 406 us -> 363 us (0.89)
  blocking collectives: 38.1 us -> 13.2 us
  Pallas kernels: 121 us -> 97.7 us
  waiting for transfers between devices: 92.2 us -> 114 us
  local copies, waits for them, and re-layouts: 48.3 us -> 30.3 us
  starting transfers between devices: 80 us -> 84.8 us
    ppermute x32 -> x39, waiting for transfers between devices: 12.9 us -> 41.4 us  [shift(): lax.ppermute(block, axis, [(i, (i + step) % SIDE) for i in range(SIDE)])]
    all_to_all x2 -> x1, blocking collectives: 38.1 us -> 13.2 us  [sum_over_tensor(): lax.all_to_all(copies, TENSOR_AXES, 0, 0, tiled=True).reshape(rows, rank)]
    pallas_call x14 -> x11, Pallas kernels: 99 us -> 81.5 us  [the longest x4 33.8 us: project(): pl.pallas_call(body, out_shape=tuple((jax.ShapeDtypeStruct((tokens, w), d...]
    ppermute x32 -> x39, starting transfers between devices: 50.4 us -> 60.5 us  [shift(): lax.ppermute(block, axis, [(i, (i + step) % SIDE) for i in range(SIDE)])]
    unnamed x70 -> x68, local copies, waits for them, and re-layouts: 19.2 us -> 9.42 us
    all_to_all x4 -> x3, starting transfers between devices: 18.9 us -> 11.8 us  [the longest x2 7.74 us: sum_over_tensor(): lax.all_to_all(partial.reshape(ways, rows // ways, rank), TENSOR_AXES, 0,...]
    ppermute x1, waiting for transfers between devices: 5.99 us -> 0.01 us  [on_device(): other = lax.ppermute(mine, 'x', [(i, i ^ 1) for i in range(SIDE)])]
    all_to_all x4 -> x3, waiting for transfers between devices: 46.7 us -> 46.5 us  [the longest x2 45.8 us: sum_over_tensor(): lax.all_to_all(partial.reshape(ways, rows // ways, rank), TENSOR_AXES, 0,...]
  transfers between devices with their start and end apart: 41 -> 46, of which waited for: 7 -> 12; matrix products, arithmetic and copies ran while one was open for 12% -> 8% of each run, Pallas kernels for 25% -> 22%
where the time goes in v2:
time: 363 us; the launch traced here: 361 us
  waiting for transfers between devices  114 us (31%)
  Pallas kernels  97.7 us (27%)
  starting transfers between devices  84.8 us (23%)
  local copies, waits for them, and re-layouts  30.3 us (8%)
  between operations  14.1 us (4%)
  blocking collectives  13.2 us (4%)
  other arithmetic  6.55 us (2%)
    ppermute x39, starting transfers between devices, shift(): lax.ppermute(block, axis, [(i, (i + step) % SIDE) for i in range(SIDE)])  60.5 us
    all_to_all x2, waiting for transfers between devices, sum_over_tensor(): lax.all_to_all(partial.reshape(ways, rows // ways, rank), TENSOR_AXES, 0,...  45.8 us
    ppermute x39, waiting for transfers between devices, shift(): lax.ppermute(block, axis, [(i, (i + step) % SIDE) for i in range(SIDE)])  41.4 us
    pallas_call x4, Pallas kernels, project(): pl.pallas_call(body, out_shape=tuple((jax.ShapeDtypeStruct((tokens, w), d...  33.8 us
    pallas_call x4, Pallas kernels, output_partial(): pl.pallas_call(body, out_shape=tuple((jax.ShapeDtypeStruct((tokens, width...  28.7 us
    all_to_all x1, waiting for transfers between devices, on_device(): down = lax.all_to_all(down_out, ADAPTER_AXES, 0, 0, tiled=True)  26.6 us
    all_to_all x1, blocking collectives, sum_over_tensor(): lax.all_to_all(copies, TENSOR_AXES, 0, 0, tiled=True).reshape(rows, rank)  13.2 us
    pallas_call x2, Pallas kernels, attention(): pl.pallas_call(body, out_shape=(jax.ShapeDtypeStruct((count * BLOCK, wide...  13 us
  transfers between devices with their start and end apart: 46, of which 12 were waited for; matrix products, arithmetic and copies ran while one was open for 8% of the time, Pallas kernels for 22%

profile of v2, /device:TPU:0, one launch (start us, length us, event | category | flops | bytes accessed | tf_op | source)
XLA Modules:
  0.0 361.1 jit_solution(9392522293325090933)
XLA Ops:
  11.0 12.6 %collective-permute-done = bf16[1024,256]{1,0:T(8,128)(2,1)S(1)} collective-permute-done((bf16[1024,256]{1,0:T(8,128)(2,1)S(1)}, bf16[1024,256]{1,0:T(8,128)(2,1)S(1)}, u32[]{:S(2)}, u32[]{:S(2)}) %collective-permute-start) | collective-permute-done | bytes 524320 | tf_op jit(solution)/shard_map/ppermute | solution.py:32
  23.7 7.2 %shard_map.121 = (bf16[8,256,512]{2,1,0:T(8,128)(2,1)}, bf16[8,64,1152]{2,1,0:T(8,128)(2,1)}) custom-call(s32[8]{0:T(128)} %get-tuple-element.73.pick_ref, bf16[8,192,512]{2,1,0:T(8,128)(2,1)} %bitcast.92, bf16[8,64,512]{2,1,0:T(8,128)(2,1)} %uq, bf16[8,64,128]{2,1,0:T(8,128)(2,1)} %ukv, bf16[8,64,512]{2,1,0:T(8,128)(2,1)} %bitcast.94, bf16[8,64,512]{2,1,0:T(8,128)(2,1)} %uo), custom_call_target="tpu_custom_call" | custom-call | bytes 6553600 | tf_op jit(solution)/shard_map/pallas_call | solution.py:66
  30.8 5.4 %all-to-all-start = ((bf16[8,256,512]{2,1,0:T(8,128)(2,1)}), bf16[8,256,512]{2,1,0:T(8,128)(2,1)S(1)}, u32[]{:S(2)}, u32[]{:S(2)}) async-start(bf16[8,256,512]{2,1,0:T(8,128)(2,1)} %get-tuple-element.45), calls=%async_computation | async-start | bytes 4194304 | tf_op jit(solution)/shard_map/all_to_all | solution.py:494
  36.9 26.6 %all-to-all-done.rest_0_.rest_1_.d_ref = bf16[8,256,512]{2,1,0:T(8,128)(2,1)S(1)} async-done(((bf16[8,256,512]{2,1,0:T(8,128)(2,1)}), bf16[8,256,512]{2,1,0:T(8,128)(2,1)S(1)}, u32[]{:S(2)}, u32[]{:S(2)}) %all-to-all-start) | async-done | bytes 2097184 | tf_op jit(solution)/shard_map/all_to_all | solution.py:494
  63.4 4.1 %shard_map.125 = bf16[4,512,256]{2,1,0:T(8,128)(2,1)} custom-call(s32[4]{0:T(128)} %fusion.5.index_ref, bf16[512,8192]{1,0:T(8,128)(2,1)} %m_ref), custom_call_target="tpu_custom_call" | custom-call | bytes 2097152 | tf_op jit(solution)/shard_map/pallas_call | solution.py:306
  74.1 4.1 %collective-permute-done.21 = bf16[512,256]{1,0:T(8,128)(2,1)S(1)} collective-permute-done((bf16[512,256]{1,0:T(8,128)(2,1)S(1)}, bf16[512,256]{1,0:T(8,128)(2,1)S(1)}, u32[]{:S(2)}, u32[]{:S(2)}) %collective-permute-start.21) | collective-permute-done | bytes 262176 | tf_op jit(solution)/shard_map/ppermute | solution.py:32
  78.2 4.8 %collective-permute-done.22 = bf16[512,256]{1,0:T(8,128)(2,1)S(1)} collective-permute-done((bf16[512,256]{1,0:T(8,128)(2,1)S(1)}, bf16[512,256]{1,0:T(8,128)(2,1)S(1)}, u32[]{:S(2)}, u32[]{:S(2)}) %collective-permute-start.22) | collective-permute-done | bytes 262176 | tf_op jit(solution)/shard_map/ppermute | solution.py:32
  91.4 7.2 %collective-permute-done.1 = bf16[1024,256]{1,0:T(8,128)(2,1)S(1)} collective-permute-done((bf16[1024,256]{1,0:T(8,128)(2,1)S(1)}, bf16[1024,256]{1,0:T(8,128)(2,1)S(1)}, u32[]{:S(2)}, u32[]{:S(2)}) %collective-permute-start.1) | collective-permute-done | bytes 524320 | tf_op jit(solution)/shard_map/ppermute | solution.py:32
  109.7 3.2 collective-permute-start.6
  118.7 5.0 %shard_map.122 = f32[1024,192]{1,0:T(8,128)} custom-call(s32[5,8]{1,0:T(8,128)} %stack.170.meta_ref, bf16[1024,512]{1,0:T(8,128)(2,1)} %x_ref.1, bf16[8,256,512]{2,1,0:T(8,128)(2,1)} %copy-done, bf16[8,256,512]{2,1,0:T(8,128)(2,1)} %copy-done), custom_call_target="tpu_custom_call" | custom-call | flops 201326592 | bytes 2621440 | tf_op jit(solution)/shard_map/pallas_call | solution.py:101
  123.7 3.7 %all-to-all-start.1 = ((f32[16,64,192]{2,1,0:T(8,128)}), f32[16,64,192]{2,1,0:T(8,128)S(1)}, u32[]{:S(2)}, u32[]{:S(2)}) async-start(f32[16,64,192]{2,1,0:T(8,128)} %bitcast.91), calls=%async_computation.1 | async-start | bytes 2097152 | tf_op jit(solution)/shard_map/all_to_all | solution.py:119
  127.4 43.6 %all-to-all-done.1 = f32[16,64,192]{2,1,0:T(8,128)S(1)} async-done(((f32[16,64,192]{2,1,0:T(8,128)}), f32[16,64,192]{2,1,0:T(8,128)S(1)}, u32[]{:S(2)}, u32[]{:S(2)}) %all-to-all-start.1) | async-done | bytes 786464 | tf_op jit(solution)/shard_map/all_to_all | solution.py:119
  172.0 3.6 all-to-all-start.3
  196.7 8.0 %shard_map.118 = (f32[1024,512]{1,0:T(8,128)}, f32[1024,128]{1,0:T(8,128)}) custom-call(s32[8]{0:T(128)} %stack.212.index_ref, s32[5,8]{1,0:T(8,128)} %stack.170.meta_ref, bf16[1024,1024]{1,0:T(8,128)(2,1)} %constant_dynamic-update-slice_fusion.refs_0_, bf16[1024,1024]{1,0:T(8,128)(2,1)} %constant_dynamic-update-slice_fusion.5.refs_1_, ...), custom_call_target="tpu_custom_call" | custom-call | flops 2684354560 | bytes 12058624 | tf_op jit(solution)/shard_map/pallas_call | solution.py:171
  205.7 4.0 %all-to-all-start.2 = ((bf16[16,64,192]{2,1,0:T(8,128)(2,1)}), bf16[16,64,192]{2,1,0:T(8,128)(2,1)S(1)}, u32[]{:S(2)}, u32[]{:S(2)}) async-start(bf16[16,64,192]{2,1,0:T(8,128)(2,1)} %broadcast_in_dim.76), calls=%async_computation.2 | async-start | bytes 1048576 | tf_op jit(solution)/shard_map/all_to_all | solution.py:124
  209.7 13.2 %shard_map.119 = (f32[1024,512]{1,0:T(8,128)}, f32[1024,128]{1,0:T(8,128)}) custom-call(s32[16]{0:T(128)} %stack.203.index_ref, s32[5,8]{1,0:T(8,128)} %stack.170.meta_ref, bf16[1024,1024]{1,0:T(8,128)(2,1)} %copy-done.3, bf16[1024,1024]{1,0:T(8,128)(2,1)} %collective-permute-done.6.refs_1_, ...), custom_call_target="tpu_custom_call", output_to_operand_aliasing={{0}: (38, {}), {1}: (39, {})} | custom-call | flops 5368709120 | bytes 18874368 | tf_op jit(solution)/shard_map/pallas_call | solution.py:171
  224.8 5.5 %shard_map.123.m_ref = bf16[1024,128]{1,0:T(8,128)(2,1)} custom-call(s32[8]{0:T(128)} %stack.186.index_ref, s32[5,8]{1,0:T(8,128)} %stack.170.meta_ref, bf16[1024,512]{1,0:T(8,128)(2,1)} %collective-permute-done.5.refs_0_, bf16[1024,512]{1,0:T(8,128)(2,1)} %collective-permute-done.7.refs_1_, bf16[1024,512]{1,0:T(8,128)(2,1)} %copy-done.4, ...), custom_call_target="tpu_custom_call" | custom-call | flops 536870912 | bytes 5767168 | tf_op jit(solution)/shard_map/pallas_call | solution.py:171
  230.3 3.5 collective-permute-start.16
  233.8 7.1 %shard_map.120.q_ref = f32[1024,512]{1,0:T(8,128)} custom-call(s32[8]{0:T(128)} %stack.186.index_ref, s32[5,8]{1,0:T(8,128)} %stack.170.meta_ref, bf16[1024,512]{1,0:T(8,128)(2,1)} %collective-permute-done.5.refs_0_, bf16[1024,512]{1,0:T(8,128)(2,1)} %collective-permute-done.7.refs_1_, bf16[1024,512]{1,0:T(8,128)(2,1)} %copy-done.4, ...), custom_call_target="tpu_custom_call", output_to_operand_aliasing={{}: (14, {})} | custom-call | flops 2147483648 | bytes 10485760 | tf_op jit(solution)/shard_map/pallas_call | solution.py:171
  241.6 6.5 %shard_map.128 = (bf16[512,512]{1,0:T(8,128)(2,1)}, f32[512,64]{1,0:T(8,128)}) custom-call(s32[5,8]{1,0:T(8,128)} %stack.170.meta_ref, f32[1024,512]{1,0:T(8,128)} %shard_map.120.q_ref, bf16[1024,192]{1,0:T(8,128)(2,1)} %bitcast.89, bf16[8,64,1152]{2,1,0:T(8,128)(2,1)} %copy-done.1, bf16[8,256,512]{2,1,0:T(8,128)(2,1)} %copy-done, ...), custom_call_target="tpu_custom_call" | custom-call | flops 402653184 | bytes 2097152 | tf_op jit(solution)/shard_map/pallas_call | solution.py:268
  251.4 6.5 %shard_map.124 = (bf16[512,512]{1,0:T(8,128)(2,1)}, f32[512,64]{1,0:T(8,128)}) custom-call(s32[5,8]{1,0:T(8,128)} %stack.170.meta_ref, f32[1024,512]{1,0:T(8,128)} %shard_map.120.q_ref, bf16[1024,192]{1,0:T(8,128)(2,1)} %bitcast.90, bf16[8,64,1152]{2,1,0:T(8,128)(2,1)} %copy-done.1, bf16[8,256,512]{2,1,0:T(8,128)(2,1)} %copy-done, ...), custom_call_target="tpu_custom_call" | custom-call | flops 402653184 | bytes 2097152 | tf_op jit(solution)/shard_map/pallas_call | solution.py:268
  258.0 3.2 collective-permute-start.18
  263.7 3.3 collective-permute-start.33
  268.3 6.5 %collective-permute-done.17.refs_1_ = bf16[512,512]{1,0:T(8,128)(2,1)S(1)} collective-permute-done((bf16[512,512]{1,0:T(8,128)(2,1)}, bf16[512,512]{1,0:T(8,128)(2,1)S(1)}, u32[]{:S(2)}, u32[]{:S(2)}) %collective-permute-start.17) | collective-permute-done | bytes 524320 | tf_op jit(solution)/shard_map/ppermute | solution.py:32
  274.9 3.5 collective-permute-start.20
  281.1 4.8 %shard_map.130 = (bf16[512,256]{1,0:T(8,128)(2,1)}, bf16[512,256]{1,0:T(8,128)(2,1)}) custom-call(s32[6]{0:T(128)} %stack.220.index_ref, bf16[512,512]{1,0:T(8,128)(2,1)} %get-tuple-element.58.refs_0_, bf16[512,512]{1,0:T(8,128)(2,1)} %copy-done.9, bf16[512,512]{1,0:T(8,128)(2,1)} %copy-done.10, bf16[512,256]{1,0:T(8,128)(2,1)} %copy-done.27, ...), custom_call_target="tpu_custom_call" | custom-call | flops 1073741824 | bytes 4194304 | tf_op jit(solution)/shard_map/pallas_call | solution.py:341
  288.0 9.5 %shard_map.129 = (bf16[512,256]{1,0:T(8,128)(2,1)}, bf16[512,256]{1,0:T(8,128)(2,1)}, bf16[512,256]{1,0:T(8,128)(2,1)}, bf16[512,256]{1,0:T(8,128)(2,1)}, f32[512,256]{1,0:T(8,128)}, /*index=5*/f32[512,256]{1,0:T(8,128)}) custom-call(s32[10]{0:T(128)} %stack.177.index_ref, bf16[512,512]{1,0:T(8,128)(2,1)} %get-tuple-element.58.refs_0_, ...), custom_call_target="tpu_custom_call" | custom-call | flops 3221225472 | bytes 8388608 | tf_op jit(solution)/shard_map/pallas_call | solution.py:341
  299.1 4.8 %shard_map.127 = (bf16[512,256]{1,0:T(8,128)(2,1)}, bf16[512,256]{1,0:T(8,128)(2,1)}) custom-call(s32[6]{0:T(128)} %stack.220.index_ref, bf16[512,512]{1,0:T(8,128)(2,1)} %get-tuple-element.48.refs_0_, bf16[512,512]{1,0:T(8,128)(2,1)} %copy-done.7, bf16[512,512]{1,0:T(8,128)(2,1)} %copy-done.8, bf16[512,256]{1,0:T(8,128)(2,1)} %collective-permute-done.19.refs_3_, ...), custom_call_target="tpu_custom_call" | custom-call | flops 1073741824 | bytes 4194304 | tf_op jit(solution)/shard_map/pallas_call | solution.py:341
  306.0 9.6 %shard_map.126 = (bf16[512,256]{1,0:T(8,128)(2,1)}, bf16[512,256]{1,0:T(8,128)(2,1)}, bf16[512,256]{1,0:T(8,128)(2,1)}, bf16[512,256]{1,0:T(8,128)(2,1)}, f32[512,256]{1,0:T(8,128)}, /*index=5*/f32[512,256]{1,0:T(8,128)}) custom-call(s32[10]{0:T(128)} %stack.177.index_ref, bf16[512,512]{1,0:T(8,128)(2,1)} %get-tuple-element.48.refs_0_, ...), custom_call_target="tpu_custom_call" | custom-call | flops 3221225472 | bytes 8388608 | tf_op jit(solution)/shard_map/pallas_call | solution.py:341
  319.7 4.1 %all-to-all-start.4 = ((f32[16,32,128]{2,1,0:T(8,128)}), f32[16,32,128]{2,1,0:T(8,128)S(1)}, u32[]{:S(2)}, u32[]{:S(2)}) async-start(f32[16,32,128]{2,1,0:T(8,128)} %bitcast.61), calls=%async_computation.4 | async-start | bytes 524288 | tf_op jit(solution)/shard_map/all_to_all | solution.py:119
  334.1 13.2 %all_to_all.30 = bf16[16,32,128]{2,1,0:T(8,128)(2,1)} all-to-all(bf16[16,32,128]{2,1,0:T(8,128)(2,1)S(1)} %broadcast_in_dim.77), channel_id=1, replica_groups=mesh['z'=4,'c'=2,'y'=4,'x'=4] {'y','x'}, dimensions={0} | all-to-all | bytes 262144 | tf_op jit(solution)/shard_map/all_to_all | solution.py:124
  348.4 5.9 %shard_map.131 = f32[1024,512]{1,0:T(8,128)} custom-call(s32[5,8]{1,0:T(8,128)} %stack.170.meta_ref, f32[512,256]{1,0:T(8,128)} %get-tuple-element.50.refs_0_, bf16[512,256]{1,0:T(8,128)(2,1)} %copy-done.18, bf16[512,256]{1,0:T(8,128)(2,1)} %copy-done.26, f32[512,256]{1,0:T(8,128)} %get-tuple-element.54.refs_3_, bf16[512,256]{1,0:T(8,128)(2,1)} %copy-done.19, ...), custom_call_target="tpu_custom_call" | custom-call | flops 67108864 | bytes 7340032 | tf_op jit(solution)/shard_map/pallas_call | solution.py:420
  (192 shorter events, 93.3 us)
Async XLA Ops:
  30.8 32.6 %all-to-all-start = ((bf16[8,256,512]{2,1,0:T(8,128)(2,1)}), bf16[8,256,512]{2,1,0:T(8,128)(2,1)S(1)}, u32[]{:S(2)}, u32[]{:S(2)}) async-start(bf16[8,256,512]{2,1,0:T(8,128)(2,1)} %get-tuple-element.45), calls=%async_computation | async-start | bytes 4194304 | tf_op jit(solution)/shard_map/all_to_all | solution.py:494
  36.2 244.1 %all-gather.3.cloned.1.call-start = ((), (), s32[]{:S(2)}) async-start(), calls=%async_computation.6 | async-start | bytes 9437184 | tf_op jit(solution)/shard_map/all_gather | solution.py:503
  90.8 17.4 %collective-permute-start.2 = (bf16[1024,128]{1,0:T(8,128)(2,1)S(1)}, bf16[1024,128]{1,0:T(8,128)(2,1)S(1)}, u32[]{:S(2)}, u32[]{:S(2)}) collective-permute-start(bf16[1024,128]{1,0:T(8,128)(2,1)S(1)} %slice.72), channel_id=1, source_target_pairs={{0,1},{1,2},{2,3},{3,0},{4,5},{5,6},{6,7},{7,4},{8,9},{9,10},{10,1... | collective-permute-start | bytes 786440 | tf_op jit(solution)/shard_map/ppermute | solution.py:32
  109.7 70.9 %collective-permute-start.4 = (bf16[1024,1024]{1,0:T(8,128)(2,1)}, bf16[1024,1024]{1,0:T(8,128)(2,1)S(1)}, u32[]{:S(2)}, u32[]{:S(2)}) collective-permute-start(bf16[1024,1024]{1,0:T(8,128)(2,1)} %constant_dynamic-update-slice_fusion.refs_0_), channel_id=1, source_target_pairs={{0,4},{4,8},{8,12},{12,0},{1,5},{5,9},{9,13},{13,1},{2,6},{6,10},{... | collective-permute-start | bytes 6291464 | tf_op jit(solution)/shard_map/ppermute | solution.py:32
  109.7 72.7 %collective-permute-start.6 = (bf16[1024,1024]{1,0:T(8,128)(2,1)}, bf16[1024,1024]{1,0:T(8,128)(2,1)}, u32[]{:S(2)}, u32[]{:S(2)}) collective-permute-start(bf16[1024,1024]{1,0:T(8,128)(2,1)} %constant_dynamic-update-slice_fusion.refs_0_), channel_id=1, source_target_pairs={{0,12},{4,0},{8,4},{12,8},{1,13},{5,1},{9,5},{13,9},{2,14},{6,2},{... | collective-permute-start | bytes 6291464 | tf_op jit(solution)/shard_map/ppermute | solution.py:32
  114.4 72.9 %collective-permute-start.12 = (bf16[1024,1024]{1,0:T(8,128)(2,1)}, bf16[1024,1024]{1,0:T(8,128)(2,1)}, u32[]{:S(2)}, u32[]{:S(2)}) collective-permute-start(bf16[1024,1024]{1,0:T(8,128)(2,1)} %constant_dynamic-update-slice_fusion.5.refs_1_), channel_id=1, source_target_pairs={{0,1},{1,2},{2,3},{3,0},{4,5},{5,6},{6,7},{7,4},{8,9},{9,10},{10,1... | collective-permute-start | bytes 6291464 | tf_op jit(solution)/shard_map/ppermute | solution.py:32
  114.5 75.7 %collective-permute-start.14 = (bf16[1024,1024]{1,0:T(8,128)(2,1)}, bf16[1024,1024]{1,0:T(8,128)(2,1)}, u32[]{:S(2)}, u32[]{:S(2)}) collective-permute-start(bf16[1024,1024]{1,0:T(8,128)(2,1)} %constant_dynamic-update-slice_fusion.5.refs_1_), channel_id=1, source_target_pairs={{0,3},{1,0},{2,1},{3,2},{4,7},{5,4},{6,5},{7,6},{8,11},{9,8},{10,9... | collective-permute-start | bytes 6291464 | tf_op jit(solution)/shard_map/ppermute | solution.py:32
  123.7 47.4 %all-to-all-start.1 = ((f32[16,64,192]{2,1,0:T(8,128)}), f32[16,64,192]{2,1,0:T(8,128)S(1)}, u32[]{:S(2)}, u32[]{:S(2)}) async-start(f32[16,64,192]{2,1,0:T(8,128)} %bitcast.91), calls=%async_computation.1 | async-start | bytes 2097152 | tf_op jit(solution)/shard_map/all_to_all | solution.py:119
  172.0 32.7 %all-to-all-start.3 = ((bf16[8,64,1152]{2,1,0:T(8,128)(2,1)}), bf16[8,64,1152]{2,1,0:T(8,128)(2,1)S(1)}, u32[]{:S(2)}, u32[]{:S(2)}) async-start(bf16[8,64,1152]{2,1,0:T(8,128)(2,1)} %get-tuple-element.46), calls=%async_computation.3 | async-start | bytes 2359296 | tf_op jit(solution)/shard_map/all_to_all | solution.py:495
  181.8 41.9 %collective-permute-start.5 = (bf16[1024,512]{1,0:T(8,128)(2,1)}, bf16[1024,512]{1,0:T(8,128)(2,1)}, u32[]{:S(2)}, u32[]{:S(2)}) collective-permute-start(bf16[1024,512]{1,0:T(8,128)(2,1)} %slice.74), channel_id=1, source_target_pairs={{0,4},{4,8},{8,12},{12,0},{1,5},{5,9},{9,13},{13,1},{2,6},{6,10},{... | collective-permute-start | bytes 3145736 | tf_op jit(solution)/shard_map/ppermute | solution.py:32
  184.6 39.1 %collective-permute-start.7 = (bf16[1024,512]{1,0:T(8,128)(2,1)}, bf16[1024,512]{1,0:T(8,128)(2,1)}, u32[]{:S(2)}, u32[]{:S(2)}) collective-permute-start(bf16[1024,512]{1,0:T(8,128)(2,1)} %slice.75), channel_id=1, source_target_pairs={{0,12},{4,0},{8,4},{12,8},{1,13},{5,1},{9,5},{13,9},{2,14},{6,2},{... | collective-permute-start | bytes 3145736 | tf_op jit(solution)/shard_map/ppermute | solution.py:32
  189.6 34.1 %collective-permute-start.13 = (bf16[1024,512]{1,0:T(8,128)(2,1)}, bf16[1024,512]{1,0:T(8,128)(2,1)S(1)}, u32[]{:S(2)}, u32[]{:S(2)}) collective-permute-start(bf16[1024,512]{1,0:T(8,128)(2,1)} %slice.78), channel_id=1, source_target_pairs={{0,1},{1,2},{2,3},{3,0},{4,5},{5,6},{6,7},{7,4},{8,9},{9,10},{10,1... | collective-permute-start | bytes 3145736 | tf_op jit(solution)/shard_map/ppermute | solution.py:32
  192.6 31.2 %collective-permute-start.15 = (bf16[1024,512]{1,0:T(8,128)(2,1)}, bf16[1024,512]{1,0:T(8,128)(2,1)}, u32[]{:S(2)}, u32[]{:S(2)}) collective-permute-start(bf16[1024,512]{1,0:T(8,128)(2,1)} %slice.79), channel_id=1, source_target_pairs={{0,3},{1,0},{2,1},{3,2},{4,7},{5,4},{6,5},{7,6},{8,11},{9,8},{10,9... | collective-permute-start | bytes 3145736 | tf_op jit(solution)/shard_map/ppermute | solution.py:32
  205.7 18.0 %all-to-all-start.2 = ((bf16[16,64,192]{2,1,0:T(8,128)(2,1)}), bf16[16,64,192]{2,1,0:T(8,128)(2,1)S(1)}, u32[]{:S(2)}, u32[]{:S(2)}) async-start(bf16[16,64,192]{2,1,0:T(8,128)(2,1)} %broadcast_in_dim.76), calls=%async_computation.2 | async-start | bytes 1048576 | tf_op jit(solution)/shard_map/all_to_all | solution.py:124
  248.2 15.3 %collective-permute-start.30 = (bf16[512,512]{1,0:T(8,128)(2,1)}, bf16[512,512]{1,0:T(8,128)(2,1)S(1)}, u32[]{:S(2)}, u32[]{:S(2)}) collective-permute-start(bf16[512,512]{1,0:T(8,128)(2,1)} %get-tuple-element.58.refs_0_), channel_id=1, source_target_pairs={{0,4},{4,8},{8,12},{12,0},{1,5},{5,9},{9,13},{13,1},{2,6},{6,10},{... | collective-permute-start | bytes 1572872 | tf_op jit(solution)/shard_map/ppermute | solution.py:32
  257.9 16.8 %collective-permute-start.17 = (bf16[512,512]{1,0:T(8,128)(2,1)}, bf16[512,512]{1,0:T(8,128)(2,1)S(1)}, u32[]{:S(2)}, u32[]{:S(2)}) collective-permute-start(bf16[512,512]{1,0:T(8,128)(2,1)} %get-tuple-element.48.refs_0_), channel_id=1, source_target_pairs={{0,4},{4,8},{8,12},{12,0},{1,5},{5,9},{9,13},{13,1},{2,6},{6,10},{... | collective-permute-start | bytes 1572872 | tf_op jit(solution)/shard_map/ppermute | solution.py:32
  258.0 16.9 %collective-permute-start.18 = (bf16[512,512]{1,0:T(8,128)(2,1)}, bf16[512,512]{1,0:T(8,128)(2,1)S(1)}, u32[]{:S(2)}, u32[]{:S(2)}) collective-permute-start(bf16[512,512]{1,0:T(8,128)(2,1)} %get-tuple-element.48.refs_0_), channel_id=1, source_target_pairs={{0,12},{4,0},{8,4},{12,8},{1,13},{5,1},{9,5},{13,9},{2,14},{6,2},{... | collective-permute-start | bytes 1572872 | tf_op jit(solution)/shard_map/ppermute | solution.py:32
  263.5 16.8 %collective-permute-start.32 = (bf16[512,256]{1,0:T(8,128)(2,1)S(1)}, bf16[512,256]{1,0:T(8,128)(2,1)S(1)}, u32[]{:S(2)}, u32[]{:S(2)}) collective-permute-start(bf16[512,256]{1,0:T(8,128)(2,1)S(1)} %slice.86), channel_id=1, source_target_pairs={{0,4},{4,8},{8,12},{12,0},{1,5},{5,9},{9,13},{13,1},{2,6},{6,10},{... | collective-permute-start | bytes 786440 | tf_op jit(solution)/shard_map/ppermute | solution.py:32
  263.7 16.7 %collective-permute-start.33 = (bf16[512,256]{1,0:T(8,128)(2,1)S(1)}, bf16[512,256]{1,0:T(8,128)(2,1)}, u32[]{:S(2)}, u32[]{:S(2)}) collective-permute-start(bf16[512,256]{1,0:T(8,128)(2,1)S(1)} %slice.87), channel_id=1, source_target_pairs={{0,12},{4,0},{8,4},{12,8},{1,13},{5,1},{9,5},{13,9},{2,14},{6,2},{... | collective-permute-start | bytes 786440 | tf_op jit(solution)/shard_map/ppermute | solution.py:32
  274.8 24.4 %collective-permute-start.19 = (bf16[512,256]{1,0:T(8,128)(2,1)S(1)}, bf16[512,256]{1,0:T(8,128)(2,1)}, u32[]{:S(2)}, u32[]{:S(2)}) collective-permute-start(bf16[512,256]{1,0:T(8,128)(2,1)S(1)} %slice.80), channel_id=1, source_target_pairs={{0,4},{4,8},{8,12},{12,0},{1,5},{5,9},{9,13},{13,1},{2,6},{6,10},{... | collective-permute-start | bytes 786440 | tf_op jit(solution)/shard_map/ppermute | solution.py:32
  274.9 24.3 %collective-permute-start.20 = (bf16[512,256]{1,0:T(8,128)(2,1)S(1)}, bf16[512,256]{1,0:T(8,128)(2,1)}, u32[]{:S(2)}, u32[]{:S(2)}) collective-permute-start(bf16[512,256]{1,0:T(8,128)(2,1)S(1)} %slice.81), channel_id=1, source_target_pairs={{0,12},{4,0},{8,4},{12,8},{1,13},{5,1},{9,5},{13,9},{2,14},{6,2},{... | collective-permute-start | bytes 786440 | tf_op jit(solution)/shard_map/ppermute | solution.py:32
  285.9 29.7 %collective-permute-start.38 = (bf16[512,256]{1,0:T(8,128)(2,1)}, bf16[512,256]{1,0:T(8,128)(2,1)S(1)}, u32[]{:S(2)}, u32[]{:S(2)}) collective-permute-start(bf16[512,256]{1,0:T(8,128)(2,1)} %get-tuple-element.66), channel_id=1, source_target_pairs={{0,3},{1,0},{2,1},{3,2},{4,7},{5,4},{6,5},{7,6},{8,11},{9,8},{10,9... | collective-permute-start | bytes 786440 | tf_op jit(solution)/shard_map/ppermute | solution.py:32
  286.4 29.7 %collective-permute-start.35 = (bf16[512,256]{1,0:T(8,128)(2,1)}, bf16[512,256]{1,0:T(8,128)(2,1)S(1)}, u32[]{:S(2)}, u32[]{:S(2)}) collective-permute-start(bf16[512,256]{1,0:T(8,128)(2,1)} %get-tuple-element.62), channel_id=1, source_target_pairs={{0,1},{1,2},{2,3},{3,0},{4,5},{5,6},{6,7},{7,4},{8,9},{9,10},{10,1... | collective-permute-start | bytes 786440 | tf_op jit(solution)/shard_map/ppermute | solution.py:32
  297.5 31.0 %collective-permute-start.34 = (bf16[512,256]{1,0:T(8,128)(2,1)}, bf16[512,256]{1,0:T(8,128)(2,1)S(1)}, u32[]{:S(2)}, u32[]{:S(2)}) collective-permute-start(bf16[512,256]{1,0:T(8,128)(2,1)} %get-tuple-element.60), channel_id=1, source_target_pairs={{0,3},{1,0},{2,1},{3,2},{4,7},{5,4},{6,5},{7,6},{8,11},{9,8},{10,9... | collective-permute-start | bytes 786440 | tf_op jit(solution)/shard_map/ppermute | solution.py:32
  304.0 20.0 %collective-permute-start.28 = (bf16[512,256]{1,0:T(8,128)(2,1)}, bf16[512,256]{1,0:T(8,128)(2,1)S(1)}, u32[]{:S(2)}, u32[]{:S(2)}) collective-permute-start(bf16[512,256]{1,0:T(8,128)(2,1)} %get-tuple-element.57), channel_id=1, source_target_pairs={{0,3},{1,0},{2,1},{3,2},{4,7},{5,4},{6,5},{7,6},{8,11},{9,8},{10,9... | collective-permute-start | bytes 786440 | tf_op jit(solution)/shard_map/ppermute | solution.py:32
  304.3 22.8 %collective-permute-start.25 = (bf16[512,256]{1,0:T(8,128)(2,1)}, bf16[512,256]{1,0:T(8,128)(2,1)S(1)}, u32[]{:S(2)}, u32[]{:S(2)}) collective-permute-start(bf16[512,256]{1,0:T(8,128)(2,1)} %get-tuple-element.53), channel_id=1, source_target_pairs={{0,1},{1,2},{2,3},{3,0},{4,5},{5,6},{6,7},{7,4},{8,9},{9,10},{10,1... | collective-permute-start | bytes 786440 | tf_op jit(solution)/shard_map/ppermute | solution.py:32
  316.1 15.8 %collective-permute-start.24 = (bf16[512,256]{1,0:T(8,128)(2,1)}, bf16[512,256]{1,0:T(8,128)(2,1)S(1)}, u32[]{:S(2)}, u32[]{:S(2)}) collective-permute-start(bf16[512,256]{1,0:T(8,128)(2,1)} %get-tuple-element.51), channel_id=1, source_target_pairs={{0,3},{1,0},{2,1},{3,2},{4,7},{5,4},{6,5},{7,6},{8,11},{9,8},{10,9... | collective-permute-start | bytes 786440 | tf_op jit(solution)/shard_map/ppermute | solution.py:32
  324.0 23.2 %collective-permute-start.27 = (bf16[512,256]{1,0:T(8,128)(2,1)}, bf16[512,256]{1,0:T(8,128)(2,1)S(1)}, u32[]{:S(2)}, u32[]{:S(2)}) collective-permute-start(bf16[512,256]{1,0:T(8,128)(2,1)} %get-tuple-element.55), channel_id=1, source_target_pairs={{0,1},{1,2},{2,3},{3,0},{4,5},{5,6},{6,7},{7,4},{8,9},{9,10},{10,1... | collective-permute-start | bytes 786440 | tf_op jit(solution)/shard_map/ppermute | solution.py:32
  327.0 20.2 %collective-permute-start.39 = (bf16[512,256]{1,0:T(8,128)(2,1)S(1)}, bf16[512,256]{1,0:T(8,128)(2,1)S(1)}, u32[]{:S(2)}, u32[]{:S(2)}) collective-permute-start(bf16[512,256]{1,0:T(8,128)(2,1)S(1)} %add.315), channel_id=1, source_target_pairs={{0,3},{1,0},{2,1},{3,2},{4,7},{5,4},{6,5},{7,6},{8,11},{9,8},{10,9... | collective-permute-start | bytes 786440 | tf_op jit(solution)/shard_map/ppermute | solution.py:32
  328.5 18.8 %collective-permute-start.36 = (bf16[512,256]{1,0:T(8,128)(2,1)S(1)}, bf16[512,256]{1,0:T(8,128)(2,1)S(1)}, u32[]{:S(2)}, u32[]{:S(2)}) collective-permute-start(bf16[512,256]{1,0:T(8,128)(2,1)S(1)} %add.314), channel_id=1, source_target_pairs={{0,1},{1,2},{2,3},{3,0},{4,5},{5,6},{6,7},{7,4},{8,9},{9,10},{10,1... | collective-permute-start | bytes 786440 | tf_op jit(solution)/shard_map/ppermute | solution.py:32
  329.3 18.0 %collective-permute-start.29 = (bf16[512,256]{1,0:T(8,128)(2,1)S(1)}, bf16[512,256]{1,0:T(8,128)(2,1)S(1)}, u32[]{:S(2)}, u32[]{:S(2)}) collective-permute-start(bf16[512,256]{1,0:T(8,128)(2,1)S(1)} %add.313), channel_id=1, source_target_pairs={{0,3},{1,0},{2,1},{3,2},{4,7},{5,4},{6,5},{7,6},{8,11},{9,8},{10,9... | collective-permute-start | bytes 786440 | tf_op jit(solution)/shard_map/ppermute | solution.py:32
  331.8 15.5 %collective-permute-start.26 = (bf16[512,256]{1,0:T(8,128)(2,1)S(1)}, bf16[512,256]{1,0:T(8,128)(2,1)S(1)}, u32[]{:S(2)}, u32[]{:S(2)}) collective-permute-start(bf16[512,256]{1,0:T(8,128)(2,1)S(1)} %add.312), channel_id=1, source_target_pairs={{0,1},{1,2},{2,3},{3,0},{4,5},{5,6},{6,7},{7,4},{8,9},{9,10},{10,1... | collective-permute-start | bytes 786440 | tf_op jit(solution)/shard_map/ppermute | solution.py:32
  (45 other events, 463.6 us)
Sparse Core Ops, SparseCore 0:
  86.1 46.8 all-gather.2

commit v3 on v2

--- a/solution.py
+++ b/solution.py
@@ -41,6 +41,11 @@
     return block, behind, ahead, far_low, far_high
 
 
+def second_gather(low, high, axis):
+    onward = shift(low, axis, 1), shift(high, axis, -1)
+    return onward, (shift(high, axis, 1), shift(low, axis, -1))
+
+
 def ring_order(index):
     return [index, (index + SIDE - 1) % SIDE, (index + 1) % SIDE, (index + 2) % SIDE]
 
@@ -114,14 +119,23 @@
 
 
 def sum_over_tensor(partial):
+    mine, spread = sum_over_tensor_in_two(partial)
+    return spread(mine)
+
+
+def sum_over_tensor_in_two(partial):
     rows, rank = partial.shape
     ways = SIDE * SIDE
     pieces = lax.all_to_all(
         partial.reshape(ways, rows // ways, rank), TENSOR_AXES, 0, 0, tiled=True
     )
     mine = jnp.sum(pieces, axis=0).astype(bf16)
-    copies = jnp.broadcast_to(mine[None], (ways,) + mine.shape)
-    return lax.all_to_all(copies, TENSOR_AXES, 0, 0, tiled=True).reshape(rows, rank)
+
+    def spread(mine):
+        copies = jnp.broadcast_to(mine[None], (ways,) + mine.shape)
+        return lax.all_to_all(copies, TENSOR_AXES, 0, 0, tiled=True).reshape(rows, rank)
+
+    return mine, spread
 
 
 def project(index, total, blocks, weights, tile, last=None, rows=256):
@@ -471,9 +485,17 @@
 
     half = local // 2
     ys, xs = ring_order(y), ring_order(xi)
-    flat_first = ring_gather(x[:, :half], "x")
-    flat_a = jnp.concatenate(flat_first, axis=1)
-    flat_b = jnp.concatenate(ring_gather(x[:, half:], "y"), axis=1)
+    first_a = ring_gather(x[:, :half], "x")
+    first_b = ring_gather(x[:, half:], "y")
+    low_a, high_a = jnp.concatenate(first_a[:2], axis=1), jnp.concatenate(first_a[2:], axis=1)
+    low_b, high_b = jnp.concatenate(first_b[:2], axis=1), jnp.concatenate(first_b[2:], axis=1)
+
+    stores = (jnp.swapaxes(down_qkv, 1, 2), up_q, up_kv, jnp.swapaxes(down_o, 1, 2), up_o)
+    down_out, up_out = pick_adapters(pick, *stores)
+    down = lax.all_to_all(down_out, ADAPTER_AXES, 0, 0, tiled=True)
+
+    far_a, next_a = second_gather(low_a, high_a, "y")
+    far_b, next_b = second_gather(low_b, high_b, "x")
 
     def rows_a(k, cols):
         return [(ys[k] * SIDE + xs[j]) * 2 for j in cols]
@@ -485,50 +507,65 @@
         return jnp.stack(rows).astype(i32)
 
     every = range(SIDE)
-    a0, a1, a2, a3, a4 = ring_gather(flat_a, "y")
-    b0, b1, b2, b3, b4 = ring_gather(flat_b, "x")
-
-    stores = (jnp.swapaxes(down_qkv, 1, 2), up_q, up_kv, jnp.swapaxes(down_o, 1, 2), up_o)
-    stores, _ = lax.optimization_barrier((stores, flat_first[1]))
-    down_out, up_out = pick_adapters(pick, *stores)
-    down = lax.all_to_all(down_out, ADAPTER_AXES, 0, 0, tiled=True)
+    low, high = (0, 1), (2, 3)
+    total = project(
+        (index_of(rows_a(0, every) + rows_b(0, every)), meta),
+        None,
+        [low_a, high_a, low_b, high_b],
+        [wq, wkv],
+        512,
+    )
+
+    own, down, _ = lax.optimization_barrier((x, down, (low_a, high_a, low_b, high_b)))
+    partial = rank_partial(meta, own, down, 3 * rank)
+    shrunk = sum_over_tensor(partial)
+    up_out, _ = lax.optimization_barrier((up_out, partial))
     up = lax.all_to_all(up_out, ADAPTER_AXES, 0, 0, tiled=True)
-    shrunk = sum_over_tensor(rank_partial(meta, x, down, 3 * rank))
 
     unit = wo.shape[1] // (SIDE * SIDE * 2)
-    tied, _ = lax.optimization_barrier((wo, down))
+    tied, total = lax.optimization_barrier((wo, total))
     order = ring_order(y)
     sent = pick_columns(jnp.stack(order).astype(i32) * (2 * SIDE) + group, tied, unit)
     got = [sent[0], shift(sent[2], "y", 1), shift(sent[1], "y", -1), shift(sent[3], "y", 2)]
     wo_all = lax.all_gather(jnp.concatenate(got, axis=0), ADAPTER_AXES, axis=0)
 
+    far_a, total = lax.optimization_barrier((far_a, total))
+    a_low, a_high = shift(far_a[0], "y", 1), shift(far_a[1], "y", -1)
+    b_low, b_high = shift(far_b[0], "x", 1), shift(far_b[1], "x", -1)
     total = project(
-        (index_of(rows_a(0, every) + rows_b(0, every)), meta), None, [a0, b0], [wq, wkv], 512
-    )
-    total = project(
-        (index_of(rows_a(1, every) + rows_a(2, every) + rows_b(1, every) + rows_b(2, every)), meta),
+        (
+            index_of(
+                rows_a(1, low) + rows_a(2, high) + rows_b(1, low) + rows_b(2, high)
+                + rows_a(1, high) + rows_a(2, low) + rows_b(1, high) + rows_b(2, low)
+            ),
+            meta,
+        ),
         total,
-        [a1, a2, b1, b2],
+        [*far_a, *far_b, *next_a, *next_b],
         [wq, wkv],
         512,
     )
     final = (index_of(rows_a(3, every) + rows_b(3, every)), meta)
-    far = [a3, a4, b3, b4]
+    far = [a_low, a_high, b_low, b_high]
     tail = key_value_tail(shrunk, up, cosine, sine, wide, wkv.shape[1], 512)
     (mine,) = project(final, total[1:], far, [wkv], 512, tail)
     other = lax.ppermute(mine, "x", [(i, i ^ 1) for i in range(SIDE)])
     (q,) = project(final, total[:1], far, [wq], 512)
 
     cuts = 2
-    parts, ranks = [], []
+    pieces, ranks = [], []
     for cut in range(cuts):
         attended, head = attention(
             meta, q, shrunk, up, down, mine, other, cosine, sine, cut * blocks // cuts, blocks // cuts
         )
         ranks.append(head)
-        parts.append(output_ring(ring_gather(attended, "y"), wo_all, "x", [jnp.int32(k) for k in range(SIDE)]))
-    head_rank = sum_over_tensor(jnp.concatenate(ranks, axis=1))
-    return finish(meta, parts, head_rank, up, wide)
+        pieces.append(ring_gather(attended, "y"))
+    mine_rank, spread = sum_over_tensor_in_two(jnp.concatenate(ranks, axis=1))
+    places = [jnp.int32(k) for k in range(SIDE)]
+    parts = [output_ring(pieces[0], wo_all, "x", places)]
+    last, mine_rank = lax.optimization_barrier((pieces[1], mine_rank))
+    parts.append(output_ring(last, wo_all, "x", places))
+    return finish(meta, parts, spread(mine_rank), up, wide)
 
 
 def solution(mesh):

time: 363 us -> 368 us (1.014)
  waiting for transfers between devices: 114 us -> 125 us
  local copies, waits for them, and re-layouts: 30.3 us -> 19.6 us
    all_to_all x3, waiting for transfers between devices: 46.5 us -> 21.1 us  [the longest x2 18.1 us: sum_over_tensor_in_two(): lax.all_to_all(partial.reshape(ways, rows // ways, rank), TENSOR_AXES, 0,...]
    all_to_all x1, waiting for transfers between devices: 26.6 us -> 46.1 us  [on_device(): down = lax.all_to_all(down_out, ADAPTER_AXES, 0, 0, tiled=True)]
    ppermute x39 -> x43, waiting for transfers between devices: 41.4 us -> 57.2 us  [shift(): lax.ppermute(block, axis, [(i, (i + step) % SIDE) for i in range(SIDE)])]
    slice x6 -> x4, local copies, waits for them, and re-layouts: 4.62 us -> 0.07 us  [ring_gather(): far_high = shift(ahead[:, half:], axis, -1)]
    ppermute x39 -> x43, starting transfers between devices: 60.5 us -> 63.4 us  [shift(): lax.ppermute(block, axis, [(i, (i + step) % SIDE) for i in range(SIDE)])]
    unnamed x68 -> x58, local copies, waits for them, and re-layouts: 9.42 us -> 7.79 us
  transfers between devices with their start and end apart: 46 -> 50, of which waited for: 12 -> 14; matrix products, arithmetic and copies ran while one was open for 8% -> 6% of each run, Pallas kernels for 22% -> 22%
where the time goes in v3:
time: 368 us; the launch traced here: 366 us
  waiting for transfers between devices  125 us (34%)
  Pallas kernels  97.6 us (27%)
  starting transfers between devices  87.1 us (24%)
  local copies, waits for them, and re-layouts  19.6 us (5%)
  between operations  14 us (4%)
  blocking collectives  13.3 us (4%)
  other arithmetic  9.71 us (3%)
    ppermute x43, starting transfers between devices, shift(): lax.ppermute(block, axis, [(i, (i + step) % SIDE) for i in range(SIDE)])  63.4 us
    ppermute x43, waiting for transfers between devices, shift(): lax.ppermute(block, axis, [(i, (i + step) % SIDE) for i in range(SIDE)])  57.2 us
    all_to_all x1, waiting for transfers between devices, on_device(): down = lax.all_to_all(down_out, ADAPTER_AXES, 0, 0, tiled=True)  46.1 us
    pallas_call x4, Pallas kernels, project(): pl.pallas_call(body, out_shape=tuple((jax.ShapeDtypeStruct((tokens, w), d...  33.8 us
    pallas_call x4, Pallas kernels, output_partial(): pl.pallas_call(body, out_shape=tuple((jax.ShapeDtypeStruct((tokens, width...  28.8 us
    all_to_all x2, waiting for transfers between devices, sum_over_tensor_in_two(): lax.all_to_all(partial.reshape(ways, rows // ways, rank), TENSOR_AXES, 0,...  18.1 us
    all_to_all x1, blocking collectives, spread(): lax.all_to_all(copies, TENSOR_AXES, 0, 0, tiled=True).reshape(rows, rank)  13.3 us
    pallas_call x2, Pallas kernels, attention(): pl.pallas_call(body, out_shape=(jax.ShapeDtypeStruct((count * BLOCK, wide...  13 us
  transfers between devices with their start and end apart: 50, of which 14 were waited for; matrix products, arithmetic and copies ran while one was open for 6% of the time, Pallas kernels for 22%

profile of v3, /device:TPU:0, one launch (start us, length us, event | category | flops | bytes accessed | tf_op | source)
XLA Modules:
  0.0 365.8 jit_solution(5620272778330649323)
XLA Ops:
  7.9 3.2 collective-permute-start.7
  16.7 9.0 %collective-permute-done.6 = bf16[1024,256]{1,0:T(8,128)(2,1)S(1)} collective-permute-done((bf16[1024,256]{1,0:T(8,128)(2,1)S(1)}, bf16[1024,256]{1,0:T(8,128)(2,1)S(1)}, u32[]{:S(2)}, u32[]{:S(2)}) %collective-permute-start.6) | collective-permute-done | bytes 524320 | tf_op jit(solution)/shard_map/ppermute | solution.py:32
  25.8 3.3 collective-permute-start.9
  39.4 8.0 %shard_map.118 = (f32[1024,512]{1,0:T(8,128)}, f32[1024,128]{1,0:T(8,128)}) custom-call(s32[8]{0:T(128)} %stack.195.index_ref, s32[5,8]{1,0:T(8,128)} %stack.170.meta_ref, bf16[1024,512]{1,0:T(8,128)(2,1)} %pad_maximum_fusion.refs_0_, bf16[1024,512]{1,0:T(8,128)(2,1)} %constant_dynamic-update-slice_fusion.refs_1_, ...), custom_call_target="tpu_custom_call" | custom-call | flops 2684354560 | bytes 12058624 | tf_op jit(solution)/shard_map/pallas_call | solution.py:185
  47.4 4.0 %shard_map.125 = bf16[4,512,256]{2,1,0:T(8,128)(2,1)} custom-call(s32[4]{0:T(128)} %fusion.5.index_ref, bf16[512,8192]{1,0:T(8,128)(2,1)} %m_ref), custom_call_target="tpu_custom_call" | custom-call | bytes 2097152 | tf_op jit(solution)/shard_map/pallas_call | solution.py:320
  52.8 3.2 collective-permute-start.26
  56.2 6.5 %collective-permute-done.25 = bf16[512,256]{1,0:T(8,128)(2,1)S(1)} collective-permute-done((bf16[512,256]{1,0:T(8,128)(2,1)S(1)}, bf16[512,256]{1,0:T(8,128)(2,1)S(1)}, u32[]{:S(2)}, u32[]{:S(2)}) %collective-permute-start.25) | collective-permute-done | bytes 262176 | tf_op jit(solution)/shard_map/ppermute | solution.py:32
  66.7 6.9 %shard_map.121 = (bf16[8,256,512]{2,1,0:T(8,128)(2,1)}, bf16[8,64,1152]{2,1,0:T(8,128)(2,1)}) custom-call(s32[8]{0:T(128)} %get-tuple-element.93.pick_ref, bf16[8,192,512]{2,1,0:T(8,128)(2,1)} %bitcast.92, bf16[8,64,512]{2,1,0:T(8,128)(2,1)} %uq.1, bf16[8,64,128]{2,1,0:T(8,128)(2,1)} %ukv.1, bf16[8,64,512]{2,1,0:T(8,128)(2,1)} %bitcast.94, ...), custom_call_target="tpu_custom_call" | custom-call | bytes 6553600 | tf_op jit(solution)/shard_map/pallas_call | solution.py:71
  73.6 5.0 %all-to-all-start = ((bf16[8,256,512]{2,1,0:T(8,128)(2,1)}), bf16[8,256,512]{2,1,0:T(8,128)(2,1)S(1)}, u32[]{:S(2)}, u32[]{:S(2)}) async-start(bf16[8,256,512]{2,1,0:T(8,128)(2,1)} %get-tuple-element.56), calls=%async_computation | async-start | bytes 4194304 | tf_op jit(solution)/shard_map/all_to_all | solution.py:495
  82.3 46.1 %all-to-all-done.rest_0_.rest_1_.d_ref = bf16[8,256,512]{2,1,0:T(8,128)(2,1)S(1)} async-done(((bf16[8,256,512]{2,1,0:T(8,128)(2,1)}), bf16[8,256,512]{2,1,0:T(8,128)(2,1)S(1)}, u32[]{:S(2)}, u32[]{:S(2)}) %all-to-all-start) | async-done | bytes 2097184 | tf_op jit(solution)/shard_map/all_to_all | solution.py:495
  129.8 5.0 %shard_map.122 = f32[1024,192]{1,0:T(8,128)} custom-call(s32[5,8]{1,0:T(8,128)} %stack.170.meta_ref, bf16[1024,512]{1,0:T(8,128)(2,1)} %x_ref, bf16[8,256,512]{2,1,0:T(8,128)(2,1)} %copy-done, bf16[8,256,512]{2,1,0:T(8,128)(2,1)} %copy-done), custom_call_target="tpu_custom_call" | custom-call | flops 201326592 | bytes 2621440 | tf_op jit(solution)/shard_map/pallas_call | solution.py:106
  134.8 5.2 %all-to-all-start.1 = ((f32[16,64,192]{2,1,0:T(8,128)}), f32[16,64,192]{2,1,0:T(8,128)S(1)}, u32[]{:S(2)}, u32[]{:S(2)}) async-start(f32[16,64,192]{2,1,0:T(8,128)} %bitcast.91), calls=%async_computation.1 | async-start | bytes 2097152 | tf_op jit(solution)/shard_map/all_to_all | solution.py:129
  147.8 10.7 %all-to-all-done.1 = f32[16,64,192]{2,1,0:T(8,128)S(1)} async-done(((f32[16,64,192]{2,1,0:T(8,128)}), f32[16,64,192]{2,1,0:T(8,128)S(1)}, u32[]{:S(2)}, u32[]{:S(2)}) %all-to-all-start.1) | async-done | bytes 786464 | tf_op jit(solution)/shard_map/all_to_all | solution.py:129
  158.6 3.6 all-to-all-start.3
  162.1 15.4 %collective-permute-done.19.refs_7_ = bf16[1024,512]{1,0:T(8,128)(2,1)} collective-permute-done((bf16[1024,512]{1,0:T(8,128)(2,1)S(1)}, bf16[1024,512]{1,0:T(8,128)(2,1)}, u32[]{:S(2)}, u32[]{:S(2)}) %collective-permute-start.19) | collective-permute-done | bytes 1048608 | tf_op jit(solution)/shard_map/ppermute | solution.py:32
  179.9 18.7 %collective-permute-done.14.refs_3_ = bf16[1024,512]{1,0:T(8,128)(2,1)} collective-permute-done((bf16[1024,512]{1,0:T(8,128)(2,1)}, bf16[1024,512]{1,0:T(8,128)(2,1)}, u32[]{:S(2)}, u32[]{:S(2)}) %collective-permute-start.14) | collective-permute-done | bytes 1048608 | tf_op jit(solution)/shard_map/ppermute | solution.py:32
  210.0 3.6 all-to-all-start.2
  213.6 13.2 %shard_map.119 = (f32[1024,512]{1,0:T(8,128)}, f32[1024,128]{1,0:T(8,128)}) custom-call(s32[16]{0:T(128)} %stack.212.index_ref, s32[5,8]{1,0:T(8,128)} %stack.170.meta_ref, bf16[1024,512]{1,0:T(8,128)(2,1)} %collective-permute-done.1.refs_0_, bf16[1024,512]{1,0:T(8,128)(2,1)} %collective-permute-done.5.refs_1_, ...), custom_call_target="tpu_custom_call", output_to_operand_aliasing={{0}: (42, {}), {1}: (43, {})} | custom-call | flops 5368709120 | bytes 18874368 | tf_op jit(solution)/shard_map/pallas_call | solution.py:185
  231.6 5.5 %shard_map.123.m_ref = bf16[1024,128]{1,0:T(8,128)(2,1)} custom-call(s32[8]{0:T(128)} %stack.186.index_ref, s32[5,8]{1,0:T(8,128)} %stack.170.meta_ref, bf16[1024,512]{1,0:T(8,128)(2,1)} %collective-permute-done.10.refs_0_, bf16[1024,512]{1,0:T(8,128)(2,1)} %collective-permute-done.11.refs_1_, bf16[1024,512]{1,0:T(8,128)(2,1)} %copy-done.3, ...), custom_call_target="tpu_custom_call" | custom-call | flops 536870912 | bytes 5767168 | tf_op jit(solution)/shard_map/pallas_call | solution.py:185
  239.5 7.1 %shard_map.120.q_ref = f32[1024,512]{1,0:T(8,128)} custom-call(s32[8]{0:T(128)} %stack.186.index_ref, s32[5,8]{1,0:T(8,128)} %stack.170.meta_ref, bf16[1024,512]{1,0:T(8,128)(2,1)} %collective-permute-done.10.refs_0_, bf16[1024,512]{1,0:T(8,128)(2,1)} %collective-permute-done.11.refs_1_, ...), custom_call_target="tpu_custom_call", output_to_operand_aliasing={{}: (14, {})} | custom-call | flops 2147483648 | bytes 10485760 | tf_op jit(solution)/shard_map/pallas_call | solution.py:185
  247.3 6.5 %shard_map.128 = (bf16[512,512]{1,0:T(8,128)(2,1)}, f32[512,64]{1,0:T(8,128)}) custom-call(s32[5,8]{1,0:T(8,128)} %stack.170.meta_ref, f32[1024,512]{1,0:T(8,128)} %shard_map.120.q_ref, bf16[1024,192]{1,0:T(8,128)(2,1)} %bitcast.89, bf16[8,64,1152]{2,1,0:T(8,128)(2,1)} %copy-done.1, bf16[8,256,512]{2,1,0:T(8,128)(2,1)} %copy-done, ...), custom_call_target="tpu_custom_call" | custom-call | flops 402653184 | bytes 2097152 | tf_op jit(solution)/shard_map/pallas_call | solution.py:282
  257.1 6.5 %shard_map.124 = (bf16[512,512]{1,0:T(8,128)(2,1)}, f32[512,64]{1,0:T(8,128)}) custom-call(s32[5,8]{1,0:T(8,128)} %stack.170.meta_ref, f32[1024,512]{1,0:T(8,128)} %shard_map.120.q_ref, bf16[1024,192]{1,0:T(8,128)(2,1)} %bitcast.90, bf16[8,64,1152]{2,1,0:T(8,128)(2,1)} %copy-done.1, bf16[8,256,512]{2,1,0:T(8,128)(2,1)} %copy-done, ...), custom_call_target="tpu_custom_call" | custom-call | flops 402653184 | bytes 2097152 | tf_op jit(solution)/shard_map/pallas_call | solution.py:282
  263.6 3.2 collective-permute-start.22
  273.5 4.0 %all-to-all-start.4 = ((f32[16,32,128]{2,1,0:T(8,128)}), f32[16,32,128]{2,1,0:T(8,128)S(1)}, u32[]{:S(2)}, u32[]{:S(2)}) async-start(f32[16,32,128]{2,1,0:T(8,128)} %bitcast.61), calls=%async_computation.4 | async-start | bytes 524288 | tf_op jit(solution)/shard_map/all_to_all | solution.py:129
  278.9 7.3 %all-to-all-done.4 = f32[16,32,128]{2,1,0:T(8,128)S(1)} async-done(((f32[16,32,128]{2,1,0:T(8,128)}), f32[16,32,128]{2,1,0:T(8,128)S(1)}, u32[]{:S(2)}, u32[]{:S(2)}) %all-to-all-start.4) | async-done | bytes 262176 | tf_op jit(solution)/shard_map/all_to_all | solution.py:129
  290.4 4.8 %shard_map.130 = (bf16[512,256]{1,0:T(8,128)(2,1)}, bf16[512,256]{1,0:T(8,128)(2,1)}) custom-call(s32[6]{0:T(128)} %stack.220.index_ref, bf16[512,512]{1,0:T(8,128)(2,1)} %get-tuple-element.75.refs_0_, bf16[512,512]{1,0:T(8,128)(2,1)} %copy-done.7, bf16[512,512]{1,0:T(8,128)(2,1)} %copy-done.8, bf16[512,256]{1,0:T(8,128)(2,1)} %copy-done.22, ...), custom_call_target="tpu_custom_call" | custom-call | flops 1073741824 | bytes 4194304 | tf_op jit(solution)/shard_map/pallas_call | solution.py:355
  297.5 9.6 %shard_map.129 = (bf16[512,256]{1,0:T(8,128)(2,1)}, bf16[512,256]{1,0:T(8,128)(2,1)}, bf16[512,256]{1,0:T(8,128)(2,1)}, bf16[512,256]{1,0:T(8,128)(2,1)}, f32[512,256]{1,0:T(8,128)}, /*index=5*/f32[512,256]{1,0:T(8,128)}) custom-call(s32[10]{0:T(128)} %stack.177.index_ref, bf16[512,512]{1,0:T(8,128)(2,1)} %get-tuple-element.75.refs_0_, ...), custom_call_target="tpu_custom_call" | custom-call | flops 3221225472 | bytes 8388608 | tf_op jit(solution)/shard_map/pallas_call | solution.py:355
  309.6 4.8 %shard_map.127 = (bf16[512,256]{1,0:T(8,128)(2,1)}, bf16[512,256]{1,0:T(8,128)(2,1)}) custom-call(s32[6]{0:T(128)} %stack.220.index_ref, bf16[512,512]{1,0:T(8,128)(2,1)} %get-tuple-element.62.refs_0_, bf16[512,512]{1,0:T(8,128)(2,1)} %copy-done.5, bf16[512,512]{1,0:T(8,128)(2,1)} %copy-done.6, bf16[512,256]{1,0:T(8,128)(2,1)} %collective-permute-done.23.refs_3_, ...), custom_call_target="tpu_custom_call" | custom-call | flops 1073741824 | bytes 4194304 | tf_op jit(solution)/shard_map/pallas_call | solution.py:355
  316.5 9.6 %shard_map.126 = (bf16[512,256]{1,0:T(8,128)(2,1)}, bf16[512,256]{1,0:T(8,128)(2,1)}, bf16[512,256]{1,0:T(8,128)(2,1)}, bf16[512,256]{1,0:T(8,128)(2,1)}, f32[512,256]{1,0:T(8,128)}, /*index=5*/f32[512,256]{1,0:T(8,128)}) custom-call(s32[10]{0:T(128)} %stack.177.index_ref, bf16[512,512]{1,0:T(8,128)(2,1)} %get-tuple-element.62.refs_0_, ...), custom_call_target="tpu_custom_call" | custom-call | flops 3221225472 | bytes 8388608 | tf_op jit(solution)/shard_map/pallas_call | solution.py:355
  330.6 3.3 collective-permute-start.43
  338.6 13.3 %all_to_all.30 = bf16[16,32,128]{2,1,0:T(8,128)(2,1)} all-to-all(bf16[16,32,128]{2,1,0:T(8,128)(2,1)S(1)} %broadcast_in_dim.77), channel_id=1, replica_groups=mesh['z'=4,'c'=2,'y'=4,'x'=4] {'y','x'}, dimensions={0} | all-to-all | bytes 262144 | tf_op jit(solution)/shard_map/all_to_all | solution.py:136
  353.0 5.9 %shard_map.131 = f32[1024,512]{1,0:T(8,128)} custom-call(s32[5,8]{1,0:T(8,128)} %stack.170.meta_ref, f32[512,256]{1,0:T(8,128)} %get-tuple-element.64.refs_0_, bf16[512,256]{1,0:T(8,128)(2,1)} %copy-done.12, bf16[512,256]{1,0:T(8,128)(2,1)} %copy-done.21, f32[512,256]{1,0:T(8,128)} %get-tuple-element.68.refs_3_, bf16[512,256]{1,0:T(8,128)(2,1)} %copy-done.13, ...), custom_call_target="tpu_custom_call" | custom-call | flops 67108864 | bytes 7340032 | tf_op jit(solution)/shard_map/pallas_call | solution.py:434
  (188 shorter events, 89.8 us)
Async XLA Ops:
  6.5 283.2 %all-gather.3.cloned.1.call-start = ((), (), s32[]{:S(2)}) async-start(), calls=%async_computation.6 | async-start | bytes 9437184 | tf_op jit(solution)/shard_map/all_gather | solution.py:530
  7.9 17.9 %collective-permute-start.7 = (bf16[1024,256]{1,0:T(8,128)(2,1)S(1)}, bf16[1024,256]{1,0:T(8,128)(2,1)S(1)}, u32[]{:S(2)}, u32[]{:S(2)}) collective-permute-start(bf16[1024,256]{1,0:T(8,128)(2,1)S(1)} %get-tuple-element.99), channel_id=1, source_target_pairs={{0,12},{4,0},{8,4},{12,8},{1,13},{5,1},{9,5},{13,9},{2,14},{6,2},{... | collective-permute-start | bytes 1572872 | tf_op jit(solution)/shard_map/ppermute | solution.py:32
  11.0 19.6 %collective-permute-start.2 = (bf16[1024,256]{1,0:T(8,128)(2,1)S(1)}, bf16[1024,256]{1,0:T(8,128)(2,1)S(1)}, u32[]{:S(2)}, u32[]{:S(2)}) collective-permute-start(bf16[1024,256]{1,0:T(8,128)(2,1)S(1)} %get-tuple-element.100), channel_id=1, source_target_pairs={{0,3},{1,0},{2,1},{3,2},{4,7},{5,4},{6,5},{7,6},{8,11},{9,8},{10,9... | collective-permute-start | bytes 1572872 | tf_op jit(solution)/shard_map/ppermute | solution.py:32
  73.6 54.8 %all-to-all-start = ((bf16[8,256,512]{2,1,0:T(8,128)(2,1)}), bf16[8,256,512]{2,1,0:T(8,128)(2,1)S(1)}, u32[]{:S(2)}, u32[]{:S(2)}) async-start(bf16[8,256,512]{2,1,0:T(8,128)(2,1)} %get-tuple-element.56), calls=%async_computation | async-start | bytes 4194304 | tf_op jit(solution)/shard_map/all_to_all | solution.py:495
  78.6 67.2 %collective-permute-start.1 = (bf16[1024,512]{1,0:T(8,128)(2,1)}, bf16[1024,512]{1,0:T(8,128)(2,1)}, u32[]{:S(2)}, u32[]{:S(2)}) collective-permute-start(bf16[1024,512]{1,0:T(8,128)(2,1)} %pad_maximum_fusion.refs_0_), channel_id=1, source_target_pairs={{0,4},{4,8},{8,12},{12,0},{1,5},{5,9},{9,13},{13,1},{2,6},{6,10},{... | collective-permute-start | bytes 3145736 | tf_op jit(solution)/shard_map/ppermute | solution.py:32
  79.8 66.8 %collective-permute-start.12 = (bf16[1024,512]{1,0:T(8,128)(2,1)S(1)}, bf16[1024,512]{1,0:T(8,128)(2,1)}, u32[]{:S(2)}, u32[]{:S(2)}) collective-permute-start(bf16[1024,512]{1,0:T(8,128)(2,1)S(1)} %copy-done.4), channel_id=1, source_target_pairs={{0,1},{1,2},{2,3},{3,0},{4,5},{5,6},{6,7},{7,4},{8,9},{9,10},{10,1... | collective-permute-start | bytes 3145736 | tf_op jit(solution)/shard_map/ppermute | solution.py:32
  79.8 68.0 %collective-permute-start.5 = (bf16[1024,512]{1,0:T(8,128)(2,1)}, bf16[1024,512]{1,0:T(8,128)(2,1)}, u32[]{:S(2)}, u32[]{:S(2)}) collective-permute-start(bf16[1024,512]{1,0:T(8,128)(2,1)} %constant_dynamic-update-slice_fusion.refs_1_), channel_id=1, source_target_pairs={{0,12},{4,0},{8,4},{12,8},{1,13},{5,1},{9,5},{13,9},{2,14},{6,2},{... | collective-permute-start | bytes 3145736 | tf_op jit(solution)/shard_map/ppermute | solution.py:32
  134.8 23.7 %all-to-all-start.1 = ((f32[16,64,192]{2,1,0:T(8,128)}), f32[16,64,192]{2,1,0:T(8,128)S(1)}, u32[]{:S(2)}, u32[]{:S(2)}) async-start(f32[16,64,192]{2,1,0:T(8,128)} %bitcast.91), calls=%async_computation.1 | async-start | bytes 2097152 | tf_op jit(solution)/shard_map/all_to_all | solution.py:129
  140.0 37.5 %collective-permute-start.19 = (bf16[1024,512]{1,0:T(8,128)(2,1)S(1)}, bf16[1024,512]{1,0:T(8,128)(2,1)}, u32[]{:S(2)}, u32[]{:S(2)}) collective-permute-start(bf16[1024,512]{1,0:T(8,128)(2,1)S(1)} %copy-done.4), channel_id=1, source_target_pairs={{0,3},{1,0},{2,1},{3,2},{4,7},{5,4},{6,5},{7,6},{8,11},{9,8},{10,9... | collective-permute-start | bytes 3145736 | tf_op jit(solution)/shard_map/ppermute | solution.py:32
  143.1 35.2 %collective-permute-start.17 = (bf16[1024,512]{1,0:T(8,128)(2,1)}, bf16[1024,512]{1,0:T(8,128)(2,1)}, u32[]{:S(2)}, u32[]{:S(2)}) collective-permute-start(bf16[1024,512]{1,0:T(8,128)(2,1)} %pad_maximum_fusion.refs_0_), channel_id=1, source_target_pairs={{0,12},{4,0},{8,4},{12,8},{1,13},{5,1},{9,5},{13,9},{2,14},{6,2},{... | collective-permute-start | bytes 3145736 | tf_op jit(solution)/shard_map/ppermute | solution.py:32
  145.8 52.8 %collective-permute-start.14 = (bf16[1024,512]{1,0:T(8,128)(2,1)}, bf16[1024,512]{1,0:T(8,128)(2,1)}, u32[]{:S(2)}, u32[]{:S(2)}) collective-permute-start(bf16[1024,512]{1,0:T(8,128)(2,1)} %constant_dynamic-update-slice_fusion.3.refs_3_), channel_id=1, source_target_pairs={{0,3},{1,0},{2,1},{3,2},{4,7},{5,4},{6,5},{7,6},{8,11},{9,8},{10,9... | collective-permute-start | bytes 3145736 | tf_op jit(solution)/shard_map/ppermute | solution.py:32
  146.7 54.6 %collective-permute-start.18 = (bf16[1024,512]{1,0:T(8,128)(2,1)}, bf16[1024,512]{1,0:T(8,128)(2,1)}, u32[]{:S(2)}, u32[]{:S(2)}) collective-permute-start(bf16[1024,512]{1,0:T(8,128)(2,1)} %constant_dynamic-update-slice_fusion.3.refs_3_), channel_id=1, source_target_pairs={{0,1},{1,2},{2,3},{3,0},{4,5},{5,6},{6,7},{7,4},{8,9},{9,10},{10,1... | collective-permute-start | bytes 3145736 | tf_op jit(solution)/shard_map/ppermute | solution.py:32
  147.8 65.7 %collective-permute-start.16 = (bf16[1024,512]{1,0:T(8,128)(2,1)}, bf16[1024,512]{1,0:T(8,128)(2,1)}, u32[]{:S(2)}, u32[]{:S(2)}) collective-permute-start(bf16[1024,512]{1,0:T(8,128)(2,1)} %constant_dynamic-update-slice_fusion.refs_1_), channel_id=1, source_target_pairs={{0,4},{4,8},{8,12},{12,0},{1,5},{5,9},{9,13},{13,1},{2,6},{6,10},{... | collective-permute-start | bytes 3145736 | tf_op jit(solution)/shard_map/ppermute | solution.py:32
  158.6 50.4 %all-to-all-start.3 = ((bf16[8,64,1152]{2,1,0:T(8,128)(2,1)}), bf16[8,64,1152]{2,1,0:T(8,128)(2,1)S(1)}, u32[]{:S(2)}, u32[]{:S(2)}) async-start(bf16[8,64,1152]{2,1,0:T(8,128)(2,1)} %get-tuple-element.60), calls=%async_computation.3 | async-start | bytes 2359296 | tf_op jit(solution)/shard_map/all_to_all | solution.py:523
  177.5 49.3 %collective-permute-start.13 = (bf16[1024,512]{1,0:T(8,128)(2,1)}, bf16[1024,512]{1,0:T(8,128)(2,1)S(1)}, u32[]{:S(2)}, u32[]{:S(2)}) collective-permute-start(bf16[1024,512]{1,0:T(8,128)(2,1)} %collective-permute-done.12.refs_2_), channel_id=1, source_target_pairs={{0,1},{1,2},{2,3},{3,0},{4,5},{5,6},{6,7},{7,4},{8,9},{9,10},{10,1... | collective-permute-start | bytes 3145736 | tf_op jit(solution)/shard_map/ppermute | solution.py:32
  178.3 48.5 %collective-permute-start.10 = (bf16[1024,512]{1,0:T(8,128)(2,1)}, bf16[1024,512]{1,0:T(8,128)(2,1)}, u32[]{:S(2)}, u32[]{:S(2)}) collective-permute-start(bf16[1024,512]{1,0:T(8,128)(2,1)} %collective-permute-done.1.refs_0_), channel_id=1, source_target_pairs={{0,4},{4,8},{8,12},{12,0},{1,5},{5,9},{9,13},{13,1},{2,6},{6,10},{... | collective-permute-start | bytes 3145736 | tf_op jit(solution)/shard_map/ppermute | solution.py:32
  198.6 28.9 %collective-permute-start.11 = (bf16[1024,512]{1,0:T(8,128)(2,1)}, bf16[1024,512]{1,0:T(8,128)(2,1)}, u32[]{:S(2)}, u32[]{:S(2)}) collective-permute-start(bf16[1024,512]{1,0:T(8,128)(2,1)} %collective-permute-done.5.refs_1_), channel_id=1, source_target_pairs={{0,12},{4,0},{8,4},{12,8},{1,13},{5,1},{9,5},{13,9},{2,14},{6,2},{... | collective-permute-start | bytes 3145736 | tf_op jit(solution)/shard_map/ppermute | solution.py:32
  201.3 26.4 %collective-permute-start.15 = (bf16[1024,512]{1,0:T(8,128)(2,1)}, bf16[1024,512]{1,0:T(8,128)(2,1)}, u32[]{:S(2)}, u32[]{:S(2)}) collective-permute-start(bf16[1024,512]{1,0:T(8,128)(2,1)} %collective-permute-done.14.refs_3_), channel_id=1, source_target_pairs={{0,3},{1,0},{2,1},{3,2},{4,7},{5,4},{6,5},{7,6},{8,11},{9,8},{10,9... | collective-permute-start | bytes 3145736 | tf_op jit(solution)/shard_map/ppermute | solution.py:32
  210.0 20.8 %all-to-all-start.2 = ((bf16[16,64,192]{2,1,0:T(8,128)(2,1)}), bf16[16,64,192]{2,1,0:T(8,128)(2,1)S(1)}, u32[]{:S(2)}, u32[]{:S(2)}) async-start(bf16[16,64,192]{2,1,0:T(8,128)(2,1)} %broadcast_in_dim.76), calls=%async_computation.2 | async-start | bytes 1048576 | tf_op jit(solution)/shard_map/all_to_all | solution.py:136
  263.6 22.7 %collective-permute-start.21 = (bf16[512,512]{1,0:T(8,128)(2,1)}, bf16[512,512]{1,0:T(8,128)(2,1)S(1)}, u32[]{:S(2)}, u32[]{:S(2)}) collective-permute-start(bf16[512,512]{1,0:T(8,128)(2,1)} %get-tuple-element.62.refs_0_), channel_id=1, source_target_pairs={{0,4},{4,8},{8,12},{12,0},{1,5},{5,9},{9,13},{13,1},{2,6},{6,10},{... | collective-permute-start | bytes 1572872 | tf_op jit(solution)/shard_map/ppermute | solution.py:32
  263.6 23.2 %collective-permute-start.22 = (bf16[512,512]{1,0:T(8,128)(2,1)}, bf16[512,512]{1,0:T(8,128)(2,1)S(1)}, u32[]{:S(2)}, u32[]{:S(2)}) collective-permute-start(bf16[512,512]{1,0:T(8,128)(2,1)} %get-tuple-element.62.refs_0_), channel_id=1, source_target_pairs={{0,12},{4,0},{8,4},{12,8},{1,13},{5,1},{9,5},{13,9},{2,14},{6,2},{... | collective-permute-start | bytes 1572872 | tf_op jit(solution)/shard_map/ppermute | solution.py:32
  268.3 21.4 %collective-permute-start.36 = (bf16[512,256]{1,0:T(8,128)(2,1)S(1)}, bf16[512,256]{1,0:T(8,128)(2,1)S(1)}, u32[]{:S(2)}, u32[]{:S(2)}) collective-permute-start(bf16[512,256]{1,0:T(8,128)(2,1)S(1)} %slice.66), channel_id=1, source_target_pairs={{0,4},{4,8},{8,12},{12,0},{1,5},{5,9},{9,13},{13,1},{2,6},{6,10},{... | collective-permute-start | bytes 786440 | tf_op jit(solution)/shard_map/ppermute | solution.py:32
  268.9 20.8 %collective-permute-start.37 = (bf16[512,256]{1,0:T(8,128)(2,1)S(1)}, bf16[512,256]{1,0:T(8,128)(2,1)}, u32[]{:S(2)}, u32[]{:S(2)}) collective-permute-start(bf16[512,256]{1,0:T(8,128)(2,1)S(1)} %slice.67), channel_id=1, source_target_pairs={{0,12},{4,0},{8,4},{12,8},{1,13},{5,1},{9,5},{13,9},{2,14},{6,2},{... | collective-permute-start | bytes 786440 | tf_op jit(solution)/shard_map/ppermute | solution.py:32
  286.3 23.3 %collective-permute-start.23 = (bf16[512,256]{1,0:T(8,128)(2,1)S(1)}, bf16[512,256]{1,0:T(8,128)(2,1)}, u32[]{:S(2)}, u32[]{:S(2)}) collective-permute-start(bf16[512,256]{1,0:T(8,128)(2,1)S(1)} %slice.60), channel_id=1, source_target_pairs={{0,4},{4,8},{8,12},{12,0},{1,5},{5,9},{9,13},{13,1},{2,6},{6,10},{... | collective-permute-start | bytes 786440 | tf_op jit(solution)/shard_map/ppermute | solution.py:32
  286.9 22.7 %collective-permute-start.24 = (bf16[512,256]{1,0:T(8,128)(2,1)S(1)}, bf16[512,256]{1,0:T(8,128)(2,1)}, u32[]{:S(2)}, u32[]{:S(2)}) collective-permute-start(bf16[512,256]{1,0:T(8,128)(2,1)S(1)} %slice.61), channel_id=1, source_target_pairs={{0,12},{4,0},{8,4},{12,8},{1,13},{5,1},{9,5},{13,9},{2,14},{6,2},{... | collective-permute-start | bytes 786440 | tf_op jit(solution)/shard_map/ppermute | solution.py:32
  295.2 30.8 %collective-permute-start.42 = (bf16[512,256]{1,0:T(8,128)(2,1)}, bf16[512,256]{1,0:T(8,128)(2,1)S(1)}, u32[]{:S(2)}, u32[]{:S(2)}) collective-permute-start(bf16[512,256]{1,0:T(8,128)(2,1)} %get-tuple-element.87), channel_id=1, source_target_pairs={{0,3},{1,0},{2,1},{3,2},{4,7},{5,4},{6,5},{7,6},{8,11},{9,8},{10,9... | collective-permute-start | bytes 786440 | tf_op jit(solution)/shard_map/ppermute | solution.py:32
  296.8 29.5 %collective-permute-start.39 = (bf16[512,256]{1,0:T(8,128)(2,1)}, bf16[512,256]{1,0:T(8,128)(2,1)S(1)}, u32[]{:S(2)}, u32[]{:S(2)}) collective-permute-start(bf16[512,256]{1,0:T(8,128)(2,1)} %get-tuple-element.83), channel_id=1, source_target_pairs={{0,1},{1,2},{2,3},{3,0},{4,5},{5,6},{6,7},{7,4},{8,9},{9,10},{10,1... | collective-permute-start | bytes 786440 | tf_op jit(solution)/shard_map/ppermute | solution.py:32
  307.1 26.9 %collective-permute-start.38 = (bf16[512,256]{1,0:T(8,128)(2,1)}, bf16[512,256]{1,0:T(8,128)(2,1)S(1)}, u32[]{:S(2)}, u32[]{:S(2)}) collective-permute-start(bf16[512,256]{1,0:T(8,128)(2,1)} %get-tuple-element.81), channel_id=1, source_target_pairs={{0,3},{1,0},{2,1},{3,2},{4,7},{5,4},{6,5},{7,6},{8,11},{9,8},{10,9... | collective-permute-start | bytes 786440 | tf_op jit(solution)/shard_map/ppermute | solution.py:32
  314.9 15.7 %collective-permute-start.29 = (bf16[512,256]{1,0:T(8,128)(2,1)}, bf16[512,256]{1,0:T(8,128)(2,1)S(1)}, u32[]{:S(2)}, u32[]{:S(2)}) collective-permute-start(bf16[512,256]{1,0:T(8,128)(2,1)} %get-tuple-element.67), channel_id=1, source_target_pairs={{0,1},{1,2},{2,3},{3,0},{4,5},{5,6},{6,7},{7,4},{8,9},{9,10},{10,1... | collective-permute-start | bytes 786440 | tf_op jit(solution)/shard_map/ppermute | solution.py:32
  329.5 22.4 %collective-permute-start.31 = (bf16[512,256]{1,0:T(8,128)(2,1)}, bf16[512,256]{1,0:T(8,128)(2,1)S(1)}, u32[]{:S(2)}, u32[]{:S(2)}) collective-permute-start(bf16[512,256]{1,0:T(8,128)(2,1)} %get-tuple-element.69), channel_id=1, source_target_pairs={{0,1},{1,2},{2,3},{3,0},{4,5},{5,6},{6,7},{7,4},{8,9},{9,10},{10,1... | collective-permute-start | bytes 786440 | tf_op jit(solution)/shard_map/ppermute | solution.py:32
  330.6 21.3 %collective-permute-start.43 = (bf16[512,256]{1,0:T(8,128)(2,1)S(1)}, bf16[512,256]{1,0:T(8,128)(2,1)S(1)}, u32[]{:S(2)}, u32[]{:S(2)}) collective-permute-start(bf16[512,256]{1,0:T(8,128)(2,1)S(1)} %add.315), channel_id=1, source_target_pairs={{0,3},{1,0},{2,1},{3,2},{4,7},{5,4},{6,5},{7,6},{8,11},{9,8},{10,9... | collective-permute-start | bytes 786440 | tf_op jit(solution)/shard_map/ppermute | solution.py:32
  334.0 18.0 %collective-permute-start.40 = (bf16[512,256]{1,0:T(8,128)(2,1)S(1)}, bf16[512,256]{1,0:T(8,128)(2,1)S(1)}, u32[]{:S(2)}, u32[]{:S(2)}) collective-permute-start(bf16[512,256]{1,0:T(8,128)(2,1)S(1)} %add.314), channel_id=1, source_target_pairs={{0,1},{1,2},{2,3},{3,0},{4,5},{5,6},{6,7},{7,4},{8,9},{9,10},{10,1... | collective-permute-start | bytes 786440 | tf_op jit(solution)/shard_map/ppermute | solution.py:32
  (45 other events, 449.6 us)
Sparse Core Ops, SparseCore 0:
  66.8 73.0 all-gather.2

commit v4 on v3

--- a/solution.py
+++ b/solution.py
@@ -2,6 +2,7 @@
 
 import jax
 import jax.numpy as jnp
+import numpy as np
 from jax import lax
 from jax.experimental import pallas as pl
 from jax.experimental.pallas import tpu as pltpu
@@ -24,6 +25,10 @@
     return pltpu.CompilerParams(vmem_limit_bytes=VMEM)
 
 
+def passive(arrays):
+    return [pl.BlockSpec(memory_space=pl.ANY)] * len(arrays)
+
+
 def cost(flops, moved, exps=0):
     return pl.CostEstimate(flops=flops, bytes_accessed=moved, transcendentals=exps)
 
@@ -50,13 +55,16 @@
     return [index, (index + SIDE - 1) % SIDE, (index + 1) % SIDE, (index + 2) % SIDE]
 
 
-def pick_adapters(pick, down_qkv, up_q, up_kv, down_o, up_o):
+def pick_adapters(pick, down_qkv, up_q, up_kv, down_o, up_o, x):
+    tokens, local = x.shape
     groups = pick.shape[0]
     rank3, depth = down_qkv.shape[1:]
     rank, wide = up_q.shape[1:]
     narrow = up_kv.shape[2]
 
-    def body(pick_ref, dq, uq, ukv, do, uo, down, up):
+    def body(pick_ref, dq, uq, ukv, do, uo, x_ref, down, up, left, right):
+        left[...] = x_ref[:, : local // 2]
+        right[...] = x_ref[:, local // 2 :]
         down[0, :rank3, :] = dq[0]
         down[0, rank3:, :] = do[0]
         up[0, :, :wide] = uq[0]
@@ -73,27 +81,31 @@
         out_shape=(
             jax.ShapeDtypeStruct(down_shape, bf16),
             jax.ShapeDtypeStruct(up_shape, bf16),
+            jax.ShapeDtypeStruct((tokens, local // 2), bf16),
+            jax.ShapeDtypeStruct((tokens, local // 2), bf16),
         ),
         grid_spec=pltpu.PrefetchScalarGridSpec(
             num_scalar_prefetch=1,
             grid=(groups,),
-            in_specs=[chosen(a) for a in (down_qkv, up_q, up_kv, down_o, up_o)],
+            in_specs=[chosen(a) for a in (down_qkv, up_q, up_kv, down_o, up_o)]
+            + [pl.BlockSpec((tokens // groups, local), lambda i, p: (i, 0))],
             out_specs=[
                 pl.BlockSpec((1,) + s[1:], lambda i, p: (i, 0, 0)) for s in (down_shape, up_shape)
-            ],
+            ]
+            + [pl.BlockSpec((tokens // groups, local // 2), lambda i, p: (i, 0))] * 2,
         ),
         compiler_params=params(),
         cost_estimate=cost(0, 2 * 2 * (math.prod(down_shape) + math.prod(up_shape))),
-    )(pick, down_qkv, up_q, up_kv, down_o, up_o)
-
-
-def rank_partial(meta, x, down, rank3):
+    )(pick, down_qkv, up_q, up_kv, down_o, up_o, x)
+
+
+def rank_partial(meta, x, down, rank3, after):
     tokens, depth = x.shape
     per = 2
     rows = per * BLOCK
 
     def body(meta_ref, x_ref, *rest):
-        d_refs, out = rest[:-1], rest[-1]
+        d_refs, out = rest[:per], rest[-1]
         for k in range(per):
             at = slice(k * BLOCK, (k + 1) * BLOCK)
             out[at, :] = lax.dot_general(
@@ -110,32 +122,71 @@
             num_scalar_prefetch=1,
             grid=(tokens // rows,),
             in_specs=[pl.BlockSpec((rows, depth), lambda i, m: (i, 0))]
-            + [chosen(k) for k in range(per)],
+            + [chosen(k) for k in range(per)]
+            + passive(after),
             out_specs=pl.BlockSpec((rows, rank3), lambda i, m: (i, 0)),
         ),
         compiler_params=params(),
         cost_estimate=cost(2 * tokens * depth * rank3, 2 * tokens * depth + 8 * tokens * rank3),
-    )(meta, x, *[down] * per)
-
-
-def sum_over_tensor(partial):
-    mine, spread = sum_over_tensor_in_two(partial)
-    return spread(mine)
-
-
-def sum_over_tensor_in_two(partial):
+    )(meta, x, *[down] * per, *after)
+
+
+def join(groups, after):
+    tokens = groups[0][0].shape[0]
+    rows = 256
+    flat = [b for group in groups for b in group]
+    widths = [sum(b.shape[1] for b in group) for group in groups]
+
+    def body(*refs):
+        ins, outs = refs[: len(flat)], refs[len(flat) + len(after) :]
+        at = 0
+        for out, group in zip(outs, groups):
+            col = 0
+            for b in group:
+                out[:, col : col + b.shape[1]] = ins[at][...]
+                col += b.shape[1]
+                at += 1
+
+    return pl.pallas_call(
+        body,
+        out_shape=tuple(jax.ShapeDtypeStruct((tokens, w), bf16) for w in widths),
+        grid=(tokens // rows,),
+        in_specs=[pl.BlockSpec((rows, b.shape[1]), lambda i: (i, 0)) for b in flat]
+        + passive(after),
+        out_specs=[pl.BlockSpec((rows, w), lambda i: (i, 0)) for w in widths],
+        compiler_params=params(),
+        cost_estimate=cost(0, 4 * tokens * sum(widths)),
+    )(*flat, *after)
+
+
+def share_sum(pieces, after):
+    ways, rows, rank = pieces.shape
+
+    def body(p_ref, *refs):
+        total = p_ref[0]
+        for k in range(1, ways):
+            total = total + p_ref[k]
+        for k in range(ways):
+            refs[-1][k] = total.astype(bf16)
+
+    whole = pl.BlockSpec(pieces.shape, lambda i: (0, 0, 0))
+    return pl.pallas_call(
+        body,
+        out_shape=jax.ShapeDtypeStruct(pieces.shape, bf16),
+        grid=(1,),
+        in_specs=[whole] + passive(after),
+        out_specs=whole,
+        compiler_params=params(),
+        cost_estimate=cost(ways * rows * rank, 6 * ways * rows * rank),
+    )(pieces, *after)
+
+
+def scatter_rows(partial):
     rows, rank = partial.shape
     ways = SIDE * SIDE
-    pieces = lax.all_to_all(
+    return lax.all_to_all(
         partial.reshape(ways, rows // ways, rank), TENSOR_AXES, 0, 0, tiled=True
     )
-    mine = jnp.sum(pieces, axis=0).astype(bf16)
-
-    def spread(mine):
-        copies = jnp.broadcast_to(mine[None], (ways,) + mine.shape)
-        return lax.all_to_all(copies, TENSOR_AXES, 0, 0, tiled=True).reshape(rows, rank)
-
-    return mine, spread
 
 
 def project(index, total, blocks, weights, tile, last=None, rows=256):
@@ -228,6 +279,18 @@
         pl.BlockSpec(sine.shape, lambda i, p, m: (0, 0, 0)),
     ]
     return tail, [shrunk, up, cosine, sine], specs, bf16
+
+
+def rotation_tables():
+    freq = np.exp(-(2.0 * np.arange(HEAD // 2, dtype=np.float32) / HEAD) * math.log(ROPE_BASE))
+    angle = np.arange(3 * BLOCK, dtype=np.float32)[:, None] * freq.astype(np.float32)[None, :]
+    cosine = np.concatenate([np.cos(angle)] * 2, axis=1)
+    sine = np.concatenate([-np.sin(angle), np.sin(angle)], axis=1)
+    shape = (3, BLOCK, HEAD)
+    return (
+        jnp.asarray(cosine.reshape(shape), f32),
+        jnp.asarray(sine.reshape(shape), f32),
+    )
 
 
 def attention(meta, q, shrunk, up, down, mine, other, cosine, sine, begin, count):
@@ -310,12 +373,12 @@
     )(meta, q, shrunk, up, down, mine, other, cosine, sine)
 
 
-def pick_columns(index, matrix, width):
+def pick_columns(index, matrix, width, after):
     depth = matrix.shape[0]
     count = index.shape[0]
 
-    def body(index_ref, m_ref, out):
-        out[0] = m_ref[...]
+    def body(index_ref, m_ref, *refs):
+        refs[-1][0] = m_ref[...]
 
     return pl.pallas_call(
         body,
@@ -323,15 +386,15 @@
         grid_spec=pltpu.PrefetchScalarGridSpec(
             num_scalar_prefetch=1,
             grid=(count,),
-            in_specs=[pl.BlockSpec((depth, width), lambda i, p: (0, p[i]))],
+            in_specs=[pl.BlockSpec((depth, width), lambda i, p: (0, p[i]))] + passive(after),
             out_specs=pl.BlockSpec((1, depth, width), lambda i, p: (i, 0, 0)),
         ),
         compiler_params=params(),
         cost_estimate=cost(0, 4 * count * depth * width),
-    )(index, matrix)
-
-
-def output_partial(index, pieces, weights, dtypes):
+    )(index, matrix, *after)
+
+
+def output_partial(index, pieces, weights, dtypes, after):
     tokens = pieces[0].shape[0]
     depth, width = weights.shape[1:]
     unit = depth // SIDE
@@ -339,7 +402,7 @@
     places = [(0, 0), (1, 0), (2, 0), (3, 0), (3, unit // 2)]
 
     def body(index_ref, *refs):
-        x_refs, w_ref, outs = refs[: len(pieces)], refs[len(pieces)], refs[len(pieces) + 1 :]
+        x_refs, w_ref, outs = refs[: len(pieces)], refs[len(pieces)], refs[-count:]
         total = None
         for x_ref, (place, offset) in zip(x_refs, places):
             start = pl.multiple_of(index_ref[place] * unit + offset, 128)
@@ -359,21 +422,23 @@
             num_scalar_prefetch=1,
             grid=(count,),
             in_specs=[pl.BlockSpec(p.shape, lambda j, d: (0, 0)) for p in pieces]
-            + [pl.BlockSpec((1, depth, width), lambda j, d: (d[SIDE + j], 0, 0))],
+            + [pl.BlockSpec((1, depth, width), lambda j, d: (d[SIDE + j], 0, 0))]
+            + passive(after),
             out_specs=[pl.BlockSpec((tokens, width), lambda j, d: (0, 0))] * count,
         ),
         compiler_params=params(),
         cost_estimate=cost(
             2 * tokens * depth * count * width, 2 * depth * (tokens + count * width)
         ),
-    )(index, *pieces, weights)
-
-
-def output_ring(pieces, weights, axis, places):
+    )(index, *pieces, weights, *after)
+
+
+def output_ring(pieces, weights, axis, places, ahead_of):
     me, behind, ahead, far = ring_order(lax.axis_index(axis))
 
-    def partial(shards, dtypes):
-        return output_partial(jnp.stack(places + shards).astype(i32), pieces, weights, dtypes)
+    def partial(shards, dtypes, after=()):
+        index = jnp.stack(places + shards).astype(i32)
+        return output_partial(index, pieces, weights, dtypes, after)
 
     far_low, far_high = partial([2 * far, 2 * far + 1], [bf16] * 2)
     via_behind = shift(far_low, axis, 1)
@@ -381,6 +446,7 @@
     ahead_high, behind_low, ahead_low, behind_high, low, high = partial(
         [2 * ahead + 1, 2 * behind, 2 * ahead, 2 * behind + 1, 2 * me, 2 * me + 1],
         [bf16] * 4 + [f32] * 2,
+        [ahead_of],
     )
     return (
         (low, shift(behind_low, axis, -1), shift(ahead_low + via_behind, axis, 1)),
@@ -478,22 +544,18 @@
     is_key = jnp.broadcast_to(1 - xi % 2, (blocks,)).astype(i32)
     meta = jnp.stack([slot, block - first, first * BLOCK, is_key, limit]).astype(i32)
 
-    freq = jnp.exp(-(2.0 * jnp.arange(HEAD // 2, dtype=f32) / HEAD) * math.log(ROPE_BASE))
-    angle = jnp.arange(3 * BLOCK, dtype=f32)[:, None] * freq[None, :]
-    cosine = jnp.tile(jnp.cos(angle), (1, 2)).reshape(3, BLOCK, HEAD)
-    sine = jnp.concatenate([-jnp.sin(angle), jnp.sin(angle)], axis=1).reshape(3, BLOCK, HEAD)
-
-    half = local // 2
+    cosine, sine = rotation_tables()
+
+    stores = (jnp.swapaxes(down_qkv, 1, 2), up_q, up_kv, jnp.swapaxes(down_o, 1, 2), up_o)
+    down_out, up_out, x_a, x_b = pick_adapters(pick, *stores, x)
+    down = lax.all_to_all(down_out, ADAPTER_AXES, 0, 0, tiled=True)
+
     ys, xs = ring_order(y), ring_order(xi)
-    first_a = ring_gather(x[:, :half], "x")
-    first_b = ring_gather(x[:, half:], "y")
-    low_a, high_a = jnp.concatenate(first_a[:2], axis=1), jnp.concatenate(first_a[2:], axis=1)
-    low_b, high_b = jnp.concatenate(first_b[:2], axis=1), jnp.concatenate(first_b[2:], axis=1)
-
-    stores = (jnp.swapaxes(down_qkv, 1, 2), up_q, up_kv, jnp.swapaxes(down_o, 1, 2), up_o)
-    down_out, up_out = pick_adapters(pick, *stores)
-    down = lax.all_to_all(down_out, ADAPTER_AXES, 0, 0, tiled=True)
-
+    first_a = ring_gather(x_a, "x")
+    first_b = ring_gather(x_b, "y")
+    low_a, high_a, low_b, high_b = join(
+        [first_a[:2], first_a[2:], first_b[:2], first_b[2:]], [down]
+    )
     far_a, next_a = second_gather(low_a, high_a, "y")
     far_b, next_b = second_gather(low_b, high_b, "x")
 
@@ -516,20 +578,17 @@
         512,
     )
 
-    own, down, _ = lax.optimization_barrier((x, down, (low_a, high_a, low_b, high_b)))
-    partial = rank_partial(meta, own, down, 3 * rank)
-    shrunk = sum_over_tensor(partial)
-    up_out, _ = lax.optimization_barrier((up_out, partial))
+    pieces = scatter_rows(rank_partial(meta, x, down, 3 * rank, [low_a]))
+    copies = share_sum(pieces, [*far_a, *far_b])
+    shrunk = lax.all_to_all(copies, TENSOR_AXES, 0, 0, tiled=True).reshape(tokens, 3 * rank)
     up = lax.all_to_all(up_out, ADAPTER_AXES, 0, 0, tiled=True)
 
     unit = wo.shape[1] // (SIDE * SIDE * 2)
-    tied, total = lax.optimization_barrier((wo, total))
     order = ring_order(y)
-    sent = pick_columns(jnp.stack(order).astype(i32) * (2 * SIDE) + group, tied, unit)
+    sent = pick_columns(jnp.stack(order).astype(i32) * (2 * SIDE) + group, wo, unit, first_a[1:3] + first_b[1:3])
     got = [sent[0], shift(sent[2], "y", 1), shift(sent[1], "y", -1), shift(sent[3], "y", 2)]
     wo_all = lax.all_gather(jnp.concatenate(got, axis=0), ADAPTER_AXES, axis=0)
 
-    far_a, total = lax.optimization_barrier((far_a, total))
     a_low, a_high = shift(far_a[0], "y", 1), shift(far_a[1], "y", -1)
     b_low, b_high = shift(far_b[0], "x", 1), shift(far_b[1], "x", -1)
     total = project(
@@ -560,12 +619,14 @@
         )
         ranks.append(head)
         pieces.append(ring_gather(attended, "y"))
-    mine_rank, spread = sum_over_tensor_in_two(jnp.concatenate(ranks, axis=1))
+    rank_mine = jnp.sum(scatter_rows(jnp.concatenate(ranks, axis=1)), axis=0).astype(bf16)
+    head_rank = lax.all_gather(rank_mine, TENSOR_AXES, axis=0, tiled=True)
     places = [jnp.int32(k) for k in range(SIDE)]
-    parts = [output_ring(pieces[0], wo_all, "x", places)]
-    last, mine_rank = lax.optimization_barrier((pieces[1], mine_rank))
-    parts.append(output_ring(last, wo_all, "x", places))
-    return finish(meta, parts, spread(mine_rank), up, wide)
+    parts = [
+        output_ring(pieces[0], wo_all, "x", places, rank_mine),
+        output_ring(pieces[1], wo_all, "x", places, head_rank),
+    ]
+    return finish(meta, parts, head_rank, up, wide)
 
 
 def solution(mesh):

time: 368 us -> 364 us (0.989)
  waiting for transfers between devices: 125 us -> 105 us
  blocking collectives: 13.3 us -> 25.4 us
  Pallas kernels: 97.6 us -> 105 us
  local copies, waits for them, and re-layouts: 19.6 us -> 13.6 us
  starting transfers between devices: 87.1 us -> 93 us
    all_gather x0 -> x1, blocking collectives: none -> 25.4 us  [on_device(): head_rank = lax.all_gather(rank_mine, TENSOR_AXES, axis=0, tiled=True)]
    all_to_all x1, waiting for transfers between devices: 46.1 us -> 30 us  [on_device(): down = lax.all_to_all(down_out, ADAPTER_AXES, 0, 0, tiled=True)]
    all_to_all x1 -> x0, blocking collectives: 13.3 us -> none  [spread(): lax.all_to_all(copies, TENSOR_AXES, 0, 0, tiled=True).reshape(rows, rank)]
    pallas_call x0 -> x2, Pallas kernels: none -> 6.9 us  [the longest x1 4.77 us: join(): pl.pallas_call(body, out_shape=tuple((jax.ShapeDtypeStruct((tokens, w), b...]
    all_to_all x3, waiting for transfers between devices: 21.1 us -> 15.3 us  [the longest x2 9 us: scatter_rows(): lax.all_to_all(partial.reshape(ways, rows // ways, rank), TENSOR_AXES, 0,...]
    unnamed x58 -> x78, local copies, waits for them, and re-layouts: 7.79 us -> 6.21 us
  transfers between devices with their start and end apart: 50 -> 50, of which waited for: 14 -> 22; matrix products, arithmetic and copies ran while one was open for 6% -> 3% of each run, Pallas kernels for 22% -> 24%
where the time goes in v4:
time: 364 us; the launch traced here: 362 us
  Pallas kernels  105 us (29%)
  waiting for transfers between devices  105 us (29%)
  starting transfers between devices  93 us (26%)
  blocking collectives  25.4 us (7%)
  between operations  14 us (4%)
  local copies, waits for them, and re-layouts  13.6 us (4%)
  other arithmetic  6.24 us (2%)
    ppermute x43, starting transfers between devices, shift(): lax.ppermute(block, axis, [(i, (i + step) % SIDE) for i in range(SIDE)])  67 us
    ppermute x43, waiting for transfers between devices, shift(): lax.ppermute(block, axis, [(i, (i + step) % SIDE) for i in range(SIDE)])  59.7 us
    pallas_call x4, Pallas kernels, project(): pl.pallas_call(body, out_shape=tuple((jax.ShapeDtypeStruct((tokens, w), d...  33.9 us
    all_to_all x1, waiting for transfers between devices, on_device(): down = lax.all_to_all(down_out, ADAPTER_AXES, 0, 0, tiled=True)  30 us
    pallas_call x4, Pallas kernels, output_partial(): pl.pallas_call(body, out_shape=tuple((jax.ShapeDtypeStruct((tokens, width...  28.8 us
    all_gather x1, blocking collectives, on_device(): head_rank = lax.all_gather(rank_mine, TENSOR_AXES, axis=0, tiled=True)  25.4 us
    pallas_call x2, Pallas kernels, attention(): pl.pallas_call(body, out_shape=(jax.ShapeDtypeStruct((count * BLOCK, wide...  13 us
    all_to_all x2, starting transfers between devices, scatter_rows(): lax.all_to_all(partial.reshape(ways, rows // ways, rank), TENSOR_AXES, 0,...  9.56 us
  transfers between devices with their start and end apart: 50, of which 22 were waited for; matrix products, arithmetic and copies ran while one was open for 3% of the time, Pallas kernels for 24%

profile of v4, /device:TPU:0, one launch (start us, length us, event | category | flops | bytes accessed | tf_op | source)
XLA Modules:
  0.0 362.2 jit_solution(12411413298685262380)
XLA Ops:
  7.8 7.4 %shard_map.136 = (bf16[8,256,512]{2,1,0:T(8,128)(2,1)}, bf16[8,64,1152]{2,1,0:T(8,128)(2,1)}, bf16[1024,256]{1,0:T(8,128)(2,1)}, bf16[1024,256]{1,0:T(8,128)(2,1)}) custom-call(s32[8]{0:T(128)} %get-tuple-element.73.pick_ref, bf16[8,192,512]{2,1,0:T(8,128)(2,1)} %bitcast.89, bf16[8,64,512]{2,1,0:T(8,128)(2,1)} %uq.1, bf16[8,64,128]{2,1,0:T(8,128)(2,1)} %ukv.1, ...), custom_call_target="tpu_custom_call" | custom-call | bytes 6553600 | tf_op jit(solution)/shard_map/pallas_call | solution.py:79
  22.4 7.6 %collective-permute-done.refs_1_.refs_0_ = bf16[1024,256]{1,0:T(8,128)(2,1)S(1)} collective-permute-done((bf16[1024,256]{1,0:T(8,128)(2,1)}, bf16[1024,256]{1,0:T(8,128)(2,1)S(1)}, u32[]{:S(2)}, u32[]{:S(2)}) %collective-permute-start) | collective-permute-done | bytes 524320 | tf_op jit(solution)/shard_map/ppermute | solution.py:37
  34.5 4.0 %shard_map.145 = bf16[4,512,256]{2,1,0:T(8,128)(2,1)} custom-call(s32[4]{0:T(128)} %fusion.4.index_ref, bf16[512,8192]{1,0:T(8,128)(2,1)} %m_ref.1, bf16[1024,256]{1,0:T(8,128)(2,1)} %copy-done.7, bf16[1024,256]{1,0:T(8,128)(2,1)} %copy-done.9, bf16[1024,256]{1,0:T(8,128)(2,1)} %copy-done.11, bf16[1024,256]{1,0:T(8,128)(2,1)} %copy-done.12), custom_call_target="tpu_custom_call" | custom-call | bytes 2097152 | tf_op jit(solution)/shard_map/pallas_call | solution.py:383
  44.0 6.3 %collective-permute-done.25 = bf16[512,256]{1,0:T(8,128)(2,1)S(1)} collective-permute-done((bf16[512,256]{1,0:T(8,128)(2,1)S(1)}, bf16[512,256]{1,0:T(8,128)(2,1)S(1)}, u32[]{:S(2)}, u32[]{:S(2)}) %collective-permute-start.25) | collective-permute-done | bytes 262176 | tf_op jit(solution)/shard_map/ppermute | solution.py:37
  54.4 6.4 %all-to-all-start = ((bf16[8,256,512]{2,1,0:T(8,128)(2,1)}), bf16[8,256,512]{2,1,0:T(8,128)(2,1)S(1)}, u32[]{:S(2)}, u32[]{:S(2)}) async-start(bf16[8,256,512]{2,1,0:T(8,128)(2,1)} %get-tuple-element.39), calls=%async_computation | async-start | bytes 4194304 | tf_op jit(solution)/shard_map/all_to_all | solution.py:551
  70.9 3.8 %collective-permute-done.6.refs_8_ = bf16[1024,128]{1,0:T(8,128)(2,1)S(1)} collective-permute-done((bf16[1024,128]{1,0:T(8,128)(2,1)S(1)}, bf16[1024,128]{1,0:T(8,128)(2,1)S(1)}, u32[]{:S(2)}, u32[]{:S(2)}) %collective-permute-start.6) | collective-permute-done | bytes 262176 | tf_op jit(solution)/shard_map/ppermute | solution.py:37
  75.4 30.0 %all-to-all-done.refs_10_.rest_0_.rest_1_.d_ref = bf16[8,256,512]{2,1,0:T(8,128)(2,1)S(1)} async-done(((bf16[8,256,512]{2,1,0:T(8,128)(2,1)}), bf16[8,256,512]{2,1,0:T(8,128)(2,1)S(1)}, u32[]{:S(2)}, u32[]{:S(2)}) %all-to-all-start) | async-done | bytes 2097184 | tf_op jit(solution)/shard_map/all_to_all | solution.py:551
  106.8 4.8 %shard_map.137 = (bf16[1024,512]{1,0:T(8,128)(2,1)}, bf16[1024,512]{1,0:T(8,128)(2,1)}, bf16[1024,512]{1,0:T(8,128)(2,1)}, bf16[1024,512]{1,0:T(8,128)(2,1)}) custom-call(bf16[1024,256]{1,0:T(8,128)(2,1)} %get-tuple-element.37.refs_0_, bf16[1024,256]{1,0:T(8,128)(2,1)} %copy-done.7, bf16[1024,256]{1,0:T(8,128)(2,1)} %copy-done.9, ...), custom_call_target="tpu_custom_call" | custom-call | bytes 8388608 | tf_op jit(solution)/shard_map/pallas_call | solution.py:150
  116.0 4.9 %shard_map.141 = f32[1024,192]{1,0:T(8,128)} custom-call(s32[5,8]{1,0:T(8,128)} %stack.170.meta_ref, bf16[1024,512]{1,0:T(8,128)(2,1)} %x_ref.3, bf16[8,256,512]{2,1,0:T(8,128)(2,1)} %copy-done, bf16[8,256,512]{2,1,0:T(8,128)(2,1)} %copy-done, bf16[1024,512]{1,0:T(8,128)(2,1)} %get-tuple-element.40.refs_0_.rest_2_), custom_call_target="tpu_custom_call" | custom-call | flops 201326592 | bytes 2621440 | tf_op jit(solution)/shard_map/pallas_call | solution.py:118
  120.9 6.0 %all-to-all-start.1 = ((f32[16,64,192]{2,1,0:T(8,128)}), f32[16,64,192]{2,1,0:T(8,128)}, u32[]{:S(2)}, u32[]{:S(2)}) async-start(f32[16,64,192]{2,1,0:T(8,128)} %bitcast.88), calls=%async_computation.1 | async-start | bytes 2097152 | tf_op jit(solution)/shard_map/all_to_all | solution.py:187
  132.7 12.2 %collective-permute-done.8.refs_0_ = bf16[1024,512]{1,0:T(8,128)(2,1)S(1)} collective-permute-done((bf16[1024,512]{1,0:T(8,128)(2,1)}, bf16[1024,512]{1,0:T(8,128)(2,1)S(1)}, u32[]{:S(2)}, u32[]{:S(2)}) %collective-permute-start.8) | collective-permute-done | bytes 1048608 | tf_op jit(solution)/shard_map/ppermute | solution.py:37
  150.3 3.8 %all-to-all-done.1.p_ref = f32[16,64,192]{2,1,0:T(8,128)} async-done(((f32[16,64,192]{2,1,0:T(8,128)}), f32[16,64,192]{2,1,0:T(8,128)}, u32[]{:S(2)}, u32[]{:S(2)}) %all-to-all-start.1) | async-done | bytes 786464 | tf_op jit(solution)/shard_map/all_to_all | solution.py:187
  154.1 3.6 all-to-all-start.3
  157.7 6.7 %collective-permute-done.14.refs_3_ = bf16[1024,512]{1,0:T(8,128)(2,1)} collective-permute-done((bf16[1024,512]{1,0:T(8,128)(2,1)}, bf16[1024,512]{1,0:T(8,128)(2,1)}, u32[]{:S(2)}, u32[]{:S(2)}) %collective-permute-start.14) | collective-permute-done | bytes 1048608 | tf_op jit(solution)/shard_map/ppermute | solution.py:37
  165.9 4.1 %collective-permute-done.17.refs_5_ = bf16[1024,512]{1,0:T(8,128)(2,1)} collective-permute-done((bf16[1024,512]{1,0:T(8,128)(2,1)S(1)}, bf16[1024,512]{1,0:T(8,128)(2,1)}, u32[]{:S(2)}, u32[]{:S(2)}) %collective-permute-start.17) | collective-permute-done | bytes 1048608 | tf_op jit(solution)/shard_map/ppermute | solution.py:37
  170.0 3.8 %collective-permute-start.11 = (bf16[1024,512]{1,0:T(8,128)(2,1)}, bf16[1024,512]{1,0:T(8,128)(2,1)}, u32[]{:S(2)}, u32[]{:S(2)}) collective-permute-start(bf16[1024,512]{1,0:T(8,128)(2,1)} %copy-done.6), channel_id=1, source_target_pairs={{0,12},{4,0},{8,4},{12,8},{1,13},{5,1},{9,5},{13,9},{2,14},{6,2},{... | collective-permute-start | bytes 3145736 | tf_op jit(solution)/shard_map/ppermute | solution.py:37
  179.6 8.0 %shard_map.138 = (f32[1024,512]{1,0:T(8,128)}, f32[1024,128]{1,0:T(8,128)}) custom-call(s32[8]{0:T(128)} %stack.212.index_ref, s32[5,8]{1,0:T(8,128)} %stack.170.meta_ref, bf16[1024,512]{1,0:T(8,128)(2,1)} %get-tuple-element.40.refs_0_.rest_2_, bf16[1024,512]{1,0:T(8,128)(2,1)} %get-tuple-element.41.refs_1_, bf16[1024,512]{1,0:T(8,128)(2,1)} %get-tuple-element.42.refs_2_, ...), custom_call_target="tpu_custom_call" | custom-call | flops 2684354560 | bytes 12058624 | tf_op jit(solution)/shard_map/pallas_call | solution.py:236
  189.8 3.6 all-to-all-start.2
  193.4 13.3 %shard_map.139 = (f32[1024,512]{1,0:T(8,128)}, f32[1024,128]{1,0:T(8,128)}) custom-call(s32[16]{0:T(128)} %stack.203.index_ref, s32[5,8]{1,0:T(8,128)} %stack.170.meta_ref, bf16[1024,512]{1,0:T(8,128)(2,1)} %copy-done.5, bf16[1024,512]{1,0:T(8,128)(2,1)} %copy-done.6, ...), custom_call_target="tpu_custom_call", output_to_operand_aliasing={{0}: (42, {}), {1}: (43, {})} | custom-call | flops 5368709120 | bytes 18874368 | tf_op jit(solution)/shard_map/pallas_call | solution.py:236
  206.6 6.3 %all-to-all-done.2 = bf16[16,64,192]{2,1,0:T(8,128)(2,1)S(1)} async-done(((bf16[16,64,192]{2,1,0:T(8,128)(2,1)}), bf16[16,64,192]{2,1,0:T(8,128)(2,1)S(1)}, u32[]{:S(2)}, u32[]{:S(2)}) %all-to-all-start.2) | async-done | bytes 393248 | tf_op jit(solution)/shard_map/all_to_all | solution.py:583
  214.2 5.5 %shard_map.143.m_ref = bf16[1024,128]{1,0:T(8,128)(2,1)} custom-call(s32[8]{0:T(128)} %stack.186.index_ref, s32[5,8]{1,0:T(8,128)} %stack.170.meta_ref, bf16[1024,512]{1,0:T(8,128)(2,1)} %copy-done.4, bf16[1024,512]{1,0:T(8,128)(2,1)} %collective-permute-done.11.refs_1_, bf16[1024,512]{1,0:T(8,128)(2,1)} %collective-permute-done.13.refs_2_, ...), custom_call_target="tpu_custom_call" | custom-call | flops 536870912 | bytes 5767168 | tf_op jit(solution)/shard_map/pallas_call | solution.py:236
  222.5 7.1 %shard_map.140.q_ref = f32[1024,512]{1,0:T(8,128)} custom-call(s32[8]{0:T(128)} %stack.186.index_ref, s32[5,8]{1,0:T(8,128)} %stack.170.meta_ref, bf16[1024,512]{1,0:T(8,128)(2,1)} %copy-done.4, bf16[1024,512]{1,0:T(8,128)(2,1)} %collective-permute-done.11.refs_1_, ...), custom_call_target="tpu_custom_call", output_to_operand_aliasing={{}: (14, {})} | custom-call | flops 2147483648 | bytes 10485760 | tf_op jit(solution)/shard_map/pallas_call | solution.py:236
  230.3 6.5 %shard_map.146 = (bf16[512,512]{1,0:T(8,128)(2,1)}, f32[512,64]{1,0:T(8,128)}) custom-call(s32[5,8]{1,0:T(8,128)} %stack.170.meta_ref, f32[1024,512]{1,0:T(8,128)} %shard_map.140.q_ref, bf16[1024,192]{1,0:T(8,128)(2,1)} %bitcast.86, bf16[8,64,1152]{2,1,0:T(8,128)(2,1)} %copy-done.1, bf16[8,256,512]{2,1,0:T(8,128)(2,1)} %copy-done, ...), custom_call_target="tpu_custom_call" | custom-call | flops 402653184 | bytes 2097152 | tf_op jit(solution)/shard_map/pallas_call | solution.py:345
  240.2 6.5 %shard_map.144 = (bf16[512,512]{1,0:T(8,128)(2,1)}, f32[512,64]{1,0:T(8,128)}) custom-call(s32[5,8]{1,0:T(8,128)} %stack.170.meta_ref, f32[1024,512]{1,0:T(8,128)} %shard_map.140.q_ref, bf16[1024,192]{1,0:T(8,128)(2,1)} %bitcast.87, bf16[8,64,1152]{2,1,0:T(8,128)(2,1)} %copy-done.1, bf16[8,256,512]{2,1,0:T(8,128)(2,1)} %copy-done, ...), custom_call_target="tpu_custom_call" | custom-call | flops 402653184 | bytes 2097152 | tf_op jit(solution)/shard_map/pallas_call | solution.py:345
  260.0 5.2 %all-to-all-done.4 = f32[16,32,128]{2,1,0:T(8,128)S(1)} async-done(((f32[16,32,128]{2,1,0:T(8,128)}), f32[16,32,128]{2,1,0:T(8,128)S(1)}, u32[]{:S(2)}, u32[]{:S(2)}) %all-to-all-start.4) | async-done | bytes 262176 | tf_op jit(solution)/shard_map/all_to_all | solution.py:187
  265.2 25.4 %all_gather.11.refs_6_.refs_12_ = bf16[512,128]{1,0:T(8,128)(2,1)} all-gather(bf16[32,128]{1,0:T(8,128)(2,1)S(1)} %reduce_sum.81.refs_6_), channel_id=1, replica_groups=mesh['z'=4,'c'=2,'y'=4,'x'=4] {'y','x'}, dimensions={0}, use_global_device_ids=true | all-gather | bytes 139264 | tf_op jit(solution)/shard_map/all_gather | solution.py:623
  295.0 4.8 %shard_map.150 = (bf16[512,256]{1,0:T(8,128)(2,1)}, bf16[512,256]{1,0:T(8,128)(2,1)}) custom-call(s32[6]{0:T(128)} %stack.220.index_ref, bf16[512,512]{1,0:T(8,128)(2,1)} %get-tuple-element.60.refs_0_, bf16[512,512]{1,0:T(8,128)(2,1)} %copy-done.15, bf16[512,512]{1,0:T(8,128)(2,1)} %copy-done.16, bf16[512,256]{1,0:T(8,128)(2,1)} %copy-done.34, ...), custom_call_target="tpu_custom_call" | custom-call | flops 1073741824 | bytes 4194304 | tf_op jit(solution)/shard_map/pallas_call | solution.py:418
  302.0 9.6 %shard_map.149 = (bf16[512,256]{1,0:T(8,128)(2,1)}, bf16[512,256]{1,0:T(8,128)(2,1)}, bf16[512,256]{1,0:T(8,128)(2,1)}, bf16[512,256]{1,0:T(8,128)(2,1)}, f32[512,256]{1,0:T(8,128)}, /*index=5*/f32[512,256]{1,0:T(8,128)}) custom-call(s32[10]{0:T(128)} %stack.177.index_ref, bf16[512,512]{1,0:T(8,128)(2,1)} %get-tuple-element.60.refs_0_, ...), custom_call_target="tpu_custom_call" | custom-call | flops 3221225472 | bytes 8388608 | tf_op jit(solution)/shard_map/pallas_call | solution.py:418
  313.4 4.8 %shard_map.148 = (bf16[512,256]{1,0:T(8,128)(2,1)}, bf16[512,256]{1,0:T(8,128)(2,1)}) custom-call(s32[6]{0:T(128)} %stack.220.index_ref, bf16[512,512]{1,0:T(8,128)(2,1)} %get-tuple-element.49.refs_0_, bf16[512,512]{1,0:T(8,128)(2,1)} %copy-done.13, bf16[512,512]{1,0:T(8,128)(2,1)} %copy-done.14, bf16[512,256]{1,0:T(8,128)(2,1)} %collective-permute-done.23.refs_3_, ...), custom_call_target="tpu_custom_call" | custom-call | flops 1073741824 | bytes 4194304 | tf_op jit(solution)/shard_map/pallas_call | solution.py:418
  320.2 9.6 %shard_map.147 = (bf16[512,256]{1,0:T(8,128)(2,1)}, bf16[512,256]{1,0:T(8,128)(2,1)}, bf16[512,256]{1,0:T(8,128)(2,1)}, bf16[512,256]{1,0:T(8,128)(2,1)}, f32[512,256]{1,0:T(8,128)}, /*index=5*/f32[512,256]{1,0:T(8,128)}) custom-call(s32[10]{0:T(128)} %stack.177.index_ref, bf16[512,512]{1,0:T(8,128)(2,1)} %get-tuple-element.49.refs_0_, ...), custom_call_target="tpu_custom_call" | custom-call | flops 3221225472 | bytes 8388608 | tf_op jit(solution)/shard_map/pallas_call | solution.py:418
  341.6 3.9 %collective-permute-done.40.refs_8_ = bf16[512,256]{1,0:T(8,128)(2,1)S(1)} collective-permute-done((bf16[512,256]{1,0:T(8,128)(2,1)S(1)}, bf16[512,256]{1,0:T(8,128)(2,1)S(1)}, u32[]{:S(2)}, u32[]{:S(2)}) %collective-permute-start.40) | collective-permute-done | bytes 262176 | tf_op jit(solution)/shard_map/ppermute | solution.py:37
  349.4 5.9 %shard_map.151 = f32[1024,512]{1,0:T(8,128)} custom-call(s32[5,8]{1,0:T(8,128)} %stack.170.meta_ref, f32[512,256]{1,0:T(8,128)} %get-tuple-element.52.refs_0_, bf16[512,256]{1,0:T(8,128)(2,1)} %copy-done.20, bf16[512,256]{1,0:T(8,128)(2,1)} %copy-done.31, f32[512,256]{1,0:T(8,128)} %get-tuple-element.56.refs_3_, bf16[512,256]{1,0:T(8,128)(2,1)} %copy-done.22, ...), custom_call_target="tpu_custom_call" | custom-call | flops 67108864 | bytes 7340032 | tf_op jit(solution)/shard_map/pallas_call | solution.py:500
  (194 shorter events, 106.9 us)
Async XLA Ops:
  6.5 287.8 %all-gather.3.cloned.1.call-start = ((), (), s32[]{:S(2)}) async-start(), calls=%async_computation.5 | async-start | bytes 9437184 | tf_op jit(solution)/shard_map/all_gather | solution.py:590
  15.2 14.7 %collective-permute-start = (bf16[1024,256]{1,0:T(8,128)(2,1)}, bf16[1024,256]{1,0:T(8,128)(2,1)S(1)}, u32[]{:S(2)}, u32[]{:S(2)}) collective-permute-start(bf16[1024,256]{1,0:T(8,128)(2,1)} %get-tuple-element.37.refs_0_), channel_id=1, source_target_pairs={{0,1},{1,2},{2,3},{3,0},{4,5},{5,6},{6,7},{7,4},{8,9},{9,10},{10,1... | collective-permute-start | bytes 1572872 | tf_op jit(solution)/shard_map/ppermute | solution.py:37
  18.5 14.4 %collective-permute-start.4 = (bf16[1024,256]{1,0:T(8,128)(2,1)}, bf16[1024,256]{1,0:T(8,128)(2,1)S(1)}, u32[]{:S(2)}, u32[]{:S(2)}) collective-permute-start(bf16[1024,256]{1,0:T(8,128)(2,1)} %get-tuple-element.38.refs_5_), channel_id=1, source_target_pairs={{0,4},{4,8},{8,12},{12,0},{1,5},{5,9},{9,13},{13,1},{2,6},{6,10},{... | collective-permute-start | bytes 1572872 | tf_op jit(solution)/shard_map/ppermute | solution.py:37
  54.4 51.1 %all-to-all-start = ((bf16[8,256,512]{2,1,0:T(8,128)(2,1)}), bf16[8,256,512]{2,1,0:T(8,128)(2,1)S(1)}, u32[]{:S(2)}, u32[]{:S(2)}) async-start(bf16[8,256,512]{2,1,0:T(8,128)(2,1)} %get-tuple-element.39), calls=%async_computation | async-start | bytes 4194304 | tf_op jit(solution)/shard_map/all_to_all | solution.py:551
  111.6 33.3 %collective-permute-start.8 = (bf16[1024,512]{1,0:T(8,128)(2,1)}, bf16[1024,512]{1,0:T(8,128)(2,1)S(1)}, u32[]{:S(2)}, u32[]{:S(2)}) collective-permute-start(bf16[1024,512]{1,0:T(8,128)(2,1)} %get-tuple-element.40.refs_0_.rest_2_), channel_id=1, source_target_pairs={{0,4},{4,8},{8,12},{12,0},{1,5},{5,9},{9,13},{13,1},{2,6},{6,10},{... | collective-permute-start | bytes 3145736 | tf_op jit(solution)/shard_map/ppermute | solution.py:37
  112.4 34.6 %collective-permute-start.10 = (bf16[1024,512]{1,0:T(8,128)(2,1)}, bf16[1024,512]{1,0:T(8,128)(2,1)S(1)}, u32[]{:S(2)}, u32[]{:S(2)}) collective-permute-start(bf16[1024,512]{1,0:T(8,128)(2,1)} %get-tuple-element.41.refs_1_), channel_id=1, source_target_pairs={{0,12},{4,0},{8,4},{12,8},{1,13},{5,1},{9,5},{13,9},{2,14},{6,2},{... | collective-permute-start | bytes 3145736 | tf_op jit(solution)/shard_map/ppermute | solution.py:37
  115.2 32.6 %collective-permute-start.12 = (bf16[1024,512]{1,0:T(8,128)(2,1)}, bf16[1024,512]{1,0:T(8,128)(2,1)}, u32[]{:S(2)}, u32[]{:S(2)}) collective-permute-start(bf16[1024,512]{1,0:T(8,128)(2,1)} %get-tuple-element.42.refs_2_), channel_id=1, source_target_pairs={{0,1},{1,2},{2,3},{3,0},{4,5},{5,6},{6,7},{7,4},{8,9},{9,10},{10,1... | collective-permute-start | bytes 3145736 | tf_op jit(solution)/shard_map/ppermute | solution.py:37
  120.9 33.3 %all-to-all-start.1 = ((f32[16,64,192]{2,1,0:T(8,128)}), f32[16,64,192]{2,1,0:T(8,128)}, u32[]{:S(2)}, u32[]{:S(2)}) async-start(f32[16,64,192]{2,1,0:T(8,128)} %bitcast.88), calls=%async_computation.1 | async-start | bytes 2097152 | tf_op jit(solution)/shard_map/all_to_all | solution.py:187
  126.9 37.5 %collective-permute-start.14 = (bf16[1024,512]{1,0:T(8,128)(2,1)}, bf16[1024,512]{1,0:T(8,128)(2,1)}, u32[]{:S(2)}, u32[]{:S(2)}) collective-permute-start(bf16[1024,512]{1,0:T(8,128)(2,1)} %get-tuple-element.43.refs_3_), channel_id=1, source_target_pairs={{0,3},{1,0},{2,1},{3,2},{4,7},{5,4},{6,5},{7,6},{8,11},{9,8},{10,9... | collective-permute-start | bytes 3145736 | tf_op jit(solution)/shard_map/ppermute | solution.py:37
  130.0 40.0 %collective-permute-start.17 = (bf16[1024,512]{1,0:T(8,128)(2,1)S(1)}, bf16[1024,512]{1,0:T(8,128)(2,1)}, u32[]{:S(2)}, u32[]{:S(2)}) collective-permute-start(bf16[1024,512]{1,0:T(8,128)(2,1)S(1)} %copy-done.3), channel_id=1, source_target_pairs={{0,12},{4,0},{8,4},{12,8},{1,13},{5,1},{9,5},{13,9},{2,14},{6,2},{... | collective-permute-start | bytes 3145736 | tf_op jit(solution)/shard_map/ppermute | solution.py:37
  144.8 29.5 %collective-permute-start.16 = (bf16[1024,512]{1,0:T(8,128)(2,1)}, bf16[1024,512]{1,0:T(8,128)(2,1)}, u32[]{:S(2)}, u32[]{:S(2)}) collective-permute-start(bf16[1024,512]{1,0:T(8,128)(2,1)} %get-tuple-element.41.refs_1_), channel_id=1, source_target_pairs={{0,4},{4,8},{8,12},{12,0},{1,5},{5,9},{9,13},{13,1},{2,6},{6,10},{... | collective-permute-start | bytes 3145736 | tf_op jit(solution)/shard_map/ppermute | solution.py:37
  147.1 27.2 %collective-permute-start.18 = (bf16[1024,512]{1,0:T(8,128)(2,1)}, bf16[1024,512]{1,0:T(8,128)(2,1)}, u32[]{:S(2)}, u32[]{:S(2)}) collective-permute-start(bf16[1024,512]{1,0:T(8,128)(2,1)} %get-tuple-element.43.refs_3_), channel_id=1, source_target_pairs={{0,1},{1,2},{2,3},{3,0},{4,5},{5,6},{6,7},{7,4},{8,9},{9,10},{10,1... | collective-permute-start | bytes 3145736 | tf_op jit(solution)/shard_map/ppermute | solution.py:37
  147.8 45.6 %collective-permute-start.19 = (bf16[1024,512]{1,0:T(8,128)(2,1)}, bf16[1024,512]{1,0:T(8,128)(2,1)}, u32[]{:S(2)}, u32[]{:S(2)}) collective-permute-start(bf16[1024,512]{1,0:T(8,128)(2,1)} %get-tuple-element.42.refs_2_), channel_id=1, source_target_pairs={{0,3},{1,0},{2,1},{3,2},{4,7},{5,4},{6,5},{7,6},{8,11},{9,8},{10,9... | collective-permute-start | bytes 3145736 | tf_op jit(solution)/shard_map/ppermute | solution.py:37
  154.1 35.7 %all-to-all-start.3 = ((bf16[8,64,1152]{2,1,0:T(8,128)(2,1)}), bf16[8,64,1152]{2,1,0:T(8,128)(2,1)S(1)}, u32[]{:S(2)}, u32[]{:S(2)}) async-start(bf16[8,64,1152]{2,1,0:T(8,128)(2,1)} %get-tuple-element.47), calls=%async_computation.3 | async-start | bytes 2359296 | tf_op jit(solution)/shard_map/all_to_all | solution.py:584
  164.4 48.5 %collective-permute-start.9 = (bf16[1024,512]{1,0:T(8,128)(2,1)}, bf16[1024,512]{1,0:T(8,128)(2,1)S(1)}, u32[]{:S(2)}, u32[]{:S(2)}) collective-permute-start(bf16[1024,512]{1,0:T(8,128)(2,1)} %copy-done.5), channel_id=1, source_target_pairs={{0,4},{4,8},{8,12},{12,0},{1,5},{5,9},{9,13},{13,1},{2,6},{6,10},{... | collective-permute-start | bytes 3145736 | tf_op jit(solution)/shard_map/ppermute | solution.py:37
  170.0 43.0 %collective-permute-start.11 = (bf16[1024,512]{1,0:T(8,128)(2,1)}, bf16[1024,512]{1,0:T(8,128)(2,1)}, u32[]{:S(2)}, u32[]{:S(2)}) collective-permute-start(bf16[1024,512]{1,0:T(8,128)(2,1)} %copy-done.6), channel_id=1, source_target_pairs={{0,12},{4,0},{8,4},{12,8},{1,13},{5,1},{9,5},{13,9},{2,14},{6,2},{... | collective-permute-start | bytes 3145736 | tf_op jit(solution)/shard_map/ppermute | solution.py:37
  174.3 38.7 %collective-permute-start.13 = (bf16[1024,512]{1,0:T(8,128)(2,1)}, bf16[1024,512]{1,0:T(8,128)(2,1)}, u32[]{:S(2)}, u32[]{:S(2)}) collective-permute-start(bf16[1024,512]{1,0:T(8,128)(2,1)} %collective-permute-done.12.refs_2_), channel_id=1, source_target_pairs={{0,1},{1,2},{2,3},{3,0},{4,5},{5,6},{6,7},{7,4},{8,9},{9,10},{10,1... | collective-permute-start | bytes 3145736 | tf_op jit(solution)/shard_map/ppermute | solution.py:37
  174.3 38.7 %collective-permute-start.15 = (bf16[1024,512]{1,0:T(8,128)(2,1)}, bf16[1024,512]{1,0:T(8,128)(2,1)}, u32[]{:S(2)}, u32[]{:S(2)}) collective-permute-start(bf16[1024,512]{1,0:T(8,128)(2,1)} %collective-permute-done.14.refs_3_), channel_id=1, source_target_pairs={{0,3},{1,0},{2,1},{3,2},{4,7},{5,4},{6,5},{7,6},{8,11},{9,8},{10,9... | collective-permute-start | bytes 3145736 | tf_op jit(solution)/shard_map/ppermute | solution.py:37
  189.8 23.2 %all-to-all-start.2 = ((bf16[16,64,192]{2,1,0:T(8,128)(2,1)}), bf16[16,64,192]{2,1,0:T(8,128)(2,1)S(1)}, u32[]{:S(2)}, u32[]{:S(2)}) async-start(bf16[16,64,192]{2,1,0:T(8,128)(2,1)} %shard_map.142), calls=%async_computation.2 | async-start | bytes 1048576 | tf_op jit(solution)/shard_map/all_to_all | solution.py:583
  236.9 18.4 %collective-permute-start.34 = (bf16[512,512]{1,0:T(8,128)(2,1)}, bf16[512,512]{1,0:T(8,128)(2,1)S(1)}, u32[]{:S(2)}, u32[]{:S(2)}) collective-permute-start(bf16[512,512]{1,0:T(8,128)(2,1)} %get-tuple-element.60.refs_0_), channel_id=1, source_target_pairs={{0,4},{4,8},{8,12},{12,0},{1,5},{5,9},{9,13},{13,1},{2,6},{6,10},{... | collective-permute-start | bytes 1572872 | tf_op jit(solution)/shard_map/ppermute | solution.py:37
  236.9 20.3 %collective-permute-start.35 = (bf16[512,512]{1,0:T(8,128)(2,1)}, bf16[512,512]{1,0:T(8,128)(2,1)S(1)}, u32[]{:S(2)}, u32[]{:S(2)}) collective-permute-start(bf16[512,512]{1,0:T(8,128)(2,1)} %get-tuple-element.60.refs_0_), channel_id=1, source_target_pairs={{0,12},{4,0},{8,4},{12,8},{1,13},{5,1},{9,5},{13,9},{2,14},{6,2},{... | collective-permute-start | bytes 1572872 | tf_op jit(solution)/shard_map/ppermute | solution.py:37
  246.7 44.0 %collective-permute-start.21 = (bf16[512,512]{1,0:T(8,128)(2,1)}, bf16[512,512]{1,0:T(8,128)(2,1)S(1)}, u32[]{:S(2)}, u32[]{:S(2)}) collective-permute-start(bf16[512,512]{1,0:T(8,128)(2,1)} %get-tuple-element.49.refs_0_), channel_id=1, source_target_pairs={{0,4},{4,8},{8,12},{12,0},{1,5},{5,9},{9,13},{13,1},{2,6},{6,10},{... | collective-permute-start | bytes 1572872 | tf_op jit(solution)/shard_map/ppermute | solution.py:37
  246.7 44.1 %collective-permute-start.22 = (bf16[512,512]{1,0:T(8,128)(2,1)}, bf16[512,512]{1,0:T(8,128)(2,1)S(1)}, u32[]{:S(2)}, u32[]{:S(2)}) collective-permute-start(bf16[512,512]{1,0:T(8,128)(2,1)} %get-tuple-element.49.refs_0_), channel_id=1, source_target_pairs={{0,12},{4,0},{8,4},{12,8},{1,13},{5,1},{9,5},{13,9},{2,14},{6,2},{... | collective-permute-start | bytes 1572872 | tf_op jit(solution)/shard_map/ppermute | solution.py:37
  255.3 39.0 %collective-permute-start.36 = (bf16[512,256]{1,0:T(8,128)(2,1)S(1)}, bf16[512,256]{1,0:T(8,128)(2,1)S(1)}, u32[]{:S(2)}, u32[]{:S(2)}) collective-permute-start(bf16[512,256]{1,0:T(8,128)(2,1)S(1)} %slice.58), channel_id=1, source_target_pairs={{0,4},{4,8},{8,12},{12,0},{1,5},{5,9},{9,13},{13,1},{2,6},{6,10},{... | collective-permute-start | bytes 786440 | tf_op jit(solution)/shard_map/ppermute | solution.py:37
  257.2 37.1 %collective-permute-start.37 = (bf16[512,256]{1,0:T(8,128)(2,1)S(1)}, bf16[512,256]{1,0:T(8,128)(2,1)}, u32[]{:S(2)}, u32[]{:S(2)}) collective-permute-start(bf16[512,256]{1,0:T(8,128)(2,1)S(1)} %slice.59), channel_id=1, source_target_pairs={{0,12},{4,0},{8,4},{12,8},{1,13},{5,1},{9,5},{13,9},{2,14},{6,2},{... | collective-permute-start | bytes 786440 | tf_op jit(solution)/shard_map/ppermute | solution.py:37
  290.7 22.7 %collective-permute-start.23 = (bf16[512,256]{1,0:T(8,128)(2,1)S(1)}, bf16[512,256]{1,0:T(8,128)(2,1)}, u32[]{:S(2)}, u32[]{:S(2)}) collective-permute-start(bf16[512,256]{1,0:T(8,128)(2,1)S(1)} %slice.52), channel_id=1, source_target_pairs={{0,4},{4,8},{8,12},{12,0},{1,5},{5,9},{9,13},{13,1},{2,6},{6,10},{... | collective-permute-start | bytes 786440 | tf_op jit(solution)/shard_map/ppermute | solution.py:37
  290.8 22.5 %collective-permute-start.24 = (bf16[512,256]{1,0:T(8,128)(2,1)S(1)}, bf16[512,256]{1,0:T(8,128)(2,1)}, u32[]{:S(2)}, u32[]{:S(2)}) collective-permute-start(bf16[512,256]{1,0:T(8,128)(2,1)S(1)} %slice.53), channel_id=1, source_target_pairs={{0,12},{4,0},{8,4},{12,8},{1,13},{5,1},{9,5},{13,9},{2,14},{6,2},{... | collective-permute-start | bytes 786440 | tf_op jit(solution)/shard_map/ppermute | solution.py:37
  299.9 30.0 %collective-permute-start.42 = (bf16[512,256]{1,0:T(8,128)(2,1)}, bf16[512,256]{1,0:T(8,128)(2,1)S(1)}, u32[]{:S(2)}, u32[]{:S(2)}) collective-permute-start(bf16[512,256]{1,0:T(8,128)(2,1)} %get-tuple-element.68), channel_id=1, source_target_pairs={{0,3},{1,0},{2,1},{3,2},{4,7},{5,4},{6,5},{7,6},{8,11},{9,8},{10,9... | collective-permute-start | bytes 786440 | tf_op jit(solution)/shard_map/ppermute | solution.py:37
  300.5 29.6 %collective-permute-start.39 = (bf16[512,256]{1,0:T(8,128)(2,1)}, bf16[512,256]{1,0:T(8,128)(2,1)S(1)}, u32[]{:S(2)}, u32[]{:S(2)}) collective-permute-start(bf16[512,256]{1,0:T(8,128)(2,1)} %get-tuple-element.64), channel_id=1, source_target_pairs={{0,1},{1,2},{2,3},{3,0},{4,5},{5,6},{6,7},{7,4},{8,9},{9,10},{10,1... | collective-permute-start | bytes 786440 | tf_op jit(solution)/shard_map/ppermute | solution.py:37
  311.6 26.2 %collective-permute-start.38 = (bf16[512,256]{1,0:T(8,128)(2,1)}, bf16[512,256]{1,0:T(8,128)(2,1)S(1)}, u32[]{:S(2)}, u32[]{:S(2)}) collective-permute-start(bf16[512,256]{1,0:T(8,128)(2,1)} %get-tuple-element.62), channel_id=1, source_target_pairs={{0,3},{1,0},{2,1},{3,2},{4,7},{5,4},{6,5},{7,6},{8,11},{9,8},{10,9... | collective-permute-start | bytes 786440 | tf_op jit(solution)/shard_map/ppermute | solution.py:37
  318.2 15.1 %collective-permute-start.32 = (bf16[512,256]{1,0:T(8,128)(2,1)}, bf16[512,256]{1,0:T(8,128)(2,1)S(1)}, u32[]{:S(2)}, u32[]{:S(2)}) collective-permute-start(bf16[512,256]{1,0:T(8,128)(2,1)} %get-tuple-element.59), channel_id=1, source_target_pairs={{0,3},{1,0},{2,1},{3,2},{4,7},{5,4},{6,5},{7,6},{8,11},{9,8},{10,9... | collective-permute-start | bytes 786440 | tf_op jit(solution)/shard_map/ppermute | solution.py:37
  318.4 16.0 %collective-permute-start.29 = (bf16[512,256]{1,0:T(8,128)(2,1)}, bf16[512,256]{1,0:T(8,128)(2,1)S(1)}, u32[]{:S(2)}, u32[]{:S(2)}) collective-permute-start(bf16[512,256]{1,0:T(8,128)(2,1)} %get-tuple-element.55), channel_id=1, source_target_pairs={{0,1},{1,2},{2,3},{3,0},{4,5},{5,6},{6,7},{7,4},{8,9},{9,10},{10,1... | collective-permute-start | bytes 786440 | tf_op jit(solution)/shard_map/ppermute | solution.py:37
  (57 other events, 714.8 us)
Sparse Core Ops, SparseCore 0:
  54.5 68.7 all-gather.2

commit v5 on v4

--- a/solution.py
+++ b/solution.py
@@ -55,14 +55,16 @@
     return [index, (index + SIDE - 1) % SIDE, (index + 1) % SIDE, (index + 2) % SIDE]
 
 
-def pick_adapters(pick, down_qkv, up_q, up_kv, down_o, up_o, x):
+def pick_local(pick, down_qkv, up_q, up_kv, down_o, up_o, x, wo, unit):
     tokens, local = x.shape
-    groups = pick.shape[0]
+    groups = pick.shape[0] - SIDE
     rank3, depth = down_qkv.shape[1:]
     rank, wide = up_q.shape[1:]
     narrow = up_kv.shape[2]
-
-    def body(pick_ref, dq, uq, ukv, do, uo, x_ref, down, up, left, right):
+    rows = wo.shape[0] // groups
+
+    def body(pick_ref, dq, uq, ukv, do, uo, x_ref, *refs):
+        w_refs, (down, up, left, right), w_outs = refs[:SIDE], refs[SIDE : SIDE + 4], refs[SIDE + 4 :]
         left[...] = x_ref[:, : local // 2]
         right[...] = x_ref[:, local // 2 :]
         down[0, :rank3, :] = dq[0]
@@ -70,33 +72,61 @@
         up[0, :, :wide] = uq[0]
         up[0, :, wide : 2 * wide] = uo[0]
         up[0, :, 2 * wide :] = ukv[0]
+        for w_ref, w_out in zip(w_refs, w_outs):
+            w_out[...] = w_ref[...]
 
     def chosen(a):
         return pl.BlockSpec((1,) + a.shape[1:], lambda i, p: (p[i], 0, 0))
 
+    def columns(k):
+        return pl.BlockSpec((rows, unit), lambda i, p: (i, p[groups + k]))
+
     down_shape = (groups, rank3 + rank, depth)
     up_shape = (groups, rank, 2 * wide + narrow)
-    return pl.pallas_call(
-        body,
-        out_shape=(
-            jax.ShapeDtypeStruct(down_shape, bf16),
-            jax.ShapeDtypeStruct(up_shape, bf16),
-            jax.ShapeDtypeStruct((tokens, local // 2), bf16),
-            jax.ShapeDtypeStruct((tokens, local // 2), bf16),
+    half = (tokens, local // 2)
+    share = (wo.shape[0], unit)
+    return pl.pallas_call(
+        body,
+        out_shape=tuple(
+            jax.ShapeDtypeStruct(s, bf16)
+            for s in (down_shape, up_shape, half, half, share, share, share, share)
         ),
         grid_spec=pltpu.PrefetchScalarGridSpec(
             num_scalar_prefetch=1,
             grid=(groups,),
             in_specs=[chosen(a) for a in (down_qkv, up_q, up_kv, down_o, up_o)]
-            + [pl.BlockSpec((tokens // groups, local), lambda i, p: (i, 0))],
+            + [pl.BlockSpec((tokens // groups, local), lambda i, p: (i, 0))]
+            + [columns(k) for k in range(SIDE)],
             out_specs=[
                 pl.BlockSpec((1,) + s[1:], lambda i, p: (i, 0, 0)) for s in (down_shape, up_shape)
             ]
-            + [pl.BlockSpec((tokens // groups, local // 2), lambda i, p: (i, 0))] * 2,
+            + [pl.BlockSpec((tokens // groups, local // 2), lambda i, p: (i, 0))] * 2
+            + [pl.BlockSpec((rows, unit), lambda i, p: (i, 0))] * SIDE,
         ),
         compiler_params=params(),
         cost_estimate=cost(0, 2 * 2 * (math.prod(down_shape) + math.prod(up_shape))),
-    )(pick, down_qkv, up_q, up_kv, down_o, up_o, x)
+    )(pick, down_qkv, up_q, up_kv, down_o, up_o, x, wo, wo, wo, wo)
+
+
+def stack_rows(blocks, after):
+    rows, width = blocks[0].shape
+    count = len(blocks)
+
+    def body(*refs):
+        out = refs[-1]
+        for k in range(count):
+            out[k * rows : (k + 1) * rows, :] = refs[k][...]
+
+    spec = pl.BlockSpec((rows, width), lambda i: (0, 0))
+    return pl.pallas_call(
+        body,
+        out_shape=jax.ShapeDtypeStruct((count * rows, width), bf16),
+        grid=(1,),
+        in_specs=[spec] * count + passive(after),
+        out_specs=pl.BlockSpec((count * rows, width), lambda i: (0, 0)),
+        compiler_params=params(),
+        cost_estimate=cost(0, 4 * count * rows * width),
+    )(*blocks, *after)
 
 
 def rank_partial(meta, x, down, rank3, after):
@@ -373,27 +403,6 @@
     )(meta, q, shrunk, up, down, mine, other, cosine, sine)
 
 
-def pick_columns(index, matrix, width, after):
-    depth = matrix.shape[0]
-    count = index.shape[0]
-
-    def body(index_ref, m_ref, *refs):
-        refs[-1][0] = m_ref[...]
-
-    return pl.pallas_call(
-        body,
-        out_shape=jax.ShapeDtypeStruct((count, depth, width), bf16),
-        grid_spec=pltpu.PrefetchScalarGridSpec(
-            num_scalar_prefetch=1,
-            grid=(count,),
-            in_specs=[pl.BlockSpec((depth, width), lambda i, p: (0, p[i]))] + passive(after),
-            out_specs=pl.BlockSpec((1, depth, width), lambda i, p: (i, 0, 0)),
-        ),
-        compiler_params=params(),
-        cost_estimate=cost(0, 4 * count * depth * width),
-    )(index, matrix, *after)
-
-
 def output_partial(index, pieces, weights, dtypes, after):
     tokens = pieces[0].shape[0]
     depth, width = weights.shape[1:]
@@ -547,14 +556,23 @@
     cosine, sine = rotation_tables()
 
     stores = (jnp.swapaxes(down_qkv, 1, 2), up_q, up_kv, jnp.swapaxes(down_o, 1, 2), up_o)
-    down_out, up_out, x_a, x_b = pick_adapters(pick, *stores, x)
+    ys, xs = ring_order(y), ring_order(xi)
+    unit = wo.shape[1] // (SIDE * SIDE * 2)
+    wo_cols = jnp.stack(ys) * (2 * SIDE) + group
+    down_out, up_out, x_a, x_b, *sent = pick_local(
+        jnp.concatenate([pick, wo_cols.astype(i32)]), *stores, x, wo, unit
+    )
     down = lax.all_to_all(down_out, ADAPTER_AXES, 0, 0, tiled=True)
 
-    ys, xs = ring_order(y), ring_order(xi)
     first_a = ring_gather(x_a, "x")
     first_b = ring_gather(x_b, "y")
+
+    got = [sent[0], shift(sent[2], "y", 1), shift(sent[1], "y", -1), shift(sent[3], "y", 2)]
+    wo_mine = stack_rows(got, first_a[1:3] + first_b[1:3])
+    wo_all = lax.all_gather(wo_mine, ADAPTER_AXES, axis=0)
+
     low_a, high_a, low_b, high_b = join(
-        [first_a[:2], first_a[2:], first_b[:2], first_b[2:]], [down]
+        [first_a[:2], first_a[2:], first_b[:2], first_b[2:]], [wo_mine]
     )
     far_a, next_a = second_gather(low_a, high_a, "y")
     far_b, next_b = second_gather(low_b, high_b, "x")
@@ -578,16 +596,10 @@
         512,
     )
 
-    pieces = scatter_rows(rank_partial(meta, x, down, 3 * rank, [low_a]))
-    copies = share_sum(pieces, [*far_a, *far_b])
+    pieces = scatter_rows(rank_partial(meta, x, down, 3 * rank, [*far_a, *far_b]))
+    copies = share_sum(pieces, [])
     shrunk = lax.all_to_all(copies, TENSOR_AXES, 0, 0, tiled=True).reshape(tokens, 3 * rank)
     up = lax.all_to_all(up_out, ADAPTER_AXES, 0, 0, tiled=True)
-
-    unit = wo.shape[1] // (SIDE * SIDE * 2)
-    order = ring_order(y)
-    sent = pick_columns(jnp.stack(order).astype(i32) * (2 * SIDE) + group, wo, unit, first_a[1:3] + first_b[1:3])
-    got = [sent[0], shift(sent[2], "y", 1), shift(sent[1], "y", -1), shift(sent[3], "y", 2)]
-    wo_all = lax.all_gather(jnp.concatenate(got, axis=0), ADAPTER_AXES, axis=0)
 
     a_low, a_high = shift(far_a[0], "y", 1), shift(far_a[1], "y", -1)
     b_low, b_high = shift(far_b[0], "x", 1), shift(far_b[1], "x", -1)
@@ -619,11 +631,11 @@
         )
         ranks.append(head)
         pieces.append(ring_gather(attended, "y"))
-    rank_mine = jnp.sum(scatter_rows(jnp.concatenate(ranks, axis=1)), axis=0).astype(bf16)
-    head_rank = lax.all_gather(rank_mine, TENSOR_AXES, axis=0, tiled=True)
+    copies = share_sum(scatter_rows(jnp.concatenate(ranks, axis=1)), [])
+    head_rank = lax.all_to_all(copies, TENSOR_AXES, 0, 0, tiled=True).reshape(tokens // 2, 2 * rank)
     places = [jnp.int32(k) for k in range(SIDE)]
     parts = [
-        output_ring(pieces[0], wo_all, "x", places, rank_mine),
+        output_ring(pieces[0], wo_all, "x", places, copies),
         output_ring(pieces[1], wo_all, "x", places, head_rank),
     ]
     return finish(meta, parts, head_rank, up, wide)

time: 364 us -> 322 us (0.88)
  blocking collectives: 25.4 us -> 0 us
  waiting for transfers between devices: 105 us -> 86.9 us
    all_to_all x1, waiting for transfers between devices: 30 us -> 0.01 us  [on_device(): down = lax.all_to_all(down_out, ADAPTER_AXES, 0, 0, tiled=True)]
    all_gather x1 -> x0, blocking collectives: 25.4 us -> none  [on_device(): head_rank = lax.all_gather(rank_mine, TENSOR_AXES, axis=0, tiled=True)]
    all_to_all x2, waiting for transfers between devices: 9 us -> 18.2 us  [scatter_rows(): lax.all_to_all(partial.reshape(ways, rows // ways, rank), TENSOR_AXES, 0,...]
    ppermute x43, waiting for transfers between devices: 59.7 us -> 68.6 us  [shift(): lax.ppermute(block, axis, [(i, (i + step) % SIDE) for i in range(SIDE)])]
    all_to_all x1 -> x2, waiting for transfers between devices: 6.32 us -> 0.01 us  [on_device(): lax.all_to_all(copies, TENSOR_AXES, 0, 0, tiled=True)]
    all_to_all x1 -> x2, starting transfers between devices: 3.57 us -> 9.31 us  [on_device(): lax.all_to_all(copies, TENSOR_AXES, 0, 0, tiled=True)]
  transfers between devices with their start and end apart: 50 -> 51, of which waited for: 22 -> 17; matrix products, arithmetic and copies ran while one was open for 3% -> 3% of each run, Pallas kernels for 24% -> 28%
where the time goes in v5:
time: 322 us; the launch traced here: 320 us
  Pallas kernels  105 us (33%)
  starting transfers between devices  96.4 us (30%)
  waiting for transfers between devices  86.9 us (27%)
  between operations  14 us (4%)
  local copies, waits for them, and re-layouts  13.3 us (4%)
  other arithmetic  4.65 us (1%)
    ppermute x43, waiting for transfers between devices, shift(): lax.ppermute(block, axis, [(i, (i + step) % SIDE) for i in range(SIDE)])  68.6 us
    ppermute x43, starting transfers between devices, shift(): lax.ppermute(block, axis, [(i, (i + step) % SIDE) for i in range(SIDE)])  66.2 us
    pallas_call x4, Pallas kernels, project(): pl.pallas_call(body, out_shape=tuple((jax.ShapeDtypeStruct((tokens, w), d...  33.8 us
    pallas_call x4, Pallas kernels, output_partial(): pl.pallas_call(body, out_shape=tuple((jax.ShapeDtypeStruct((tokens, width...  28.9 us
    all_to_all x2, waiting for transfers between devices, scatter_rows(): lax.all_to_all(partial.reshape(ways, rows // ways, rank), TENSOR_AXES, 0,...  18.2 us
    pallas_call x2, Pallas kernels, attention(): pl.pallas_call(body, out_shape=(jax.ShapeDtypeStruct((count * BLOCK, wide...  13 us
    all_to_all x2, starting transfers between devices, scatter_rows(): lax.all_to_all(partial.reshape(ways, rows // ways, rank), TENSOR_AXES, 0,...  9.68 us
    all_to_all x2, starting transfers between devices, on_device(): lax.all_to_all(copies, TENSOR_AXES, 0, 0, tiled=True)  9.31 us
  transfers between devices with their start and end apart: 51, of which 17 were waited for; matrix products, arithmetic and copies ran while one was open for 3% of the time, Pallas kernels for 28%

profile of v5, /device:TPU:0, one launch (start us, length us, event | category | flops | bytes accessed | tf_op | source)
XLA Modules:
  0.0 320.3 jit_solution(14150877463036571479)
XLA Ops:
  8.0 7.8 %shard_map.136 = (bf16[8,256,512]{2,1,0:T(8,128)(2,1)}, bf16[8,64,1152]{2,1,0:T(8,128)(2,1)}, bf16[1024,256]{1,0:T(8,128)(2,1)}, bf16[1024,256]{1,0:T(8,128)(2,1...) custom-call(s32[12]{0:T(128)} %pad_add_fusion.pick_ref, ...), custom_call_target="tpu_custom_call" | custom-call | bytes 6553600 | tf_op jit(solution)/shard_map/pallas_call | solution.py:88
  15.8 3.4 %collective-permute-start.10 = (bf16[512,256]{1,0:T(8,128)(2,1)}, bf16[512,256]{1,0:T(8,128)(2,1)S(1)}, u32[]{:S(2)}, u32[]{:S(2)}) collective-permute-start(bf16[512,256]{1,0:T(8,128)(2,1)} %get-tuple-element.46), channel_id=1, source_target_pairs={{0,8},{4,12},{8,0},{12,4},{1,9},{5,13},{9,1},{13,5},{2,10},{6,14},... | collective-permute-start | bytes 786440 | tf_op jit(solution)/shard_map/ppermute | solution.py:37
  23.0 3.7 %collective-permute-done.10.refs_3_ = bf16[512,256]{1,0:T(8,128)(2,1)S(1)} collective-permute-done((bf16[512,256]{1,0:T(8,128)(2,1)}, bf16[512,256]{1,0:T(8,128)(2,1)S(1)}, u32[]{:S(2)}, u32[]{:S(2)}) %collective-permute-start.10) | collective-permute-done | bytes 262176 | tf_op jit(solution)/shard_map/ppermute | solution.py:37
  33.0 12.2 %collective-permute-done.9.refs_2_ = bf16[512,256]{1,0:T(8,128)(2,1)S(1)} collective-permute-done((bf16[512,256]{1,0:T(8,128)(2,1)}, bf16[512,256]{1,0:T(8,128)(2,1)S(1)}, u32[]{:S(2)}, u32[]{:S(2)}) %collective-permute-start.9) | collective-permute-done | bytes 262176 | tf_op jit(solution)/shard_map/ppermute | solution.py:37
  48.9 5.4 %all-to-all-start = ((bf16[8,256,512]{2,1,0:T(8,128)(2,1)}), bf16[8,256,512]{2,1,0:T(8,128)(2,1)S(1)}, u32[]{:S(2)}, u32[]{:S(2)}) async-start(bf16[8,256,512]{2,1,0:T(8,128)(2,1)} %get-tuple-element.54), calls=%async_computation | async-start | bytes 4194304 | tf_op jit(solution)/shard_map/all_to_all | solution.py:565
  64.4 4.3 %collective-permute-done.6.refs_8_ = bf16[1024,128]{1,0:T(8,128)(2,1)S(1)} collective-permute-done((bf16[1024,128]{1,0:T(8,128)(2,1)S(1)}, bf16[1024,128]{1,0:T(8,128)(2,1)S(1)}, u32[]{:S(2)}, u32[]{:S(2)}) %collective-permute-start.6) | collective-permute-done | bytes 262176 | tf_op jit(solution)/shard_map/ppermute | solution.py:37
  70.1 4.9 %shard_map.138 = (bf16[1024,512]{1,0:T(8,128)(2,1)}, bf16[1024,512]{1,0:T(8,128)(2,1)}, bf16[1024,512]{1,0:T(8,128)(2,1)}, bf16[1024,512]{1,0:T(8,128)(2,1)}) custom-call(bf16[1024,256]{1,0:T(8,128)(2,1)} %get-tuple-element.41.refs_0_, bf16[1024,256]{1,0:T(8,128)(2,1)} %copy-done.6, bf16[1024,256]{1,0:T(8,128)(2,1)} %copy-done.8, ...), custom_call_target="tpu_custom_call" | custom-call | bytes 8388608 | tf_op jit(solution)/shard_map/pallas_call | solution.py:180
  82.8 18.3 %collective-permute-done.11.refs_0_.rest_2_ = bf16[1024,512]{1,0:T(8,128)(2,1)S(1)} collective-permute-done((bf16[1024,512]{1,0:T(8,128)(2,1)}, bf16[1024,512]{1,0:T(8,128)(2,1)S(1)}, u32[]{:S(2)}, u32[]{:S(2)}) %collective-permute-start.11) | collective-permute-done | bytes 1048608 | tf_op jit(solution)/shard_map/ppermute | solution.py:37
  105.3 4.9 %shard_map.142 = f32[1024,192]{1,0:T(8,128)} custom-call(s32[5,8]{1,0:T(8,128)} %stack.170.meta_ref, bf16[1024,512]{1,0:T(8,128)(2,1)} %x_ref.3, bf16[8,256,512]{2,1,0:T(8,128)(2,1)} %copy-done, bf16[8,256,512]{2,1,0:T(8,128)(2,1)} %copy-done, bf16[1024,512]{1,0:T(8,128)(2,1)} %copy-done.3, bf16[1024,512]{1,0:T(8,128)(2,1)} %collective-permute-done.13.refs_1_.rest_3_, ...), custom_call_target="tpu_custom_call" | custom-call | flops 201326592 | bytes 2621440 | tf_op jit(solution)/shard_map/pallas_call | solution.py:148
  110.1 5.6 %all-to-all-start.1 = ((f32[16,64,192]{2,1,0:T(8,128)}), f32[16,64,192]{2,1,0:T(8,128)S(1)}, u32[]{:S(2)}, u32[]{:S(2)}) async-start(f32[16,64,192]{2,1,0:T(8,128)} %bitcast.81), calls=%async_computation.1 | async-start | bytes 2097152 | tf_op jit(solution)/shard_map/all_to_all | solution.py:217
  122.2 12.1 %all-to-all-done.1.p_ref = f32[16,64,192]{2,1,0:T(8,128)S(1)} async-done(((f32[16,64,192]{2,1,0:T(8,128)}), f32[16,64,192]{2,1,0:T(8,128)S(1)}, u32[]{:S(2)}, u32[]{:S(2)}) %all-to-all-start.1) | async-done | bytes 786464 | tf_op jit(solution)/shard_map/all_to_all | solution.py:217
  134.3 4.0 %all-to-all-start.3 = ((bf16[8,64,1152]{2,1,0:T(8,128)(2,1)}), bf16[8,64,1152]{2,1,0:T(8,128)(2,1)S(1)}, u32[]{:S(2)}, u32[]{:S(2)}) async-start(bf16[8,64,1152]{2,1,0:T(8,128)(2,1)} %get-tuple-element.55), calls=%async_computation.3 | async-start | bytes 2359296 | tf_op jit(solution)/shard_map/all_to_all | solution.py:602
  138.4 14.1 %collective-permute-done.19.refs_4_ = bf16[1024,512]{1,0:T(8,128)(2,1)} collective-permute-done((bf16[1024,512]{1,0:T(8,128)(2,1)}, bf16[1024,512]{1,0:T(8,128)(2,1)}, u32[]{:S(2)}, u32[]{:S(2)}) %collective-permute-start.19) | collective-permute-done | bytes 1048608 | tf_op jit(solution)/shard_map/ppermute | solution.py:37
  158.9 8.0 %shard_map.139 = (f32[1024,512]{1,0:T(8,128)}, f32[1024,128]{1,0:T(8,128)}) custom-call(s32[8]{0:T(128)} %stack.217.index_ref, s32[5,8]{1,0:T(8,128)} %stack.170.meta_ref, bf16[1024,512]{1,0:T(8,128)(2,1)} %get-tuple-element.47.refs_0_, bf16[1024,512]{1,0:T(8,128)(2,1)} %get-tuple-element.48.refs_1_, bf16[1024,512]{1,0:T(8,128)(2,1)} %get-tuple-element.49.refs_2_, ...), custom_call_target="tpu_custom_call" | custom-call | flops 2684354560 | bytes 12058624 | tf_op jit(solution)/shard_map/pallas_call | solution.py:266
  169.1 3.6 %all-to-all-start.2 = ((bf16[16,64,192]{2,1,0:T(8,128)(2,1)}), bf16[16,64,192]{2,1,0:T(8,128)(2,1)S(1)}, u32[]{:S(2)}, u32[]{:S(2)}) async-start(bf16[16,64,192]{2,1,0:T(8,128)(2,1)} %shard_map.143), calls=%async_computation.2 | async-start | bytes 1048576 | tf_op jit(solution)/shard_map/all_to_all | solution.py:601
  172.7 13.2 %shard_map.140 = (f32[1024,512]{1,0:T(8,128)}, f32[1024,128]{1,0:T(8,128)}) custom-call(s32[16]{0:T(128)} %stack.208.index_ref, s32[5,8]{1,0:T(8,128)} %stack.170.meta_ref, bf16[1024,512]{1,0:T(8,128)(2,1)} %copy-done.3, bf16[1024,512]{1,0:T(8,128)(2,1)} %collective-permute-done.13.refs_1_.rest_3_, ...), custom_call_target="tpu_custom_call", output_to_operand_aliasing={{0}: (42, {}), {1}: (43, {})} | custom-call | flops 5368709120 | bytes 18874368 | tf_op jit(solution)/shard_map/pallas_call | solution.py:266
  186.8 5.5 %shard_map.144.m_ref = bf16[1024,128]{1,0:T(8,128)(2,1)} custom-call(s32[8]{0:T(128)} %stack.186.index_ref, s32[5,8]{1,0:T(8,128)} %stack.170.meta_ref, bf16[1024,512]{1,0:T(8,128)(2,1)} %collective-permute-done.12.refs_0_, bf16[1024,512]{1,0:T(8,128)(2,1)} %collective-permute-done.14.refs_1_, bf16[1024,512]{1,0:T(8,128)(2,1)} %collective-permute-done.16.refs_2_, ...), custom_call_target="tpu_custom_call" | custom-call | flops 536870912 | bytes 5767168 | tf_op jit(solution)/shard_map/pallas_call | solution.py:266
  194.1 7.1 %shard_map.141.q_ref = f32[1024,512]{1,0:T(8,128)} custom-call(s32[8]{0:T(128)} %stack.186.index_ref, s32[5,8]{1,0:T(8,128)} %stack.170.meta_ref, bf16[1024,512]{1,0:T(8,128)(2,1)} %collective-permute-done.12.refs_0_, bf16[1024,512]{1,0:T(8,128)(2,1)} %collective-permute-done.14.refs_1_, ...), custom_call_target="tpu_custom_call", output_to_operand_aliasing={{}: (14, {})} | custom-call | flops 2147483648 | bytes 10485760 | tf_op jit(solution)/shard_map/pallas_call | solution.py:266
  201.9 6.5 %shard_map.146 = (bf16[512,512]{1,0:T(8,128)(2,1)}, f32[512,64]{1,0:T(8,128)}) custom-call(s32[5,8]{1,0:T(8,128)} %stack.170.meta_ref, f32[1024,512]{1,0:T(8,128)} %shard_map.141.q_ref, bf16[1024,192]{1,0:T(8,128)(2,1)} %bitcast.79, bf16[8,64,1152]{2,1,0:T(8,128)(2,1)} %copy-done.1, bf16[8,256,512]{2,1,0:T(8,128)(2,1)} %copy-done, ...), custom_call_target="tpu_custom_call" | custom-call | flops 402653184 | bytes 2097152 | tf_op jit(solution)/shard_map/pallas_call | solution.py:375
  211.8 6.5 %shard_map.145 = (bf16[512,512]{1,0:T(8,128)(2,1)}, f32[512,64]{1,0:T(8,128)}) custom-call(s32[5,8]{1,0:T(8,128)} %stack.170.meta_ref, f32[1024,512]{1,0:T(8,128)} %shard_map.141.q_ref, bf16[1024,192]{1,0:T(8,128)(2,1)} %bitcast.80, bf16[8,64,1152]{2,1,0:T(8,128)(2,1)} %copy-done.1, bf16[8,256,512]{2,1,0:T(8,128)(2,1)} %copy-done, ...), custom_call_target="tpu_custom_call" | custom-call | flops 402653184 | bytes 2097152 | tf_op jit(solution)/shard_map/pallas_call | solution.py:375
  223.3 4.1 %all-to-all-start.4 = ((f32[16,32,128]{2,1,0:T(8,128)}), f32[16,32,128]{2,1,0:T(8,128)S(1)}, u32[]{:S(2)}, u32[]{:S(2)}) async-start(f32[16,32,128]{2,1,0:T(8,128)} %bitcast.55), calls=%async_computation.4 | async-start | bytes 524288 | tf_op jit(solution)/shard_map/all_to_all | solution.py:217
  230.9 6.1 %all-to-all-done.4.p_ref = f32[16,32,128]{2,1,0:T(8,128)S(1)} async-done(((f32[16,32,128]{2,1,0:T(8,128)}), f32[16,32,128]{2,1,0:T(8,128)S(1)}, u32[]{:S(2)}, u32[]{:S(2)}) %all-to-all-start.4) | async-done | bytes 262176 | tf_op jit(solution)/shard_map/all_to_all | solution.py:217
  239.3 5.7 %all-to-all-start.5 = ((bf16[16,32,128]{2,1,0:T(8,128)(2,1)}), bf16[16,32,128]{2,1,0:T(8,128)(2,1)S(1)}, u32[]{:S(2)}, u32[]{:S(2)}) async-start(bf16[16,32,128]{2,1,0:T(8,128)(2,1)} %shard_map.147.refs_6_), calls=%async_computation.5 | async-start | bytes 262144 | tf_op jit(solution)/shard_map/all_to_all | solution.py:635
  249.9 4.8 %shard_map.151 = (bf16[512,256]{1,0:T(8,128)(2,1)}, bf16[512,256]{1,0:T(8,128)(2,1)}) custom-call(s32[6]{0:T(128)} %stack.220.index_ref, bf16[512,512]{1,0:T(8,128)(2,1)} %get-tuple-element.68.refs_0_, bf16[512,512]{1,0:T(8,128)(2,1)} %copy-done.14, bf16[512,512]{1,0:T(8,128)(2,1)} %copy-done.15, bf16[512,256]{1,0:T(8,128)(2,1)} %collective-permute-done.36.refs_3_, ...), custom_call_target="tpu_custom_call" | custom-call | flops 1073741824 | bytes 4194304 | tf_op jit(solution)/shard_map/pallas_call | solution.py:427
  254.7 3.2 collective-permute-start.42
  258.6 9.6 %shard_map.150 = (bf16[512,256]{1,0:T(8,128)(2,1)}, bf16[512,256]{1,0:T(8,128)(2,1)}, bf16[512,256]{1,0:T(8,128)(2,1)}, bf16[512,256]{1,0:T(8,128)(2,1)}, f32[512,256]{1,0:T(8,128)}, /*index=5*/f32[512,256]{1,0:T(8,128)}) custom-call(s32[10]{0:T(128)} %stack.177.index_ref, bf16[512,512]{1,0:T(8,128)(2,1)} %get-tuple-element.68.refs_0_, ...), custom_call_target="tpu_custom_call" | custom-call | flops 3221225472 | bytes 8388608 | tf_op jit(solution)/shard_map/pallas_call | solution.py:427
  268.2 3.2 %collective-permute-start.38 = (bf16[512,256]{1,0:T(8,128)(2,1)}, bf16[512,256]{1,0:T(8,128)(2,1)S(1)}, u32[]{:S(2)}, u32[]{:S(2)}) collective-permute-start(bf16[512,256]{1,0:T(8,128)(2,1)} %get-tuple-element.70), channel_id=1, source_target_pairs={{0,3},{1,0},{2,1},{3,2},{4,7},{5,4},{6,5},{7,6},{8,11},{9,8},{10,9... | collective-permute-start | bytes 786440 | tf_op jit(solution)/shard_map/ppermute | solution.py:37
  271.4 4.8 %shard_map.149 = (bf16[512,256]{1,0:T(8,128)(2,1)}, bf16[512,256]{1,0:T(8,128)(2,1)}) custom-call(s32[6]{0:T(128)} %stack.220.index_ref, bf16[512,512]{1,0:T(8,128)(2,1)} %get-tuple-element.57.refs_0_, bf16[512,512]{1,0:T(8,128)(2,1)} %copy-done.12, bf16[512,512]{1,0:T(8,128)(2,1)} %copy-done.13, bf16[512,256]{1,0:T(8,128)(2,1)} %collective-permute-done.26.refs_3_, ...), custom_call_target="tpu_custom_call" | custom-call | flops 1073741824 | bytes 4194304 | tf_op jit(solution)/shard_map/pallas_call | solution.py:427
  278.3 9.7 %shard_map.148 = (bf16[512,256]{1,0:T(8,128)(2,1)}, bf16[512,256]{1,0:T(8,128)(2,1)}, bf16[512,256]{1,0:T(8,128)(2,1)}, bf16[512,256]{1,0:T(8,128)(2,1)}, f32[512,256]{1,0:T(8,128)}, /*index=5*/f32[512,256]{1,0:T(8,128)}) custom-call(s32[10]{0:T(128)} %stack.177.index_ref, bf16[512,512]{1,0:T(8,128)(2,1)} %get-tuple-element.57.refs_0_, ...), custom_call_target="tpu_custom_call" | custom-call | flops 3221225472 | bytes 8388608 | tf_op jit(solution)/shard_map/pallas_call | solution.py:427
  288.2 3.1 collective-permute-start.28
  292.5 3.3 %collective-permute-start.43 = (bf16[512,256]{1,0:T(8,128)(2,1)S(1)}, bf16[512,256]{1,0:T(8,128)(2,1)S(1)}, u32[]{:S(2)}, u32[]{:S(2)}) collective-permute-start(bf16[512,256]{1,0:T(8,128)(2,1)S(1)} %add.304), channel_id=1, source_target_pairs={{0,3},{1,0},{2,1},{3,2},{4,7},{5,4},{6,5},{7,6},{8,11},{9,8},{10,9... | collective-permute-start | bytes 786440 | tf_op jit(solution)/shard_map/ppermute | solution.py:37
  307.5 5.9 %shard_map.152 = f32[1024,512]{1,0:T(8,128)} custom-call(s32[5,8]{1,0:T(8,128)} %stack.170.meta_ref, f32[512,256]{1,0:T(8,128)} %get-tuple-element.60.refs_0_, bf16[512,256]{1,0:T(8,128)(2,1)} %copy-done.21, bf16[512,256]{1,0:T(8,128)(2,1)} %copy-done.33, f32[512,256]{1,0:T(8,128)} %get-tuple-element.64.refs_3_, bf16[512,256]{1,0:T(8,128)(2,1)} %copy-done.23, ...), custom_call_target="tpu_custom_call" | custom-call | flops 67108864 | bytes 7340032 | tf_op jit(solution)/shard_map/pallas_call | solution.py:509
  (198 shorter events, 91.8 us)
Async XLA Ops:
  6.5 243.4 %all-gather.3.cloned.1.call-start = ((), (), s32[]{:S(2)}) async-start(), calls=%async_computation.6 | async-start | bytes 9437184 | tf_op jit(solution)/shard_map/all_gather | solution.py:572
  19.8 25.4 %collective-permute-start = (bf16[1024,256]{1,0:T(8,128)(2,1)}, bf16[1024,256]{1,0:T(8,128)(2,1)S(1)}, u32[]{:S(2)}, u32[]{:S(2)}) collective-permute-start(bf16[1024,256]{1,0:T(8,128)(2,1)} %get-tuple-element.41.refs_0_), channel_id=1, source_target_pairs={{0,1},{1,2},{2,3},{3,0},{4,5},{5,6},{6,7},{7,4},{8,9},{9,10},{10,1... | collective-permute-start | bytes 1572872 | tf_op jit(solution)/shard_map/ppermute | solution.py:37
  21.3 23.9 %collective-permute-start.1 = (bf16[1024,256]{1,0:T(8,128)(2,1)}, bf16[1024,256]{1,0:T(8,128)(2,1)S(1)}, u32[]{:S(2)}, u32[]{:S(2)}) collective-permute-start(bf16[1024,256]{1,0:T(8,128)(2,1)} %get-tuple-element.41.refs_0_), channel_id=1, source_target_pairs={{0,3},{1,0},{2,1},{3,2},{4,7},{5,4},{6,5},{7,6},{8,11},{9,8},{10,9... | collective-permute-start | bytes 1572872 | tf_op jit(solution)/shard_map/ppermute | solution.py:37
  23.0 22.2 %collective-permute-start.4 = (bf16[1024,256]{1,0:T(8,128)(2,1)}, bf16[1024,256]{1,0:T(8,128)(2,1)S(1)}, u32[]{:S(2)}, u32[]{:S(2)}) collective-permute-start(bf16[1024,256]{1,0:T(8,128)(2,1)} %get-tuple-element.42.refs_5_), channel_id=1, source_target_pairs={{0,4},{4,8},{8,12},{12,0},{1,5},{5,9},{9,13},{13,1},{2,6},{6,10},{... | collective-permute-start | bytes 1572872 | tf_op jit(solution)/shard_map/ppermute | solution.py:37
  26.8 18.5 %collective-permute-start.5 = (bf16[1024,256]{1,0:T(8,128)(2,1)}, bf16[1024,256]{1,0:T(8,128)(2,1)S(1)}, u32[]{:S(2)}, u32[]{:S(2)}) collective-permute-start(bf16[1024,256]{1,0:T(8,128)(2,1)} %get-tuple-element.42.refs_5_), channel_id=1, source_target_pairs={{0,12},{4,0},{8,4},{12,8},{1,13},{5,1},{9,5},{13,9},{2,14},{6,2},{... | collective-permute-start | bytes 1572872 | tf_op jit(solution)/shard_map/ppermute | solution.py:37
  48.9 55.1 %all-to-all-start = ((bf16[8,256,512]{2,1,0:T(8,128)(2,1)}), bf16[8,256,512]{2,1,0:T(8,128)(2,1)S(1)}, u32[]{:S(2)}, u32[]{:S(2)}) async-start(bf16[8,256,512]{2,1,0:T(8,128)(2,1)} %get-tuple-element.54), calls=%async_computation | async-start | bytes 4194304 | tf_op jit(solution)/shard_map/all_to_all | solution.py:565
  75.0 26.1 %collective-permute-start.11 = (bf16[1024,512]{1,0:T(8,128)(2,1)}, bf16[1024,512]{1,0:T(8,128)(2,1)S(1)}, u32[]{:S(2)}, u32[]{:S(2)}) collective-permute-start(bf16[1024,512]{1,0:T(8,128)(2,1)} %get-tuple-element.47.refs_0_), channel_id=1, source_target_pairs={{0,4},{4,8},{8,12},{12,0},{1,5},{5,9},{9,13},{13,1},{2,6},{6,10},{... | collective-permute-start | bytes 3145736 | tf_op jit(solution)/shard_map/ppermute | solution.py:37
  76.6 24.5 %collective-permute-start.13 = (bf16[1024,512]{1,0:T(8,128)(2,1)}, bf16[1024,512]{1,0:T(8,128)(2,1)}, u32[]{:S(2)}, u32[]{:S(2)}) collective-permute-start(bf16[1024,512]{1,0:T(8,128)(2,1)} %get-tuple-element.48.refs_1_), channel_id=1, source_target_pairs={{0,12},{4,0},{8,4},{12,8},{1,13},{5,1},{9,5},{13,9},{2,14},{6,2},{... | collective-permute-start | bytes 3145736 | tf_op jit(solution)/shard_map/ppermute | solution.py:37
  78.5 25.5 %collective-permute-start.15 = (bf16[1024,512]{1,0:T(8,128)(2,1)}, bf16[1024,512]{1,0:T(8,128)(2,1)}, u32[]{:S(2)}, u32[]{:S(2)}) collective-permute-start(bf16[1024,512]{1,0:T(8,128)(2,1)} %get-tuple-element.49.refs_2_), channel_id=1, source_target_pairs={{0,1},{1,2},{2,3},{3,0},{4,5},{5,6},{6,7},{7,4},{8,9},{9,10},{10,1... | collective-permute-start | bytes 3145736 | tf_op jit(solution)/shard_map/ppermute | solution.py:37
  78.7 25.2 %collective-permute-start.17 = (bf16[1024,512]{1,0:T(8,128)(2,1)}, bf16[1024,512]{1,0:T(8,128)(2,1)}, u32[]{:S(2)}, u32[]{:S(2)}) collective-permute-start(bf16[1024,512]{1,0:T(8,128)(2,1)} %get-tuple-element.50.refs_3_), channel_id=1, source_target_pairs={{0,3},{1,0},{2,1},{3,2},{4,7},{5,4},{6,5},{7,6},{8,11},{9,8},{10,9... | collective-permute-start | bytes 3145736 | tf_op jit(solution)/shard_map/ppermute | solution.py:37
  110.1 24.2 %all-to-all-start.1 = ((f32[16,64,192]{2,1,0:T(8,128)}), f32[16,64,192]{2,1,0:T(8,128)S(1)}, u32[]{:S(2)}, u32[]{:S(2)}) async-start(f32[16,64,192]{2,1,0:T(8,128)} %bitcast.81), calls=%async_computation.1 | async-start | bytes 2097152 | tf_op jit(solution)/shard_map/all_to_all | solution.py:217
  115.7 36.7 %collective-permute-start.19 = (bf16[1024,512]{1,0:T(8,128)(2,1)}, bf16[1024,512]{1,0:T(8,128)(2,1)}, u32[]{:S(2)}, u32[]{:S(2)}) collective-permute-start(bf16[1024,512]{1,0:T(8,128)(2,1)} %get-tuple-element.48.refs_1_), channel_id=1, source_target_pairs={{0,4},{4,8},{8,12},{12,0},{1,5},{5,9},{9,13},{13,1},{2,6},{6,10},{... | collective-permute-start | bytes 3145736 | tf_op jit(solution)/shard_map/ppermute | solution.py:37
  117.6 36.1 %collective-permute-start.20 = (bf16[1024,512]{1,0:T(8,128)(2,1)}, bf16[1024,512]{1,0:T(8,128)(2,1)}, u32[]{:S(2)}, u32[]{:S(2)}) collective-permute-start(bf16[1024,512]{1,0:T(8,128)(2,1)} %get-tuple-element.47.refs_0_), channel_id=1, source_target_pairs={{0,12},{4,0},{8,4},{12,8},{1,13},{5,1},{9,5},{13,9},{2,14},{6,2},{... | collective-permute-start | bytes 3145736 | tf_op jit(solution)/shard_map/ppermute | solution.py:37
  119.0 35.4 %collective-permute-start.21 = (bf16[1024,512]{1,0:T(8,128)(2,1)}, bf16[1024,512]{1,0:T(8,128)(2,1)}, u32[]{:S(2)}, u32[]{:S(2)}) collective-permute-start(bf16[1024,512]{1,0:T(8,128)(2,1)} %get-tuple-element.50.refs_3_), channel_id=1, source_target_pairs={{0,1},{1,2},{2,3},{3,0},{4,5},{5,6},{6,7},{7,4},{8,9},{9,10},{10,1... | collective-permute-start | bytes 3145736 | tf_op jit(solution)/shard_map/ppermute | solution.py:37
  120.9 51.8 %collective-permute-start.22 = (bf16[1024,512]{1,0:T(8,128)(2,1)}, bf16[1024,512]{1,0:T(8,128)(2,1)}, u32[]{:S(2)}, u32[]{:S(2)}) collective-permute-start(bf16[1024,512]{1,0:T(8,128)(2,1)} %get-tuple-element.49.refs_2_), channel_id=1, source_target_pairs={{0,3},{1,0},{2,1},{3,2},{4,7},{5,4},{6,5},{7,6},{8,11},{9,8},{10,9... | collective-permute-start | bytes 3145736 | tf_op jit(solution)/shard_map/ppermute | solution.py:37
  134.3 34.7 %all-to-all-start.3 = ((bf16[8,64,1152]{2,1,0:T(8,128)(2,1)}), bf16[8,64,1152]{2,1,0:T(8,128)(2,1)S(1)}, u32[]{:S(2)}, u32[]{:S(2)}) async-start(bf16[8,64,1152]{2,1,0:T(8,128)(2,1)} %get-tuple-element.55), calls=%async_computation.3 | async-start | bytes 2359296 | tf_op jit(solution)/shard_map/all_to_all | solution.py:602
  138.3 47.6 %collective-permute-start.12 = (bf16[1024,512]{1,0:T(8,128)(2,1)S(1)}, bf16[1024,512]{1,0:T(8,128)(2,1)}, u32[]{:S(2)}, u32[]{:S(2)}) collective-permute-start(bf16[1024,512]{1,0:T(8,128)(2,1)S(1)} %copy-done.4), channel_id=1, source_target_pairs={{0,4},{4,8},{8,12},{12,0},{1,5},{5,9},{9,13},{13,1},{2,6},{6,10},{... | collective-permute-start | bytes 3145736 | tf_op jit(solution)/shard_map/ppermute | solution.py:37
  152.4 33.5 %collective-permute-start.14 = (bf16[1024,512]{1,0:T(8,128)(2,1)}, bf16[1024,512]{1,0:T(8,128)(2,1)}, u32[]{:S(2)}, u32[]{:S(2)}) collective-permute-start(bf16[1024,512]{1,0:T(8,128)(2,1)} %collective-permute-done.13.refs_1_.rest_3_), channel_id=1, source_target_pairs={{0,12},{4,0},{8,4},{12,8},{1,13},{5,1},{9,5},{13,9},{2,14},{6,2},{... | collective-permute-start | bytes 3145736 | tf_op jit(solution)/shard_map/ppermute | solution.py:37
  153.7 32.2 %collective-permute-start.16 = (bf16[1024,512]{1,0:T(8,128)(2,1)}, bf16[1024,512]{1,0:T(8,128)(2,1)}, u32[]{:S(2)}, u32[]{:S(2)}) collective-permute-start(bf16[1024,512]{1,0:T(8,128)(2,1)} %collective-permute-done.15.refs_2_.rest_4_), channel_id=1, source_target_pairs={{0,1},{1,2},{2,3},{3,0},{4,5},{5,6},{6,7},{7,4},{8,9},{9,10},{10,1... | collective-permute-start | bytes 3145736 | tf_op jit(solution)/shard_map/ppermute | solution.py:37
  154.4 31.5 %collective-permute-start.18 = (bf16[1024,512]{1,0:T(8,128)(2,1)}, bf16[1024,512]{1,0:T(8,128)(2,1)}, u32[]{:S(2)}, u32[]{:S(2)}) collective-permute-start(bf16[1024,512]{1,0:T(8,128)(2,1)} %collective-permute-done.17.refs_3_.rest_5_), channel_id=1, source_target_pairs={{0,3},{1,0},{2,1},{3,2},{4,7},{5,4},{6,5},{7,6},{8,11},{9,8},{10,9... | collective-permute-start | bytes 3145736 | tf_op jit(solution)/shard_map/ppermute | solution.py:37
  208.4 19.0 %collective-permute-start.34 = (bf16[512,512]{1,0:T(8,128)(2,1)}, bf16[512,512]{1,0:T(8,128)(2,1)S(1)}, u32[]{:S(2)}, u32[]{:S(2)}) collective-permute-start(bf16[512,512]{1,0:T(8,128)(2,1)} %get-tuple-element.68.refs_0_), channel_id=1, source_target_pairs={{0,4},{4,8},{8,12},{12,0},{1,5},{5,9},{9,13},{13,1},{2,6},{6,10},{... | collective-permute-start | bytes 1572872 | tf_op jit(solution)/shard_map/ppermute | solution.py:37
  210.0 19.5 %collective-permute-start.35 = (bf16[512,512]{1,0:T(8,128)(2,1)}, bf16[512,512]{1,0:T(8,128)(2,1)S(1)}, u32[]{:S(2)}, u32[]{:S(2)}) collective-permute-start(bf16[512,512]{1,0:T(8,128)(2,1)} %get-tuple-element.68.refs_0_), channel_id=1, source_target_pairs={{0,12},{4,0},{8,4},{12,8},{1,13},{5,1},{9,5},{13,9},{2,14},{6,2},{... | collective-permute-start | bytes 1572872 | tf_op jit(solution)/shard_map/ppermute | solution.py:37
  218.3 28.0 %collective-permute-start.24 = (bf16[512,512]{1,0:T(8,128)(2,1)}, bf16[512,512]{1,0:T(8,128)(2,1)S(1)}, u32[]{:S(2)}, u32[]{:S(2)}) collective-permute-start(bf16[512,512]{1,0:T(8,128)(2,1)} %get-tuple-element.57.refs_0_), channel_id=1, source_target_pairs={{0,4},{4,8},{8,12},{12,0},{1,5},{5,9},{9,13},{13,1},{2,6},{6,10},{... | collective-permute-start | bytes 1572872 | tf_op jit(solution)/shard_map/ppermute | solution.py:37
  218.5 29.7 %collective-permute-start.25 = (bf16[512,512]{1,0:T(8,128)(2,1)}, bf16[512,512]{1,0:T(8,128)(2,1)S(1)}, u32[]{:S(2)}, u32[]{:S(2)}) collective-permute-start(bf16[512,512]{1,0:T(8,128)(2,1)} %get-tuple-element.57.refs_0_), channel_id=1, source_target_pairs={{0,12},{4,0},{8,4},{12,8},{1,13},{5,1},{9,5},{13,9},{2,14},{6,2},{... | collective-permute-start | bytes 1572872 | tf_op jit(solution)/shard_map/ppermute | solution.py:37
  227.5 22.5 %collective-permute-start.36 = (bf16[512,256]{1,0:T(8,128)(2,1)S(1)}, bf16[512,256]{1,0:T(8,128)(2,1)}, u32[]{:S(2)}, u32[]{:S(2)}) collective-permute-start(bf16[512,256]{1,0:T(8,128)(2,1)S(1)} %slice.38), channel_id=1, source_target_pairs={{0,4},{4,8},{8,12},{12,0},{1,5},{5,9},{9,13},{13,1},{2,6},{6,10},{... | collective-permute-start | bytes 786440 | tf_op jit(solution)/shard_map/ppermute | solution.py:37
  229.5 20.4 %collective-permute-start.37 = (bf16[512,256]{1,0:T(8,128)(2,1)S(1)}, bf16[512,256]{1,0:T(8,128)(2,1)}, u32[]{:S(2)}, u32[]{:S(2)}) collective-permute-start(bf16[512,256]{1,0:T(8,128)(2,1)S(1)} %slice.39), channel_id=1, source_target_pairs={{0,12},{4,0},{8,4},{12,8},{1,13},{5,1},{9,5},{13,9},{2,14},{6,2},{... | collective-permute-start | bytes 786440 | tf_op jit(solution)/shard_map/ppermute | solution.py:37
  239.3 18.6 %all-to-all-start.5 = ((bf16[16,32,128]{2,1,0:T(8,128)(2,1)}), bf16[16,32,128]{2,1,0:T(8,128)(2,1)S(1)}, u32[]{:S(2)}, u32[]{:S(2)}) async-start(bf16[16,32,128]{2,1,0:T(8,128)(2,1)} %shard_map.147.refs_6_), calls=%async_computation.5 | async-start | bytes 262144 | tf_op jit(solution)/shard_map/all_to_all | solution.py:635
  246.3 25.2 %collective-permute-start.26 = (bf16[512,256]{1,0:T(8,128)(2,1)S(1)}, bf16[512,256]{1,0:T(8,128)(2,1)}, u32[]{:S(2)}, u32[]{:S(2)}) collective-permute-start(bf16[512,256]{1,0:T(8,128)(2,1)S(1)} %slice.36), channel_id=1, source_target_pairs={{0,4},{4,8},{8,12},{12,0},{1,5},{5,9},{9,13},{13,1},{2,6},{6,10},{... | collective-permute-start | bytes 786440 | tf_op jit(solution)/shard_map/ppermute | solution.py:37
  248.3 23.1 %collective-permute-start.27 = (bf16[512,256]{1,0:T(8,128)(2,1)S(1)}, bf16[512,256]{1,0:T(8,128)(2,1)}, u32[]{:S(2)}, u32[]{:S(2)}) collective-permute-start(bf16[512,256]{1,0:T(8,128)(2,1)S(1)} %slice.37), channel_id=1, source_target_pairs={{0,12},{4,0},{8,4},{12,8},{1,13},{5,1},{9,5},{13,9},{2,14},{6,2},{... | collective-permute-start | bytes 786440 | tf_op jit(solution)/shard_map/ppermute | solution.py:37
  254.7 33.2 %collective-permute-start.42 = (bf16[512,256]{1,0:T(8,128)(2,1)}, bf16[512,256]{1,0:T(8,128)(2,1)S(1)}, u32[]{:S(2)}, u32[]{:S(2)}) collective-permute-start(bf16[512,256]{1,0:T(8,128)(2,1)} %get-tuple-element.76), channel_id=1, source_target_pairs={{0,3},{1,0},{2,1},{3,2},{4,7},{5,4},{6,5},{7,6},{8,11},{9,8},{10,9... | collective-permute-start | bytes 786440 | tf_op jit(solution)/shard_map/ppermute | solution.py:37
  257.9 30.2 %collective-permute-start.39 = (bf16[512,256]{1,0:T(8,128)(2,1)}, bf16[512,256]{1,0:T(8,128)(2,1)S(1)}, u32[]{:S(2)}, u32[]{:S(2)}) collective-permute-start(bf16[512,256]{1,0:T(8,128)(2,1)} %get-tuple-element.72), channel_id=1, source_target_pairs={{0,1},{1,2},{2,3},{3,0},{4,5},{5,6},{6,7},{7,4},{8,9},{9,10},{10,1... | collective-permute-start | bytes 786440 | tf_op jit(solution)/shard_map/ppermute | solution.py:37
  268.2 27.7 %collective-permute-start.38 = (bf16[512,256]{1,0:T(8,128)(2,1)}, bf16[512,256]{1,0:T(8,128)(2,1)S(1)}, u32[]{:S(2)}, u32[]{:S(2)}) collective-permute-start(bf16[512,256]{1,0:T(8,128)(2,1)} %get-tuple-element.70), channel_id=1, source_target_pairs={{0,3},{1,0},{2,1},{3,2},{4,7},{5,4},{6,5},{7,6},{8,11},{9,8},{10,9... | collective-permute-start | bytes 786440 | tf_op jit(solution)/shard_map/ppermute | solution.py:37
  (60 other events, 559.3 us)
Sparse Core Ops, SparseCore 0:
  49.0 67.6 all-gather.2

commit v6 on v5

--- a/solution.py
+++ b/solution.py
@@ -187,6 +187,26 @@
         compiler_params=params(),
         cost_estimate=cost(0, 4 * tokens * sum(widths)),
     )(*flat, *after)
+
+
+def side_by_side(blocks, after):
+    rows, width = blocks[0].shape
+
+    def body(*refs):
+        for k in range(len(blocks)):
+            refs[-1][:, k * width : (k + 1) * width] = refs[k][...]
+
+    spec = pl.BlockSpec((rows, width), lambda i: (0, 0))
+    shape = (rows, width * len(blocks))
+    return pl.pallas_call(
+        body,
+        out_shape=jax.ShapeDtypeStruct(shape, f32),
+        grid=(1,),
+        in_specs=[spec] * len(blocks) + passive(after),
+        out_specs=pl.BlockSpec(shape, lambda i: (0, 0)),
+        compiler_params=params(),
+        cost_estimate=cost(0, 8 * math.prod(shape)),
+    )(*blocks, *after)
 
 
 def share_sum(pieces, after):
@@ -442,7 +462,28 @@
     )(index, *pieces, weights, *after)
 
 
-def output_ring(pieces, weights, axis, places, ahead_of):
+def add_pairs(pairs, after):
+    rows, width = pairs[0][0].shape
+    count = len(pairs)
+
+    def body(*refs):
+        for k in range(count):
+            total = refs[2 * k][...].astype(f32) + refs[2 * k + 1][...].astype(f32)
+            refs[len(refs) - count + k][...] = total.astype(bf16)
+
+    spec = pl.BlockSpec((rows, width), lambda i: (0, 0))
+    return pl.pallas_call(
+        body,
+        out_shape=tuple(jax.ShapeDtypeStruct((rows, width), bf16) for _ in pairs),
+        grid=(1,),
+        in_specs=[spec] * (2 * count) + passive(after),
+        out_specs=[spec] * count,
+        compiler_params=params(),
+        cost_estimate=cost(count * rows * width, 6 * count * rows * width),
+    )(*[a for pair in pairs for a in pair], *after)
+
+
+def output_ring(pieces, weights, axis, places):
     me, behind, ahead, far = ring_order(lax.axis_index(axis))
 
     def partial(shards, dtypes, after=()):
@@ -450,17 +491,24 @@
         return output_partial(index, pieces, weights, dtypes, after)
 
     far_low, far_high = partial([2 * far, 2 * far + 1], [bf16] * 2)
-    via_behind = shift(far_low, axis, 1)
-    via_ahead = shift(far_high, axis, -1)
-    ahead_high, behind_low, ahead_low, behind_high, low, high = partial(
-        [2 * ahead + 1, 2 * behind, 2 * ahead, 2 * behind + 1, 2 * me, 2 * me + 1],
-        [bf16] * 4 + [f32] * 2,
-        [ahead_of],
-    )
-    return (
-        (low, shift(behind_low, axis, -1), shift(ahead_low + via_behind, axis, 1)),
-        (high, shift(ahead_high, axis, 1), shift(behind_high + via_ahead, axis, -1)),
-    )
+
+    def rest(after, later):
+        via_behind = shift(far_low, axis, 1)
+        via_ahead = shift(far_high, axis, -1)
+        ahead_high, behind_low, ahead_low, behind_high, low, high = partial(
+            [2 * ahead + 1, 2 * behind, 2 * ahead, 2 * behind + 1, 2 * me, 2 * me + 1],
+            [bf16] * 4 + [f32] * 2,
+            after,
+        )
+        to_ahead, to_behind = add_pairs(
+            [(ahead_low, via_behind), (behind_high, via_ahead)], later
+        )
+        return (
+            (low, shift(behind_low, axis, -1), shift(to_ahead, axis, 1)),
+            (high, shift(ahead_high, axis, 1), shift(to_behind, axis, -1)),
+        )
+
+    return (far_low, far_high), rest
 
 
 def finish(meta, parts, head_rank, up, wide):
@@ -568,12 +616,11 @@
     first_b = ring_gather(x_b, "y")
 
     got = [sent[0], shift(sent[2], "y", 1), shift(sent[1], "y", -1), shift(sent[3], "y", 2)]
-    wo_mine = stack_rows(got, first_a[1:3] + first_b[1:3])
+    low_a, high_a, low_b, high_b = join(
+        [first_a[:2], first_a[2:], first_b[:2], first_b[2:]], got[1:]
+    )
+    wo_mine = stack_rows(got, [down, low_a])
     wo_all = lax.all_gather(wo_mine, ADAPTER_AXES, axis=0)
-
-    low_a, high_a, low_b, high_b = join(
-        [first_a[:2], first_a[2:], first_b[:2], first_b[2:]], [wo_mine]
-    )
     far_a, next_a = second_gather(low_a, high_a, "y")
     far_b, next_b = second_gather(low_b, high_b, "x")
 
@@ -596,8 +643,8 @@
         512,
     )
 
-    pieces = scatter_rows(rank_partial(meta, x, down, 3 * rank, [*far_a, *far_b]))
-    copies = share_sum(pieces, [])
+    pieces = scatter_rows(rank_partial(meta, x, down, 3 * rank, [low_a]))
+    copies = share_sum(pieces, [total[1]])
     shrunk = lax.all_to_all(copies, TENSOR_AXES, 0, 0, tiled=True).reshape(tokens, 3 * rank)
     up = lax.all_to_all(up_out, ADAPTER_AXES, 0, 0, tiled=True)
 
@@ -605,14 +652,21 @@
     b_low, b_high = shift(far_b[0], "x", 1), shift(far_b[1], "x", -1)
     total = project(
         (
-            index_of(
-                rows_a(1, low) + rows_a(2, high) + rows_b(1, low) + rows_b(2, high)
-                + rows_a(1, high) + rows_a(2, low) + rows_b(1, high) + rows_b(2, low)
-            ),
+            index_of(rows_a(1, low) + rows_a(2, high) + rows_b(1, low) + rows_b(2, high)),
             meta,
         ),
         total,
-        [*far_a, *far_b, *next_a, *next_b],
+        [*far_a, *far_b],
+        [wq, wkv],
+        512,
+    )
+    total = project(
+        (
+            index_of(rows_a(1, high) + rows_a(2, low) + rows_b(1, high) + rows_b(2, low)),
+            meta,
+        ),
+        total,
+        [*next_a, *next_b],
         [wq, wkv],
         512,
     )
@@ -631,13 +685,12 @@
         )
         ranks.append(head)
         pieces.append(ring_gather(attended, "y"))
-    copies = share_sum(scatter_rows(jnp.concatenate(ranks, axis=1)), [])
+    places = [jnp.int32(k) for k in range(SIDE)]
+    rings = [output_ring(p, wo_all, "x", places) for p in pieces]
+    (first_far, first_rest), (last_far, last_rest) = rings
+    copies = share_sum(scatter_rows(side_by_side(ranks, [first_far[0]])), [])
     head_rank = lax.all_to_all(copies, TENSOR_AXES, 0, 0, tiled=True).reshape(tokens // 2, 2 * rank)
-    places = [jnp.int32(k) for k in range(SIDE)]
-    parts = [
-        output_ring(pieces[0], wo_all, "x", places, copies),
-        output_ring(pieces[1], wo_all, "x", places, head_rank),
-    ]
+    parts = [first_rest([], []), last_rest([copies], [head_rank])]
     return finish(meta, parts, head_rank, up, wide)
 
 

time: 322 us -> 317 us (0.984)
  Pallas kernels: 105 us -> 115 us
  waiting for transfers between devices: 86.9 us -> 80 us
  starting transfers between devices: 96.4 us -> 92.8 us
    all_to_all x2, waiting for transfers between devices: 18.2 us -> 6.44 us  [scatter_rows(): lax.all_to_all(partial.reshape(ways, rows // ways, rank), TENSOR_AXES, 0,...]
    pallas_call x0 -> x3, Pallas kernels: none -> 5.98 us  [the longest x2 4.11 us: add_pairs(): pl.pallas_call(body, out_shape=tuple((jax.ShapeDtypeStruct((rows, width),...]
    all_to_all x2, waiting for transfers between devices: 0.01 us -> 4.99 us  [on_device(): lax.all_to_all(copies, TENSOR_AXES, 0, 0, tiled=True)]
    ppermute x43, starting transfers between devices: 66.2 us -> 61.6 us  [shift(): lax.ppermute(block, axis, [(i, (i + step) % SIDE) for i in range(SIDE)])]
    pallas_call x4 -> x5, Pallas kernels: 33.8 us -> 37.8 us  [project(): pl.pallas_call(body, out_shape=tuple((jax.ShapeDtypeStruct((tokens, w), d...]
    unnamed x82 -> x84, local copies, waits for them, and re-layouts: 7.25 us -> 6.36 us
  transfers between devices with their start and end apart: 51 -> 51, of which waited for: 17 -> 21; matrix products, arithmetic and copies ran while one was open for 3% -> 2% of each run, Pallas kernels for 28% -> 32%
where the time goes in v6:
time: 317 us; the launch traced here: 315 us
  Pallas kernels  115 us (36%)
  starting transfers between devices  92.8 us (29%)
  waiting for transfers between devices  80 us (25%)
  between operations  14 us (4%)
  local copies, waits for them, and re-layouts  11.2 us (4%)
    ppermute x43, waiting for transfers between devices, shift(): lax.ppermute(block, axis, [(i, (i + step) % SIDE) for i in range(SIDE)])  68.6 us
    ppermute x43, starting transfers between devices, shift(): lax.ppermute(block, axis, [(i, (i + step) % SIDE) for i in range(SIDE)])  61.6 us
    pallas_call x5, Pallas kernels, project(): pl.pallas_call(body, out_shape=tuple((jax.ShapeDtypeStruct((tokens, w), d...  37.8 us
    pallas_call x4, Pallas kernels, output_partial(): pl.pallas_call(body, out_shape=tuple((jax.ShapeDtypeStruct((tokens, width...  28.9 us
    pallas_call x2, Pallas kernels, attention(): pl.pallas_call(body, out_shape=(jax.ShapeDtypeStruct((count * BLOCK, wide...  13 us
    all_to_all x2, starting transfers between devices, scatter_rows(): lax.all_to_all(partial.reshape(ways, rows // ways, rank), TENSOR_AXES, 0,...  11.3 us
    all_to_all x2, starting transfers between devices, on_device(): lax.all_to_all(copies, TENSOR_AXES, 0, 0, tiled=True)  7.92 us
    pallas_call x1, Pallas kernels, pick_local(): pl.pallas_call(body, out_shape=tuple((jax.ShapeDtypeStruct(s, bf16) for s...  7.55 us
  transfers between devices with their start and end apart: 51, of which 21 were waited for; matrix products, arithmetic and copies ran while one was open for 2% of the time, Pallas kernels for 32%

profile of v6, /device:TPU:0, one launch (start us, length us, event | category | flops | bytes accessed | tf_op | source)
XLA Modules:
  0.0 314.5 jit_solution(9955142573677859077)
XLA Ops:
  8.0 7.6 %shard_map.136 = (bf16[8,256,512]{2,1,0:T(8,128)(2,1)}, bf16[8,64,1152]{2,1,0:T(8,128)(2,1)}, bf16[1024,256]{1,0:T(8,128)(2,1)}, bf16[1024,256]{1,0:T(8,128)(2,1...) custom-call(s32[12]{0:T(128)} %pad_add_fusion.pick_ref, ...), custom_call_target="tpu_custom_call" | custom-call | bytes 6553600 | tf_op jit(solution)/shard_map/pallas_call | solution.py:88
  15.5 5.3 %all-to-all-start = ((bf16[8,256,512]{2,1,0:T(8,128)(2,1)}), bf16[8,256,512]{2,1,0:T(8,128)(2,1)S(1)}, u32[]{:S(2)}, u32[]{:S(2)}) async-start(bf16[8,256,512]{2,1,0:T(8,128)(2,1)} %get-tuple-element.61), calls=%async_computation | async-start | bytes 4194304 | tf_op jit(solution)/shard_map/all_to_all | solution.py:613
  29.4 7.0 %collective-permute-done.refs_1_ = bf16[1024,256]{1,0:T(8,128)(2,1)S(1)} collective-permute-done((bf16[1024,256]{1,0:T(8,128)(2,1)S(1)}, bf16[1024,256]{1,0:T(8,128)(2,1)S(1)}, u32[]{:S(2)}, u32[]{:S(2)}) %collective-permute-start) | collective-permute-done | bytes 524320 | tf_op jit(solution)/shard_map/ppermute | solution.py:37
  43.3 4.0 %collective-permute-done.10.refs_12_.refs_3_ = bf16[512,256]{1,0:T(8,128)(2,1)S(1)} collective-permute-done((bf16[512,256]{1,0:T(8,128)(2,1)}, bf16[512,256]{1,0:T(8,128)(2,1)S(1)}, u32[]{:S(2)}, u32[]{:S(2)}) %collective-permute-start.10) | collective-permute-done | bytes 262176 | tf_op jit(solution)/shard_map/ppermute | solution.py:37
  59.5 4.8 %shard_map.137 = (bf16[1024,512]{1,0:T(8,128)(2,1)}, bf16[1024,512]{1,0:T(8,128)(2,1)}, bf16[1024,512]{1,0:T(8,128)(2,1)}, bf16[1024,512]{1,0:T(8,128)(2,1)}) custom-call(bf16[1024,256]{1,0:T(8,128)(2,1)} %get-tuple-element.47.refs_0_, bf16[1024,256]{1,0:T(8,128)(2,1)} %copy-done.6, bf16[1024,256]{1,0:T(8,128)(2,1)} %copy-done.7, ...), custom_call_target="tpu_custom_call" | custom-call | bytes 8388608 | tf_op jit(solution)/shard_map/pallas_call | solution.py:180
  72.6 4.9 %shard_map.142 = f32[1024,192]{1,0:T(8,128)} custom-call(s32[5,8]{1,0:T(8,128)} %stack.173.meta_ref, bf16[1024,512]{1,0:T(8,128)(2,1)} %x_ref.3, bf16[8,256,512]{2,1,0:T(8,128)(2,1)} %copy-done, bf16[8,256,512]{2,1,0:T(8,128)(2,1)} %copy-done, bf16[1024,512]{1,0:T(8,128)(2,1)} %get-tuple-element.52.refs_0_.rest_2_.refs_5_), custom_call_target="tpu_custom_call" | custom-call | flops 201326592 | bytes 2621440 | tf_op jit(solution)/shard_map/pallas_call | solution.py:148
  77.5 4.8 %all-to-all-start.1 = ((f32[16,64,192]{2,1,0:T(8,128)}), f32[16,64,192]{2,1,0:T(8,128)S(1)}, u32[]{:S(2)}, u32[]{:S(2)}) async-start(f32[16,64,192]{2,1,0:T(8,128)} %bitcast.81), calls=%async_computation.1 | async-start | bytes 2097152 | tf_op jit(solution)/shard_map/all_to_all | solution.py:237
  87.0 15.6 %collective-permute-done.11.refs_0_ = bf16[1024,512]{1,0:T(8,128)(2,1)S(1)} collective-permute-done((bf16[1024,512]{1,0:T(8,128)(2,1)}, bf16[1024,512]{1,0:T(8,128)(2,1)S(1)}, u32[]{:S(2)}, u32[]{:S(2)}) %collective-permute-start.11) | collective-permute-done | bytes 1048608 | tf_op jit(solution)/shard_map/ppermute | solution.py:37
  104.4 6.4 %all-to-all-done.1.p_ref = f32[16,64,192]{2,1,0:T(8,128)S(1)} async-done(((f32[16,64,192]{2,1,0:T(8,128)}), f32[16,64,192]{2,1,0:T(8,128)S(1)}, u32[]{:S(2)}, u32[]{:S(2)}) %all-to-all-start.1) | async-done | bytes 786464 | tf_op jit(solution)/shard_map/all_to_all | solution.py:237
  110.8 4.8 %all-to-all-start.3 = ((bf16[8,64,1152]{2,1,0:T(8,128)(2,1)}), bf16[8,64,1152]{2,1,0:T(8,128)(2,1)S(1)}, u32[]{:S(2)}, u32[]{:S(2)}) async-start(bf16[8,64,1152]{2,1,0:T(8,128)(2,1)} %get-tuple-element.62), calls=%async_computation.3 | async-start | bytes 2359296 | tf_op jit(solution)/shard_map/all_to_all | solution.py:649
  117.8 11.5 %collective-permute-done.19.refs_0_ = bf16[1024,512]{1,0:T(8,128)(2,1)} collective-permute-done((bf16[1024,512]{1,0:T(8,128)(2,1)}, bf16[1024,512]{1,0:T(8,128)(2,1)}, u32[]{:S(2)}, u32[]{:S(2)}) %collective-permute-start.19) | collective-permute-done | bytes 1048608 | tf_op jit(solution)/shard_map/ppermute | solution.py:37
  136.4 8.0 %shard_map.138 = (f32[1024,512]{1,0:T(8,128)}, f32[1024,128]{1,0:T(8,128)}) custom-call(s32[8]{0:T(128)} %stack.221.index_ref, s32[5,8]{1,0:T(8,128)} %stack.173.meta_ref, bf16[1024,512]{1,0:T(8,128)(2,1)} %get-tuple-element.52.refs_0_.rest_2_.refs_5_, bf16[1024,512]{1,0:T(8,128)(2,1)} %get-tuple-element.53.refs_1_, ...), custom_call_target="tpu_custom_call" | custom-call | flops 2684354560 | bytes 12058624 | tf_op jit(solution)/shard_map/pallas_call | solution.py:286
  146.5 3.6 %all-to-all-start.2 = ((bf16[16,64,192]{2,1,0:T(8,128)(2,1)}), bf16[16,64,192]{2,1,0:T(8,128)(2,1)S(1)}, u32[]{:S(2)}, u32[]{:S(2)}) async-start(bf16[16,64,192]{2,1,0:T(8,128)(2,1)} %shard_map.143), calls=%async_computation.2 | async-start | bytes 1048576 | tf_op jit(solution)/shard_map/all_to_all | solution.py:648
  150.1 8.6 %shard_map.139 = (f32[1024,512]{1,0:T(8,128)}, f32[1024,128]{1,0:T(8,128)}) custom-call(s32[8]{0:T(128)} %stack.212.index_ref, s32[5,8]{1,0:T(8,128)} %stack.173.meta_ref, bf16[1024,512]{1,0:T(8,128)(2,1)} %copy-done.14, bf16[1024,512]{1,0:T(8,128)(2,1)} %copy-done.15, ...), custom_call_target="tpu_custom_call", output_to_operand_aliasing={{0}: (22, {}), {1}: (23, {})} | custom-call | flops 2684354560 | bytes 12058624 | tf_op jit(solution)/shard_map/pallas_call | solution.py:286
  158.7 8.6 %shard_map.140 = (f32[1024,512]{1,0:T(8,128)}, f32[1024,128]{1,0:T(8,128)}) custom-call(s32[8]{0:T(128)} %stack.203.index_ref, s32[5,8]{1,0:T(8,128)} %stack.173.meta_ref, bf16[1024,512]{1,0:T(8,128)(2,1)} %collective-permute-done.19.refs_0_, bf16[1024,512]{1,0:T(8,128)(2,1)} %collective-permute-done.20.refs_1_, ...), custom_call_target="tpu_custom_call", output_to_operand_aliasing={{0}: (22, {}), {1}: (23, {})} | custom-call | flops 2684354560 | bytes 12058624 | tf_op jit(solution)/shard_map/pallas_call | solution.py:286
  170.0 5.5 %shard_map.144.m_ref = bf16[1024,128]{1,0:T(8,128)(2,1)} custom-call(s32[8]{0:T(128)} %stack.189.index_ref, s32[5,8]{1,0:T(8,128)} %stack.173.meta_ref, bf16[1024,512]{1,0:T(8,128)(2,1)} %copy-done.3, bf16[1024,512]{1,0:T(8,128)(2,1)} %collective-permute-done.14.refs_1_, bf16[1024,512]{1,0:T(8,128)(2,1)} %collective-permute-done.16.refs_2_, ...), custom_call_target="tpu_custom_call" | custom-call | flops 536870912 | bytes 5767168 | tf_op jit(solution)/shard_map/pallas_call | solution.py:286
  177.4 7.1 %shard_map.141.q_ref = f32[1024,512]{1,0:T(8,128)} custom-call(s32[8]{0:T(128)} %stack.189.index_ref, s32[5,8]{1,0:T(8,128)} %stack.173.meta_ref, bf16[1024,512]{1,0:T(8,128)(2,1)} %copy-done.3, bf16[1024,512]{1,0:T(8,128)(2,1)} %collective-permute-done.14.refs_1_, ...), custom_call_target="tpu_custom_call", output_to_operand_aliasing={{}: (14, {})} | custom-call | flops 2147483648 | bytes 10485760 | tf_op jit(solution)/shard_map/pallas_call | solution.py:286
  185.2 6.5 %shard_map.150 = (bf16[512,512]{1,0:T(8,128)(2,1)}, f32[512,64]{1,0:T(8,128)}) custom-call(s32[5,8]{1,0:T(8,128)} %stack.173.meta_ref, f32[1024,512]{1,0:T(8,128)} %shard_map.141.q_ref, bf16[1024,192]{1,0:T(8,128)(2,1)} %bitcast.79, bf16[8,64,1152]{2,1,0:T(8,128)(2,1)} %copy-done.1, bf16[8,256,512]{2,1,0:T(8,128)(2,1)} %copy-done, ...), custom_call_target="tpu_custom_call" | custom-call | flops 402653184 | bytes 2097152 | tf_op jit(solution)/shard_map/pallas_call | solution.py:395
  191.7 3.2 %collective-permute-start.35 = (bf16[512,512]{1,0:T(8,128)(2,1)}, bf16[512,512]{1,0:T(8,128)(2,1)S(1)}, u32[]{:S(2)}, u32[]{:S(2)}) collective-permute-start(bf16[512,512]{1,0:T(8,128)(2,1)} %get-tuple-element.76.refs_0_), channel_id=1, source_target_pairs={{0,12},{4,0},{8,4},{12,8},{1,13},{5,1},{9,5},{13,9},{2,14},{6,2},{... | collective-permute-start | bytes 1572872 | tf_op jit(solution)/shard_map/ppermute | solution.py:37
  194.9 6.5 %shard_map.145 = (bf16[512,512]{1,0:T(8,128)(2,1)}, f32[512,64]{1,0:T(8,128)}) custom-call(s32[5,8]{1,0:T(8,128)} %stack.173.meta_ref, f32[1024,512]{1,0:T(8,128)} %shard_map.141.q_ref, bf16[1024,192]{1,0:T(8,128)(2,1)} %bitcast.80, bf16[8,64,1152]{2,1,0:T(8,128)(2,1)} %copy-done.1, bf16[8,256,512]{2,1,0:T(8,128)(2,1)} %copy-done, ...), custom_call_target="tpu_custom_call" | custom-call | flops 402653184 | bytes 2097152 | tf_op jit(solution)/shard_map/pallas_call | solution.py:395
  201.5 3.2 %collective-permute-start.25 = (bf16[512,512]{1,0:T(8,128)(2,1)}, bf16[512,512]{1,0:T(8,128)(2,1)S(1)}, u32[]{:S(2)}, u32[]{:S(2)}) collective-permute-start(bf16[512,512]{1,0:T(8,128)(2,1)} %get-tuple-element.64.refs_0_), channel_id=1, source_target_pairs={{0,12},{4,0},{8,4},{12,8},{1,13},{5,1},{9,5},{13,9},{2,14},{6,2},{... | collective-permute-start | bytes 1572872 | tf_op jit(solution)/shard_map/ppermute | solution.py:37
  204.7 3.3 %collective-permute-done.34.refs_1_ = bf16[512,512]{1,0:T(8,128)(2,1)S(1)} collective-permute-done((bf16[512,512]{1,0:T(8,128)(2,1)}, bf16[512,512]{1,0:T(8,128)(2,1)S(1)}, u32[]{:S(2)}, u32[]{:S(2)}) %collective-permute-start.34) | collective-permute-done | bytes 524320 | tf_op jit(solution)/shard_map/ppermute | solution.py:37
  208.1 3.3 %collective-permute-start.37 = (bf16[512,256]{1,0:T(8,128)(2,1)S(1)}, bf16[512,256]{1,0:T(8,128)(2,1)}, u32[]{:S(2)}, u32[]{:S(2)}) collective-permute-start(bf16[512,256]{1,0:T(8,128)(2,1)S(1)} %slice.39), channel_id=1, source_target_pairs={{0,12},{4,0},{8,4},{12,8},{1,13},{5,1},{9,5},{13,9},{2,14},{6,2},{... | collective-permute-start | bytes 786440 | tf_op jit(solution)/shard_map/ppermute | solution.py:37
  211.4 7.8 %collective-permute-done.24.refs_1_ = bf16[512,512]{1,0:T(8,128)(2,1)S(1)} collective-permute-done((bf16[512,512]{1,0:T(8,128)(2,1)}, bf16[512,512]{1,0:T(8,128)(2,1)S(1)}, u32[]{:S(2)}, u32[]{:S(2)}) %collective-permute-start.24) | collective-permute-done | bytes 524320 | tf_op jit(solution)/shard_map/ppermute | solution.py:37
  219.4 3.3 %collective-permute-start.27 = (bf16[512,256]{1,0:T(8,128)(2,1)S(1)}, bf16[512,256]{1,0:T(8,128)(2,1)}, u32[]{:S(2)}, u32[]{:S(2)}) collective-permute-start(bf16[512,256]{1,0:T(8,128)(2,1)S(1)} %slice.37), channel_id=1, source_target_pairs={{0,12},{4,0},{8,4},{12,8},{1,13},{5,1},{9,5},{13,9},{2,14},{6,2},{... | collective-permute-start | bytes 786440 | tf_op jit(solution)/shard_map/ppermute | solution.py:37
  225.5 4.8 %shard_map.154 = (bf16[512,256]{1,0:T(8,128)(2,1)}, bf16[512,256]{1,0:T(8,128)(2,1)}) custom-call(s32[6]{0:T(128)} %stack.224.index_ref, bf16[512,512]{1,0:T(8,128)(2,1)} %get-tuple-element.76.refs_0_, bf16[512,512]{1,0:T(8,128)(2,1)} %copy-done.10, bf16[512,512]{1,0:T(8,128)(2,1)} %copy-done.11, bf16[512,256]{1,0:T(8,128)(2,1)} %copy-done.38, ...), custom_call_target="tpu_custom_call" | custom-call | flops 1073741824 | bytes 4194304 | tf_op jit(solution)/shard_map/pallas_call | solution.py:447
  233.7 4.8 %shard_map.148 = (bf16[512,256]{1,0:T(8,128)(2,1)}, bf16[512,256]{1,0:T(8,128)(2,1)}) custom-call(s32[6]{0:T(128)} %stack.224.index_ref, bf16[512,512]{1,0:T(8,128)(2,1)} %get-tuple-element.64.refs_0_, bf16[512,512]{1,0:T(8,128)(2,1)} %copy-done.12, bf16[512,512]{1,0:T(8,128)(2,1)} %copy-done.13, bf16[512,256]{1,0:T(8,128)(2,1)} %collective-permute-done.26.refs_3_, ...), custom_call_target="tpu_custom_call" | custom-call | flops 1073741824 | bytes 4194304 | tf_op jit(solution)/shard_map/pallas_call | solution.py:447
  240.4 6.4 %all-to-all-start.4 = ((f32[16,32,128]{2,1,0:T(8,128)}), f32[16,32,128]{2,1,0:T(8,128)S(1)}, u32[]{:S(2)}, u32[]{:S(2)}) async-start(f32[16,32,128]{2,1,0:T(8,128)} %bitcast.85), calls=%async_computation.4 | async-start | bytes 524288 | tf_op jit(solution)/shard_map/all_to_all | solution.py:237
  249.9 9.6 %shard_map.147 = (bf16[512,256]{1,0:T(8,128)(2,1)}, bf16[512,256]{1,0:T(8,128)(2,1)}, bf16[512,256]{1,0:T(8,128)(2,1)}, bf16[512,256]{1,0:T(8,128)(2,1)}, f32[512,256]{1,0:T(8,128)}, /*index=5*/f32[512,256]{1,0:T(8,128)}) custom-call(s32[10]{0:T(128)} %stack.180.index_ref, bf16[512,512]{1,0:T(8,128)(2,1)} %get-tuple-element.64.refs_0_, ...), custom_call_target="tpu_custom_call" | custom-call | flops 3221225472 | bytes 8388608 | tf_op jit(solution)/shard_map/pallas_call | solution.py:447
  262.7 9.7 %shard_map.153 = (bf16[512,256]{1,0:T(8,128)(2,1)}, bf16[512,256]{1,0:T(8,128)(2,1)}, bf16[512,256]{1,0:T(8,128)(2,1)}, bf16[512,256]{1,0:T(8,128)(2,1)}, f32[512,256]{1,0:T(8,128)}, /*index=5*/f32[512,256]{1,0:T(8,128)}) custom-call(s32[10]{0:T(128)} %stack.180.index_ref, bf16[512,512]{1,0:T(8,128)(2,1)} %get-tuple-element.76.refs_0_, ...), custom_call_target="tpu_custom_call" | custom-call | flops 3221225472 | bytes 8388608 | tf_op jit(solution)/shard_map/pallas_call | solution.py:447
  275.8 4.4 %all-to-all-start.5 = ((bf16[16,32,128]{2,1,0:T(8,128)(2,1)}), bf16[16,32,128]{2,1,0:T(8,128)(2,1)S(1)}, u32[]{:S(2)}, u32[]{:S(2)}) async-start(bf16[16,32,128]{2,1,0:T(8,128)(2,1)} %shard_map.152.refs_6_), calls=%async_computation.5 | async-start | bytes 262144 | tf_op jit(solution)/shard_map/all_to_all | solution.py:692
  301.8 5.9 %shard_map.156 = f32[1024,512]{1,0:T(8,128)} custom-call(s32[5,8]{1,0:T(8,128)} %stack.173.meta_ref, f32[512,256]{1,0:T(8,128)} %get-tuple-element.66.refs_0_, bf16[512,256]{1,0:T(8,128)(2,1)} %copy-done.22, bf16[512,256]{1,0:T(8,128)(2,1)} %copy-done.26, f32[512,256]{1,0:T(8,128)} %get-tuple-element.73.refs_3_, bf16[512,256]{1,0:T(8,128)(2,1)} %copy-done.23, ...), custom_call_target="tpu_custom_call" | custom-call | flops 67108864 | bytes 7340032 | tf_op jit(solution)/shard_map/pallas_call | solution.py:557
  (200 shorter events, 99.9 us)
Async XLA Ops:
  15.5 48.8 %all-to-all-start = ((bf16[8,256,512]{2,1,0:T(8,128)(2,1)}), bf16[8,256,512]{2,1,0:T(8,128)(2,1)S(1)}, u32[]{:S(2)}, u32[]{:S(2)}) async-start(bf16[8,256,512]{2,1,0:T(8,128)(2,1)} %get-tuple-element.61), calls=%async_computation | async-start | bytes 4194304 | tf_op jit(solution)/shard_map/all_to_all | solution.py:613
  20.8 204.0 %all-gather.3.cloned.1.call-start = ((), (), s32[]{:S(2)}) async-start(), calls=%async_computation.6 | async-start | bytes 9437184 | tf_op jit(solution)/shard_map/all_gather | solution.py:623
  25.8 17.6 %collective-permute-start.5 = (bf16[1024,256]{1,0:T(8,128)(2,1)}, bf16[1024,256]{1,0:T(8,128)(2,1)S(1)}, u32[]{:S(2)}, u32[]{:S(2)}) collective-permute-start(bf16[1024,256]{1,0:T(8,128)(2,1)} %get-tuple-element.48.refs_5_), channel_id=1, source_target_pairs={{0,12},{4,0},{8,4},{12,8},{1,13},{5,1},{9,5},{13,9},{2,14},{6,2},{... | collective-permute-start | bytes 1572872 | tf_op jit(solution)/shard_map/ppermute | solution.py:37
  27.4 19.9 %collective-permute-start.10 = (bf16[512,256]{1,0:T(8,128)(2,1)}, bf16[512,256]{1,0:T(8,128)(2,1)S(1)}, u32[]{:S(2)}, u32[]{:S(2)}) collective-permute-start(bf16[512,256]{1,0:T(8,128)(2,1)} %get-tuple-element.51), channel_id=1, source_target_pairs={{0,8},{4,12},{8,0},{12,4},{1,9},{5,13},{9,1},{13,5},{2,10},{6,14},... | collective-permute-start | bytes 786440 | tf_op jit(solution)/shard_map/ppermute | solution.py:37
  67.9 34.6 %collective-permute-start.11 = (bf16[1024,512]{1,0:T(8,128)(2,1)}, bf16[1024,512]{1,0:T(8,128)(2,1)S(1)}, u32[]{:S(2)}, u32[]{:S(2)}) collective-permute-start(bf16[1024,512]{1,0:T(8,128)(2,1)} %get-tuple-element.52.refs_0_.rest_2_.refs_5_), channel_id=1, source_target_pairs={{0,4},{4,8},{8,12},{12,0},{1,5},{5,9},{9,13},{13,1},{2,6},{6,10},{... | collective-permute-start | bytes 3145736 | tf_op jit(solution)/shard_map/ppermute | solution.py:37
  68.2 35.4 %collective-permute-start.13 = (bf16[1024,512]{1,0:T(8,128)(2,1)}, bf16[1024,512]{1,0:T(8,128)(2,1)S(1)}, u32[]{:S(2)}, u32[]{:S(2)}) collective-permute-start(bf16[1024,512]{1,0:T(8,128)(2,1)} %get-tuple-element.53.refs_1_), channel_id=1, source_target_pairs={{0,12},{4,0},{8,4},{12,8},{1,13},{5,1},{9,5},{13,9},{2,14},{6,2},{... | collective-permute-start | bytes 3145736 | tf_op jit(solution)/shard_map/ppermute | solution.py:37
  71.6 43.9 %collective-permute-start.15 = (bf16[1024,512]{1,0:T(8,128)(2,1)}, bf16[1024,512]{1,0:T(8,128)(2,1)}, u32[]{:S(2)}, u32[]{:S(2)}) collective-permute-start(bf16[1024,512]{1,0:T(8,128)(2,1)} %get-tuple-element.54.refs_2_), channel_id=1, source_target_pairs={{0,1},{1,2},{2,3},{3,0},{4,5},{5,6},{6,7},{7,4},{8,9},{9,10},{10,1... | collective-permute-start | bytes 3145736 | tf_op jit(solution)/shard_map/ppermute | solution.py:37
  77.5 33.3 %all-to-all-start.1 = ((f32[16,64,192]{2,1,0:T(8,128)}), f32[16,64,192]{2,1,0:T(8,128)S(1)}, u32[]{:S(2)}, u32[]{:S(2)}) async-start(f32[16,64,192]{2,1,0:T(8,128)} %bitcast.81), calls=%async_computation.1 | async-start | bytes 2097152 | tf_op jit(solution)/shard_map/all_to_all | solution.py:237
  82.4 34.0 %collective-permute-start.17 = (bf16[1024,512]{1,0:T(8,128)(2,1)}, bf16[1024,512]{1,0:T(8,128)(2,1)}, u32[]{:S(2)}, u32[]{:S(2)}) collective-permute-start(bf16[1024,512]{1,0:T(8,128)(2,1)} %get-tuple-element.55.refs_3_), channel_id=1, source_target_pairs={{0,3},{1,0},{2,1},{3,2},{4,7},{5,4},{6,5},{7,6},{8,11},{9,8},{10,9... | collective-permute-start | bytes 3145736 | tf_op jit(solution)/shard_map/ppermute | solution.py:37
  85.5 43.8 %collective-permute-start.19 = (bf16[1024,512]{1,0:T(8,128)(2,1)}, bf16[1024,512]{1,0:T(8,128)(2,1)}, u32[]{:S(2)}, u32[]{:S(2)}) collective-permute-start(bf16[1024,512]{1,0:T(8,128)(2,1)} %get-tuple-element.53.refs_1_), channel_id=1, source_target_pairs={{0,4},{4,8},{8,12},{12,0},{1,5},{5,9},{9,13},{13,1},{2,6},{6,10},{... | collective-permute-start | bytes 3145736 | tf_op jit(solution)/shard_map/ppermute | solution.py:37
  102.5 27.9 %collective-permute-start.20 = (bf16[1024,512]{1,0:T(8,128)(2,1)}, bf16[1024,512]{1,0:T(8,128)(2,1)}, u32[]{:S(2)}, u32[]{:S(2)}) collective-permute-start(bf16[1024,512]{1,0:T(8,128)(2,1)} %get-tuple-element.52.refs_0_.rest_2_.refs_5_), channel_id=1, source_target_pairs={{0,12},{4,0},{8,4},{12,8},{1,13},{5,1},{9,5},{13,9},{2,14},{6,2},{... | collective-permute-start | bytes 3145736 | tf_op jit(solution)/shard_map/ppermute | solution.py:37
  103.6 27.7 %collective-permute-start.21 = (bf16[1024,512]{1,0:T(8,128)(2,1)}, bf16[1024,512]{1,0:T(8,128)(2,1)}, u32[]{:S(2)}, u32[]{:S(2)}) collective-permute-start(bf16[1024,512]{1,0:T(8,128)(2,1)} %get-tuple-element.55.refs_3_), channel_id=1, source_target_pairs={{0,1},{1,2},{2,3},{3,0},{4,5},{5,6},{6,7},{7,4},{8,9},{9,10},{10,1... | collective-permute-start | bytes 3145736 | tf_op jit(solution)/shard_map/ppermute | solution.py:37
  110.8 35.7 %all-to-all-start.3 = ((bf16[8,64,1152]{2,1,0:T(8,128)(2,1)}), bf16[8,64,1152]{2,1,0:T(8,128)(2,1)S(1)}, u32[]{:S(2)}, u32[]{:S(2)}) async-start(bf16[8,64,1152]{2,1,0:T(8,128)(2,1)} %get-tuple-element.62), calls=%async_computation.3 | async-start | bytes 2359296 | tf_op jit(solution)/shard_map/all_to_all | solution.py:649
  115.6 43.1 %collective-permute-start.22 = (bf16[1024,512]{1,0:T(8,128)(2,1)}, bf16[1024,512]{1,0:T(8,128)(2,1)}, u32[]{:S(2)}, u32[]{:S(2)}) collective-permute-start(bf16[1024,512]{1,0:T(8,128)(2,1)} %get-tuple-element.54.refs_2_), channel_id=1, source_target_pairs={{0,3},{1,0},{2,1},{3,2},{4,7},{5,4},{6,5},{7,6},{8,11},{9,8},{10,9... | collective-permute-start | bytes 3145736 | tf_op jit(solution)/shard_map/ppermute | solution.py:37
  116.4 51.0 %collective-permute-start.12 = (bf16[1024,512]{1,0:T(8,128)(2,1)}, bf16[1024,512]{1,0:T(8,128)(2,1)S(1)}, u32[]{:S(2)}, u32[]{:S(2)}) collective-permute-start(bf16[1024,512]{1,0:T(8,128)(2,1)} %copy-done.14), channel_id=1, source_target_pairs={{0,4},{4,8},{8,12},{12,0},{1,5},{5,9},{9,13},{13,1},{2,6},{6,10},{... | collective-permute-start | bytes 3145736 | tf_op jit(solution)/shard_map/ppermute | solution.py:37
  129.3 38.0 %collective-permute-start.14 = (bf16[1024,512]{1,0:T(8,128)(2,1)}, bf16[1024,512]{1,0:T(8,128)(2,1)}, u32[]{:S(2)}, u32[]{:S(2)}) collective-permute-start(bf16[1024,512]{1,0:T(8,128)(2,1)} %copy-done.15), channel_id=1, source_target_pairs={{0,12},{4,0},{8,4},{12,8},{1,13},{5,1},{9,5},{13,9},{2,14},{6,2},{... | collective-permute-start | bytes 3145736 | tf_op jit(solution)/shard_map/ppermute | solution.py:37
  130.4 36.9 %collective-permute-start.16 = (bf16[1024,512]{1,0:T(8,128)(2,1)}, bf16[1024,512]{1,0:T(8,128)(2,1)}, u32[]{:S(2)}, u32[]{:S(2)}) collective-permute-start(bf16[1024,512]{1,0:T(8,128)(2,1)} %collective-permute-done.15.refs_2_), channel_id=1, source_target_pairs={{0,1},{1,2},{2,3},{3,0},{4,5},{5,6},{6,7},{7,4},{8,9},{9,10},{10,1... | collective-permute-start | bytes 3145736 | tf_op jit(solution)/shard_map/ppermute | solution.py:37
  131.3 36.1 %collective-permute-start.18 = (bf16[1024,512]{1,0:T(8,128)(2,1)}, bf16[1024,512]{1,0:T(8,128)(2,1)}, u32[]{:S(2)}, u32[]{:S(2)}) collective-permute-start(bf16[1024,512]{1,0:T(8,128)(2,1)} %collective-permute-done.17.refs_3_), channel_id=1, source_target_pairs={{0,3},{1,0},{2,1},{3,2},{4,7},{5,4},{6,5},{7,6},{8,11},{9,8},{10,9... | collective-permute-start | bytes 3145736 | tf_op jit(solution)/shard_map/ppermute | solution.py:37
  146.5 22.6 %all-to-all-start.2 = ((bf16[16,64,192]{2,1,0:T(8,128)(2,1)}), bf16[16,64,192]{2,1,0:T(8,128)(2,1)S(1)}, u32[]{:S(2)}, u32[]{:S(2)}) async-start(bf16[16,64,192]{2,1,0:T(8,128)(2,1)} %shard_map.143), calls=%async_computation.2 | async-start | bytes 1048576 | tf_op jit(solution)/shard_map/all_to_all | solution.py:648
  191.7 16.4 %collective-permute-start.35 = (bf16[512,512]{1,0:T(8,128)(2,1)}, bf16[512,512]{1,0:T(8,128)(2,1)S(1)}, u32[]{:S(2)}, u32[]{:S(2)}) collective-permute-start(bf16[512,512]{1,0:T(8,128)(2,1)} %get-tuple-element.76.refs_0_), channel_id=1, source_target_pairs={{0,12},{4,0},{8,4},{12,8},{1,13},{5,1},{9,5},{13,9},{2,14},{6,2},{... | collective-permute-start | bytes 1572872 | tf_op jit(solution)/shard_map/ppermute | solution.py:37
  201.5 17.8 %collective-permute-start.24 = (bf16[512,512]{1,0:T(8,128)(2,1)}, bf16[512,512]{1,0:T(8,128)(2,1)S(1)}, u32[]{:S(2)}, u32[]{:S(2)}) collective-permute-start(bf16[512,512]{1,0:T(8,128)(2,1)} %get-tuple-element.64.refs_0_), channel_id=1, source_target_pairs={{0,4},{4,8},{8,12},{12,0},{1,5},{5,9},{9,13},{13,1},{2,6},{6,10},{... | collective-permute-start | bytes 1572872 | tf_op jit(solution)/shard_map/ppermute | solution.py:37
  201.5 17.9 %collective-permute-start.25 = (bf16[512,512]{1,0:T(8,128)(2,1)}, bf16[512,512]{1,0:T(8,128)(2,1)S(1)}, u32[]{:S(2)}, u32[]{:S(2)}) collective-permute-start(bf16[512,512]{1,0:T(8,128)(2,1)} %get-tuple-element.64.refs_0_), channel_id=1, source_target_pairs={{0,12},{4,0},{8,4},{12,8},{1,13},{5,1},{9,5},{13,9},{2,14},{6,2},{... | collective-permute-start | bytes 1572872 | tf_op jit(solution)/shard_map/ppermute | solution.py:37
  208.0 16.8 %collective-permute-start.36 = (bf16[512,256]{1,0:T(8,128)(2,1)S(1)}, bf16[512,256]{1,0:T(8,128)(2,1)S(1)}, u32[]{:S(2)}, u32[]{:S(2)}) collective-permute-start(bf16[512,256]{1,0:T(8,128)(2,1)S(1)} %slice.38), channel_id=1, source_target_pairs={{0,4},{4,8},{8,12},{12,0},{1,5},{5,9},{9,13},{13,1},{2,6},{6,10},{... | collective-permute-start | bytes 786440 | tf_op jit(solution)/shard_map/ppermute | solution.py:37
  208.1 16.7 %collective-permute-start.37 = (bf16[512,256]{1,0:T(8,128)(2,1)S(1)}, bf16[512,256]{1,0:T(8,128)(2,1)}, u32[]{:S(2)}, u32[]{:S(2)}) collective-permute-start(bf16[512,256]{1,0:T(8,128)(2,1)S(1)} %slice.39), channel_id=1, source_target_pairs={{0,12},{4,0},{8,4},{12,8},{1,13},{5,1},{9,5},{13,9},{2,14},{6,2},{... | collective-permute-start | bytes 786440 | tf_op jit(solution)/shard_map/ppermute | solution.py:37
  230.4 51.8 %collective-permute-start.39 = (bf16[512,256]{1,0:T(8,128)(2,1)}, bf16[512,256]{1,0:T(8,128)(2,1)S(1)}, u32[]{:S(2)}, u32[]{:S(2)}) collective-permute-start(bf16[512,256]{1,0:T(8,128)(2,1)} %get-tuple-element.82), channel_id=1, source_target_pairs={{0,1},{1,2},{2,3},{3,0},{4,5},{5,6},{6,7},{7,4},{8,9},{9,10},{10,1... | collective-permute-start | bytes 786440 | tf_op jit(solution)/shard_map/ppermute | solution.py:37
  230.7 53.4 %collective-permute-start.40 = (bf16[512,256]{1,0:T(8,128)(2,1)}, bf16[512,256]{1,0:T(8,128)(2,1)S(1)}, u32[]{:S(2)}, u32[]{:S(2)}) collective-permute-start(bf16[512,256]{1,0:T(8,128)(2,1)} %get-tuple-element.84), channel_id=1, source_target_pairs={{0,3},{1,0},{2,1},{3,2},{4,7},{5,4},{6,5},{7,6},{8,11},{9,8},{10,9... | collective-permute-start | bytes 786440 | tf_op jit(solution)/shard_map/ppermute | solution.py:37
  238.5 33.9 %collective-permute-start.29 = (bf16[512,256]{1,0:T(8,128)(2,1)}, bf16[512,256]{1,0:T(8,128)(2,1)S(1)}, u32[]{:S(2)}, u32[]{:S(2)}) collective-permute-start(bf16[512,256]{1,0:T(8,128)(2,1)} %get-tuple-element.69.refs_2_), channel_id=1, source_target_pairs={{0,1},{1,2},{2,3},{3,0},{4,5},{5,6},{6,7},{7,4},{8,9},{9,10},{10,1... | collective-permute-start | bytes 786440 | tf_op jit(solution)/shard_map/ppermute | solution.py:37
  240.4 20.0 %all-to-all-start.4 = ((f32[16,32,128]{2,1,0:T(8,128)}), f32[16,32,128]{2,1,0:T(8,128)S(1)}, u32[]{:S(2)}, u32[]{:S(2)}) async-start(f32[16,32,128]{2,1,0:T(8,128)} %bitcast.85), calls=%async_computation.4 | async-start | bytes 524288 | tf_op jit(solution)/shard_map/all_to_all | solution.py:237
  246.8 26.9 %collective-permute-start.30 = (bf16[512,256]{1,0:T(8,128)(2,1)}, bf16[512,256]{1,0:T(8,128)(2,1)S(1)}, u32[]{:S(2)}, u32[]{:S(2)}) collective-permute-start(bf16[512,256]{1,0:T(8,128)(2,1)} %get-tuple-element.71), channel_id=1, source_target_pairs={{0,3},{1,0},{2,1},{3,2},{4,7},{5,4},{6,5},{7,6},{8,11},{9,8},{10,9... | collective-permute-start | bytes 786440 | tf_op jit(solution)/shard_map/ppermute | solution.py:37
  259.5 32.1 %collective-permute-start.28 = (bf16[512,256]{1,0:T(8,128)(2,1)}, bf16[512,256]{1,0:T(8,128)(2,1)S(1)}, u32[]{:S(2)}, u32[]{:S(2)}) collective-permute-start(bf16[512,256]{1,0:T(8,128)(2,1)} %get-tuple-element.67), channel_id=1, source_target_pairs={{0,3},{1,0},{2,1},{3,2},{4,7},{5,4},{6,5},{7,6},{8,11},{9,8},{10,9... | collective-permute-start | bytes 786440 | tf_op jit(solution)/shard_map/ppermute | solution.py:37
  272.5 19.7 %collective-permute-start.32 = (bf16[512,256]{1,0:T(8,128)(2,1)S(1)}, bf16[512,256]{1,0:T(8,128)(2,1)S(1)}, u32[]{:S(2)}, u32[]{:S(2)}) collective-permute-start(bf16[512,256]{1,0:T(8,128)(2,1)S(1)} %copy-done.41), channel_id=1, source_target_pairs={{0,1},{1,2},{2,3},{3,0},{4,5},{5,6},{6,7},{7,4},{8,9},{9,10},{10,1... | collective-permute-start | bytes 786440 | tf_op jit(solution)/shard_map/ppermute | solution.py:37
  273.7 20.0 %collective-permute-start.38 = (bf16[512,256]{1,0:T(8,128)(2,1)}, bf16[512,256]{1,0:T(8,128)(2,1)S(1)}, u32[]{:S(2)}, u32[]{:S(2)}) collective-permute-start(bf16[512,256]{1,0:T(8,128)(2,1)} %get-tuple-element.80), channel_id=1, source_target_pairs={{0,3},{1,0},{2,1},{3,2},{4,7},{5,4},{6,5},{7,6},{8,11},{9,8},{10,9... | collective-permute-start | bytes 786440 | tf_op jit(solution)/shard_map/ppermute | solution.py:37
  (61 other events, 568.5 us)
Sparse Core Ops, SparseCore 0:
  68.0 49.7 all-gather.2

commit v7 on v5

--- a/solution.py
+++ b/solution.py
@@ -37,8 +37,7 @@
     return lax.ppermute(block, axis, [(i, (i + step) % SIDE) for i in range(SIDE)])
 
 
-def ring_gather(block, axis):
-    half = block.shape[1] // 2
+def ring_gather(block, axis, half):
     behind = shift(block, axis, 1)
     ahead = shift(block, axis, -1)
     far_low = shift(behind[:, :half], axis, 1)
@@ -219,7 +218,7 @@
     )
 
 
-def project(index, total, blocks, weights, tile, last=None, rows=256):
+def project(index, total, blocks, weights, tile, last=None, after=(), rows=256):
     tokens = blocks[0].shape[0]
     counts = [b.shape[1] // rows for b in blocks]
     pieces = sum(counts)
@@ -242,7 +241,7 @@
                 acc = add if acc is None else acc + add
                 at += n
             if tail is not None:
-                acc = tail(meta_ref, acc, rest[kinds : len(rest) - kinds])
+                acc = tail(meta_ref, acc, rest[kinds : kinds + len(tail_operands)])
             outs[kind][...] = acc
 
     def weight(k, width):
@@ -269,7 +268,7 @@
         grid_spec=pltpu.PrefetchScalarGridSpec(
             num_scalar_prefetch=2,
             grid=(tokens // tile,),
-            in_specs=in_specs + tail_specs,
+            in_specs=in_specs + tail_specs + passive(after),
             out_specs=row_specs,
         ),
         input_output_aliases=aliases,
@@ -278,7 +277,7 @@
             2 * tokens * depth * sum(widths),
             2 * depth * (tokens + sum(widths)) + 8 * tokens * sum(widths),
         ),
-    )(index, meta, *operands, *tail_operands)
+    )(index, meta, *operands, *tail_operands, *after)
 
 
 def key_value_tail(shrunk, up, cosine, sine, wide, narrow, tile):
@@ -330,7 +329,7 @@
     window = min(3 * BLOCK, tokens)
     scale = 1.0 / math.sqrt(HEAD)
 
-    def body(meta_ref, q_ref, s_ref, up_ref, d_ref, m_ref, o_ref, c_ref, n_ref, att, head):
+    def body(meta_ref, q_ref, s_ref, up_ref, d_ref, m_ref, o_ref, c_ref, n_ref, att):
         i = begin + pl.program_id(0)
         is_key = meta_ref[3, 0] == 1
         first = meta_ref[2, i]
@@ -366,18 +365,17 @@
             weights = weights * (1.0 / jnp.sum(weights, axis=1, keepdims=True))
             mixed = jnp.dot(weights.astype(bf16), values, preferred_element_type=f32)
             att[:, at] = mixed.astype(bf16)
-        head[...] = lax.dot_general(
-            att[...], d_ref[0], (((1,), (1,)), ((), ())), preferred_element_type=f32
+        head = lax.dot_general(
+            att[:, :wide], d_ref[0], (((1,), (1,)), ((), ())), preferred_element_type=f32
         )
+        att[:, wide : wide + rank] = head.astype(bf16)
+        att[:, wide + rank :] = jnp.zeros((BLOCK, HEAD - rank), bf16)
 
     table = pl.BlockSpec((1, BLOCK, HEAD), lambda i, m: (m[1, i + begin], 0, 0))
     whole = pl.BlockSpec((tokens, HEAD), lambda i, m: (0, 0))
     return pl.pallas_call(
         body,
-        out_shape=(
-            jax.ShapeDtypeStruct((count * BLOCK, wide), bf16),
-            jax.ShapeDtypeStruct((count * BLOCK, rank), f32),
-        ),
+        out_shape=jax.ShapeDtypeStruct((count * BLOCK, wide + HEAD), bf16),
         grid_spec=pltpu.PrefetchScalarGridSpec(
             num_scalar_prefetch=1,
             grid=(count,),
@@ -391,10 +389,7 @@
                 table,
                 table,
             ],
-            out_specs=[
-                pl.BlockSpec((BLOCK, wide), lambda i, m: (i, 0)),
-                pl.BlockSpec((BLOCK, rank), lambda i, m: (i, 0)),
-            ],
+            out_specs=pl.BlockSpec((BLOCK, wide + HEAD), lambda i, m: (i, 0)),
         ),
         compiler_params=params(),
         cost_estimate=cost(
@@ -403,107 +398,136 @@
     )(meta, q, shrunk, up, down, mine, other, cosine, sine)
 
 
-def output_partial(index, pieces, weights, dtypes, after):
+def output_partial(shards, pieces, weights):
     tokens = pieces[0].shape[0]
-    depth, width = weights.shape[1:]
+    count, (depth, width) = len(shards), weights.shape[1:]
     unit = depth // SIDE
-    count = len(dtypes)
-    places = [(0, 0), (1, 0), (2, 0), (3, 0), (3, unit // 2)]
+    far_cut = pieces[3].shape[1]
+    whole = 2 * width + HEAD
 
     def body(index_ref, *refs):
-        x_refs, w_ref, outs = refs[: len(pieces)], refs[len(pieces)], refs[-count:]
-        total = None
-        for x_ref, (place, offset) in zip(x_refs, places):
-            start = pl.multiple_of(index_ref[place] * unit + offset, 128)
-            rows = w_ref[0, pl.ds(start, x_ref.shape[1]), :]
-            add = jnp.dot(x_ref[...], rows, preferred_element_type=f32)
-            total = add if total is None else total + add
-        for k, out in enumerate(outs):
-
-            @pl.when(pl.program_id(0) == k)
+        own, behind, ahead, far_low, far_high, w_ref = refs[:6]
+        out_far_low, out_far_high, out_ahead, out_behind, out_mine, x_all = refs[6:]
+        step = pl.program_id(0)
+
+        @pl.when(step == 0)
+        def _():
+            for k, ref in enumerate((own, behind, ahead)):
+                x_all[:, k * unit : (k + 1) * unit] = ref[:, :unit]
+            x_all[:, 3 * unit : 3 * unit + far_cut] = far_low[...]
+            x_all[:, 3 * unit + far_cut :] = far_high[:, : unit - far_cut]
+            rank = (
+                own[:, unit:].astype(f32)
+                + behind[:, unit:].astype(f32)
+                + ahead[:, unit:].astype(f32)
+                + far_high[:, unit - far_cut :].astype(f32)
+            )
+            for out in (out_far_low, out_ahead, out_behind, out_mine):
+                out[:, width : width + HEAD] = rank.astype(out.dtype)
+
+        total = jnp.dot(x_all[...], w_ref[0], preferred_element_type=f32)
+        low, high = slice(0, width), slice(width + HEAD, whole)
+        targets = [(out_far_low, low), (out_far_high, low)]
+        targets += [(out, at) for out in (out_ahead, out_behind, out_mine) for at in (low, high)]
+        for k, (out, at) in enumerate(targets):
+
+            @pl.when(step == k)
             def _():
-                out[...] = total.astype(out.dtype)
-
-    return pl.pallas_call(
-        body,
-        out_shape=tuple(jax.ShapeDtypeStruct((tokens, width), d) for d in dtypes),
+                out[:, at] = total.astype(out.dtype)
+
+    shapes = [(width + HEAD, bf16), (width, bf16), (whole, bf16), (whole, bf16), (whole, f32)]
+    return pl.pallas_call(
+        body,
+        out_shape=tuple(jax.ShapeDtypeStruct((tokens, w), d) for w, d in shapes),
         grid_spec=pltpu.PrefetchScalarGridSpec(
             num_scalar_prefetch=1,
             grid=(count,),
             in_specs=[pl.BlockSpec(p.shape, lambda j, d: (0, 0)) for p in pieces]
-            + [pl.BlockSpec((1, depth, width), lambda j, d: (d[SIDE + j], 0, 0))]
-            + passive(after),
-            out_specs=[pl.BlockSpec((tokens, width), lambda j, d: (0, 0))] * count,
+            + [pl.BlockSpec((1, depth, width), lambda j, d: (d[j], 0, 0))],
+            out_specs=[pl.BlockSpec((tokens, w), lambda j, d: (0, 0)) for w, _ in shapes],
+            scratch_shapes=[pltpu.VMEM((tokens, depth), bf16)],
         ),
         compiler_params=params(),
         cost_estimate=cost(
             2 * tokens * depth * count * width, 2 * depth * (tokens + count * width)
         ),
-    )(index, *pieces, weights, *after)
-
-
-def output_ring(pieces, weights, axis, places, ahead_of):
+    )(jnp.stack(shards).astype(i32), *pieces, weights)
+
+
+def add_far(ahead, via_behind, behind, via_ahead):
+    rows, whole = ahead.shape
+    low = via_behind.shape[1]
+
+    def body(a_ref, va_ref, b_ref, vb_ref, out_a, out_b):
+        out_a[:, :low] = (a_ref[:, :low].astype(f32) + va_ref[...].astype(f32)).astype(bf16)
+        out_a[:, low:] = a_ref[:, low:]
+        out_b[:, :low] = b_ref[:, :low]
+        out_b[:, low:] = (b_ref[:, low:].astype(f32) + vb_ref[...].astype(f32)).astype(bf16)
+
+    arrays = (ahead, via_behind, behind, via_ahead)
+    return pl.pallas_call(
+        body,
+        out_shape=(jax.ShapeDtypeStruct((rows, whole), bf16),) * 2,
+        grid=(1,),
+        in_specs=[pl.BlockSpec(a.shape, lambda i: (0, 0)) for a in arrays],
+        out_specs=[pl.BlockSpec((rows, whole), lambda i: (0, 0))] * 2,
+        compiler_params=params(),
+        cost_estimate=cost(2 * rows * whole, 10 * rows * whole),
+    )(*arrays)
+
+
+def output_ring(pieces, weights, axis):
     me, behind, ahead, far = ring_order(lax.axis_index(axis))
-
-    def partial(shards, dtypes, after=()):
-        index = jnp.stack(places + shards).astype(i32)
-        return output_partial(index, pieces, weights, dtypes, after)
-
-    far_low, far_high = partial([2 * far, 2 * far + 1], [bf16] * 2)
-    via_behind = shift(far_low, axis, 1)
-    via_ahead = shift(far_high, axis, -1)
-    ahead_high, behind_low, ahead_low, behind_high, low, high = partial(
-        [2 * ahead + 1, 2 * behind, 2 * ahead, 2 * behind + 1, 2 * me, 2 * me + 1],
-        [bf16] * 4 + [f32] * 2,
-        [ahead_of],
-    )
-    return (
-        (low, shift(behind_low, axis, -1), shift(ahead_low + via_behind, axis, 1)),
-        (high, shift(ahead_high, axis, 1), shift(behind_high + via_ahead, axis, -1)),
-    )
-
-
-def finish(meta, parts, head_rank, up, wide):
+    shards = [2 * place + side for place in (far, ahead, behind, me) for side in range(2)]
+    far_low, far_high, to_ahead, to_behind, mine = output_partial(shards, pieces, weights)
+    to_ahead, to_behind = add_far(
+        to_ahead, shift(far_low, axis, 1), to_behind, shift(far_high, axis, -1)
+    )
+    return mine, shift(to_behind, axis, -1), shift(to_ahead, axis, 1)
+
+
+def finish(meta, parts, up, rank, wide):
     cuts = len(parts)
-    rows, width = parts[0][0][0].shape
+    rows, whole = parts[0][0].shape
+    width = (whole - HEAD) // 2
     per = 2
     steps = rows // (per * BLOCK)
-    rank = head_rank.shape[1] // cuts
-    terms = [t for cut in parts for side in cut for t in side]
-    each = len(parts[0][0])
+    terms = [t for cut in parts for t in cut]
+    each = len(parts[0])
 
     def body(meta_ref, *refs):
-        h_ref, up_ref, out = refs[len(terms) :]
+        up_ref, out = refs[len(terms) :]
         i = pl.program_id(0)
 
-        def put(cut):
+        def put(mine):
             for k in range(per):
                 at = slice(k * BLOCK, (k + 1) * BLOCK)
                 block = i * per + k
+                total = mine[0][at, :].astype(f32)
+                for ref in mine[1:]:
+                    total = total + ref[at, :].astype(f32)
                 extra = jnp.dot(
-                    h_ref[at, cut * rank : (cut + 1) * rank],
+                    total[:, width : width + rank].astype(bf16),
                     up_ref[meta_ref[0, block]],
                     preferred_element_type=f32,
                 )
                 row = block * BLOCK + lax.broadcasted_iota(i32, (BLOCK, width), 0)
                 valid = row < meta_ref[4, block]
-                for side in range(2):
+                for side, begin in enumerate((0, width + HEAD)):
                     cols = slice(side * width, (side + 1) * width)
-                    total = extra[:, cols]
-                    begin = (cut * 2 + side) * each
-                    for ref in refs[begin : begin + each]:
-                        total = total + ref[at, :].astype(f32)
-                    out[at, cols] = jnp.where(valid, total, 0.0)
+                    out[at, cols] = jnp.where(
+                        valid, total[:, begin : begin + width] + extra[:, cols], 0.0
+                    )
 
         for cut in range(cuts):
 
             @pl.when(i // steps == cut)
             def _():
-                put(cut)
+                put(refs[cut * each : (cut + 1) * each])
 
     def term_spec(cut):
         return pl.BlockSpec(
-            (per * BLOCK, width), lambda i, m: (jnp.clip(i - cut * steps, 0, steps - 1), 0)
+            (per * BLOCK, whole), lambda i, m: (jnp.clip(i - cut * steps, 0, steps - 1), 0)
         )
 
     return pl.pallas_call(
@@ -512,16 +536,13 @@
         grid_spec=pltpu.PrefetchScalarGridSpec(
             num_scalar_prefetch=1,
             grid=(cuts * steps,),
-            in_specs=[term_spec(cut) for cut in range(cuts) for _ in range(2 * each)]
-            + [
-                pl.BlockSpec((per * BLOCK, cuts * rank), lambda i, m: (lax.rem(i, steps), 0)),
-                pl.BlockSpec((up.shape[0], rank, wide), lambda i, m: (0, 0, 1)),
-            ],
+            in_specs=[term_spec(cut) for cut in range(cuts) for _ in range(each)]
+            + [pl.BlockSpec((up.shape[0], rank, wide), lambda i, m: (0, 0, 1))],
             out_specs=pl.BlockSpec((per * BLOCK, 2 * width), lambda i, m: (i, 0)),
         ),
         compiler_params=params(),
         cost_estimate=cost(4 * cuts * rows * rank * width, 28 * cuts * rows * width),
-    )(meta, *terms, head_rank, up)
+    )(meta, *terms, up)
 
 
 def on_device(x, wq, wkv, wo, down_qkv, up_q, up_kv, down_o, up_o, choice, counts, tails):
@@ -564,16 +585,15 @@
     )
     down = lax.all_to_all(down_out, ADAPTER_AXES, 0, 0, tiled=True)
 
-    first_a = ring_gather(x_a, "x")
-    first_b = ring_gather(x_b, "y")
+    first_a = ring_gather(x_a, "x", x_a.shape[1] // 2)
+    first_b = ring_gather(x_b, "y", x_b.shape[1] // 2)
 
     got = [sent[0], shift(sent[2], "y", 1), shift(sent[1], "y", -1), shift(sent[3], "y", 2)]
-    wo_mine = stack_rows(got, first_a[1:3] + first_b[1:3])
+    low_a, high_a, low_b, high_b = join(
+        [first_a[:2], first_a[2:], first_b[:2], first_b[2:]], got[1:]
+    )
+    wo_mine = stack_rows(got, [down, low_a])
     wo_all = lax.all_gather(wo_mine, ADAPTER_AXES, axis=0)
-
-    low_a, high_a, low_b, high_b = join(
-        [first_a[:2], first_a[2:], first_b[:2], first_b[2:]], [wo_mine]
-    )
     far_a, next_a = second_gather(low_a, high_a, "y")
     far_b, next_b = second_gather(low_b, high_b, "x")
 
@@ -588,34 +608,38 @@
 
     every = range(SIDE)
     low, high = (0, 1), (2, 3)
-    total = project(
-        (index_of(rows_a(0, every) + rows_b(0, every)), meta),
-        None,
-        [low_a, high_a, low_b, high_b],
-        [wq, wkv],
-        512,
-    )
-
-    pieces = scatter_rows(rank_partial(meta, x, down, 3 * rank, [*far_a, *far_b]))
+    pieces = scatter_rows(rank_partial(meta, x, down, 3 * rank, [low_a]))
+    up = lax.all_to_all(up_out, ADAPTER_AXES, 0, 0, tiled=True)
+
     copies = share_sum(pieces, [])
-    shrunk = lax.all_to_all(copies, TENSOR_AXES, 0, 0, tiled=True).reshape(tokens, 3 * rank)
-    up = lax.all_to_all(up_out, ADAPTER_AXES, 0, 0, tiled=True)
 
     a_low, a_high = shift(far_a[0], "y", 1), shift(far_a[1], "y", -1)
     b_low, b_high = shift(far_b[0], "x", 1), shift(far_b[1], "x", -1)
     total = project(
         (
             index_of(
-                rows_a(1, low) + rows_a(2, high) + rows_b(1, low) + rows_b(2, high)
-                + rows_a(1, high) + rows_a(2, low) + rows_b(1, high) + rows_b(2, low)
+                rows_a(0, every) + rows_b(0, every)
+                + rows_a(1, low) + rows_a(2, high) + rows_b(1, low) + rows_b(2, high)
             ),
             meta,
         ),
-        total,
-        [*far_a, *far_b, *next_a, *next_b],
+        None,
+        [low_a, high_a, low_b, high_b, *far_a, *far_b],
         [wq, wkv],
         512,
-    )
+        after=[copies],
+    )
+    total = project(
+        (
+            index_of(rows_a(1, high) + rows_a(2, low) + rows_b(1, high) + rows_b(2, low)),
+            meta,
+        ),
+        total,
+        [*next_a, *next_b],
+        [wq, wkv],
+        512,
+    )
+    shrunk = lax.all_to_all(copies, TENSOR_AXES, 0, 0, tiled=True).reshape(tokens, 3 * rank)
     final = (index_of(rows_a(3, every) + rows_b(3, every)), meta)
     far = [a_low, a_high, b_low, b_high]
     tail = key_value_tail(shrunk, up, cosine, sine, wide, wkv.shape[1], 512)
@@ -624,21 +648,14 @@
     (q,) = project(final, total[:1], far, [wq], 512)
 
     cuts = 2
-    pieces, ranks = [], []
+    each = blocks // cuts
+    parts = []
     for cut in range(cuts):
-        attended, head = attention(
-            meta, q, shrunk, up, down, mine, other, cosine, sine, cut * blocks // cuts, blocks // cuts
+        attended = attention(
+            meta, q, shrunk, up, down, mine, other, cosine, sine, cut * each, each
         )
-        ranks.append(head)
-        pieces.append(ring_gather(attended, "y"))
-    copies = share_sum(scatter_rows(jnp.concatenate(ranks, axis=1)), [])
-    head_rank = lax.all_to_all(copies, TENSOR_AXES, 0, 0, tiled=True).reshape(tokens // 2, 2 * rank)
-    places = [jnp.int32(k) for k in range(SIDE)]
-    parts = [
-        output_ring(pieces[0], wo_all, "x", places, copies),
-        output_ring(pieces[1], wo_all, "x", places, head_rank),
-    ]
-    return finish(meta, parts, head_rank, up, wide)
+        parts.append(output_ring(ring_gather(attended, "y", wide // 2), wo_all, "x"))
+    return finish(meta, parts, up, rank, wide)
 
 
 def solution(mesh):

time: 322 us -> 316 us (0.981)
  starting transfers between devices: 96.4 us -> 78.4 us
  waiting for transfers between devices: 86.9 us -> 103 us
    ppermute x43 -> x39, waiting for transfers between devices: 68.6 us -> 101 us  [shift(): lax.ppermute(block, axis, [(i, (i + step) % SIDE) for i in range(SIDE)])]
    all_to_all x2 -> x1, waiting for transfers between devices: 18.2 us -> 1.96 us  [scatter_rows(): lax.all_to_all(partial.reshape(ways, rows // ways, rank), TENSOR_AXES, 0,...]
    ppermute x43 -> x39, starting transfers between devices: 66.2 us -> 57.7 us  [shift(): lax.ppermute(block, axis, [(i, (i + step) % SIDE) for i in range(SIDE)])]
    all_to_all x2 -> x1, starting transfers between devices: 9.68 us -> 3.72 us  [scatter_rows(): lax.all_to_all(partial.reshape(ways, rows // ways, rank), TENSOR_AXES, 0,...]
    all_to_all x2 -> x1, starting transfers between devices: 9.31 us -> 4.51 us  [on_device(): lax.all_to_all(copies, TENSOR_AXES, 0, 0, tiled=True)]
    unnamed x82 -> x72, local copies, waits for them, and re-layouts: 7.25 us -> 7.44 us
  transfers between devices with their start and end apart: 51 -> 45, of which waited for: 17 -> 19; matrix products, arithmetic and copies ran while one was open for 3% -> 1% of each run, Pallas kernels for 28% -> 29%
where the time goes in v7:
time: 316 us; the launch traced here: 314 us
  Pallas kernels  106 us (34%)
  waiting for transfers between devices  103 us (33%)
  starting transfers between devices  78.4 us (25%)
  between operations  13.8 us (4%)
  local copies, waits for them, and re-layouts  11 us (3%)
    ppermute x39, waiting for transfers between devices, shift(): lax.ppermute(block, axis, [(i, (i + step) % SIDE) for i in range(SIDE)])  101 us
    ppermute x39, starting transfers between devices, shift(): lax.ppermute(block, axis, [(i, (i + step) % SIDE) for i in range(SIDE)])  57.7 us
    pallas_call x4, Pallas kernels, project(): pl.pallas_call(body, out_shape=tuple((jax.ShapeDtypeStruct((tokens, w), d...  34.1 us
    pallas_call x2, Pallas kernels, output_partial(): pl.pallas_call(body, out_shape=tuple((jax.ShapeDtypeStruct((tokens, w), d...  25.1 us
    pallas_call x2, Pallas kernels, attention(): pl.pallas_call(body, out_shape=jax.ShapeDtypeStruct((count * BLOCK, wide...  13.3 us
    pallas_call x1, Pallas kernels, pick_local(): pl.pallas_call(body, out_shape=tuple((jax.ShapeDtypeStruct(s, bf16) for s...  7.52 us
    unnamed x72, local copies, waits for them, and re-layouts  7.44 us
  transfers between devices with their start and end apart: 45, of which 19 were waited for; matrix products, arithmetic and copies ran while one was open for 1% of the time, Pallas kernels for 29%

profile of v7, /device:TPU:0, one launch (start us, length us, event | category | flops | bytes accessed | tf_op | source)
XLA Modules:
  0.0 313.8 jit_solution(9300314600612270796)
XLA Ops:
  7.9 7.5 %shard_map.136 = (bf16[8,256,512]{2,1,0:T(8,128)(2,1)}, bf16[8,64,1152]{2,1,0:T(8,128)(2,1)}, bf16[1024,256]{1,0:T(8,128)(2,1)}, bf16[1024,256]{1,0:T(8,128)(2,1...) custom-call(s32[12]{0:T(128)} %pad_add_fusion.pick_ref, ...), custom_call_target="tpu_custom_call" | custom-call | bytes 6553600 | tf_op jit(solution)/shard_map/pallas_call | solution.py:87
  15.5 5.7 %all-to-all-start = ((bf16[8,256,512]{2,1,0:T(8,128)(2,1)}), bf16[8,256,512]{2,1,0:T(8,128)(2,1)S(1)}, u32[]{:S(2)}, u32[]{:S(2)}) async-start(bf16[8,256,512]{2,1,0:T(8,128)(2,1)} %get-tuple-element.44), calls=%async_computation | async-start | bytes 4194304 | tf_op jit(solution)/shard_map/all_to_all | solution.py:586
  29.8 7.0 %collective-permute-done.refs_1_ = bf16[1024,256]{1,0:T(8,128)(2,1)S(1)} collective-permute-done((bf16[1024,256]{1,0:T(8,128)(2,1)S(1)}, bf16[1024,256]{1,0:T(8,128)(2,1)S(1)}, u32[]{:S(2)}, u32[]{:S(2)}) %collective-permute-start) | collective-permute-done | bytes 524320 | tf_op jit(solution)/shard_map/ppermute | solution.py:37
  43.7 4.0 %collective-permute-done.10.refs_12_.refs_3_ = bf16[512,256]{1,0:T(8,128)(2,1)S(1)} collective-permute-done((bf16[512,256]{1,0:T(8,128)(2,1)}, bf16[512,256]{1,0:T(8,128)(2,1)S(1)}, u32[]{:S(2)}, u32[]{:S(2)}) %collective-permute-start.10) | collective-permute-done | bytes 262176 | tf_op jit(solution)/shard_map/ppermute | solution.py:37
  53.9 3.2 %collective-permute-done.6.refs_8_ = bf16[1024,128]{1,0:T(8,128)(2,1)S(1)} collective-permute-done((bf16[1024,128]{1,0:T(8,128)(2,1)S(1)}, bf16[1024,128]{1,0:T(8,128)(2,1)S(1)}, u32[]{:S(2)}, u32[]{:S(2)}) %collective-permute-start.6) | collective-permute-done | bytes 262176 | tf_op jit(solution)/shard_map/ppermute | solution.py:37
  59.9 4.7 %shard_map.137 = (bf16[1024,512]{1,0:T(8,128)(2,1)}, bf16[1024,512]{1,0:T(8,128)(2,1)}, bf16[1024,512]{1,0:T(8,128)(2,1)}, bf16[1024,512]{1,0:T(8,128)(2,1)}) custom-call(bf16[1024,256]{1,0:T(8,128)(2,1)} %get-tuple-element.35.refs_0_, bf16[1024,256]{1,0:T(8,128)(2,1)} %copy-done.5, bf16[1024,256]{1,0:T(8,128)(2,1)} %copy-done.6, ...), custom_call_target="tpu_custom_call" | custom-call | bytes 8388608 | tf_op jit(solution)/shard_map/pallas_call | solution.py:179
  72.6 5.1 %shard_map.138 = f32[1024,192]{1,0:T(8,128)} custom-call(s32[5,8]{1,0:T(8,128)} %stack.166.meta_ref, bf16[1024,512]{1,0:T(8,128)(2,1)} %x_ref.3, bf16[8,256,512]{2,1,0:T(8,128)(2,1)} %copy-done, bf16[8,256,512]{2,1,0:T(8,128)(2,1)} %copy-done, bf16[1024,512]{1,0:T(8,128)(2,1)} %get-tuple-element.40.rest_2_.refs_0_.refs_5_), custom_call_target="tpu_custom_call" | custom-call | flops 201326592 | bytes 2621440 | tf_op jit(solution)/shard_map/pallas_call | solution.py:147
  77.7 3.7 %all-to-all-start.1 = ((f32[16,64,192]{2,1,0:T(8,128)}), f32[16,64,192]{2,1,0:T(8,128)S(1)}, u32[]{:S(2)}, u32[]{:S(2)}) async-start(f32[16,64,192]{2,1,0:T(8,128)} %bitcast.75), calls=%async_computation.1 | async-start | bytes 2097152 | tf_op jit(solution)/shard_map/all_to_all | solution.py:216
  86.6 18.4 %collective-permute-done.11.refs_4_ = bf16[1024,512]{1,0:T(8,128)(2,1)S(1)} collective-permute-done((bf16[1024,512]{1,0:T(8,128)(2,1)}, bf16[1024,512]{1,0:T(8,128)(2,1)S(1)}, u32[]{:S(2)}, u32[]{:S(2)}) %collective-permute-start.11) | collective-permute-done | bytes 1048608 | tf_op jit(solution)/shard_map/ppermute | solution.py:37
  107.7 4.8 %all-to-all-start.3 = ((bf16[8,64,1152]{2,1,0:T(8,128)(2,1)}), bf16[8,64,1152]{2,1,0:T(8,128)(2,1)S(1)}, u32[]{:S(2)}, u32[]{:S(2)}) async-start(bf16[8,64,1152]{2,1,0:T(8,128)(2,1)} %get-tuple-element.48), calls=%async_computation.3 | async-start | bytes 2359296 | tf_op jit(solution)/shard_map/all_to_all | solution.py:612
  112.5 5.6 %collective-permute-done.15.refs_6_ = bf16[1024,512]{1,0:T(8,128)(2,1)} collective-permute-done((bf16[1024,512]{1,0:T(8,128)(2,1)}, bf16[1024,512]{1,0:T(8,128)(2,1)}, u32[]{:S(2)}, u32[]{:S(2)}) %collective-permute-start.15) | collective-permute-done | bytes 1048608 | tf_op jit(solution)/shard_map/ppermute | solution.py:37
  122.6 7.1 %collective-permute-done.19.refs_0_ = bf16[1024,512]{1,0:T(8,128)(2,1)} collective-permute-done((bf16[1024,512]{1,0:T(8,128)(2,1)}, bf16[1024,512]{1,0:T(8,128)(2,1)}, u32[]{:S(2)}, u32[]{:S(2)}) %collective-permute-start.19) | collective-permute-done | bytes 1048608 | tf_op jit(solution)/shard_map/ppermute | solution.py:37
  131.1 9.5 %collective-permute-done.21.refs_2_ = bf16[1024,512]{1,0:T(8,128)(2,1)} collective-permute-done((bf16[1024,512]{1,0:T(8,128)(2,1)}, bf16[1024,512]{1,0:T(8,128)(2,1)}, u32[]{:S(2)}, u32[]{:S(2)}) %collective-permute-start.21) | collective-permute-done | bytes 1048608 | tf_op jit(solution)/shard_map/ppermute | solution.py:37
  147.6 4.5 %all-to-all-start.2 = ((bf16[16,64,192]{2,1,0:T(8,128)(2,1)}), bf16[16,64,192]{2,1,0:T(8,128)(2,1)S(1)}, u32[]{:S(2)}, u32[]{:S(2)}) async-start(bf16[16,64,192]{2,1,0:T(8,128)(2,1)} %shard_map.139.refs_40_), calls=%async_computation.2 | async-start | bytes 1048576 | tf_op jit(solution)/shard_map/all_to_all | solution.py:642
  152.1 12.9 %shard_map.140 = (f32[1024,512]{1,0:T(8,128)}, f32[1024,128]{1,0:T(8,128)}) custom-call(s32[16]{0:T(128)} %stack.215.index_ref, s32[5,8]{1,0:T(8,128)} %stack.166.meta_ref, bf16[1024,512]{1,0:T(8,128)(2,1)} %get-tuple-element.40.rest_2_.refs_0_.refs_5_, bf16[1024,512]{1,0:T(8,128)(2,1)} %get-tuple-element.41.refs_1_, ...), custom_call_target="tpu_custom_call" | custom-call | flops 5368709120 | bytes 18874368 | tf_op jit(solution)/shard_map/pallas_call | solution.py:265
  165.0 8.6 %shard_map.141 = (f32[1024,512]{1,0:T(8,128)}, f32[1024,128]{1,0:T(8,128)}) custom-call(s32[8]{0:T(128)} %stack.198.index_ref, s32[5,8]{1,0:T(8,128)} %stack.166.meta_ref, bf16[1024,512]{1,0:T(8,128)(2,1)} %collective-permute-done.19.refs_0_, bf16[1024,512]{1,0:T(8,128)(2,1)} %collective-permute-done.20.refs_1_, ...), custom_call_target="tpu_custom_call", output_to_operand_aliasing={{0}: (22, {}), {1}: (23, {})} | custom-call | flops 2684354560 | bytes 12058624 | tf_op jit(solution)/shard_map/pallas_call | solution.py:265
  174.8 5.5 %shard_map.143.m_ref = bf16[1024,128]{1,0:T(8,128)(2,1)} custom-call(s32[8]{0:T(128)} %stack.184.index_ref, s32[5,8]{1,0:T(8,128)} %stack.166.meta_ref, bf16[1024,512]{1,0:T(8,128)(2,1)} %copy-done.3, bf16[1024,512]{1,0:T(8,128)(2,1)} %collective-permute-done.14.refs_1_, bf16[1024,512]{1,0:T(8,128)(2,1)} %collective-permute-done.16.refs_2_, ...), custom_call_target="tpu_custom_call" | custom-call | flops 536870912 | bytes 5767168 | tf_op jit(solution)/shard_map/pallas_call | solution.py:265
  182.2 7.1 %shard_map.142.q_ref = f32[1024,512]{1,0:T(8,128)} custom-call(s32[8]{0:T(128)} %stack.184.index_ref, s32[5,8]{1,0:T(8,128)} %stack.166.meta_ref, bf16[1024,512]{1,0:T(8,128)(2,1)} %copy-done.3, bf16[1024,512]{1,0:T(8,128)(2,1)} %collective-permute-done.14.refs_1_, ...), custom_call_target="tpu_custom_call", output_to_operand_aliasing={{}: (14, {})} | custom-call | flops 2147483648 | bytes 10485760 | tf_op jit(solution)/shard_map/pallas_call | solution.py:265
  190.1 6.6 %shard_map.148.refs_0_ = bf16[512,640]{1,0:T(8,128)(2,1)} custom-call(s32[5,8]{1,0:T(8,128)} %stack.166.meta_ref, f32[1024,512]{1,0:T(8,128)} %shard_map.142.q_ref, bf16[1024,192]{1,0:T(8,128)(2,1)} %bitcast.73, bf16[8,64,1152]{2,1,0:T(8,128)(2,1)} %copy-done.1, bf16[8,256,512]{2,1,0:T(8,128)(2,1)} %copy-done, bf16[1024,128]{1,0:T(8,128)(2,1)} %shard_map.143.m_ref, ...), custom_call_target="tpu_custom_call" | custom-call | flops 402653184 | bytes 2097152 | tf_op jit(solution)/shard_map/pallas_call | solution.py:376
  199.4 6.6 %shard_map.144.refs_0_ = bf16[512,640]{1,0:T(8,128)(2,1)} custom-call(s32[5,8]{1,0:T(8,128)} %stack.166.meta_ref, f32[1024,512]{1,0:T(8,128)} %shard_map.142.q_ref, bf16[1024,192]{1,0:T(8,128)(2,1)} %bitcast.74, bf16[8,64,1152]{2,1,0:T(8,128)(2,1)} %copy-done.1, bf16[8,256,512]{2,1,0:T(8,128)(2,1)} %copy-done, bf16[1024,128]{1,0:T(8,128)(2,1)} %shard_map.143.m_ref, ...), custom_call_target="tpu_custom_call" | custom-call | flops 402653184 | bytes 2097152 | tf_op jit(solution)/shard_map/pallas_call | solution.py:376
  206.0 3.2 %collective-permute-start.25 = (bf16[512,640]{1,0:T(8,128)(2,1)}, bf16[512,640]{1,0:T(8,128)(2,1)S(1)}, u32[]{:S(2)}, u32[]{:S(2)}) collective-permute-start(bf16[512,640]{1,0:T(8,128)(2,1)} %shard_map.144.refs_0_), channel_id=1, source_target_pairs={{0,12},{4,0},{8,4},{12,8},{1,13},{5,1},{9,5},{13,9},{2,14},{6,2},{... | collective-permute-start | bytes 1966088 | tf_op jit(solution)/shard_map/ppermute | solution.py:37
  209.2 3.4 %collective-permute-done.33.refs_2_ = bf16[512,640]{1,0:T(8,128)(2,1)S(1)} collective-permute-done((bf16[512,640]{1,0:T(8,128)(2,1)}, bf16[512,640]{1,0:T(8,128)(2,1)S(1)}, u32[]{:S(2)}, u32[]{:S(2)}) %collective-permute-start.33) | collective-permute-done | bytes 655392 | tf_op jit(solution)/shard_map/ppermute | solution.py:37
  212.7 3.7 %collective-permute-start.35 = (bf16[512,384]{1,0:T(8,128)(2,1)S(1)}, bf16[512,384]{1,0:T(8,128)(2,1)}, u32[]{:S(2)}, u32[]{:S(2)}) collective-permute-start(bf16[512,384]{1,0:T(8,128)(2,1)S(1)} %slice.39), channel_id=1, source_target_pairs={{0,12},{4,0},{8,4},{12,8},{1,13},{5,1},{9,5},{13,9},{2,14},{6,2},{... | collective-permute-start | bytes 1179656 | tf_op jit(solution)/shard_map/ppermute | solution.py:37
  218.0 8.7 %collective-permute-done.25.refs_2_ = bf16[512,640]{1,0:T(8,128)(2,1)S(1)} collective-permute-done((bf16[512,640]{1,0:T(8,128)(2,1)}, bf16[512,640]{1,0:T(8,128)(2,1)S(1)}, u32[]{:S(2)}, u32[]{:S(2)}) %collective-permute-start.25) | collective-permute-done | bytes 655392 | tf_op jit(solution)/shard_map/ppermute | solution.py:37
  226.7 3.7 %collective-permute-start.27 = (bf16[512,384]{1,0:T(8,128)(2,1)S(1)}, bf16[512,384]{1,0:T(8,128)(2,1)}, u32[]{:S(2)}, u32[]{:S(2)}) collective-permute-start(bf16[512,384]{1,0:T(8,128)(2,1)S(1)} %slice.37), channel_id=1, source_target_pairs={{0,12},{4,0},{8,4},{12,8},{1,13},{5,1},{9,5},{13,9},{2,14},{6,2},{... | collective-permute-start | bytes 1179656 | tf_op jit(solution)/shard_map/ppermute | solution.py:37
  230.5 3.3 %collective-permute-done.34.refs_3_ = bf16[512,256]{1,0:T(8,128)(2,1)S(1)} collective-permute-done((bf16[512,256]{1,0:T(8,128)(2,1)S(1)}, bf16[512,256]{1,0:T(8,128)(2,1)S(1)}, u32[]{:S(2)}, u32[]{:S(2)}) %collective-permute-start.34) | collective-permute-done | bytes 262176 | tf_op jit(solution)/shard_map/ppermute | solution.py:37
  234.6 12.5 %shard_map.149 = (bf16[512,384]{1,0:T(8,128)(2,1)}, bf16[512,256]{1,0:T(8,128)(2,1)}, bf16[512,640]{1,0:T(8,128)(2,1)}, bf16[512,640]{1,0:T(8,128)(2,1)}, f32[512,640]{1,0:T(8,128)}) custom-call(s32[8]{0:T(128)} %stack.175.index_ref, bf16[512,640]{1,0:T(8,128)(2,1)} %shard_map.148.refs_0_, bf16[512,640]{1,0:T(8,128)(2,1)} %copy-done.31, ...), custom_call_target="tpu_custom_call" | custom-call | flops 4294967296 | bytes 10485760 | tf_op jit(solution)/shard_map/pallas_call | solution.py:439
  248.0 12.5 %shard_map.146 = (bf16[512,384]{1,0:T(8,128)(2,1)}, bf16[512,256]{1,0:T(8,128)(2,1)}, bf16[512,640]{1,0:T(8,128)(2,1)}, bf16[512,640]{1,0:T(8,128)(2,1)}, f32[512,640]{1,0:T(8,128)}) custom-call(s32[8]{0:T(128)} %stack.175.index_ref, bf16[512,640]{1,0:T(8,128)(2,1)} %shard_map.144.refs_0_, bf16[512,640]{1,0:T(8,128)(2,1)} %copy-done.30, ...), custom_call_target="tpu_custom_call" | custom-call | flops 4294967296 | bytes 10485760 | tf_op jit(solution)/shard_map/pallas_call | solution.py:439
  265.2 6.5 %collective-permute-done.37.vb_ref = bf16[512,256]{1,0:T(8,128)(2,1)S(1)} collective-permute-done((bf16[512,256]{1,0:T(8,128)(2,1)S(1)}, bf16[512,256]{1,0:T(8,128)(2,1)S(1)}, u32[]{:S(2)}, u32[]{:S(2)}) %collective-permute-start.37) | collective-permute-done | bytes 262176 | tf_op jit(solution)/shard_map/ppermute | solution.py:37
  283.3 9.4 %collective-permute-done.38.refs_4_ = bf16[512,640]{1,0:T(8,128)(2,1)S(1)} collective-permute-done((bf16[512,640]{1,0:T(8,128)(2,1)}, bf16[512,640]{1,0:T(8,128)(2,1)S(1)}, u32[]{:S(2)}, u32[]{:S(2)}) %collective-permute-start.38) | collective-permute-done | bytes 655392 | tf_op jit(solution)/shard_map/ppermute | solution.py:37
  292.7 7.0 %collective-permute-done.30.refs_1_ = bf16[512,640]{1,0:T(8,128)(2,1)S(1)} collective-permute-done((bf16[512,640]{1,0:T(8,128)(2,1)}, bf16[512,640]{1,0:T(8,128)(2,1)S(1)}, u32[]{:S(2)}, u32[]{:S(2)}) %collective-permute-start.30) | collective-permute-done | bytes 655392 | tf_op jit(solution)/shard_map/ppermute | solution.py:37
  300.8 6.2 %shard_map.151 = f32[1024,512]{1,0:T(8,128)} custom-call(s32[5,8]{1,0:T(8,128)} %stack.166.meta_ref, f32[512,640]{1,0:T(8,128)} %get-tuple-element.51.refs_0_, bf16[512,640]{1,0:T(8,128)(2,1)} %copy-done.17, bf16[512,640]{1,0:T(8,128)(2,1)} %copy-done.18, f32[512,640]{1,0:T(8,128)} %get-tuple-element.58.refs_3_, bf16[512,640]{1,0:T(8,128)(2,1)} %copy-done.15, ...), custom_call_target="tpu_custom_call" | custom-call | flops 67108864 | bytes 7340032 | tf_op jit(solution)/shard_map/pallas_call | solution.py:533
  (169 shorter events, 81.5 us)
Async XLA Ops:
  15.5 49.2 %all-to-all-start = ((bf16[8,256,512]{2,1,0:T(8,128)(2,1)}), bf16[8,256,512]{2,1,0:T(8,128)(2,1)S(1)}, u32[]{:S(2)}, u32[]{:S(2)}) async-start(bf16[8,256,512]{2,1,0:T(8,128)(2,1)} %get-tuple-element.44), calls=%async_computation | async-start | bytes 4194304 | tf_op jit(solution)/shard_map/all_to_all | solution.py:586
  21.2 213.3 %all-gather.3.cloned.1.call-start = ((), (), s32[]{:S(2)}) async-start(), calls=%async_computation.4 | async-start | bytes 9437184 | tf_op jit(solution)/shard_map/all_gather | solution.py:596
  26.2 17.6 %collective-permute-start.5 = (bf16[1024,256]{1,0:T(8,128)(2,1)}, bf16[1024,256]{1,0:T(8,128)(2,1)S(1)}, u32[]{:S(2)}, u32[]{:S(2)}) collective-permute-start(bf16[1024,256]{1,0:T(8,128)(2,1)} %get-tuple-element.36.refs_5_), channel_id=1, source_target_pairs={{0,12},{4,0},{8,4},{12,8},{1,13},{5,1},{9,5},{13,9},{2,14},{6,2},{... | collective-permute-start | bytes 1572872 | tf_op jit(solution)/shard_map/ppermute | solution.py:37
  27.8 19.9 %collective-permute-start.10 = (bf16[512,256]{1,0:T(8,128)(2,1)}, bf16[512,256]{1,0:T(8,128)(2,1)S(1)}, u32[]{:S(2)}, u32[]{:S(2)}) collective-permute-start(bf16[512,256]{1,0:T(8,128)(2,1)} %get-tuple-element.39), channel_id=1, source_target_pairs={{0,8},{4,12},{8,0},{12,4},{1,9},{5,13},{9,1},{13,5},{2,10},{6,14},... | collective-permute-start | bytes 786440 | tf_op jit(solution)/shard_map/ppermute | solution.py:37
  68.3 36.7 %collective-permute-start.11 = (bf16[1024,512]{1,0:T(8,128)(2,1)}, bf16[1024,512]{1,0:T(8,128)(2,1)S(1)}, u32[]{:S(2)}, u32[]{:S(2)}) collective-permute-start(bf16[1024,512]{1,0:T(8,128)(2,1)} %get-tuple-element.40.rest_2_.refs_0_.refs_5_), channel_id=1, source_target_pairs={{0,4},{4,8},{8,12},{12,0},{1,5},{5,9},{9,13},{13,1},{2,6},{6,10},{... | collective-permute-start | bytes 3145736 | tf_op jit(solution)/shard_map/ppermute | solution.py:37
  68.6 36.8 %collective-permute-start.13 = (bf16[1024,512]{1,0:T(8,128)(2,1)}, bf16[1024,512]{1,0:T(8,128)(2,1)S(1)}, u32[]{:S(2)}, u32[]{:S(2)}) collective-permute-start(bf16[1024,512]{1,0:T(8,128)(2,1)} %get-tuple-element.41.refs_1_), channel_id=1, source_target_pairs={{0,12},{4,0},{8,4},{12,8},{1,13},{5,1},{9,5},{13,9},{2,14},{6,2},{... | collective-permute-start | bytes 3145736 | tf_op jit(solution)/shard_map/ppermute | solution.py:37
  77.7 29.9 %all-to-all-start.1 = ((f32[16,64,192]{2,1,0:T(8,128)}), f32[16,64,192]{2,1,0:T(8,128)S(1)}, u32[]{:S(2)}, u32[]{:S(2)}) async-start(f32[16,64,192]{2,1,0:T(8,128)} %bitcast.75), calls=%async_computation.1 | async-start | bytes 2097152 | tf_op jit(solution)/shard_map/all_to_all | solution.py:216
  81.5 36.6 %collective-permute-start.15 = (bf16[1024,512]{1,0:T(8,128)(2,1)}, bf16[1024,512]{1,0:T(8,128)(2,1)}, u32[]{:S(2)}, u32[]{:S(2)}) collective-permute-start(bf16[1024,512]{1,0:T(8,128)(2,1)} %get-tuple-element.42.refs_2_), channel_id=1, source_target_pairs={{0,1},{1,2},{2,3},{3,0},{4,5},{5,6},{6,7},{7,4},{8,9},{9,10},{10,1... | collective-permute-start | bytes 3145736 | tf_op jit(solution)/shard_map/ppermute | solution.py:37
  83.4 37.7 %collective-permute-start.17 = (bf16[1024,512]{1,0:T(8,128)(2,1)}, bf16[1024,512]{1,0:T(8,128)(2,1)}, u32[]{:S(2)}, u32[]{:S(2)}) collective-permute-start(bf16[1024,512]{1,0:T(8,128)(2,1)} %get-tuple-element.43.refs_3_), channel_id=1, source_target_pairs={{0,3},{1,0},{2,1},{3,2},{4,7},{5,4},{6,5},{7,6},{8,11},{9,8},{10,9... | collective-permute-start | bytes 3145736 | tf_op jit(solution)/shard_map/ppermute | solution.py:37
  84.8 44.9 %collective-permute-start.19 = (bf16[1024,512]{1,0:T(8,128)(2,1)}, bf16[1024,512]{1,0:T(8,128)(2,1)}, u32[]{:S(2)}, u32[]{:S(2)}) collective-permute-start(bf16[1024,512]{1,0:T(8,128)(2,1)} %get-tuple-element.41.refs_1_), channel_id=1, source_target_pairs={{0,4},{4,8},{8,12},{12,0},{1,5},{5,9},{9,13},{13,1},{2,6},{6,10},{... | collective-permute-start | bytes 3145736 | tf_op jit(solution)/shard_map/ppermute | solution.py:37
  105.0 25.8 %collective-permute-start.20 = (bf16[1024,512]{1,0:T(8,128)(2,1)}, bf16[1024,512]{1,0:T(8,128)(2,1)}, u32[]{:S(2)}, u32[]{:S(2)}) collective-permute-start(bf16[1024,512]{1,0:T(8,128)(2,1)} %get-tuple-element.40.rest_2_.refs_0_.refs_5_), channel_id=1, source_target_pairs={{0,12},{4,0},{8,4},{12,8},{1,13},{5,1},{9,5},{13,9},{2,14},{6,2},{... | collective-permute-start | bytes 3145736 | tf_op jit(solution)/shard_map/ppermute | solution.py:37
  105.4 35.2 %collective-permute-start.21 = (bf16[1024,512]{1,0:T(8,128)(2,1)}, bf16[1024,512]{1,0:T(8,128)(2,1)}, u32[]{:S(2)}, u32[]{:S(2)}) collective-permute-start(bf16[1024,512]{1,0:T(8,128)(2,1)} %get-tuple-element.43.refs_3_), channel_id=1, source_target_pairs={{0,1},{1,2},{2,3},{3,0},{4,5},{5,6},{6,7},{7,4},{8,9},{9,10},{10,1... | collective-permute-start | bytes 3145736 | tf_op jit(solution)/shard_map/ppermute | solution.py:37
  107.7 40.0 %all-to-all-start.3 = ((bf16[8,64,1152]{2,1,0:T(8,128)(2,1)}), bf16[8,64,1152]{2,1,0:T(8,128)(2,1)S(1)}, u32[]{:S(2)}, u32[]{:S(2)}) async-start(bf16[8,64,1152]{2,1,0:T(8,128)(2,1)} %get-tuple-element.48), calls=%async_computation.3 | async-start | bytes 2359296 | tf_op jit(solution)/shard_map/all_to_all | solution.py:612
  118.1 46.9 %collective-permute-start.22 = (bf16[1024,512]{1,0:T(8,128)(2,1)}, bf16[1024,512]{1,0:T(8,128)(2,1)}, u32[]{:S(2)}, u32[]{:S(2)}) collective-permute-start(bf16[1024,512]{1,0:T(8,128)(2,1)} %get-tuple-element.42.refs_2_), channel_id=1, source_target_pairs={{0,3},{1,0},{2,1},{3,2},{4,7},{5,4},{6,5},{7,6},{8,11},{9,8},{10,9... | collective-permute-start | bytes 3145736 | tf_op jit(solution)/shard_map/ppermute | solution.py:37
  121.1 52.6 %collective-permute-start.12 = (bf16[1024,512]{1,0:T(8,128)(2,1)}, bf16[1024,512]{1,0:T(8,128)(2,1)S(1)}, u32[]{:S(2)}, u32[]{:S(2)}) collective-permute-start(bf16[1024,512]{1,0:T(8,128)(2,1)} %copy-done.9), channel_id=1, source_target_pairs={{0,4},{4,8},{8,12},{12,0},{1,5},{5,9},{9,13},{13,1},{2,6},{6,10},{... | collective-permute-start | bytes 3145736 | tf_op jit(solution)/shard_map/ppermute | solution.py:37
  129.7 44.0 %collective-permute-start.14 = (bf16[1024,512]{1,0:T(8,128)(2,1)}, bf16[1024,512]{1,0:T(8,128)(2,1)}, u32[]{:S(2)}, u32[]{:S(2)}) collective-permute-start(bf16[1024,512]{1,0:T(8,128)(2,1)} %copy-done.10), channel_id=1, source_target_pairs={{0,12},{4,0},{8,4},{12,8},{1,13},{5,1},{9,5},{13,9},{2,14},{6,2},{... | collective-permute-start | bytes 3145736 | tf_op jit(solution)/shard_map/ppermute | solution.py:37
  130.8 42.9 %collective-permute-start.16 = (bf16[1024,512]{1,0:T(8,128)(2,1)}, bf16[1024,512]{1,0:T(8,128)(2,1)}, u32[]{:S(2)}, u32[]{:S(2)}) collective-permute-start(bf16[1024,512]{1,0:T(8,128)(2,1)} %collective-permute-done.15.refs_6_), channel_id=1, source_target_pairs={{0,1},{1,2},{2,3},{3,0},{4,5},{5,6},{6,7},{7,4},{8,9},{9,10},{10,1... | collective-permute-start | bytes 3145736 | tf_op jit(solution)/shard_map/ppermute | solution.py:37
  140.6 33.1 %collective-permute-start.18 = (bf16[1024,512]{1,0:T(8,128)(2,1)}, bf16[1024,512]{1,0:T(8,128)(2,1)}, u32[]{:S(2)}, u32[]{:S(2)}) collective-permute-start(bf16[1024,512]{1,0:T(8,128)(2,1)} %collective-permute-done.17.refs_7_), channel_id=1, source_target_pairs={{0,3},{1,0},{2,1},{3,2},{4,7},{5,4},{6,5},{7,6},{8,11},{9,8},{10,9... | collective-permute-start | bytes 3145736 | tf_op jit(solution)/shard_map/ppermute | solution.py:37
  147.6 26.1 %all-to-all-start.2 = ((bf16[16,64,192]{2,1,0:T(8,128)(2,1)}), bf16[16,64,192]{2,1,0:T(8,128)(2,1)S(1)}, u32[]{:S(2)}, u32[]{:S(2)}) async-start(bf16[16,64,192]{2,1,0:T(8,128)(2,1)} %shard_map.139.refs_40_), calls=%async_computation.2 | async-start | bytes 1048576 | tf_op jit(solution)/shard_map/all_to_all | solution.py:642
  199.4 17.0 %collective-permute-start.32 = (bf16[512,640]{1,0:T(8,128)(2,1)}, bf16[512,640]{1,0:T(8,128)(2,1)S(1)}, u32[]{:S(2)}, u32[]{:S(2)}) collective-permute-start(bf16[512,640]{1,0:T(8,128)(2,1)} %shard_map.148.refs_0_), channel_id=1, source_target_pairs={{0,4},{4,8},{8,12},{12,0},{1,5},{5,9},{9,13},{13,1},{2,6},{6,10},{... | collective-permute-start | bytes 1966088 | tf_op jit(solution)/shard_map/ppermute | solution.py:37
  206.0 20.7 %collective-permute-start.25 = (bf16[512,640]{1,0:T(8,128)(2,1)}, bf16[512,640]{1,0:T(8,128)(2,1)S(1)}, u32[]{:S(2)}, u32[]{:S(2)}) collective-permute-start(bf16[512,640]{1,0:T(8,128)(2,1)} %shard_map.144.refs_0_), channel_id=1, source_target_pairs={{0,12},{4,0},{8,4},{12,8},{1,13},{5,1},{9,5},{13,9},{2,14},{6,2},{... | collective-permute-start | bytes 1966088 | tf_op jit(solution)/shard_map/ppermute | solution.py:37
  209.2 21.2 %collective-permute-start.24 = (bf16[512,640]{1,0:T(8,128)(2,1)}, bf16[512,640]{1,0:T(8,128)(2,1)S(1)}, u32[]{:S(2)}, u32[]{:S(2)}) collective-permute-start(bf16[512,640]{1,0:T(8,128)(2,1)} %shard_map.144.refs_0_), channel_id=1, source_target_pairs={{0,4},{4,8},{8,12},{12,0},{1,5},{5,9},{9,13},{13,1},{2,6},{6,10},{... | collective-permute-start | bytes 1966088 | tf_op jit(solution)/shard_map/ppermute | solution.py:37
  212.7 21.8 %collective-permute-start.35 = (bf16[512,384]{1,0:T(8,128)(2,1)S(1)}, bf16[512,384]{1,0:T(8,128)(2,1)}, u32[]{:S(2)}, u32[]{:S(2)}) collective-permute-start(bf16[512,384]{1,0:T(8,128)(2,1)S(1)} %slice.39), channel_id=1, source_target_pairs={{0,12},{4,0},{8,4},{12,8},{1,13},{5,1},{9,5},{13,9},{2,14},{6,2},{... | collective-permute-start | bytes 1179656 | tf_op jit(solution)/shard_map/ppermute | solution.py:37
  217.2 16.6 %collective-permute-start.34 = (bf16[512,256]{1,0:T(8,128)(2,1)S(1)}, bf16[512,256]{1,0:T(8,128)(2,1)S(1)}, u32[]{:S(2)}, u32[]{:S(2)}) collective-permute-start(bf16[512,256]{1,0:T(8,128)(2,1)S(1)} %slice.38), channel_id=1, source_target_pairs={{0,4},{4,8},{8,12},{12,0},{1,5},{5,9},{9,13},{13,1},{2,6},{6,10},{... | collective-permute-start | bytes 786440 | tf_op jit(solution)/shard_map/ppermute | solution.py:37
  226.7 21.2 %collective-permute-start.27 = (bf16[512,384]{1,0:T(8,128)(2,1)S(1)}, bf16[512,384]{1,0:T(8,128)(2,1)}, u32[]{:S(2)}, u32[]{:S(2)}) collective-permute-start(bf16[512,384]{1,0:T(8,128)(2,1)S(1)} %slice.37), channel_id=1, source_target_pairs={{0,12},{4,0},{8,4},{12,8},{1,13},{5,1},{9,5},{13,9},{2,14},{6,2},{... | collective-permute-start | bytes 1179656 | tf_op jit(solution)/shard_map/ppermute | solution.py:37
  230.4 17.6 %collective-permute-start.26 = (bf16[512,256]{1,0:T(8,128)(2,1)S(1)}, bf16[512,256]{1,0:T(8,128)(2,1)}, u32[]{:S(2)}, u32[]{:S(2)}) collective-permute-start(bf16[512,256]{1,0:T(8,128)(2,1)S(1)} %slice.36), channel_id=1, source_target_pairs={{0,4},{4,8},{8,12},{12,0},{1,5},{5,9},{9,13},{13,1},{2,6},{6,10},{... | collective-permute-start | bytes 786440 | tf_op jit(solution)/shard_map/ppermute | solution.py:37
  247.1 24.6 %collective-permute-start.36 = (bf16[512,384]{1,0:T(8,128)(2,1)}, bf16[512,384]{1,0:T(8,128)(2,1)S(1)}, u32[]{:S(2)}, u32[]{:S(2)}) collective-permute-start(bf16[512,384]{1,0:T(8,128)(2,1)} %get-tuple-element.60), channel_id=1, source_target_pairs={{0,1},{1,2},{2,3},{3,0},{4,5},{5,6},{6,7},{7,4},{8,9},{9,10},{10,1... | collective-permute-start | bytes 1179656 | tf_op jit(solution)/shard_map/ppermute | solution.py:37
  260.5 16.9 %collective-permute-start.28 = (bf16[512,384]{1,0:T(8,128)(2,1)}, bf16[512,384]{1,0:T(8,128)(2,1)S(1)}, u32[]{:S(2)}, u32[]{:S(2)}) collective-permute-start(bf16[512,384]{1,0:T(8,128)(2,1)} %get-tuple-element.53), channel_id=1, source_target_pairs={{0,1},{1,2},{2,3},{3,0},{4,5},{5,6},{6,7},{7,4},{8,9},{9,10},{10,1... | collective-permute-start | bytes 1179656 | tf_op jit(solution)/shard_map/ppermute | solution.py:37
  275.2 17.5 %collective-permute-start.38 = (bf16[512,640]{1,0:T(8,128)(2,1)}, bf16[512,640]{1,0:T(8,128)(2,1)S(1)}, u32[]{:S(2)}, u32[]{:S(2)}) collective-permute-start(bf16[512,640]{1,0:T(8,128)(2,1)} %get-tuple-element.63), channel_id=1, source_target_pairs={{0,3},{1,0},{2,1},{3,2},{4,7},{5,4},{6,5},{7,6},{8,11},{9,8},{10,9... | collective-permute-start | bytes 1966088 | tf_op jit(solution)/shard_map/ppermute | solution.py:37
  276.5 16.2 %collective-permute-start.39 = (bf16[512,640]{1,0:T(8,128)(2,1)}, bf16[512,640]{1,0:T(8,128)(2,1)S(1)}, u32[]{:S(2)}, u32[]{:S(2)}) collective-permute-start(bf16[512,640]{1,0:T(8,128)(2,1)} %get-tuple-element.64), channel_id=1, source_target_pairs={{0,1},{1,2},{2,3},{3,0},{4,5},{5,6},{6,7},{7,4},{8,9},{9,10},{10,1... | collective-permute-start | bytes 1966088 | tf_op jit(solution)/shard_map/ppermute | solution.py:37
  280.9 18.8 %collective-permute-start.30 = (bf16[512,640]{1,0:T(8,128)(2,1)}, bf16[512,640]{1,0:T(8,128)(2,1)S(1)}, u32[]{:S(2)}, u32[]{:S(2)}) collective-permute-start(bf16[512,640]{1,0:T(8,128)(2,1)} %get-tuple-element.56), channel_id=1, source_target_pairs={{0,3},{1,0},{2,1},{3,2},{4,7},{5,4},{6,5},{7,6},{8,11},{9,8},{10,9... | collective-permute-start | bytes 1966088 | tf_op jit(solution)/shard_map/ppermute | solution.py:37
  283.3 16.5 %collective-permute-start.31 = (bf16[512,640]{1,0:T(8,128)(2,1)}, bf16[512,640]{1,0:T(8,128)(2,1)S(1)}, u32[]{:S(2)}, u32[]{:S(2)}) collective-permute-start(bf16[512,640]{1,0:T(8,128)(2,1)} %get-tuple-element.57), channel_id=1, source_target_pairs={{0,1},{1,2},{2,3},{3,0},{4,5},{5,6},{6,7},{7,4},{8,9},{9,10},{10,1... | collective-permute-start | bytes 1966088 | tf_op jit(solution)/shard_map/ppermute | solution.py:37
  (49 other events, 470.3 us)
Sparse Core Ops, SparseCore 0:
  68.4 49.7 all-gather.2

commit v8 on v7

--- a/solution.py
+++ b/solution.py
@@ -54,18 +54,16 @@
     return [index, (index + SIDE - 1) % SIDE, (index + 1) % SIDE, (index + 2) % SIDE]
 
 
-def pick_local(pick, down_qkv, up_q, up_kv, down_o, up_o, x, wo, unit):
-    tokens, local = x.shape
+def pick_local(pick, down_qkv, up_q, up_kv, down_o, up_o, wo, unit, after):
     groups = pick.shape[0] - SIDE
     rank3, depth = down_qkv.shape[1:]
     rank, wide = up_q.shape[1:]
     narrow = up_kv.shape[2]
     rows = wo.shape[0] // groups
 
-    def body(pick_ref, dq, uq, ukv, do, uo, x_ref, *refs):
-        w_refs, (down, up, left, right), w_outs = refs[:SIDE], refs[SIDE : SIDE + 4], refs[SIDE + 4 :]
-        left[...] = x_ref[:, : local // 2]
-        right[...] = x_ref[:, local // 2 :]
+    def body(pick_ref, dq, uq, ukv, do, uo, *refs):
+        w_refs, w_outs = refs[:SIDE], refs[-SIDE:]
+        down, up = refs[-SIDE - 2 : -SIDE]
         down[0, :rank3, :] = dq[0]
         down[0, rank3:, :] = do[0]
         up[0, :, :wide] = uq[0]
@@ -82,29 +80,27 @@
 
     down_shape = (groups, rank3 + rank, depth)
     up_shape = (groups, rank, 2 * wide + narrow)
-    half = (tokens, local // 2)
     share = (wo.shape[0], unit)
     return pl.pallas_call(
         body,
         out_shape=tuple(
             jax.ShapeDtypeStruct(s, bf16)
-            for s in (down_shape, up_shape, half, half, share, share, share, share)
+            for s in (down_shape, up_shape, share, share, share, share)
         ),
         grid_spec=pltpu.PrefetchScalarGridSpec(
             num_scalar_prefetch=1,
             grid=(groups,),
             in_specs=[chosen(a) for a in (down_qkv, up_q, up_kv, down_o, up_o)]
-            + [pl.BlockSpec((tokens // groups, local), lambda i, p: (i, 0))]
-            + [columns(k) for k in range(SIDE)],
+            + [columns(k) for k in range(SIDE)]
+            + passive(after),
             out_specs=[
                 pl.BlockSpec((1,) + s[1:], lambda i, p: (i, 0, 0)) for s in (down_shape, up_shape)
             ]
-            + [pl.BlockSpec((tokens // groups, local // 2), lambda i, p: (i, 0))] * 2
             + [pl.BlockSpec((rows, unit), lambda i, p: (i, 0))] * SIDE,
         ),
         compiler_params=params(),
         cost_estimate=cost(0, 2 * 2 * (math.prod(down_shape) + math.prod(up_shape))),
-    )(pick, down_qkv, up_q, up_kv, down_o, up_o, x, wo, wo, wo, wo)
+    )(pick, down_qkv, up_q, up_kv, down_o, up_o, wo, wo, wo, wo, *after)
 
 
 def stack_rows(blocks, after):
@@ -406,8 +402,8 @@
     whole = 2 * width + HEAD
 
     def body(index_ref, *refs):
-        own, behind, ahead, far_low, far_high, w_ref = refs[:6]
-        out_far_low, out_far_high, out_ahead, out_behind, out_mine, x_all = refs[6:]
+        own, behind, ahead, far_low, far_high, w_low, w_high = refs[:7]
+        out_far_low, out_far_high, out_ahead, out_behind, out_mine, x_all = refs[7:]
         step = pl.program_id(0)
 
         @pl.when(step == 0)
@@ -425,15 +421,21 @@
             for out in (out_far_low, out_ahead, out_behind, out_mine):
                 out[:, width : width + HEAD] = rank.astype(out.dtype)
 
-        total = jnp.dot(x_all[...], w_ref[0], preferred_element_type=f32)
+        first = jnp.dot(x_all[...], w_low[0], preferred_element_type=f32)
+        second = jnp.dot(x_all[...], w_high[0], preferred_element_type=f32)
         low, high = slice(0, width), slice(width + HEAD, whole)
-        targets = [(out_far_low, low), (out_far_high, low)]
-        targets += [(out, at) for out in (out_ahead, out_behind, out_mine) for at in (low, high)]
-        for k, (out, at) in enumerate(targets):
-
-            @pl.when(step == k)
+
+        @pl.when(step == 0)
+        def _():
+            out_far_low[:, low] = first.astype(bf16)
+            out_far_high[...] = second.astype(bf16)
+
+        for k, out in enumerate((out_ahead, out_behind, out_mine)):
+
+            @pl.when(step == k + 1)
             def _():
-                out[:, at] = total.astype(out.dtype)
+                out[:, low] = first.astype(out.dtype)
+                out[:, high] = second.astype(out.dtype)
 
     shapes = [(width + HEAD, bf16), (width, bf16), (whole, bf16), (whole, bf16), (whole, f32)]
     return pl.pallas_call(
@@ -441,9 +443,10 @@
         out_shape=tuple(jax.ShapeDtypeStruct((tokens, w), d) for w, d in shapes),
         grid_spec=pltpu.PrefetchScalarGridSpec(
             num_scalar_prefetch=1,
-            grid=(count,),
+            grid=(count // 2,),
             in_specs=[pl.BlockSpec(p.shape, lambda j, d: (0, 0)) for p in pieces]
-            + [pl.BlockSpec((1, depth, width), lambda j, d: (d[j], 0, 0))],
+            + [pl.BlockSpec((1, depth, width), lambda j, d: (d[2 * j], 0, 0))]
+            + [pl.BlockSpec((1, depth, width), lambda j, d: (d[2 * j + 1], 0, 0))],
             out_specs=[pl.BlockSpec((tokens, w), lambda j, d: (0, 0)) for w, _ in shapes],
             scratch_shapes=[pltpu.VMEM((tokens, depth), bf16)],
         ),
@@ -451,7 +454,7 @@
         cost_estimate=cost(
             2 * tokens * depth * count * width, 2 * depth * (tokens + count * width)
         ),
-    )(jnp.stack(shards).astype(i32), *pieces, weights)
+    )(jnp.stack(shards).astype(i32), *pieces, weights, weights)
 
 
 def add_far(ahead, via_behind, behind, via_ahead):
@@ -576,26 +579,31 @@
 
     cosine, sine = rotation_tables()
 
+    half = local // 2
+    ys, xs = ring_order(y), ring_order(xi)
+    first_a = ring_gather(x[:, :half], "x", half // 2)
+    first_b = ring_gather(x[:, half:], "y", half // 2)
+    low_a, high_a, low_b, high_b = join(
+        [first_a[:2], first_a[2:], first_b[:2], first_b[2:]], []
+    )
+    far_a, next_a = second_gather(low_a, high_a, "y")
+    far_b, next_b = second_gather(low_b, high_b, "x")
+
     stores = (jnp.swapaxes(down_qkv, 1, 2), up_q, up_kv, jnp.swapaxes(down_o, 1, 2), up_o)
-    ys, xs = ring_order(y), ring_order(xi)
     unit = wo.shape[1] // (SIDE * SIDE * 2)
     wo_cols = jnp.stack(ys) * (2 * SIDE) + group
-    down_out, up_out, x_a, x_b, *sent = pick_local(
-        jnp.concatenate([pick, wo_cols.astype(i32)]), *stores, x, wo, unit
+    down_out, up_out, *sent = pick_local(
+        jnp.concatenate([pick, wo_cols.astype(i32)]),
+        *stores,
+        wo,
+        unit,
+        first_a[1:3] + first_b[1:3],
     )
     down = lax.all_to_all(down_out, ADAPTER_AXES, 0, 0, tiled=True)
 
-    first_a = ring_gather(x_a, "x", x_a.shape[1] // 2)
-    first_b = ring_gather(x_b, "y", x_b.shape[1] // 2)
-
     got = [sent[0], shift(sent[2], "y", 1), shift(sent[1], "y", -1), shift(sent[3], "y", 2)]
-    low_a, high_a, low_b, high_b = join(
-        [first_a[:2], first_a[2:], first_b[:2], first_b[2:]], got[1:]
-    )
-    wo_mine = stack_rows(got, [down, low_a])
+    wo_mine = stack_rows(got, [down, *far_a, *far_b])
     wo_all = lax.all_gather(wo_mine, ADAPTER_AXES, axis=0)
-    far_a, next_a = second_gather(low_a, high_a, "y")
-    far_b, next_b = second_gather(low_b, high_b, "x")
 
     def rows_a(k, cols):
         return [(ys[k] * SIDE + xs[j]) * 2 for j in cols]
@@ -608,27 +616,32 @@
 
     every = range(SIDE)
     low, high = (0, 1), (2, 3)
-    pieces = scatter_rows(rank_partial(meta, x, down, 3 * rank, [low_a]))
+    total = project(
+        (index_of(rows_a(0, every) + rows_b(0, every)), meta),
+        None,
+        [low_a, high_a, low_b, high_b],
+        [wq, wkv],
+        512,
+    )
+
+    pieces = scatter_rows(
+        rank_partial(meta, x, down, 3 * rank, [*far_a, *far_b, total[1]])
+    )
     up = lax.all_to_all(up_out, ADAPTER_AXES, 0, 0, tiled=True)
-
-    copies = share_sum(pieces, [])
+    total = project(
+        (
+            index_of(rows_a(1, low) + rows_a(2, high) + rows_b(1, low) + rows_b(2, high)),
+            meta,
+        ),
+        total,
+        [*far_a, *far_b],
+        [wq, wkv],
+        512,
+    )
+    copies = share_sum(pieces, [total[1]])
 
     a_low, a_high = shift(far_a[0], "y", 1), shift(far_a[1], "y", -1)
     b_low, b_high = shift(far_b[0], "x", 1), shift(far_b[1], "x", -1)
-    total = project(
-        (
-            index_of(
-                rows_a(0, every) + rows_b(0, every)
-                + rows_a(1, low) + rows_a(2, high) + rows_b(1, low) + rows_b(2, high)
-            ),
-            meta,
-        ),
-        None,
-        [low_a, high_a, low_b, high_b, *far_a, *far_b],
-        [wq, wkv],
-        512,
-        after=[copies],
-    )
     total = project(
         (
             index_of(rows_a(1, high) + rows_a(2, low) + rows_b(1, high) + rows_b(2, low)),

time: 316 us -> 353 us (1.12)
  waiting for transfers between devices: 103 us -> 142 us
  local copies, waits for them, and re-layouts: 11 us -> 18.4 us
  starting transfers between devices: 78.4 us -> 71.8 us
    ppermute x39, waiting for transfers between devices: 101 us -> 123 us  [shift(): lax.ppermute(block, axis, [(i, (i + step) % SIDE) for i in range(SIDE)])]
    all_to_all x1, waiting for transfers between devices: 1.96 us -> 13.5 us  [scatter_rows(): lax.all_to_all(partial.reshape(ways, rows // ways, rank), TENSOR_AXES, 0,...]
    all_to_all x1, waiting for transfers between devices: 0.01 us -> 4.92 us  [on_device(): lax.all_to_all(copies, TENSOR_AXES, 0, 0, tiled=True)]
    ppermute x39, starting transfers between devices: 57.7 us -> 53.3 us  [shift(): lax.ppermute(block, axis, [(i, (i + step) % SIDE) for i in range(SIDE)])]
    pallas_call x2, Pallas kernels: 25.1 us -> 21.2 us  [output_partial(): pl.pallas_call(body, out_shape=tuple((jax.ShapeDtypeStruct((tokens, w), d...]
    pallas_call x4 -> x5, Pallas kernels: 34.1 us -> 37.7 us  [project(): pl.pallas_call(body, out_shape=tuple((jax.ShapeDtypeStruct((tokens, w), d...]
    unnamed x72 -> x86, local copies, waits for them, and re-layouts: 7.44 us -> 9.55 us
  transfers between devices with their start and end apart: 45 -> 45, of which waited for: 19 -> 22; matrix products, arithmetic and copies ran while one was open for 1% -> 2% of each run, Pallas kernels for 29% -> 25%
where the time goes in v8:
time: 353 us; the launch traced here: 352 us
  waiting for transfers between devices  142 us (40%)
  Pallas kernels  105 us (30%)
  starting transfers between devices  71.8 us (20%)
  local copies, waits for them, and re-layouts  18.4 us (5%)
  between operations  13.9 us (4%)
    ppermute x39, waiting for transfers between devices, shift(): lax.ppermute(block, axis, [(i, (i + step) % SIDE) for i in range(SIDE)])  123 us
    ppermute x39, starting transfers between devices, shift(): lax.ppermute(block, axis, [(i, (i + step) % SIDE) for i in range(SIDE)])  53.3 us
    pallas_call x5, Pallas kernels, project(): pl.pallas_call(body, out_shape=tuple((jax.ShapeDtypeStruct((tokens, w), d...  37.7 us
    pallas_call x2, Pallas kernels, output_partial(): pl.pallas_call(body, out_shape=tuple((jax.ShapeDtypeStruct((tokens, w), d...  21.2 us
    all_to_all x1, waiting for transfers between devices, scatter_rows(): lax.all_to_all(partial.reshape(ways, rows // ways, rank), TENSOR_AXES, 0,...  13.5 us
    pallas_call x2, Pallas kernels, attention(): pl.pallas_call(body, out_shape=jax.ShapeDtypeStruct((count * BLOCK, wide...  13.2 us
    unnamed x86, local copies, waits for them, and re-layouts  9.55 us
    pallas_call x1, Pallas kernels, pick_local(): pl.pallas_call(body, out_shape=tuple((jax.ShapeDtypeStruct(s, bf16) for s...  7.08 us
  transfers between devices with their start and end apart: 45, of which 22 were waited for; matrix products, arithmetic and copies ran while one was open for 2% of the time, Pallas kernels for 25%

profile of v8, /device:TPU:0, one launch (start us, length us, event | category | flops | bytes accessed | tf_op | source)
XLA Modules:
  0.0 351.7 jit_solution(6225475588396112805)
XLA Ops:
  15.1 7.6 %collective-permute-done.refs_1_.refs_4_ = bf16[1024,256]{1,0:T(8,128)(2,1)S(1)} collective-permute-done((bf16[1024,256]{1,0:T(8,128)(2,1)S(1)}, bf16[1024,256]{1,0:T(8,128)(2,1)S(1)}, u32[]{:S(2)}, u32[]{:S(2)}) %collective-permute-start) | collective-permute-done | bytes 524320 | tf_op jit(solution)/shard_map/ppermute | solution.py:37
  26.6 7.1 %shard_map.141 = (bf16[8,256,512]{2,1,0:T(8,128)(2,1)}, bf16[8,64,1152]{2,1,0:T(8,128)(2,1)}, bf16[512,256]{1,0:T(8,128)(2,1)}, bf16[512,256]{1,0:T(8,128)(2,1)}...) custom-call(s32[12]{0:T(128)} %pad_add_fusion.pick_ref, bf16[8,192,512]{2,1,0:T(8,128)(2,1)} %bitcast.77, ...), custom_call_target="tpu_custom_call" | custom-call | bytes 6553600 | tf_op jit(solution)/shard_map/pallas_call | solution.py:84
  33.7 5.7 %all-to-all-start = ((bf16[8,256,512]{2,1,0:T(8,128)(2,1)}), bf16[8,256,512]{2,1,0:T(8,128)(2,1)S(1)}, u32[]{:S(2)}, u32[]{:S(2)}) async-start(bf16[8,256,512]{2,1,0:T(8,128)(2,1)} %get-tuple-element.44), calls=%async_computation | async-start | bytes 4194304 | tf_op jit(solution)/shard_map/all_to_all | solution.py:602
  49.4 3.8 %collective-permute-done.6.refs_8_ = bf16[1024,128]{1,0:T(8,128)(2,1)S(1)} collective-permute-done((bf16[1024,128]{1,0:T(8,128)(2,1)S(1)}, bf16[1024,128]{1,0:T(8,128)(2,1)S(1)}, u32[]{:S(2)}, u32[]{:S(2)}) %collective-permute-start.6) | collective-permute-done | bytes 262176 | tf_op jit(solution)/shard_map/ppermute | solution.py:37
  54.9 4.8 %shard_map.136 = (bf16[1024,512]{1,0:T(8,128)(2,1)}, bf16[1024,512]{1,0:T(8,128)(2,1)}, bf16[1024,512]{1,0:T(8,128)(2,1)}, bf16[1024,512]{1,0:T(8,128)(2,1)}) custom-call(bf16[1024,256]{1,0:T(8,128)(2,1)} %copy-done.15, bf16[1024,256]{1,0:T(8,128)(2,1)} %copy-done.8, bf16[1024,256]{1,0:T(8,128)(2,1)} %copy-done.10, bf16[1024,128]{1,0:T(8,128)(2,1)} %copy-done.27, ...), custom_call_target="tpu_custom_call" | custom-call | bytes 8388608 | tf_op jit(solution)/shard_map/pallas_call | solution.py:175
  66.4 29.7 %collective-permute-done.25.refs_1_ = bf16[512,256]{1,0:T(8,128)(2,1)S(1)} collective-permute-done((bf16[512,256]{1,0:T(8,128)(2,1)S(1)}, bf16[512,256]{1,0:T(8,128)(2,1)S(1)}, u32[]{:S(2)}, u32[]{:S(2)}) %collective-permute-start.25) | collective-permute-done | bytes 262176 | tf_op jit(solution)/shard_map/ppermute | solution.py:37
  96.1 7.5 %collective-permute-done.26.refs_2_ = bf16[512,256]{1,0:T(8,128)(2,1)S(1)} collective-permute-done((bf16[512,256]{1,0:T(8,128)(2,1)S(1)}, bf16[512,256]{1,0:T(8,128)(2,1)S(1)}, u32[]{:S(2)}, u32[]{:S(2)}) %collective-permute-start.26) | collective-permute-done | bytes 262176 | tf_op jit(solution)/shard_map/ppermute | solution.py:37
  103.5 7.9 %collective-permute-done.27.refs_3_ = bf16[512,256]{1,0:T(8,128)(2,1)S(1)} collective-permute-done((bf16[512,256]{1,0:T(8,128)(2,1)S(1)}, bf16[512,256]{1,0:T(8,128)(2,1)S(1)}, u32[]{:S(2)}, u32[]{:S(2)}) %collective-permute-start.27) | collective-permute-done | bytes 262176 | tf_op jit(solution)/shard_map/ppermute | solution.py:37
  119.0 8.0 %shard_map.137 = (f32[1024,512]{1,0:T(8,128)}, f32[1024,128]{1,0:T(8,128)}) custom-call(s32[8]{0:T(128)} %stack.214.index_ref, s32[5,8]{1,0:T(8,128)} %stack.169.meta_ref, bf16[1024,512]{1,0:T(8,128)(2,1)} %get-tuple-element.35.refs_0_, bf16[1024,512]{1,0:T(8,128)(2,1)} %get-tuple-element.36.refs_1_, bf16[1024,512]{1,0:T(8,128)(2,1)} %get-tuple-element.37.refs_2_, ...), custom_call_target="tpu_custom_call" | custom-call | flops 2684354560 | bytes 12058624 | tf_op jit(solution)/shard_map/pallas_call | solution.py:261
  127.0 4.9 %shard_map.142 = f32[1024,192]{1,0:T(8,128)} custom-call(s32[5,8]{1,0:T(8,128)} %stack.169.meta_ref, bf16[1024,512]{1,0:T(8,128)(2,1)} %x_ref.1, bf16[8,256,512]{2,1,0:T(8,128)(2,1)} %copy-done, bf16[8,256,512]{2,1,0:T(8,128)(2,1)} %copy-done, bf16[1024,512]{1,0:T(8,128)(2,1)} %collective-permute-done.8.refs_0_.rest_2_.refs_5_, bf16[1024,512]{1,0:T(8,128)(2,1)} %copy-done.2, ...), custom_call_target="tpu_custom_call" | custom-call | flops 201326592 | bytes 2621440 | tf_op jit(solution)/shard_map/pallas_call | solution.py:143
  131.9 3.8 %all-to-all-start.1 = ((f32[16,64,192]{2,1,0:T(8,128)}), f32[16,64,192]{2,1,0:T(8,128)S(1)}, u32[]{:S(2)}, u32[]{:S(2)}) async-start(f32[16,64,192]{2,1,0:T(8,128)} %bitcast.76), calls=%async_computation.1 | async-start | bytes 2097152 | tf_op jit(solution)/shard_map/all_to_all | solution.py:212
  140.8 13.5 %all-to-all-done.1.p_ref = f32[16,64,192]{2,1,0:T(8,128)S(1)} async-done(((f32[16,64,192]{2,1,0:T(8,128)}), f32[16,64,192]{2,1,0:T(8,128)S(1)}, u32[]{:S(2)}, u32[]{:S(2)}) %all-to-all-start.1) | async-done | bytes 786464 | tf_op jit(solution)/shard_map/all_to_all | solution.py:212
  155.3 4.4 %all-to-all-start.3 = ((bf16[8,64,1152]{2,1,0:T(8,128)(2,1)}), bf16[8,64,1152]{2,1,0:T(8,128)(2,1)S(1)}, u32[]{:S(2)}, u32[]{:S(2)}) async-start(bf16[8,64,1152]{2,1,0:T(8,128)(2,1)} %get-tuple-element.45), calls=%async_computation.3 | async-start | bytes 2359296 | tf_op jit(solution)/shard_map/all_to_all | solution.py:630
  160.6 6.8 %collective-permute-done.16.refs_0_ = bf16[1024,512]{1,0:T(8,128)(2,1)} collective-permute-done((bf16[1024,512]{1,0:T(8,128)(2,1)}, bf16[1024,512]{1,0:T(8,128)(2,1)}, u32[]{:S(2)}, u32[]{:S(2)}) %collective-permute-start.16) | collective-permute-done | bytes 1048608 | tf_op jit(solution)/shard_map/ppermute | solution.py:37
  173.0 8.6 %shard_map.138 = (f32[1024,512]{1,0:T(8,128)}, f32[1024,128]{1,0:T(8,128)}) custom-call(s32[8]{0:T(128)} %stack.205.index_ref, s32[5,8]{1,0:T(8,128)} %stack.169.meta_ref, bf16[1024,512]{1,0:T(8,128)(2,1)} %collective-permute-done.8.refs_0_.rest_2_.refs_5_, bf16[1024,512]{1,0:T(8,128)(2,1)} %copy-done.2, ...), custom_call_target="tpu_custom_call", output_to_operand_aliasing={{0}: (22, {}), {1}: (23, {})} | custom-call | flops 2684354560 | bytes 12058624 | tf_op jit(solution)/shard_map/pallas_call | solution.py:261
  183.7 4.2 %all-to-all-start.2 = ((bf16[16,64,192]{2,1,0:T(8,128)(2,1)}), bf16[16,64,192]{2,1,0:T(8,128)(2,1)}, u32[]{:S(2)}, u32[]{:S(2)}) async-start(bf16[16,64,192]{2,1,0:T(8,128)(2,1)} %shard_map.143), calls=%async_computation.2 | async-start | bytes 1048576 | tf_op jit(solution)/shard_map/all_to_all | solution.py:655
  189.2 8.6 %shard_map.139 = (f32[1024,512]{1,0:T(8,128)}, f32[1024,128]{1,0:T(8,128)}) custom-call(s32[8]{0:T(128)} %stack.196.index_ref, s32[5,8]{1,0:T(8,128)} %stack.169.meta_ref, bf16[1024,512]{1,0:T(8,128)(2,1)} %collective-permute-done.16.refs_0_, bf16[1024,512]{1,0:T(8,128)(2,1)} %collective-permute-done.17.refs_1_, ...), custom_call_target="tpu_custom_call", output_to_operand_aliasing={{0}: (22, {}), {1}: (23, {})} | custom-call | flops 2684354560 | bytes 12058624 | tf_op jit(solution)/shard_map/pallas_call | solution.py:261
  197.8 10.6 %collective-permute-done.15.refs_3_ = bf16[1024,512]{1,0:T(8,128)(2,1)} collective-permute-done((bf16[1024,512]{1,0:T(8,128)(2,1)}, bf16[1024,512]{1,0:T(8,128)(2,1)}, u32[]{:S(2)}, u32[]{:S(2)}) %collective-permute-start.15) | collective-permute-done | bytes 1048608 | tf_op jit(solution)/shard_map/ppermute | solution.py:37
  208.5 4.9 %all-to-all-done.2 = bf16[16,64,192]{2,1,0:T(8,128)(2,1)} async-done(((bf16[16,64,192]{2,1,0:T(8,128)(2,1)}), bf16[16,64,192]{2,1,0:T(8,128)(2,1)}, u32[]{:S(2)}, u32[]{:S(2)}) %all-to-all-start.2) | async-done | bytes 393248 | tf_op jit(solution)/shard_map/all_to_all | solution.py:655
  213.4 5.5 %shard_map.144.m_ref = bf16[1024,128]{1,0:T(8,128)(2,1)} custom-call(s32[8]{0:T(128)} %stack.187.index_ref, s32[5,8]{1,0:T(8,128)} %stack.169.meta_ref, bf16[1024,512]{1,0:T(8,128)(2,1)} %collective-permute-done.9.refs_0_, bf16[1024,512]{1,0:T(8,128)(2,1)} %collective-permute-done.11.refs_1_, bf16[1024,512]{1,0:T(8,128)(2,1)} %collective-permute-done.13.refs_2_, ...), custom_call_target="tpu_custom_call" | custom-call | flops 536870912 | bytes 5767168 | tf_op jit(solution)/shard_map/pallas_call | solution.py:261
  219.2 7.1 %shard_map.140.q_ref = f32[1024,512]{1,0:T(8,128)} custom-call(s32[8]{0:T(128)} %stack.187.index_ref, s32[5,8]{1,0:T(8,128)} %stack.169.meta_ref, bf16[1024,512]{1,0:T(8,128)(2,1)} %collective-permute-done.9.refs_0_, bf16[1024,512]{1,0:T(8,128)(2,1)} %collective-permute-done.11.refs_1_, ...), custom_call_target="tpu_custom_call", output_to_operand_aliasing={{}: (14, {})} | custom-call | flops 2147483648 | bytes 10485760 | tf_op jit(solution)/shard_map/pallas_call | solution.py:261
  227.2 6.6 %shard_map.149.refs_0_ = bf16[512,640]{1,0:T(8,128)(2,1)} custom-call(s32[5,8]{1,0:T(8,128)} %stack.169.meta_ref, f32[1024,512]{1,0:T(8,128)} %shard_map.140.q_ref, bf16[1024,192]{1,0:T(8,128)(2,1)} %bitcast.55.refs_13_.s_ref, bf16[8,64,1152]{2,1,0:T(8,128)(2,1)} %copy-done.1, bf16[8,256,512]{2,1,0:T(8,128)(2,1)} %copy-done, ...), custom_call_target="tpu_custom_call" | custom-call | flops 402653184 | bytes 2097152 | tf_op jit(solution)/shard_map/pallas_call | solution.py:372
  235.8 6.6 %shard_map.145.refs_0_ = bf16[512,640]{1,0:T(8,128)(2,1)} custom-call(s32[5,8]{1,0:T(8,128)} %stack.169.meta_ref, f32[1024,512]{1,0:T(8,128)} %shard_map.140.q_ref, bf16[1024,192]{1,0:T(8,128)(2,1)} %bitcast.55.refs_13_.s_ref, bf16[8,64,1152]{2,1,0:T(8,128)(2,1)} %copy-done.1, bf16[8,256,512]{2,1,0:T(8,128)(2,1)} %copy-done, ...), custom_call_target="tpu_custom_call" | custom-call | flops 402653184 | bytes 2097152 | tf_op jit(solution)/shard_map/pallas_call | solution.py:372
  245.6 6.1 %collective-permute-done.33.refs_2_ = bf16[512,640]{1,0:T(8,128)(2,1)S(1)} collective-permute-done((bf16[512,640]{1,0:T(8,128)(2,1)}, bf16[512,640]{1,0:T(8,128)(2,1)S(1)}, u32[]{:S(2)}, u32[]{:S(2)}) %collective-permute-start.33) | collective-permute-done | bytes 655392 | tf_op jit(solution)/shard_map/ppermute | solution.py:37
  256.4 9.3 %collective-permute-done.22.refs_2_ = bf16[512,640]{1,0:T(8,128)(2,1)S(1)} collective-permute-done((bf16[512,640]{1,0:T(8,128)(2,1)}, bf16[512,640]{1,0:T(8,128)(2,1)S(1)}, u32[]{:S(2)}, u32[]{:S(2)}) %collective-permute-start.22) | collective-permute-done | bytes 655392 | tf_op jit(solution)/shard_map/ppermute | solution.py:37
  269.8 4.8 %collective-permute-done.34.refs_3_ = bf16[512,256]{1,0:T(8,128)(2,1)} collective-permute-done((bf16[512,256]{1,0:T(8,128)(2,1)}, bf16[512,256]{1,0:T(8,128)(2,1)}, u32[]{:S(2)}, u32[]{:S(2)}) %collective-permute-start.34) | collective-permute-done | bytes 262176 | tf_op jit(solution)/shard_map/ppermute | solution.py:37
  274.6 10.6 %shard_map.150 = (bf16[512,384]{1,0:T(8,128)(2,1)}, bf16[512,256]{1,0:T(8,128)(2,1)}, bf16[512,640]{1,0:T(8,128)(2,1)}, bf16[512,640]{1,0:T(8,128)(2,1)}, f32[512,640]{1,0:T(8,128)}) custom-call(s32[8]{0:T(128)} %stack.178.index_ref, bf16[512,640]{1,0:T(8,128)(2,1)} %shard_map.149.refs_0_, bf16[512,640]{1,0:T(8,128)(2,1)} %copy-done.19, ...), custom_call_target="tpu_custom_call" | custom-call | flops 4294967296 | bytes 10485760 | tf_op jit(solution)/shard_map/pallas_call | solution.py:441
  287.2 10.6 %shard_map.147 = (bf16[512,384]{1,0:T(8,128)(2,1)}, bf16[512,256]{1,0:T(8,128)(2,1)}, bf16[512,640]{1,0:T(8,128)(2,1)}, bf16[512,640]{1,0:T(8,128)(2,1)}, f32[512,640]{1,0:T(8,128)}) custom-call(s32[8]{0:T(128)} %stack.178.index_ref, bf16[512,640]{1,0:T(8,128)(2,1)} %shard_map.145.refs_0_, bf16[512,640]{1,0:T(8,128)(2,1)} %copy-done.18, ...), custom_call_target="tpu_custom_call" | custom-call | flops 4294967296 | bytes 10485760 | tf_op jit(solution)/shard_map/pallas_call | solution.py:441
  301.5 5.2 %collective-permute-done.37.vb_ref = bf16[512,256]{1,0:T(8,128)(2,1)S(1)} collective-permute-done((bf16[512,256]{1,0:T(8,128)(2,1)S(1)}, bf16[512,256]{1,0:T(8,128)(2,1)S(1)}, u32[]{:S(2)}, u32[]{:S(2)}) %collective-permute-start.37) | collective-permute-done | bytes 262176 | tf_op jit(solution)/shard_map/ppermute | solution.py:37
  318.9 9.1 %collective-permute-done.38.refs_4_ = bf16[512,640]{1,0:T(8,128)(2,1)S(1)} collective-permute-done((bf16[512,640]{1,0:T(8,128)(2,1)}, bf16[512,640]{1,0:T(8,128)(2,1)S(1)}, u32[]{:S(2)}, u32[]{:S(2)}) %collective-permute-start.38) | collective-permute-done | bytes 655392 | tf_op jit(solution)/shard_map/ppermute | solution.py:37
  330.6 6.9 %collective-permute-done.30.refs_1_ = bf16[512,640]{1,0:T(8,128)(2,1)S(1)} collective-permute-done((bf16[512,640]{1,0:T(8,128)(2,1)}, bf16[512,640]{1,0:T(8,128)(2,1)S(1)}, u32[]{:S(2)}, u32[]{:S(2)}) %collective-permute-start.30) | collective-permute-done | bytes 655392 | tf_op jit(solution)/shard_map/ppermute | solution.py:37
  338.7 6.2 %shard_map.152 = f32[1024,512]{1,0:T(8,128)} custom-call(s32[5,8]{1,0:T(8,128)} %stack.169.meta_ref, f32[512,640]{1,0:T(8,128)} %get-tuple-element.51.refs_0_, bf16[512,640]{1,0:T(8,128)(2,1)} %copy-done.23, bf16[512,640]{1,0:T(8,128)(2,1)} %copy-done.24, f32[512,640]{1,0:T(8,128)} %get-tuple-element.58.refs_3_, bf16[512,640]{1,0:T(8,128)(2,1)} %copy-done.21, ...), custom_call_target="tpu_custom_call" | custom-call | flops 67108864 | bytes 7340032 | tf_op jit(solution)/shard_map/pallas_call | solution.py:536
  (186 shorter events, 90.9 us)
Async XLA Ops:
  7.8 14.8 %collective-permute-start = (bf16[1024,256]{1,0:T(8,128)(2,1)S(1)}, bf16[1024,256]{1,0:T(8,128)(2,1)S(1)}, u32[]{:S(2)}, u32[]{:S(2)}) collective-permute-start(bf16[1024,256]{1,0:T(8,128)(2,1)S(1)} %get-tuple-element.72.refs_0_), channel_id=1, source_target_pairs={{0,1},{1,2},{2,3},{3,0},{4,5},{5,6},{6,7},{7,4},{8,9},{9,10},{10,1... | collective-permute-start | bytes 1572872 | tf_op jit(solution)/shard_map/ppermute | solution.py:37
  33.7 79.8 %all-to-all-start = ((bf16[8,256,512]{2,1,0:T(8,128)(2,1)}), bf16[8,256,512]{2,1,0:T(8,128)(2,1)S(1)}, u32[]{:S(2)}, u32[]{:S(2)}) async-start(bf16[8,256,512]{2,1,0:T(8,128)(2,1)} %get-tuple-element.44), calls=%async_computation | async-start | bytes 4194304 | tf_op jit(solution)/shard_map/all_to_all | solution.py:602
  39.4 235.2 %all-gather.3.cloned.1.call-start = ((), (), s32[]{:S(2)}) async-start(), calls=%async_computation.4 | async-start | bytes 9437184 | tf_op jit(solution)/shard_map/all_gather | solution.py:606
  59.8 51.7 %collective-permute-start.10 = (bf16[1024,512]{1,0:T(8,128)(2,1)}, bf16[1024,512]{1,0:T(8,128)(2,1)S(1)}, u32[]{:S(2)}, u32[]{:S(2)}) collective-permute-start(bf16[1024,512]{1,0:T(8,128)(2,1)} %get-tuple-element.36.refs_1_), channel_id=1, source_target_pairs={{0,12},{4,0},{8,4},{12,8},{1,13},{5,1},{9,5},{13,9},{2,14},{6,2},{... | collective-permute-start | bytes 3145736 | tf_op jit(solution)/shard_map/ppermute | solution.py:37
  62.8 48.6 %collective-permute-start.12 = (bf16[1024,512]{1,0:T(8,128)(2,1)}, bf16[1024,512]{1,0:T(8,128)(2,1)S(1)}, u32[]{:S(2)}, u32[]{:S(2)}) collective-permute-start(bf16[1024,512]{1,0:T(8,128)(2,1)} %get-tuple-element.37.refs_2_), channel_id=1, source_target_pairs={{0,1},{1,2},{2,3},{3,0},{4,5},{5,6},{6,7},{7,4},{8,9},{9,10},{10,1... | collective-permute-start | bytes 3145736 | tf_op jit(solution)/shard_map/ppermute | solution.py:37
  62.8 48.6 %collective-permute-start.14 = (bf16[1024,512]{1,0:T(8,128)(2,1)}, bf16[1024,512]{1,0:T(8,128)(2,1)S(1)}, u32[]{:S(2)}, u32[]{:S(2)}) collective-permute-start(bf16[1024,512]{1,0:T(8,128)(2,1)} %get-tuple-element.38.refs_3_), channel_id=1, source_target_pairs={{0,3},{1,0},{2,1},{3,2},{4,7},{5,4},{6,5},{7,6},{8,11},{9,8},{10,9... | collective-permute-start | bytes 3145736 | tf_op jit(solution)/shard_map/ppermute | solution.py:37
  66.1 47.4 %collective-permute-start.8 = (bf16[1024,512]{1,0:T(8,128)(2,1)}, bf16[1024,512]{1,0:T(8,128)(2,1)}, u32[]{:S(2)}, u32[]{:S(2)}) collective-permute-start(bf16[1024,512]{1,0:T(8,128)(2,1)} %get-tuple-element.35.refs_0_), channel_id=1, source_target_pairs={{0,4},{4,8},{8,12},{12,0},{1,5},{5,9},{9,13},{13,1},{2,6},{6,10},{... | collective-permute-start | bytes 3145736 | tf_op jit(solution)/shard_map/ppermute | solution.py:37
  66.1 30.0 %collective-permute-start.25 = (bf16[512,256]{1,0:T(8,128)(2,1)S(1)}, bf16[512,256]{1,0:T(8,128)(2,1)S(1)}, u32[]{:S(2)}, u32[]{:S(2)}) collective-permute-start(bf16[512,256]{1,0:T(8,128)(2,1)S(1)} %copy-done.41), channel_id=1, source_target_pairs={{0,4},{4,8},{8,12},{12,0},{1,5},{5,9},{9,13},{13,1},{2,6},{6,10},{... | collective-permute-start | bytes 786440 | tf_op jit(solution)/shard_map/ppermute | solution.py:37
  131.9 22.3 %all-to-all-start.1 = ((f32[16,64,192]{2,1,0:T(8,128)}), f32[16,64,192]{2,1,0:T(8,128)S(1)}, u32[]{:S(2)}, u32[]{:S(2)}) async-start(f32[16,64,192]{2,1,0:T(8,128)} %bitcast.76), calls=%async_computation.1 | async-start | bytes 2097152 | tf_op jit(solution)/shard_map/all_to_all | solution.py:212
  135.7 31.7 %collective-permute-start.16 = (bf16[1024,512]{1,0:T(8,128)(2,1)}, bf16[1024,512]{1,0:T(8,128)(2,1)}, u32[]{:S(2)}, u32[]{:S(2)}) collective-permute-start(bf16[1024,512]{1,0:T(8,128)(2,1)} %get-tuple-element.36.refs_1_), channel_id=1, source_target_pairs={{0,4},{4,8},{8,12},{12,0},{1,5},{5,9},{9,13},{13,1},{2,6},{6,10},{... | collective-permute-start | bytes 3145736 | tf_op jit(solution)/shard_map/ppermute | solution.py:37
  137.6 31.4 %collective-permute-start.17 = (bf16[1024,512]{1,0:T(8,128)(2,1)}, bf16[1024,512]{1,0:T(8,128)(2,1)}, u32[]{:S(2)}, u32[]{:S(2)}) collective-permute-start(bf16[1024,512]{1,0:T(8,128)(2,1)} %get-tuple-element.35.refs_0_), channel_id=1, source_target_pairs={{0,12},{4,0},{8,4},{12,8},{1,13},{5,1},{9,5},{13,9},{2,14},{6,2},{... | collective-permute-start | bytes 3145736 | tf_op jit(solution)/shard_map/ppermute | solution.py:37
  139.0 32.6 %collective-permute-start.18 = (bf16[1024,512]{1,0:T(8,128)(2,1)}, bf16[1024,512]{1,0:T(8,128)(2,1)}, u32[]{:S(2)}, u32[]{:S(2)}) collective-permute-start(bf16[1024,512]{1,0:T(8,128)(2,1)} %get-tuple-element.38.refs_3_), channel_id=1, source_target_pairs={{0,1},{1,2},{2,3},{3,0},{4,5},{5,6},{6,7},{7,4},{8,9},{9,10},{10,1... | collective-permute-start | bytes 3145736 | tf_op jit(solution)/shard_map/ppermute | solution.py:37
  155.3 28.4 %all-to-all-start.3 = ((bf16[8,64,1152]{2,1,0:T(8,128)(2,1)}), bf16[8,64,1152]{2,1,0:T(8,128)(2,1)S(1)}, u32[]{:S(2)}, u32[]{:S(2)}) async-start(bf16[8,64,1152]{2,1,0:T(8,128)(2,1)} %get-tuple-element.45), calls=%async_computation.3 | async-start | bytes 2359296 | tf_op jit(solution)/shard_map/all_to_all | solution.py:630
  159.7 29.5 %collective-permute-start.19 = (bf16[1024,512]{1,0:T(8,128)(2,1)}, bf16[1024,512]{1,0:T(8,128)(2,1)}, u32[]{:S(2)}, u32[]{:S(2)}) collective-permute-start(bf16[1024,512]{1,0:T(8,128)(2,1)} %get-tuple-element.37.refs_2_), channel_id=1, source_target_pairs={{0,3},{1,0},{2,1},{3,2},{4,7},{5,4},{6,5},{7,6},{8,11},{9,8},{10,9... | collective-permute-start | bytes 3145736 | tf_op jit(solution)/shard_map/ppermute | solution.py:37
  159.7 38.1 %collective-permute-start.11 = (bf16[1024,512]{1,0:T(8,128)(2,1)S(1)}, bf16[1024,512]{1,0:T(8,128)(2,1)}, u32[]{:S(2)}, u32[]{:S(2)}) collective-permute-start(bf16[1024,512]{1,0:T(8,128)(2,1)S(1)} %copy-done.3), channel_id=1, source_target_pairs={{0,12},{4,0},{8,4},{12,8},{1,13},{5,1},{9,5},{13,9},{2,14},{6,2},{... | collective-permute-start | bytes 3145736 | tf_op jit(solution)/shard_map/ppermute | solution.py:37
  167.5 30.3 %collective-permute-start.13 = (bf16[1024,512]{1,0:T(8,128)(2,1)S(1)}, bf16[1024,512]{1,0:T(8,128)(2,1)}, u32[]{:S(2)}, u32[]{:S(2)}) collective-permute-start(bf16[1024,512]{1,0:T(8,128)(2,1)S(1)} %copy-done.5), channel_id=1, source_target_pairs={{0,1},{1,2},{2,3},{3,0},{4,5},{5,6},{6,7},{7,4},{8,9},{9,10},{10,1... | collective-permute-start | bytes 3145736 | tf_op jit(solution)/shard_map/ppermute | solution.py:37
  169.0 39.5 %collective-permute-start.15 = (bf16[1024,512]{1,0:T(8,128)(2,1)}, bf16[1024,512]{1,0:T(8,128)(2,1)}, u32[]{:S(2)}, u32[]{:S(2)}) collective-permute-start(bf16[1024,512]{1,0:T(8,128)(2,1)} %copy-done.6), channel_id=1, source_target_pairs={{0,3},{1,0},{2,1},{3,2},{4,7},{5,4},{6,5},{7,6},{8,11},{9,8},{10,9... | collective-permute-start | bytes 3145736 | tf_op jit(solution)/shard_map/ppermute | solution.py:37
  171.7 36.8 %collective-permute-start.9 = (bf16[1024,512]{1,0:T(8,128)(2,1)}, bf16[1024,512]{1,0:T(8,128)(2,1)}, u32[]{:S(2)}, u32[]{:S(2)}) collective-permute-start(bf16[1024,512]{1,0:T(8,128)(2,1)} %collective-permute-done.8.refs_0_.rest_2_.refs_5_), channel_id=1, source_target_pairs={{0,4},{4,8},{8,12},{12,0},{1,5},{5,9},{9,13},{13,1},{2,6},{6,10},{... | collective-permute-start | bytes 3145736 | tf_op jit(solution)/shard_map/ppermute | solution.py:37
  183.7 29.7 %all-to-all-start.2 = ((bf16[16,64,192]{2,1,0:T(8,128)(2,1)}), bf16[16,64,192]{2,1,0:T(8,128)(2,1)}, u32[]{:S(2)}, u32[]{:S(2)}) async-start(bf16[16,64,192]{2,1,0:T(8,128)(2,1)} %shard_map.143), calls=%async_computation.2 | async-start | bytes 1048576 | tf_op jit(solution)/shard_map/all_to_all | solution.py:655
  233.8 17.9 %collective-permute-start.33 = (bf16[512,640]{1,0:T(8,128)(2,1)}, bf16[512,640]{1,0:T(8,128)(2,1)S(1)}, u32[]{:S(2)}, u32[]{:S(2)}) collective-permute-start(bf16[512,640]{1,0:T(8,128)(2,1)} %shard_map.149.refs_0_), channel_id=1, source_target_pairs={{0,12},{4,0},{8,4},{12,8},{1,13},{5,1},{9,5},{13,9},{2,14},{6,2},{... | collective-permute-start | bytes 1966088 | tf_op jit(solution)/shard_map/ppermute | solution.py:37
  235.8 19.2 %collective-permute-start.32 = (bf16[512,640]{1,0:T(8,128)(2,1)}, bf16[512,640]{1,0:T(8,128)(2,1)S(1)}, u32[]{:S(2)}, u32[]{:S(2)}) collective-permute-start(bf16[512,640]{1,0:T(8,128)(2,1)} %shard_map.149.refs_0_), channel_id=1, source_target_pairs={{0,4},{4,8},{8,12},{12,0},{1,5},{5,9},{9,13},{13,1},{2,6},{6,10},{... | collective-permute-start | bytes 1966088 | tf_op jit(solution)/shard_map/ppermute | solution.py:37
  242.4 23.3 %collective-permute-start.22 = (bf16[512,640]{1,0:T(8,128)(2,1)}, bf16[512,640]{1,0:T(8,128)(2,1)S(1)}, u32[]{:S(2)}, u32[]{:S(2)}) collective-permute-start(bf16[512,640]{1,0:T(8,128)(2,1)} %shard_map.145.refs_0_), channel_id=1, source_target_pairs={{0,12},{4,0},{8,4},{12,8},{1,13},{5,1},{9,5},{13,9},{2,14},{6,2},{... | collective-permute-start | bytes 1966088 | tf_op jit(solution)/shard_map/ppermute | solution.py:37
  245.6 23.4 %collective-permute-start.21 = (bf16[512,640]{1,0:T(8,128)(2,1)}, bf16[512,640]{1,0:T(8,128)(2,1)S(1)}, u32[]{:S(2)}, u32[]{:S(2)}) collective-permute-start(bf16[512,640]{1,0:T(8,128)(2,1)} %shard_map.145.refs_0_), channel_id=1, source_target_pairs={{0,4},{4,8},{8,12},{12,0},{1,5},{5,9},{9,13},{13,1},{2,6},{6,10},{... | collective-permute-start | bytes 1966088 | tf_op jit(solution)/shard_map/ppermute | solution.py:37
  251.7 22.9 %collective-permute-start.35 = (bf16[512,384]{1,0:T(8,128)(2,1)S(1)}, bf16[512,384]{1,0:T(8,128)(2,1)}, u32[]{:S(2)}, u32[]{:S(2)}) collective-permute-start(bf16[512,384]{1,0:T(8,128)(2,1)S(1)} %slice.47), channel_id=1, source_target_pairs={{0,12},{4,0},{8,4},{12,8},{1,13},{5,1},{9,5},{13,9},{2,14},{6,2},{... | collective-permute-start | bytes 1179656 | tf_op jit(solution)/shard_map/ppermute | solution.py:37
  255.7 18.9 %collective-permute-start.34 = (bf16[512,256]{1,0:T(8,128)(2,1)}, bf16[512,256]{1,0:T(8,128)(2,1)}, u32[]{:S(2)}, u32[]{:S(2)}) collective-permute-start(bf16[512,256]{1,0:T(8,128)(2,1)} %slice.46), channel_id=1, source_target_pairs={{0,4},{4,8},{8,12},{12,0},{1,5},{5,9},{9,13},{13,1},{2,6},{6,10},{... | collective-permute-start | bytes 786440 | tf_op jit(solution)/shard_map/ppermute | solution.py:37
  265.8 21.5 %collective-permute-start.24 = (bf16[512,384]{1,0:T(8,128)(2,1)S(1)}, bf16[512,384]{1,0:T(8,128)(2,1)}, u32[]{:S(2)}, u32[]{:S(2)}) collective-permute-start(bf16[512,384]{1,0:T(8,128)(2,1)S(1)} %slice.45), channel_id=1, source_target_pairs={{0,12},{4,0},{8,4},{12,8},{1,13},{5,1},{9,5},{13,9},{2,14},{6,2},{... | collective-permute-start | bytes 1179656 | tf_op jit(solution)/shard_map/ppermute | solution.py:37
  269.8 17.4 %collective-permute-start.23 = (bf16[512,256]{1,0:T(8,128)(2,1)}, bf16[512,256]{1,0:T(8,128)(2,1)}, u32[]{:S(2)}, u32[]{:S(2)}) collective-permute-start(bf16[512,256]{1,0:T(8,128)(2,1)} %slice.44), channel_id=1, source_target_pairs={{0,4},{4,8},{8,12},{12,0},{1,5},{5,9},{9,13},{13,1},{2,6},{6,10},{... | collective-permute-start | bytes 786440 | tf_op jit(solution)/shard_map/ppermute | solution.py:37
  285.3 21.4 %collective-permute-start.36 = (bf16[512,384]{1,0:T(8,128)(2,1)}, bf16[512,384]{1,0:T(8,128)(2,1)S(1)}, u32[]{:S(2)}, u32[]{:S(2)}) collective-permute-start(bf16[512,384]{1,0:T(8,128)(2,1)} %get-tuple-element.60), channel_id=1, source_target_pairs={{0,1},{1,2},{2,3},{3,0},{4,5},{5,6},{6,7},{7,4},{8,9},{9,10},{10,1... | collective-permute-start | bytes 1179656 | tf_op jit(solution)/shard_map/ppermute | solution.py:37
  310.1 17.9 %collective-permute-start.38 = (bf16[512,640]{1,0:T(8,128)(2,1)}, bf16[512,640]{1,0:T(8,128)(2,1)S(1)}, u32[]{:S(2)}, u32[]{:S(2)}) collective-permute-start(bf16[512,640]{1,0:T(8,128)(2,1)} %get-tuple-element.63), channel_id=1, source_target_pairs={{0,3},{1,0},{2,1},{3,2},{4,7},{5,4},{6,5},{7,6},{8,11},{9,8},{10,9... | collective-permute-start | bytes 1966088 | tf_op jit(solution)/shard_map/ppermute | solution.py:37
  312.1 18.5 %collective-permute-start.39 = (bf16[512,640]{1,0:T(8,128)(2,1)}, bf16[512,640]{1,0:T(8,128)(2,1)S(1)}, u32[]{:S(2)}, u32[]{:S(2)}) collective-permute-start(bf16[512,640]{1,0:T(8,128)(2,1)} %get-tuple-element.64), channel_id=1, source_target_pairs={{0,1},{1,2},{2,3},{3,0},{4,5},{5,6},{6,7},{7,4},{8,9},{9,10},{10,1... | collective-permute-start | bytes 1966088 | tf_op jit(solution)/shard_map/ppermute | solution.py:37
  315.7 21.9 %collective-permute-start.30 = (bf16[512,640]{1,0:T(8,128)(2,1)}, bf16[512,640]{1,0:T(8,128)(2,1)S(1)}, u32[]{:S(2)}, u32[]{:S(2)}) collective-permute-start(bf16[512,640]{1,0:T(8,128)(2,1)} %get-tuple-element.56), channel_id=1, source_target_pairs={{0,3},{1,0},{2,1},{3,2},{4,7},{5,4},{6,5},{7,6},{8,11},{9,8},{10,9... | collective-permute-start | bytes 1966088 | tf_op jit(solution)/shard_map/ppermute | solution.py:37
  318.9 18.7 %collective-permute-start.31 = (bf16[512,640]{1,0:T(8,128)(2,1)}, bf16[512,640]{1,0:T(8,128)(2,1)S(1)}, u32[]{:S(2)}, u32[]{:S(2)}) collective-permute-start(bf16[512,640]{1,0:T(8,128)(2,1)} %get-tuple-element.57), channel_id=1, source_target_pairs={{0,1},{1,2},{2,3},{3,0},{4,5},{5,6},{6,7},{7,4},{8,9},{9,10},{10,1... | collective-permute-start | bytes 1966088 | tf_op jit(solution)/shard_map/ppermute | solution.py:37
  (56 other events, 580.3 us)
Sparse Core Ops, SparseCore 0:
  117.3 46.3 all-gather.2

commit v9 on v7

--- a/solution.py
+++ b/solution.py
@@ -188,26 +188,31 @@
     )(*flat, *after)
 
 
-def share_sum(pieces, after):
+def share_sum(pieces, onward, after):
     ways, rows, rank = pieces.shape
 
     def body(p_ref, *refs):
+        out = refs[-2]
         total = p_ref[0]
         for k in range(1, ways):
             total = total + p_ref[k]
         for k in range(ways):
-            refs[-1][k] = total.astype(bf16)
+            out[k] = total.astype(bf16)
 
     whole = pl.BlockSpec(pieces.shape, lambda i: (0, 0, 0))
     return pl.pallas_call(
         body,
-        out_shape=jax.ShapeDtypeStruct(pieces.shape, bf16),
+        out_shape=(
+            jax.ShapeDtypeStruct(pieces.shape, bf16),
+            jax.ShapeDtypeStruct(onward.shape, onward.dtype),
+        ),
         grid=(1,),
-        in_specs=[whole] + passive(after),
-        out_specs=whole,
+        in_specs=[whole] + passive([onward, *after]),
+        out_specs=[whole] + passive([onward]),
+        input_output_aliases={1: 1},
         compiler_params=params(),
         cost_estimate=cost(ways * rows * rank, 6 * ways * rows * rank),
-    )(pieces, *after)
+    )(pieces, onward, *after)
 
 
 def scatter_rows(partial):
@@ -406,8 +411,8 @@
     whole = 2 * width + HEAD
 
     def body(index_ref, *refs):
-        own, behind, ahead, far_low, far_high, w_ref = refs[:6]
-        out_far_low, out_far_high, out_ahead, out_behind, out_mine, x_all = refs[6:]
+        own, behind, ahead, far_low, far_high, w_low, w_high = refs[:7]
+        out_far_low, out_far_high, out_ahead, out_behind, out_mine, x_all = refs[7:]
         step = pl.program_id(0)
 
         @pl.when(step == 0)
@@ -425,15 +430,21 @@
             for out in (out_far_low, out_ahead, out_behind, out_mine):
                 out[:, width : width + HEAD] = rank.astype(out.dtype)
 
-        total = jnp.dot(x_all[...], w_ref[0], preferred_element_type=f32)
+        first = jnp.dot(x_all[...], w_low[0], preferred_element_type=f32)
+        second = jnp.dot(x_all[...], w_high[0], preferred_element_type=f32)
         low, high = slice(0, width), slice(width + HEAD, whole)
-        targets = [(out_far_low, low), (out_far_high, low)]
-        targets += [(out, at) for out in (out_ahead, out_behind, out_mine) for at in (low, high)]
-        for k, (out, at) in enumerate(targets):
-
-            @pl.when(step == k)
+
+        @pl.when(step == 0)
+        def _():
+            out_far_low[:, low] = first.astype(bf16)
+            out_far_high[...] = second.astype(bf16)
+
+        for k, out in enumerate((out_ahead, out_behind, out_mine)):
+
+            @pl.when(step == k + 1)
             def _():
-                out[:, at] = total.astype(out.dtype)
+                out[:, low] = first.astype(out.dtype)
+                out[:, high] = second.astype(out.dtype)
 
     shapes = [(width + HEAD, bf16), (width, bf16), (whole, bf16), (whole, bf16), (whole, f32)]
     return pl.pallas_call(
@@ -441,9 +452,10 @@
         out_shape=tuple(jax.ShapeDtypeStruct((tokens, w), d) for w, d in shapes),
         grid_spec=pltpu.PrefetchScalarGridSpec(
             num_scalar_prefetch=1,
-            grid=(count,),
+            grid=(count // 2,),
             in_specs=[pl.BlockSpec(p.shape, lambda j, d: (0, 0)) for p in pieces]
-            + [pl.BlockSpec((1, depth, width), lambda j, d: (d[j], 0, 0))],
+            + [pl.BlockSpec((1, depth, width), lambda j, d: (d[2 * j], 0, 0))]
+            + [pl.BlockSpec((1, depth, width), lambda j, d: (d[2 * j + 1], 0, 0))],
             out_specs=[pl.BlockSpec((tokens, w), lambda j, d: (0, 0)) for w, _ in shapes],
             scratch_shapes=[pltpu.VMEM((tokens, depth), bf16)],
         ),
@@ -451,7 +463,7 @@
         cost_estimate=cost(
             2 * tokens * depth * count * width, 2 * depth * (tokens + count * width)
         ),
-    )(jnp.stack(shards).astype(i32), *pieces, weights)
+    )(jnp.stack(shards).astype(i32), *pieces, weights, weights)
 
 
 def add_far(ahead, via_behind, behind, via_ahead):
@@ -608,26 +620,29 @@
 
     every = range(SIDE)
     low, high = (0, 1), (2, 3)
+    total = project(
+        (index_of(rows_a(0, every) + rows_b(0, every)), meta),
+        None,
+        [low_a, high_a, low_b, high_b],
+        [wq, wkv],
+        512,
+    )
+
     pieces = scatter_rows(rank_partial(meta, x, down, 3 * rank, [low_a]))
+    copies, up_out = share_sum(pieces, up_out, [total[1]])
     up = lax.all_to_all(up_out, ADAPTER_AXES, 0, 0, tiled=True)
-
-    copies = share_sum(pieces, [])
 
     a_low, a_high = shift(far_a[0], "y", 1), shift(far_a[1], "y", -1)
     b_low, b_high = shift(far_b[0], "x", 1), shift(far_b[1], "x", -1)
     total = project(
         (
-            index_of(
-                rows_a(0, every) + rows_b(0, every)
-                + rows_a(1, low) + rows_a(2, high) + rows_b(1, low) + rows_b(2, high)
-            ),
+            index_of(rows_a(1, low) + rows_a(2, high) + rows_b(1, low) + rows_b(2, high)),
             meta,
         ),
-        None,
-        [low_a, high_a, low_b, high_b, *far_a, *far_b],
+        total,
+        [*far_a, *far_b],
         [wq, wkv],
         512,
-        after=[copies],
     )
     total = project(
         (

time: 316 us -> 305 us (0.965)
  waiting for transfers between devices: 103 us -> 87.7 us
    ppermute x39, waiting for transfers between devices: 101 us -> 84.7 us  [shift(): lax.ppermute(block, axis, [(i, (i + step) % SIDE) for i in range(SIDE)])]
    pallas_call x2, Pallas kernels: 25.1 us -> 21.2 us  [output_partial(): pl.pallas_call(body, out_shape=tuple((jax.ShapeDtypeStruct((tokens, w), d...]
    pallas_call x4 -> x5, Pallas kernels: 34.1 us -> 37.9 us  [project(): pl.pallas_call(body, out_shape=tuple((jax.ShapeDtypeStruct((tokens, w), d...]
    unnamed x72 -> x70, local copies, waits for them, and re-layouts: 7.44 us -> 7.57 us
  transfers between devices with their start and end apart: 45 -> 45, of which waited for: 19 -> 22; matrix products, arithmetic and copies ran while one was open for 1% -> 2% of each run, Pallas kernels for 29% -> 30%
where the time goes in v9:
time: 305 us; the launch traced here: 303 us
  Pallas kernels  106 us (35%)
  waiting for transfers between devices  87.7 us (29%)
  starting transfers between devices  80.6 us (26%)
  between operations  13.8 us (5%)
  local copies, waits for them, and re-layouts  13.3 us (4%)
    ppermute x39, waiting for transfers between devices, shift(): lax.ppermute(block, axis, [(i, (i + step) % SIDE) for i in range(SIDE)])  84.7 us
    ppermute x39, starting transfers between devices, shift(): lax.ppermute(block, axis, [(i, (i + step) % SIDE) for i in range(SIDE)])  57.1 us
    pallas_call x5, Pallas kernels, project(): pl.pallas_call(body, out_shape=tuple((jax.ShapeDtypeStruct((tokens, w), d...  37.9 us
    pallas_call x2, Pallas kernels, output_partial(): pl.pallas_call(body, out_shape=tuple((jax.ShapeDtypeStruct((tokens, w), d...  21.2 us
    pallas_call x2, Pallas kernels, attention(): pl.pallas_call(body, out_shape=jax.ShapeDtypeStruct((count * BLOCK, wide...  13.2 us
    pallas_call x1, Pallas kernels, pick_local(): pl.pallas_call(body, out_shape=tuple((jax.ShapeDtypeStruct(s, bf16) for s...  7.66 us
    unnamed x70, local copies, waits for them, and re-layouts  7.57 us
    all_to_all x1, starting transfers between devices, on_device(): lax.all_to_all(copies, TENSOR_AXES, 0, 0, tiled=True)  7.48 us
  transfers between devices with their start and end apart: 45, of which 22 were waited for; matrix products, arithmetic and copies ran while one was open for 2% of the time, Pallas kernels for 30%

profile of v9, /device:TPU:0, one launch (start us, length us, event | category | flops | bytes accessed | tf_op | source)
XLA Modules:
  0.0 302.9 jit_solution(11010668481254453658)
XLA Ops:
  8.0 7.7 %shard_map.136 = (bf16[8,256,512]{2,1,0:T(8,128)(2,1)}, bf16[8,64,1152]{2,1,0:T(8,128)(2,1)}, bf16[1024,256]{1,0:T(8,128)(2,1)}, bf16[1024,256]{1,0:T(8,128)(2,1...) custom-call(s32[12]{0:T(128)} %pad_add_fusion.pick_ref, ...), custom_call_target="tpu_custom_call" | custom-call | bytes 6553600 | tf_op jit(solution)/shard_map/pallas_call | solution.py:87
  15.7 5.7 %all-to-all-start = ((bf16[8,256,512]{2,1,0:T(8,128)(2,1)}), bf16[8,256,512]{2,1,0:T(8,128)(2,1)S(1)}, u32[]{:S(2)}, u32[]{:S(2)}) async-start(bf16[8,256,512]{2,1,0:T(8,128)(2,1)} %get-tuple-element.53), calls=%async_computation | async-start | bytes 4194304 | tf_op jit(solution)/shard_map/all_to_all | solution.py:598
  29.9 7.0 %collective-permute-done.refs_1_ = bf16[1024,256]{1,0:T(8,128)(2,1)S(1)} collective-permute-done((bf16[1024,256]{1,0:T(8,128)(2,1)S(1)}, bf16[1024,256]{1,0:T(8,128)(2,1)S(1)}, u32[]{:S(2)}, u32[]{:S(2)}) %collective-permute-start) | collective-permute-done | bytes 524320 | tf_op jit(solution)/shard_map/ppermute | solution.py:37
  43.9 4.0 %collective-permute-done.10.refs_12_.refs_3_ = bf16[512,256]{1,0:T(8,128)(2,1)S(1)} collective-permute-done((bf16[512,256]{1,0:T(8,128)(2,1)}, bf16[512,256]{1,0:T(8,128)(2,1)S(1)}, u32[]{:S(2)}, u32[]{:S(2)}) %collective-permute-start.10) | collective-permute-done | bytes 262176 | tf_op jit(solution)/shard_map/ppermute | solution.py:37
  60.1 4.8 %shard_map.137 = (bf16[1024,512]{1,0:T(8,128)(2,1)}, bf16[1024,512]{1,0:T(8,128)(2,1)}, bf16[1024,512]{1,0:T(8,128)(2,1)}, bf16[1024,512]{1,0:T(8,128)(2,1)}) custom-call(bf16[1024,256]{1,0:T(8,128)(2,1)} %get-tuple-element.39.refs_0_, bf16[1024,256]{1,0:T(8,128)(2,1)} %copy-done.11, bf16[1024,256]{1,0:T(8,128)(2,1)} %copy-done.12, ...), custom_call_target="tpu_custom_call" | custom-call | bytes 8388608 | tf_op jit(solution)/shard_map/pallas_call | solution.py:179
  73.2 5.1 %shard_map.142 = f32[1024,192]{1,0:T(8,128)} custom-call(s32[5,8]{1,0:T(8,128)} %stack.169.meta_ref, bf16[1024,512]{1,0:T(8,128)(2,1)} %x_ref.3, bf16[8,256,512]{2,1,0:T(8,128)(2,1)} %copy-done, bf16[8,256,512]{2,1,0:T(8,128)(2,1)} %copy-done, bf16[1024,512]{1,0:T(8,128)(2,1)} %get-tuple-element.44.refs_0_.rest_2_.refs_5_), custom_call_target="tpu_custom_call" | custom-call | flops 201326592 | bytes 2621440 | tf_op jit(solution)/shard_map/pallas_call | solution.py:147
  78.3 5.0 %all-to-all-start.1 = ((f32[16,64,192]{2,1,0:T(8,128)}), f32[16,64,192]{2,1,0:T(8,128)S(1)}, u32[]{:S(2)}, u32[]{:S(2)}) async-start(f32[16,64,192]{2,1,0:T(8,128)} %bitcast.79), calls=%async_computation.1 | async-start | bytes 2097152 | tf_op jit(solution)/shard_map/all_to_all | solution.py:221
  87.8 15.2 %collective-permute-done.11.refs_0_ = bf16[1024,512]{1,0:T(8,128)(2,1)} collective-permute-done((bf16[1024,512]{1,0:T(8,128)(2,1)S(1)}, bf16[1024,512]{1,0:T(8,128)(2,1)}, u32[]{:S(2)}, u32[]{:S(2)}) %collective-permute-start.11) | collective-permute-done | bytes 1048608 | tf_op jit(solution)/shard_map/ppermute | solution.py:37
  105.7 8.1 %shard_map.138 = (f32[1024,512]{1,0:T(8,128)}, f32[1024,128]{1,0:T(8,128)}) custom-call(s32[8]{0:T(128)} %stack.219.index_ref, s32[5,8]{1,0:T(8,128)} %stack.169.meta_ref, bf16[1024,512]{1,0:T(8,128)(2,1)} %get-tuple-element.44.refs_0_.rest_2_.refs_5_, bf16[1024,512]{1,0:T(8,128)(2,1)} %get-tuple-element.45.refs_1_, ...), custom_call_target="tpu_custom_call" | custom-call | flops 2684354560 | bytes 12058624 | tf_op jit(solution)/shard_map/pallas_call | solution.py:270
  116.9 7.5 %all-to-all-start.2 = ((bf16[16,64,192]{2,1,0:T(8,128)(2,1)}), bf16[16,64,192]{2,1,0:T(8,128)(2,1)S(1)}, u32[]{:S(2)}, u32[]{:S(2)}) async-start(bf16[16,64,192]{2,1,0:T(8,128)(2,1)} %get-tuple-element.55), calls=%async_computation.2 | async-start | bytes 1048576 | tf_op jit(solution)/shard_map/all_to_all | solution.py:657
  124.4 3.2 %collective-permute-start.22 = (bf16[1024,512]{1,0:T(8,128)(2,1)}, bf16[1024,512]{1,0:T(8,128)(2,1)}, u32[]{:S(2)}, u32[]{:S(2)}) collective-permute-start(bf16[1024,512]{1,0:T(8,128)(2,1)} %get-tuple-element.46.refs_2_), channel_id=1, source_target_pairs={{0,3},{1,0},{2,1},{3,2},{4,7},{5,4},{6,5},{7,6},{8,11},{9,8},{10,9... | collective-permute-start | bytes 3145736 | tf_op jit(solution)/shard_map/ppermute | solution.py:37
  139.2 4.0 %all-to-all-start.3 = ((bf16[8,64,1152]{2,1,0:T(8,128)(2,1)}), bf16[8,64,1152]{2,1,0:T(8,128)(2,1)S(1)}, u32[]{:S(2)}, u32[]{:S(2)}) async-start(bf16[8,64,1152]{2,1,0:T(8,128)(2,1)} %get-tuple-element.56), calls=%async_computation.3 | async-start | bytes 2359296 | tf_op jit(solution)/shard_map/all_to_all | solution.py:633
  145.1 8.6 %shard_map.139 = (f32[1024,512]{1,0:T(8,128)}, f32[1024,128]{1,0:T(8,128)}) custom-call(s32[8]{0:T(128)} %stack.210.index_ref, s32[5,8]{1,0:T(8,128)} %stack.169.meta_ref, bf16[1024,512]{1,0:T(8,128)(2,1)} %collective-permute-done.11.refs_0_, bf16[1024,512]{1,0:T(8,128)(2,1)} %collective-permute-done.13.refs_1_, ...), custom_call_target="tpu_custom_call", output_to_operand_aliasing={{0}: (22, {}), {1}: (23, {})} | custom-call | flops 2684354560 | bytes 12058624 | tf_op jit(solution)/shard_map/pallas_call | solution.py:270
  156.3 8.7 %shard_map.140 = (f32[1024,512]{1,0:T(8,128)}, f32[1024,128]{1,0:T(8,128)}) custom-call(s32[8]{0:T(128)} %stack.201.index_ref, s32[5,8]{1,0:T(8,128)} %stack.169.meta_ref, bf16[1024,512]{1,0:T(8,128)(2,1)} %collective-permute-done.19.refs_0_, bf16[1024,512]{1,0:T(8,128)(2,1)} %collective-permute-done.20.refs_1_, ...), custom_call_target="tpu_custom_call", output_to_operand_aliasing={{0}: (22, {}), {1}: (23, {})} | custom-call | flops 2684354560 | bytes 12058624 | tf_op jit(solution)/shard_map/pallas_call | solution.py:270
  168.8 5.5 %shard_map.144.m_ref = bf16[1024,128]{1,0:T(8,128)(2,1)} custom-call(s32[8]{0:T(128)} %stack.187.index_ref, s32[5,8]{1,0:T(8,128)} %stack.169.meta_ref, bf16[1024,512]{1,0:T(8,128)(2,1)} %copy-done.5, bf16[1024,512]{1,0:T(8,128)(2,1)} %collective-permute-done.14.refs_1_, bf16[1024,512]{1,0:T(8,128)(2,1)} %collective-permute-done.16.refs_2_, ...), custom_call_target="tpu_custom_call" | custom-call | flops 536870912 | bytes 5767168 | tf_op jit(solution)/shard_map/pallas_call | solution.py:270
  175.7 7.1 %shard_map.141.q_ref = f32[1024,512]{1,0:T(8,128)} custom-call(s32[8]{0:T(128)} %stack.187.index_ref, s32[5,8]{1,0:T(8,128)} %stack.169.meta_ref, bf16[1024,512]{1,0:T(8,128)(2,1)} %copy-done.5, bf16[1024,512]{1,0:T(8,128)(2,1)} %collective-permute-done.14.refs_1_, ...), custom_call_target="tpu_custom_call", output_to_operand_aliasing={{}: (14, {})} | custom-call | flops 2147483648 | bytes 10485760 | tf_op jit(solution)/shard_map/pallas_call | solution.py:270
  183.5 6.6 %shard_map.149.refs_0_ = bf16[512,640]{1,0:T(8,128)(2,1)} custom-call(s32[5,8]{1,0:T(8,128)} %stack.169.meta_ref, f32[1024,512]{1,0:T(8,128)} %shard_map.141.q_ref, bf16[1024,192]{1,0:T(8,128)(2,1)} %bitcast.77, bf16[8,64,1152]{2,1,0:T(8,128)(2,1)} %copy-done.1, bf16[8,256,512]{2,1,0:T(8,128)(2,1)} %copy-done, bf16[1024,128]{1,0:T(8,128)(2,1)} %shard_map.144.m_ref, ...), custom_call_target="tpu_custom_call" | custom-call | flops 402653184 | bytes 2097152 | tf_op jit(solution)/shard_map/pallas_call | solution.py:381
  192.8 6.6 %shard_map.145.refs_0_ = bf16[512,640]{1,0:T(8,128)(2,1)} custom-call(s32[5,8]{1,0:T(8,128)} %stack.169.meta_ref, f32[1024,512]{1,0:T(8,128)} %shard_map.141.q_ref, bf16[1024,192]{1,0:T(8,128)(2,1)} %bitcast.78, bf16[8,64,1152]{2,1,0:T(8,128)(2,1)} %copy-done.1, bf16[8,256,512]{2,1,0:T(8,128)(2,1)} %copy-done, bf16[1024,128]{1,0:T(8,128)(2,1)} %shard_map.144.m_ref, ...), custom_call_target="tpu_custom_call" | custom-call | flops 402653184 | bytes 2097152 | tf_op jit(solution)/shard_map/pallas_call | solution.py:381
  199.4 3.2 %collective-permute-start.25 = (bf16[512,640]{1,0:T(8,128)(2,1)}, bf16[512,640]{1,0:T(8,128)(2,1)S(1)}, u32[]{:S(2)}, u32[]{:S(2)}) collective-permute-start(bf16[512,640]{1,0:T(8,128)(2,1)} %shard_map.145.refs_0_), channel_id=1, source_target_pairs={{0,12},{4,0},{8,4},{12,8},{1,13},{5,1},{9,5},{13,9},{2,14},{6,2},{... | collective-permute-start | bytes 1966088 | tf_op jit(solution)/shard_map/ppermute | solution.py:37
  202.7 4.4 %collective-permute-done.33.refs_2_ = bf16[512,640]{1,0:T(8,128)(2,1)S(1)} collective-permute-done((bf16[512,640]{1,0:T(8,128)(2,1)}, bf16[512,640]{1,0:T(8,128)(2,1)S(1)}, u32[]{:S(2)}, u32[]{:S(2)}) %collective-permute-start.33) | collective-permute-done | bytes 655392 | tf_op jit(solution)/shard_map/ppermute | solution.py:37
  207.2 3.4 %collective-permute-start.35 = (bf16[512,384]{1,0:T(8,128)(2,1)S(1)}, bf16[512,384]{1,0:T(8,128)(2,1)}, u32[]{:S(2)}, u32[]{:S(2)}) collective-permute-start(bf16[512,384]{1,0:T(8,128)(2,1)S(1)} %slice.39), channel_id=1, source_target_pairs={{0,12},{4,0},{8,4},{12,8},{1,13},{5,1},{9,5},{13,9},{2,14},{6,2},{... | collective-permute-start | bytes 1179656 | tf_op jit(solution)/shard_map/ppermute | solution.py:37
  212.1 9.0 %collective-permute-done.25.refs_2_ = bf16[512,640]{1,0:T(8,128)(2,1)S(1)} collective-permute-done((bf16[512,640]{1,0:T(8,128)(2,1)}, bf16[512,640]{1,0:T(8,128)(2,1)S(1)}, u32[]{:S(2)}, u32[]{:S(2)}) %collective-permute-start.25) | collective-permute-done | bytes 655392 | tf_op jit(solution)/shard_map/ppermute | solution.py:37
  221.2 3.4 %collective-permute-start.27 = (bf16[512,384]{1,0:T(8,128)(2,1)S(1)}, bf16[512,384]{1,0:T(8,128)(2,1)}, u32[]{:S(2)}, u32[]{:S(2)}) collective-permute-start(bf16[512,384]{1,0:T(8,128)(2,1)S(1)} %slice.37), channel_id=1, source_target_pairs={{0,12},{4,0},{8,4},{12,8},{1,13},{5,1},{9,5},{13,9},{2,14},{6,2},{... | collective-permute-start | bytes 1179656 | tf_op jit(solution)/shard_map/ppermute | solution.py:37
  228.0 10.6 %shard_map.150 = (bf16[512,384]{1,0:T(8,128)(2,1)}, bf16[512,256]{1,0:T(8,128)(2,1)}, bf16[512,640]{1,0:T(8,128)(2,1)}, bf16[512,640]{1,0:T(8,128)(2,1)}, f32[512,640]{1,0:T(8,128)}) custom-call(s32[8]{0:T(128)} %stack.178.index_ref, bf16[512,640]{1,0:T(8,128)(2,1)} %shard_map.149.refs_0_, bf16[512,640]{1,0:T(8,128)(2,1)} %copy-done.10, ...), custom_call_target="tpu_custom_call" | custom-call | flops 4294967296 | bytes 10485760 | tf_op jit(solution)/shard_map/pallas_call | solution.py:450
  240.6 10.6 %shard_map.147 = (bf16[512,384]{1,0:T(8,128)(2,1)}, bf16[512,256]{1,0:T(8,128)(2,1)}, bf16[512,640]{1,0:T(8,128)(2,1)}, bf16[512,640]{1,0:T(8,128)(2,1)}, f32[512,640]{1,0:T(8,128)}) custom-call(s32[8]{0:T(128)} %stack.178.index_ref, bf16[512,640]{1,0:T(8,128)(2,1)} %shard_map.145.refs_0_, bf16[512,640]{1,0:T(8,128)(2,1)} %copy-done.9, ...), custom_call_target="tpu_custom_call" | custom-call | flops 4294967296 | bytes 10485760 | tf_op jit(solution)/shard_map/pallas_call | solution.py:450
  251.2 3.2 %collective-permute-start.37 = (bf16[512,256]{1,0:T(8,128)(2,1)S(1)}, bf16[512,256]{1,0:T(8,128)(2,1)S(1)}, u32[]{:S(2)}, u32[]{:S(2)}) collective-permute-start(bf16[512,256]{1,0:T(8,128)(2,1)S(1)} %copy-done.34), channel_id=1, source_target_pairs={{0,3},{1,0},{2,1},{3,2},{4,7},{5,4},{6,5},{7,6},{8,11},{9,8},{10,9... | collective-permute-start | bytes 786440 | tf_op jit(solution)/shard_map/ppermute | solution.py:37
  254.8 6.3 %collective-permute-done.37.vb_ref = bf16[512,256]{1,0:T(8,128)(2,1)S(1)} collective-permute-done((bf16[512,256]{1,0:T(8,128)(2,1)S(1)}, bf16[512,256]{1,0:T(8,128)(2,1)S(1)}, u32[]{:S(2)}, u32[]{:S(2)}) %collective-permute-start.37) | collective-permute-done | bytes 262176 | tf_op jit(solution)/shard_map/ppermute | solution.py:37
  264.6 3.7 %collective-permute-start.38 = (bf16[512,640]{1,0:T(8,128)(2,1)}, bf16[512,640]{1,0:T(8,128)(2,1)S(1)}, u32[]{:S(2)}, u32[]{:S(2)}) collective-permute-start(bf16[512,640]{1,0:T(8,128)(2,1)} %get-tuple-element.71), channel_id=1, source_target_pairs={{0,3},{1,0},{2,1},{3,2},{4,7},{5,4},{6,5},{7,6},{8,11},{9,8},{10,9... | collective-permute-start | bytes 1966088 | tf_op jit(solution)/shard_map/ppermute | solution.py:37
  271.8 3.2 %collective-permute-start.30 = (bf16[512,640]{1,0:T(8,128)(2,1)}, bf16[512,640]{1,0:T(8,128)(2,1)S(1)}, u32[]{:S(2)}, u32[]{:S(2)}) collective-permute-start(bf16[512,640]{1,0:T(8,128)(2,1)} %get-tuple-element.64), channel_id=1, source_target_pairs={{0,3},{1,0},{2,1},{3,2},{4,7},{5,4},{6,5},{7,6},{8,11},{9,8},{10,9... | collective-permute-start | bytes 1966088 | tf_op jit(solution)/shard_map/ppermute | solution.py:37
  275.0 6.7 %collective-permute-done.38.refs_4_ = bf16[512,640]{1,0:T(8,128)(2,1)S(1)} collective-permute-done((bf16[512,640]{1,0:T(8,128)(2,1)}, bf16[512,640]{1,0:T(8,128)(2,1)S(1)}, u32[]{:S(2)}, u32[]{:S(2)}) %collective-permute-start.38) | collective-permute-done | bytes 655392 | tf_op jit(solution)/shard_map/ppermute | solution.py:37
  281.8 7.0 %collective-permute-done.30.refs_1_ = bf16[512,640]{1,0:T(8,128)(2,1)S(1)} collective-permute-done((bf16[512,640]{1,0:T(8,128)(2,1)}, bf16[512,640]{1,0:T(8,128)(2,1)S(1)}, u32[]{:S(2)}, u32[]{:S(2)}) %collective-permute-start.30) | collective-permute-done | bytes 655392 | tf_op jit(solution)/shard_map/ppermute | solution.py:37
  289.9 6.2 %shard_map.152 = f32[1024,512]{1,0:T(8,128)} custom-call(s32[5,8]{1,0:T(8,128)} %stack.169.meta_ref, f32[512,640]{1,0:T(8,128)} %get-tuple-element.59.refs_0_, bf16[512,640]{1,0:T(8,128)(2,1)} %copy-done.21, bf16[512,640]{1,0:T(8,128)(2,1)} %copy-done.22, f32[512,640]{1,0:T(8,128)} %get-tuple-element.66.refs_3_, bf16[512,640]{1,0:T(8,128)(2,1)} %copy-done.19, ...), custom_call_target="tpu_custom_call" | custom-call | flops 67108864 | bytes 7340032 | tf_op jit(solution)/shard_map/pallas_call | solution.py:545
  (169 shorter events, 88.0 us)
Async XLA Ops:
  15.7 49.2 %all-to-all-start = ((bf16[8,256,512]{2,1,0:T(8,128)(2,1)}), bf16[8,256,512]{2,1,0:T(8,128)(2,1)S(1)}, u32[]{:S(2)}, u32[]{:S(2)}) async-start(bf16[8,256,512]{2,1,0:T(8,128)(2,1)} %get-tuple-element.53), calls=%async_computation | async-start | bytes 4194304 | tf_op jit(solution)/shard_map/all_to_all | solution.py:598
  21.4 206.6 %all-gather.3.cloned.1.call-start = ((), (), s32[]{:S(2)}) async-start(), calls=%async_computation.4 | async-start | bytes 9437184 | tf_op jit(solution)/shard_map/all_gather | solution.py:608
  23.0 15.6 %collective-permute-start.1 = (bf16[1024,256]{1,0:T(8,128)(2,1)S(1)}, bf16[1024,256]{1,0:T(8,128)(2,1)S(1)}, u32[]{:S(2)}, u32[]{:S(2)}) collective-permute-start(bf16[1024,256]{1,0:T(8,128)(2,1)S(1)} %copy-done.23), channel_id=1, source_target_pairs={{0,3},{1,0},{2,1},{3,2},{4,7},{5,4},{6,5},{7,6},{8,11},{9,8},{10,9... | collective-permute-start | bytes 1572872 | tf_op jit(solution)/shard_map/ppermute | solution.py:37
  24.7 15.6 %collective-permute-start.4 = (bf16[1024,256]{1,0:T(8,128)(2,1)}, bf16[1024,256]{1,0:T(8,128)(2,1)S(1)}, u32[]{:S(2)}, u32[]{:S(2)}) collective-permute-start(bf16[1024,256]{1,0:T(8,128)(2,1)} %get-tuple-element.40.refs_5_), channel_id=1, source_target_pairs={{0,4},{4,8},{8,12},{12,0},{1,5},{5,9},{9,13},{13,1},{2,6},{6,10},{... | collective-permute-start | bytes 1572872 | tf_op jit(solution)/shard_map/ppermute | solution.py:37
  26.3 17.6 %collective-permute-start.5 = (bf16[1024,256]{1,0:T(8,128)(2,1)}, bf16[1024,256]{1,0:T(8,128)(2,1)S(1)}, u32[]{:S(2)}, u32[]{:S(2)}) collective-permute-start(bf16[1024,256]{1,0:T(8,128)(2,1)} %get-tuple-element.40.refs_5_), channel_id=1, source_target_pairs={{0,12},{4,0},{8,4},{12,8},{1,13},{5,1},{9,5},{13,9},{2,14},{6,2},{... | collective-permute-start | bytes 1572872 | tf_op jit(solution)/shard_map/ppermute | solution.py:37
  28.0 19.9 %collective-permute-start.10 = (bf16[512,256]{1,0:T(8,128)(2,1)}, bf16[512,256]{1,0:T(8,128)(2,1)S(1)}, u32[]{:S(2)}, u32[]{:S(2)}) collective-permute-start(bf16[512,256]{1,0:T(8,128)(2,1)} %get-tuple-element.43), channel_id=1, source_target_pairs={{0,8},{4,12},{8,0},{12,4},{1,9},{5,13},{9,1},{13,5},{2,10},{6,14},... | collective-permute-start | bytes 786440 | tf_op jit(solution)/shard_map/ppermute | solution.py:37
  68.5 34.5 %collective-permute-start.11 = (bf16[1024,512]{1,0:T(8,128)(2,1)S(1)}, bf16[1024,512]{1,0:T(8,128)(2,1)}, u32[]{:S(2)}, u32[]{:S(2)}) collective-permute-start(bf16[1024,512]{1,0:T(8,128)(2,1)S(1)} %copy-done.2), channel_id=1, source_target_pairs={{0,4},{4,8},{8,12},{12,0},{1,5},{5,9},{9,13},{13,1},{2,6},{6,10},{... | collective-permute-start | bytes 3145736 | tf_op jit(solution)/shard_map/ppermute | solution.py:37
  68.8 35.4 %collective-permute-start.13 = (bf16[1024,512]{1,0:T(8,128)(2,1)}, bf16[1024,512]{1,0:T(8,128)(2,1)}, u32[]{:S(2)}, u32[]{:S(2)}) collective-permute-start(bf16[1024,512]{1,0:T(8,128)(2,1)} %get-tuple-element.45.refs_1_), channel_id=1, source_target_pairs={{0,12},{4,0},{8,4},{12,8},{1,13},{5,1},{9,5},{13,9},{2,14},{6,2},{... | collective-permute-start | bytes 3145736 | tf_op jit(solution)/shard_map/ppermute | solution.py:37
  72.2 52.1 %collective-permute-start.15 = (bf16[1024,512]{1,0:T(8,128)(2,1)}, bf16[1024,512]{1,0:T(8,128)(2,1)}, u32[]{:S(2)}, u32[]{:S(2)}) collective-permute-start(bf16[1024,512]{1,0:T(8,128)(2,1)} %get-tuple-element.46.refs_2_), channel_id=1, source_target_pairs={{0,1},{1,2},{2,3},{3,0},{4,5},{5,6},{6,7},{7,4},{8,9},{9,10},{10,1... | collective-permute-start | bytes 3145736 | tf_op jit(solution)/shard_map/ppermute | solution.py:37
  78.3 35.5 %all-to-all-start.1 = ((f32[16,64,192]{2,1,0:T(8,128)}), f32[16,64,192]{2,1,0:T(8,128)S(1)}, u32[]{:S(2)}, u32[]{:S(2)}) async-start(f32[16,64,192]{2,1,0:T(8,128)} %bitcast.79), calls=%async_computation.1 | async-start | bytes 2097152 | tf_op jit(solution)/shard_map/all_to_all | solution.py:221
  83.2 44.3 %collective-permute-start.17 = (bf16[1024,512]{1,0:T(8,128)(2,1)}, bf16[1024,512]{1,0:T(8,128)(2,1)}, u32[]{:S(2)}, u32[]{:S(2)}) collective-permute-start(bf16[1024,512]{1,0:T(8,128)(2,1)} %get-tuple-element.47.refs_3_), channel_id=1, source_target_pairs={{0,3},{1,0},{2,1},{3,2},{4,7},{5,4},{6,5},{7,6},{8,11},{9,8},{10,9... | collective-permute-start | bytes 3145736 | tf_op jit(solution)/shard_map/ppermute | solution.py:37
  86.4 45.8 %collective-permute-start.19 = (bf16[1024,512]{1,0:T(8,128)(2,1)}, bf16[1024,512]{1,0:T(8,128)(2,1)}, u32[]{:S(2)}, u32[]{:S(2)}) collective-permute-start(bf16[1024,512]{1,0:T(8,128)(2,1)} %get-tuple-element.45.refs_1_), channel_id=1, source_target_pairs={{0,4},{4,8},{8,12},{12,0},{1,5},{5,9},{9,13},{13,1},{2,6},{6,10},{... | collective-permute-start | bytes 3145736 | tf_op jit(solution)/shard_map/ppermute | solution.py:37
  103.0 29.6 %collective-permute-start.20 = (bf16[1024,512]{1,0:T(8,128)(2,1)S(1)}, bf16[1024,512]{1,0:T(8,128)(2,1)}, u32[]{:S(2)}, u32[]{:S(2)}) collective-permute-start(bf16[1024,512]{1,0:T(8,128)(2,1)S(1)} %copy-done.3), channel_id=1, source_target_pairs={{0,12},{4,0},{8,4},{12,8},{1,13},{5,1},{9,5},{13,9},{2,14},{6,2},{... | collective-permute-start | bytes 3145736 | tf_op jit(solution)/shard_map/ppermute | solution.py:37
  104.2 31.9 %collective-permute-start.21 = (bf16[1024,512]{1,0:T(8,128)(2,1)}, bf16[1024,512]{1,0:T(8,128)(2,1)}, u32[]{:S(2)}, u32[]{:S(2)}) collective-permute-start(bf16[1024,512]{1,0:T(8,128)(2,1)} %get-tuple-element.47.refs_3_), channel_id=1, source_target_pairs={{0,1},{1,2},{2,3},{3,0},{4,5},{5,6},{6,7},{7,4},{8,9},{9,10},{10,1... | collective-permute-start | bytes 3145736 | tf_op jit(solution)/shard_map/ppermute | solution.py:37
  116.9 22.3 %all-to-all-start.2 = ((bf16[16,64,192]{2,1,0:T(8,128)(2,1)}), bf16[16,64,192]{2,1,0:T(8,128)(2,1)S(1)}, u32[]{:S(2)}, u32[]{:S(2)}) async-start(bf16[16,64,192]{2,1,0:T(8,128)(2,1)} %get-tuple-element.55), calls=%async_computation.2 | async-start | bytes 1048576 | tf_op jit(solution)/shard_map/all_to_all | solution.py:657
  124.4 31.9 %collective-permute-start.22 = (bf16[1024,512]{1,0:T(8,128)(2,1)}, bf16[1024,512]{1,0:T(8,128)(2,1)}, u32[]{:S(2)}, u32[]{:S(2)}) collective-permute-start(bf16[1024,512]{1,0:T(8,128)(2,1)} %get-tuple-element.46.refs_2_), channel_id=1, source_target_pairs={{0,3},{1,0},{2,1},{3,2},{4,7},{5,4},{6,5},{7,6},{8,11},{9,8},{10,9... | collective-permute-start | bytes 3145736 | tf_op jit(solution)/shard_map/ppermute | solution.py:37
  127.6 37.4 %collective-permute-start.12 = (bf16[1024,512]{1,0:T(8,128)(2,1)}, bf16[1024,512]{1,0:T(8,128)(2,1)S(1)}, u32[]{:S(2)}, u32[]{:S(2)}) collective-permute-start(bf16[1024,512]{1,0:T(8,128)(2,1)} %collective-permute-done.11.refs_0_), channel_id=1, source_target_pairs={{0,4},{4,8},{8,12},{12,0},{1,5},{5,9},{9,13},{13,1},{2,6},{6,10},{... | collective-permute-start | bytes 3145736 | tf_op jit(solution)/shard_map/ppermute | solution.py:37
  132.2 32.8 %collective-permute-start.14 = (bf16[1024,512]{1,0:T(8,128)(2,1)}, bf16[1024,512]{1,0:T(8,128)(2,1)}, u32[]{:S(2)}, u32[]{:S(2)}) collective-permute-start(bf16[1024,512]{1,0:T(8,128)(2,1)} %collective-permute-done.13.refs_1_), channel_id=1, source_target_pairs={{0,12},{4,0},{8,4},{12,8},{1,13},{5,1},{9,5},{13,9},{2,14},{6,2},{... | collective-permute-start | bytes 3145736 | tf_op jit(solution)/shard_map/ppermute | solution.py:37
  132.7 32.3 %collective-permute-start.16 = (bf16[1024,512]{1,0:T(8,128)(2,1)}, bf16[1024,512]{1,0:T(8,128)(2,1)}, u32[]{:S(2)}, u32[]{:S(2)}) collective-permute-start(bf16[1024,512]{1,0:T(8,128)(2,1)} %collective-permute-done.15.refs_2_), channel_id=1, source_target_pairs={{0,1},{1,2},{2,3},{3,0},{4,5},{5,6},{6,7},{7,4},{8,9},{9,10},{10,1... | collective-permute-start | bytes 3145736 | tf_op jit(solution)/shard_map/ppermute | solution.py:37
  136.1 31.6 %collective-permute-start.18 = (bf16[1024,512]{1,0:T(8,128)(2,1)}, bf16[1024,512]{1,0:T(8,128)(2,1)}, u32[]{:S(2)}, u32[]{:S(2)}) collective-permute-start(bf16[1024,512]{1,0:T(8,128)(2,1)} %collective-permute-done.17.refs_3_), channel_id=1, source_target_pairs={{0,3},{1,0},{2,1},{3,2},{4,7},{5,4},{6,5},{7,6},{8,11},{9,8},{10,9... | collective-permute-start | bytes 3145736 | tf_op jit(solution)/shard_map/ppermute | solution.py:37
  139.2 28.6 %all-to-all-start.3 = ((bf16[8,64,1152]{2,1,0:T(8,128)(2,1)}), bf16[8,64,1152]{2,1,0:T(8,128)(2,1)S(1)}, u32[]{:S(2)}, u32[]{:S(2)}) async-start(bf16[8,64,1152]{2,1,0:T(8,128)(2,1)} %get-tuple-element.56), calls=%async_computation.3 | async-start | bytes 2359296 | tf_op jit(solution)/shard_map/all_to_all | solution.py:633
  190.1 17.0 %collective-permute-start.33 = (bf16[512,640]{1,0:T(8,128)(2,1)}, bf16[512,640]{1,0:T(8,128)(2,1)S(1)}, u32[]{:S(2)}, u32[]{:S(2)}) collective-permute-start(bf16[512,640]{1,0:T(8,128)(2,1)} %shard_map.149.refs_0_), channel_id=1, source_target_pairs={{0,12},{4,0},{8,4},{12,8},{1,13},{5,1},{9,5},{13,9},{2,14},{6,2},{... | collective-permute-start | bytes 1966088 | tf_op jit(solution)/shard_map/ppermute | solution.py:37
  192.8 17.9 %collective-permute-start.32 = (bf16[512,640]{1,0:T(8,128)(2,1)}, bf16[512,640]{1,0:T(8,128)(2,1)S(1)}, u32[]{:S(2)}, u32[]{:S(2)}) collective-permute-start(bf16[512,640]{1,0:T(8,128)(2,1)} %shard_map.149.refs_0_), channel_id=1, source_target_pairs={{0,4},{4,8},{8,12},{12,0},{1,5},{5,9},{9,13},{13,1},{2,6},{6,10},{... | collective-permute-start | bytes 1966088 | tf_op jit(solution)/shard_map/ppermute | solution.py:37
  199.4 21.7 %collective-permute-start.25 = (bf16[512,640]{1,0:T(8,128)(2,1)}, bf16[512,640]{1,0:T(8,128)(2,1)S(1)}, u32[]{:S(2)}, u32[]{:S(2)}) collective-permute-start(bf16[512,640]{1,0:T(8,128)(2,1)} %shard_map.145.refs_0_), channel_id=1, source_target_pairs={{0,12},{4,0},{8,4},{12,8},{1,13},{5,1},{9,5},{13,9},{2,14},{6,2},{... | collective-permute-start | bytes 1966088 | tf_op jit(solution)/shard_map/ppermute | solution.py:37
  202.7 21.9 %collective-permute-start.24 = (bf16[512,640]{1,0:T(8,128)(2,1)}, bf16[512,640]{1,0:T(8,128)(2,1)S(1)}, u32[]{:S(2)}, u32[]{:S(2)}) collective-permute-start(bf16[512,640]{1,0:T(8,128)(2,1)} %shard_map.145.refs_0_), channel_id=1, source_target_pairs={{0,4},{4,8},{8,12},{12,0},{1,5},{5,9},{9,13},{13,1},{2,6},{6,10},{... | collective-permute-start | bytes 1966088 | tf_op jit(solution)/shard_map/ppermute | solution.py:37
  207.2 20.8 %collective-permute-start.35 = (bf16[512,384]{1,0:T(8,128)(2,1)S(1)}, bf16[512,384]{1,0:T(8,128)(2,1)}, u32[]{:S(2)}, u32[]{:S(2)}) collective-permute-start(bf16[512,384]{1,0:T(8,128)(2,1)S(1)} %slice.39), channel_id=1, source_target_pairs={{0,12},{4,0},{8,4},{12,8},{1,13},{5,1},{9,5},{13,9},{2,14},{6,2},{... | collective-permute-start | bytes 1179656 | tf_op jit(solution)/shard_map/ppermute | solution.py:37
  211.5 15.9 %collective-permute-start.34 = (bf16[512,256]{1,0:T(8,128)(2,1)}, bf16[512,256]{1,0:T(8,128)(2,1)}, u32[]{:S(2)}, u32[]{:S(2)}) collective-permute-start(bf16[512,256]{1,0:T(8,128)(2,1)} %slice.38), channel_id=1, source_target_pairs={{0,4},{4,8},{8,12},{12,0},{1,5},{5,9},{9,13},{13,1},{2,6},{6,10},{... | collective-permute-start | bytes 786440 | tf_op jit(solution)/shard_map/ppermute | solution.py:37
  221.2 19.4 %collective-permute-start.27 = (bf16[512,384]{1,0:T(8,128)(2,1)S(1)}, bf16[512,384]{1,0:T(8,128)(2,1)}, u32[]{:S(2)}, u32[]{:S(2)}) collective-permute-start(bf16[512,384]{1,0:T(8,128)(2,1)S(1)} %slice.37), channel_id=1, source_target_pairs={{0,12},{4,0},{8,4},{12,8},{1,13},{5,1},{9,5},{13,9},{2,14},{6,2},{... | collective-permute-start | bytes 1179656 | tf_op jit(solution)/shard_map/ppermute | solution.py:37
  238.6 22.5 %collective-permute-start.36 = (bf16[512,384]{1,0:T(8,128)(2,1)}, bf16[512,384]{1,0:T(8,128)(2,1)S(1)}, u32[]{:S(2)}, u32[]{:S(2)}) collective-permute-start(bf16[512,384]{1,0:T(8,128)(2,1)} %get-tuple-element.68), channel_id=1, source_target_pairs={{0,1},{1,2},{2,3},{3,0},{4,5},{5,6},{6,7},{7,4},{8,9},{9,10},{10,1... | collective-permute-start | bytes 1179656 | tf_op jit(solution)/shard_map/ppermute | solution.py:37
  251.2 17.1 %collective-permute-start.28 = (bf16[512,384]{1,0:T(8,128)(2,1)}, bf16[512,384]{1,0:T(8,128)(2,1)S(1)}, u32[]{:S(2)}, u32[]{:S(2)}) collective-permute-start(bf16[512,384]{1,0:T(8,128)(2,1)} %get-tuple-element.61), channel_id=1, source_target_pairs={{0,1},{1,2},{2,3},{3,0},{4,5},{5,6},{6,7},{7,4},{8,9},{9,10},{10,1... | collective-permute-start | bytes 1179656 | tf_op jit(solution)/shard_map/ppermute | solution.py:37
  264.6 17.2 %collective-permute-start.38 = (bf16[512,640]{1,0:T(8,128)(2,1)}, bf16[512,640]{1,0:T(8,128)(2,1)S(1)}, u32[]{:S(2)}, u32[]{:S(2)}) collective-permute-start(bf16[512,640]{1,0:T(8,128)(2,1)} %get-tuple-element.71), channel_id=1, source_target_pairs={{0,3},{1,0},{2,1},{3,2},{4,7},{5,4},{6,5},{7,6},{8,11},{9,8},{10,9... | collective-permute-start | bytes 1966088 | tf_op jit(solution)/shard_map/ppermute | solution.py:37
  271.8 17.0 %collective-permute-start.30 = (bf16[512,640]{1,0:T(8,128)(2,1)}, bf16[512,640]{1,0:T(8,128)(2,1)S(1)}, u32[]{:S(2)}, u32[]{:S(2)}) collective-permute-start(bf16[512,640]{1,0:T(8,128)(2,1)} %get-tuple-element.64), channel_id=1, source_target_pairs={{0,3},{1,0},{2,1},{3,2},{4,7},{5,4},{6,5},{7,6},{8,11},{9,8},{10,9... | collective-permute-start | bytes 1966088 | tf_op jit(solution)/shard_map/ppermute | solution.py:37
  (48 other events, 443.2 us)
Sparse Core Ops, SparseCore 0:
  68.6 49.7 all-gather.2

commit v10 on v9

--- a/solution.py
+++ b/solution.py
@@ -45,9 +45,18 @@
     return block, behind, ahead, far_low, far_high
 
 
-def second_gather(low, high, axis):
-    onward = shift(low, axis, 1), shift(high, axis, -1)
-    return onward, (shift(high, axis, 1), shift(low, axis, -1))
+def gather_onward(low, high, axis):
+    return shift(low, axis, 1), shift(high, axis, -1)
+
+
+def gather_next(low, high, axis):
+    return shift(high, axis, 1), shift(low, axis, -1)
+
+
+def ring_gather_whole(block, axis, step):
+    behind = shift(block, axis, 1)
+    ahead = shift(block, axis, -1)
+    return block, behind, ahead, shift(behind if step == 1 else ahead, axis, step)
 
 
 def ring_order(index):
@@ -405,96 +414,64 @@
 
 def output_partial(shards, pieces, weights):
     tokens = pieces[0].shape[0]
-    count, (depth, width) = len(shards), weights.shape[1:]
+    count, (depth, width) = len(shards) // 2, weights.shape[1:]
     unit = depth // SIDE
-    far_cut = pieces[3].shape[1]
     whole = 2 * width + HEAD
+    low, high = slice(0, width), slice(width + HEAD, whole)
 
     def body(index_ref, *refs):
-        own, behind, ahead, far_low, far_high, w_low, w_high = refs[:7]
-        out_far_low, out_far_high, out_ahead, out_behind, out_mine, x_all = refs[7:]
+        x_refs, (w_low, w_high) = refs[:SIDE], refs[SIDE : SIDE + 2]
+        outs, x_all = refs[SIDE + 2 : -1], refs[-1]
         step = pl.program_id(0)
 
         @pl.when(step == 0)
         def _():
-            for k, ref in enumerate((own, behind, ahead)):
+            for k, ref in enumerate(x_refs):
                 x_all[:, k * unit : (k + 1) * unit] = ref[:, :unit]
-            x_all[:, 3 * unit : 3 * unit + far_cut] = far_low[...]
-            x_all[:, 3 * unit + far_cut :] = far_high[:, : unit - far_cut]
-            rank = (
-                own[:, unit:].astype(f32)
-                + behind[:, unit:].astype(f32)
-                + ahead[:, unit:].astype(f32)
-                + far_high[:, unit - far_cut :].astype(f32)
-            )
-            for out in (out_far_low, out_ahead, out_behind, out_mine):
+            rank = x_refs[0][:, unit:].astype(f32)
+            for ref in x_refs[1:]:
+                rank = rank + ref[:, unit:].astype(f32)
+            for out in outs:
                 out[:, width : width + HEAD] = rank.astype(out.dtype)
 
         first = jnp.dot(x_all[...], w_low[0], preferred_element_type=f32)
         second = jnp.dot(x_all[...], w_high[0], preferred_element_type=f32)
-        low, high = slice(0, width), slice(width + HEAD, whole)
-
-        @pl.when(step == 0)
-        def _():
-            out_far_low[:, low] = first.astype(bf16)
-            out_far_high[...] = second.astype(bf16)
-
-        for k, out in enumerate((out_ahead, out_behind, out_mine)):
-
-            @pl.when(step == k + 1)
+        for k, out in enumerate(outs):
+
+            @pl.when(step == k)
             def _():
                 out[:, low] = first.astype(out.dtype)
                 out[:, high] = second.astype(out.dtype)
 
-    shapes = [(width + HEAD, bf16), (width, bf16), (whole, bf16), (whole, bf16), (whole, f32)]
-    return pl.pallas_call(
-        body,
-        out_shape=tuple(jax.ShapeDtypeStruct((tokens, w), d) for w, d in shapes),
+    dtypes = [bf16] * (count - 1) + [f32]
+    return pl.pallas_call(
+        body,
+        out_shape=tuple(jax.ShapeDtypeStruct((tokens, whole), d) for d in dtypes),
         grid_spec=pltpu.PrefetchScalarGridSpec(
             num_scalar_prefetch=1,
-            grid=(count // 2,),
+            grid=(count,),
             in_specs=[pl.BlockSpec(p.shape, lambda j, d: (0, 0)) for p in pieces]
             + [pl.BlockSpec((1, depth, width), lambda j, d: (d[2 * j], 0, 0))]
             + [pl.BlockSpec((1, depth, width), lambda j, d: (d[2 * j + 1], 0, 0))],
-            out_specs=[pl.BlockSpec((tokens, w), lambda j, d: (0, 0)) for w, _ in shapes],
+            out_specs=[pl.BlockSpec((tokens, whole), lambda j, d: (0, 0))] * count,
             scratch_shapes=[pltpu.VMEM((tokens, depth), bf16)],
         ),
         compiler_params=params(),
         cost_estimate=cost(
-            2 * tokens * depth * count * width, 2 * depth * (tokens + count * width)
+            4 * tokens * depth * count * width, 2 * depth * (tokens + 2 * count * width)
         ),
     )(jnp.stack(shards).astype(i32), *pieces, weights, weights)
 
 
-def add_far(ahead, via_behind, behind, via_ahead):
-    rows, whole = ahead.shape
-    low = via_behind.shape[1]
-
-    def body(a_ref, va_ref, b_ref, vb_ref, out_a, out_b):
-        out_a[:, :low] = (a_ref[:, :low].astype(f32) + va_ref[...].astype(f32)).astype(bf16)
-        out_a[:, low:] = a_ref[:, low:]
-        out_b[:, :low] = b_ref[:, :low]
-        out_b[:, low:] = (b_ref[:, low:].astype(f32) + vb_ref[...].astype(f32)).astype(bf16)
-
-    arrays = (ahead, via_behind, behind, via_ahead)
-    return pl.pallas_call(
-        body,
-        out_shape=(jax.ShapeDtypeStruct((rows, whole), bf16),) * 2,
-        grid=(1,),
-        in_specs=[pl.BlockSpec(a.shape, lambda i: (0, 0)) for a in arrays],
-        out_specs=[pl.BlockSpec((rows, whole), lambda i: (0, 0))] * 2,
-        compiler_params=params(),
-        cost_estimate=cost(2 * rows * whole, 10 * rows * whole),
-    )(*arrays)
-
-
-def output_ring(pieces, weights, axis):
+def output_ring(pieces, weights, axis, step):
     me, behind, ahead, far = ring_order(lax.axis_index(axis))
     shards = [2 * place + side for place in (far, ahead, behind, me) for side in range(2)]
-    far_low, far_high, to_ahead, to_behind, mine = output_partial(shards, pieces, weights)
-    to_ahead, to_behind = add_far(
-        to_ahead, shift(far_low, axis, 1), to_behind, shift(far_high, axis, -1)
-    )
+    to_far, to_ahead, to_behind, mine = output_partial(shards, pieces, weights)
+    passing = shift(to_far, axis, step)
+    if step == 1:
+        to_ahead = to_ahead + passing
+    else:
+        to_behind = to_behind + passing
     return mine, shift(to_behind, axis, -1), shift(to_ahead, axis, 1)
 
 
@@ -601,13 +578,12 @@
     first_b = ring_gather(x_b, "y", x_b.shape[1] // 2)
 
     got = [sent[0], shift(sent[2], "y", 1), shift(sent[1], "y", -1), shift(sent[3], "y", 2)]
-    low_a, high_a, low_b, high_b = join(
-        [first_a[:2], first_a[2:], first_b[:2], first_b[2:]], got[1:]
-    )
+    halves = [first_a[:2], first_a[2:], first_b[:2], first_b[2:]]
+    low_a, high_a, low_b, high_b = join(halves, got[1:])
+    far_a = gather_onward(low_a, high_a, "y")
+    far_b = gather_onward(low_b, high_b, "x")
     wo_mine = stack_rows(got, [down, low_a])
     wo_all = lax.all_gather(wo_mine, ADAPTER_AXES, axis=0)
-    far_a, next_a = second_gather(low_a, high_a, "y")
-    far_b, next_b = second_gather(low_b, high_b, "x")
 
     def rows_a(k, cols):
         return [(ys[k] * SIDE + xs[j]) * 2 for j in cols]
@@ -628,6 +604,10 @@
         512,
     )
 
+    again = join(halves, [total[1]])
+    next_a = gather_next(again[0], again[1], "y")
+    next_b = gather_next(again[2], again[3], "x")
+
     pieces = scatter_rows(rank_partial(meta, x, down, 3 * rank, [low_a]))
     copies, up_out = share_sum(pieces, up_out, [total[1]])
     up = lax.all_to_all(up_out, ADAPTER_AXES, 0, 0, tiled=True)
@@ -669,7 +649,8 @@
         attended = attention(
             meta, q, shrunk, up, down, mine, other, cosine, sine, cut * each, each
         )
-        parts.append(output_ring(ring_gather(attended, "y", wide // 2), wo_all, "x"))
+        step = 1 - 2 * cut
+        parts.append(output_ring(ring_gather_whole(attended, "y", step), wo_all, "x", step))
     return finish(meta, parts, up, rank, wide)
 
 

time: 305 us -> 307 us (level)
  waiting for transfers between devices: 87.7 us -> 101 us
  starting transfers between devices: 80.6 us -> 69.6 us
    all_to_all x1, waiting for transfers between devices: 0.01 us -> 9.03 us  [scatter_rows(): lax.all_to_all(partial.reshape(ways, rows // ways, rank), TENSOR_AXES, 0,...]
    ppermute x39 -> x35, waiting for transfers between devices: 84.7 us -> 91.4 us  [shift(): lax.ppermute(block, axis, [(i, (i + step) % SIDE) for i in range(SIDE)])]
    ppermute x39 -> x35, starting transfers between devices: 57.1 us -> 50.5 us  [shift(): lax.ppermute(block, axis, [(i, (i + step) % SIDE) for i in range(SIDE)])]
    pallas_call x4 -> x2, Pallas kernels: 26.5 us -> 21.1 us  [output_partial(): pl.pallas_call(body, out_shape=tuple((jax.ShapeDtypeStruct((tokens, whole...]
    pallas_call x1 -> x2, Pallas kernels: 4.76 us -> 9.53 us  [join(): pl.pallas_call(body, out_shape=tuple((jax.ShapeDtypeStruct((tokens, w), b...]
    all_to_all x1, starting transfers between devices: 7.48 us -> 3.57 us  [on_device(): lax.all_to_all(copies, TENSOR_AXES, 0, 0, tiled=True)]
  transfers between devices with their start and end apart: 45 -> 41, of which waited for: 22 -> 16; matrix products, arithmetic and copies ran while one was open for 2% -> 2% of each run, Pallas kernels for 30% -> 29%
where the time goes in v10:
time: 307 us; the launch traced here: 302 us
  Pallas kernels  105 us (34%)
  waiting for transfers between devices  101 us (33%)
  starting transfers between devices  69.6 us (23%)
  between operations  13.8 us (4%)
  local copies, waits for them, and re-layouts  11.5 us (4%)
    ppermute x35, waiting for transfers between devices, shift(): lax.ppermute(block, axis, [(i, (i + step) % SIDE) for i in range(SIDE)])  91.4 us
    ppermute x35, starting transfers between devices, shift(): lax.ppermute(block, axis, [(i, (i + step) % SIDE) for i in range(SIDE)])  50.5 us
    pallas_call x5, Pallas kernels, project(): pl.pallas_call(body, out_shape=tuple((jax.ShapeDtypeStruct((tokens, w), d...  37.9 us
    pallas_call x2, Pallas kernels, output_partial(): pl.pallas_call(body, out_shape=tuple((jax.ShapeDtypeStruct((tokens, whole...  21.1 us
    pallas_call x2, Pallas kernels, attention(): pl.pallas_call(body, out_shape=jax.ShapeDtypeStruct((count * BLOCK, wide...  13.2 us
    pallas_call x2, Pallas kernels, join(): pl.pallas_call(body, out_shape=tuple((jax.ShapeDtypeStruct((tokens, w), b...  9.53 us
    all_to_all x1, waiting for transfers between devices, scatter_rows(): lax.all_to_all(partial.reshape(ways, rows // ways, rank), TENSOR_AXES, 0,...  9.03 us
    unnamed x70, local copies, waits for them, and re-layouts  7.34 us
  transfers between devices with their start and end apart: 41, of which 16 were waited for; matrix products, arithmetic and copies ran while one was open for 2% of the time, Pallas kernels for 29%

profile of v10, /device:TPU:0, one launch (start us, length us, event | category | flops | bytes accessed | tf_op | source)
XLA Modules:
  0.0 302.5 jit_solution(15356184408581291066)
XLA Ops:
  7.9 7.3 %shard_map.136 = (bf16[8,256,512]{2,1,0:T(8,128)(2,1)}, bf16[8,64,1152]{2,1,0:T(8,128)(2,1)}, bf16[1024,256]{1,0:T(8,128)(2,1)}, bf16[1024,256]{1,0:T(8,128)(2,1...) custom-call(s32[12]{0:T(128)} %pad_add_fusion.pick_ref, ...), custom_call_target="tpu_custom_call" | custom-call | bytes 6553600 | tf_op jit(solution)/shard_map/pallas_call | solution.py:96
  15.2 5.9 %all-to-all-start = ((bf16[8,256,512]{2,1,0:T(8,128)(2,1)}), bf16[8,256,512]{2,1,0:T(8,128)(2,1)S(1)}, u32[]{:S(2)}, u32[]{:S(2)}) async-start(bf16[8,256,512]{2,1,0:T(8,128)(2,1)} %get-tuple-element.55), calls=%async_computation | async-start | bytes 4194304 | tf_op jit(solution)/shard_map/all_to_all | solution.py:575
  29.6 7.0 %collective-permute-done.refs_1_ = bf16[1024,256]{1,0:T(8,128)(2,1)S(1)} collective-permute-done((bf16[1024,256]{1,0:T(8,128)(2,1)S(1)}, bf16[1024,256]{1,0:T(8,128)(2,1)S(1)}, u32[]{:S(2)}, u32[]{:S(2)}) %collective-permute-start) | collective-permute-done | bytes 524320 | tf_op jit(solution)/shard_map/ppermute | solution.py:37
  43.5 3.8 %collective-permute-done.10.refs_12_.refs_3_ = bf16[512,256]{1,0:T(8,128)(2,1)S(1)} collective-permute-done((bf16[512,256]{1,0:T(8,128)(2,1)}, bf16[512,256]{1,0:T(8,128)(2,1)S(1)}, u32[]{:S(2)}, u32[]{:S(2)}) %collective-permute-start.10) | collective-permute-done | bytes 262176 | tf_op jit(solution)/shard_map/ppermute | solution.py:37
  48.8 3.0 %collective-permute-done.8.refs_10_.refs_1_ = bf16[512,256]{1,0:T(8,128)(2,1)S(1)} collective-permute-done((bf16[512,256]{1,0:T(8,128)(2,1)}, bf16[512,256]{1,0:T(8,128)(2,1)S(1)}, u32[]{:S(2)}, u32[]{:S(2)}) %collective-permute-start.8) | collective-permute-done | bytes 262176 | tf_op jit(solution)/shard_map/ppermute | solution.py:37
  53.6 3.3 %collective-permute-done.6.refs_8_ = bf16[1024,128]{1,0:T(8,128)(2,1)S(1)} collective-permute-done((bf16[1024,128]{1,0:T(8,128)(2,1)S(1)}, bf16[1024,128]{1,0:T(8,128)(2,1)S(1)}, u32[]{:S(2)}, u32[]{:S(2)}) %collective-permute-start.6) | collective-permute-done | bytes 262176 | tf_op jit(solution)/shard_map/ppermute | solution.py:37
  59.7 4.7 %shard_map.137 = (bf16[1024,512]{1,0:T(8,128)(2,1)}, bf16[1024,512]{1,0:T(8,128)(2,1)}, bf16[1024,512]{1,0:T(8,128)(2,1)}, bf16[1024,512]{1,0:T(8,128)(2,1)}) custom-call(bf16[1024,256]{1,0:T(8,128)(2,1)} %get-tuple-element.37.refs_0_, bf16[1024,256]{1,0:T(8,128)(2,1)} %copy-done.6, bf16[1024,256]{1,0:T(8,128)(2,1)} %copy-done.7, ...), custom_call_target="tpu_custom_call" | custom-call | bytes 8388608 | tf_op jit(solution)/shard_map/pallas_call | solution.py:188
  76.3 5.1 %shard_map.143 = f32[1024,192]{1,0:T(8,128)} custom-call(s32[5,8]{1,0:T(8,128)} %stack.169.meta_ref, bf16[1024,512]{1,0:T(8,128)(2,1)} %x_ref.3, bf16[8,256,512]{2,1,0:T(8,128)(2,1)} %copy-done, bf16[8,256,512]{2,1,0:T(8,128)(2,1)} %copy-done, bf16[1024,512]{1,0:T(8,128)(2,1)} %get-tuple-element.42.refs_0_.rest_2_.refs_5_), custom_call_target="tpu_custom_call" | custom-call | flops 201326592 | bytes 2621440 | tf_op jit(solution)/shard_map/pallas_call | solution.py:156
  81.4 3.7 %all-to-all-start.1 = ((f32[16,64,192]{2,1,0:T(8,128)}), f32[16,64,192]{2,1,0:T(8,128)S(1)}, u32[]{:S(2)}, u32[]{:S(2)}) async-start(f32[16,64,192]{2,1,0:T(8,128)} %bitcast.79), calls=%async_computation.1 | async-start | bytes 2097152 | tf_op jit(solution)/shard_map/all_to_all | solution.py:230
  85.1 8.1 %shard_map.138 = (f32[1024,512]{1,0:T(8,128)}, f32[1024,128]{1,0:T(8,128)}) custom-call(s32[8]{0:T(128)} %stack.210.index_ref, s32[5,8]{1,0:T(8,128)} %stack.169.meta_ref, bf16[1024,512]{1,0:T(8,128)(2,1)} %get-tuple-element.42.refs_0_.rest_2_.refs_5_, bf16[1024,512]{1,0:T(8,128)(2,1)} %get-tuple-element.43.refs_1_, ...), custom_call_target="tpu_custom_call" | custom-call | flops 2684354560 | bytes 12058624 | tf_op jit(solution)/shard_map/pallas_call | solution.py:279
  93.2 4.8 %shard_map.139 = (bf16[1024,512]{1,0:T(8,128)(2,1)}, bf16[1024,512]{1,0:T(8,128)(2,1)}, bf16[1024,512]{1,0:T(8,128)(2,1)}, bf16[1024,512]{1,0:T(8,128)(2,1)}) custom-call(bf16[1024,256]{1,0:T(8,128)(2,1)} %get-tuple-element.37.refs_0_, bf16[1024,256]{1,0:T(8,128)(2,1)} %copy-done.6, bf16[1024,256]{1,0:T(8,128)(2,1)} %copy-done.7, ...), custom_call_target="tpu_custom_call" | custom-call | bytes 8388608 | tf_op jit(solution)/shard_map/pallas_call | solution.py:188
  103.0 9.0 %all-to-all-done.1.p_ref = f32[16,64,192]{2,1,0:T(8,128)S(1)} async-done(((f32[16,64,192]{2,1,0:T(8,128)}), f32[16,64,192]{2,1,0:T(8,128)S(1)}, u32[]{:S(2)}, u32[]{:S(2)}) %all-to-all-start.1) | async-done | bytes 786464 | tf_op jit(solution)/shard_map/all_to_all | solution.py:230
  115.2 3.6 %all-to-all-start.2 = ((bf16[16,64,192]{2,1,0:T(8,128)(2,1)}), bf16[16,64,192]{2,1,0:T(8,128)(2,1)S(1)}, u32[]{:S(2)}, u32[]{:S(2)}) async-start(bf16[16,64,192]{2,1,0:T(8,128)(2,1)} %get-tuple-element.57), calls=%async_computation.2 | async-start | bytes 1048576 | tf_op jit(solution)/shard_map/all_to_all | solution.py:637
  118.8 3.1 %collective-permute-start.22 = (bf16[1024,512]{1,0:T(8,128)(2,1)}, bf16[1024,512]{1,0:T(8,128)(2,1)}, u32[]{:S(2)}, u32[]{:S(2)}) collective-permute-start(bf16[1024,512]{1,0:T(8,128)(2,1)} %get-tuple-element.50), channel_id=1, source_target_pairs={{0,3},{1,0},{2,1},{3,2},{4,7},{5,4},{6,5},{7,6},{8,11},{9,8},{10,9... | collective-permute-start | bytes 3145736 | tf_op jit(solution)/shard_map/ppermute | solution.py:37
  123.4 9.3 %collective-permute-done.19.refs_0_ = bf16[1024,512]{1,0:T(8,128)(2,1)S(1)} collective-permute-done((bf16[1024,512]{1,0:T(8,128)(2,1)}, bf16[1024,512]{1,0:T(8,128)(2,1)S(1)}, u32[]{:S(2)}, u32[]{:S(2)}) %collective-permute-start.19) | collective-permute-done | bytes 1048608 | tf_op jit(solution)/shard_map/ppermute | solution.py:37
  137.6 4.5 %all-to-all-start.3 = ((bf16[8,64,1152]{2,1,0:T(8,128)(2,1)}), bf16[8,64,1152]{2,1,0:T(8,128)(2,1)S(1)}, u32[]{:S(2)}, u32[]{:S(2)}) async-start(bf16[8,64,1152]{2,1,0:T(8,128)(2,1)} %get-tuple-element.58), calls=%async_computation.3 | async-start | bytes 2359296 | tf_op jit(solution)/shard_map/all_to_all | solution.py:613
  144.1 8.6 %shard_map.140 = (f32[1024,512]{1,0:T(8,128)}, f32[1024,128]{1,0:T(8,128)}) custom-call(s32[8]{0:T(128)} %stack.219.index_ref, s32[5,8]{1,0:T(8,128)} %stack.169.meta_ref, bf16[1024,512]{1,0:T(8,128)(2,1)} %collective-permute-done.11.refs_0_, bf16[1024,512]{1,0:T(8,128)(2,1)} %collective-permute-done.13.refs_1_, ...), custom_call_target="tpu_custom_call", output_to_operand_aliasing={{0}: (22, {}), {1}: (23, {})} | custom-call | flops 2684354560 | bytes 12058624 | tf_op jit(solution)/shard_map/pallas_call | solution.py:279
  152.7 8.6 %shard_map.141 = (f32[1024,512]{1,0:T(8,128)}, f32[1024,128]{1,0:T(8,128)}) custom-call(s32[8]{0:T(128)} %stack.201.index_ref, s32[5,8]{1,0:T(8,128)} %stack.169.meta_ref, bf16[1024,512]{1,0:T(8,128)(2,1)} %copy-done.13, bf16[1024,512]{1,0:T(8,128)(2,1)} %collective-permute-done.20.refs_1_, ...), custom_call_target="tpu_custom_call", output_to_operand_aliasing={{0}: (22, {}), {1}: (23, {})} | custom-call | flops 2684354560 | bytes 12058624 | tf_op jit(solution)/shard_map/pallas_call | solution.py:279
  161.3 4.6 %collective-permute-done.18.refs_3_ = bf16[1024,512]{1,0:T(8,128)(2,1)} collective-permute-done((bf16[1024,512]{1,0:T(8,128)(2,1)}, bf16[1024,512]{1,0:T(8,128)(2,1)}, u32[]{:S(2)}, u32[]{:S(2)}) %collective-permute-start.18) | collective-permute-done | bytes 1048608 | tf_op jit(solution)/shard_map/ppermute | solution.py:37
  167.0 5.5 %shard_map.145.m_ref = bf16[1024,128]{1,0:T(8,128)(2,1)} custom-call(s32[8]{0:T(128)} %stack.187.index_ref, s32[5,8]{1,0:T(8,128)} %stack.169.meta_ref, bf16[1024,512]{1,0:T(8,128)(2,1)} %copy-done.4, bf16[1024,512]{1,0:T(8,128)(2,1)} %collective-permute-done.14.refs_1_, bf16[1024,512]{1,0:T(8,128)(2,1)} %collective-permute-done.16.refs_2_, ...), custom_call_target="tpu_custom_call" | custom-call | flops 536870912 | bytes 5767168 | tf_op jit(solution)/shard_map/pallas_call | solution.py:279
  174.0 7.1 %shard_map.142.q_ref = f32[1024,512]{1,0:T(8,128)} custom-call(s32[8]{0:T(128)} %stack.187.index_ref, s32[5,8]{1,0:T(8,128)} %stack.169.meta_ref, bf16[1024,512]{1,0:T(8,128)(2,1)} %copy-done.4, bf16[1024,512]{1,0:T(8,128)(2,1)} %collective-permute-done.14.refs_1_, ...), custom_call_target="tpu_custom_call", output_to_operand_aliasing={{}: (14, {})} | custom-call | flops 2147483648 | bytes 10485760 | tf_op jit(solution)/shard_map/pallas_call | solution.py:279
  181.8 6.6 %shard_map.149.refs_0_ = bf16[512,640]{1,0:T(8,128)(2,1)} custom-call(s32[5,8]{1,0:T(8,128)} %stack.169.meta_ref, f32[1024,512]{1,0:T(8,128)} %shard_map.142.q_ref, bf16[1024,192]{1,0:T(8,128)(2,1)} %bitcast.77, bf16[8,64,1152]{2,1,0:T(8,128)(2,1)} %copy-done.1, bf16[8,256,512]{2,1,0:T(8,128)(2,1)} %copy-done, bf16[1024,128]{1,0:T(8,128)(2,1)} %shard_map.145.m_ref, ...), custom_call_target="tpu_custom_call" | custom-call | flops 402653184 | bytes 2097152 | tf_op jit(solution)/shard_map/pallas_call | solution.py:390
  191.2 6.6 %shard_map.146.refs_0_ = bf16[512,640]{1,0:T(8,128)(2,1)} custom-call(s32[5,8]{1,0:T(8,128)} %stack.169.meta_ref, f32[1024,512]{1,0:T(8,128)} %shard_map.142.q_ref, bf16[1024,192]{1,0:T(8,128)(2,1)} %bitcast.78, bf16[8,64,1152]{2,1,0:T(8,128)(2,1)} %copy-done.1, bf16[8,256,512]{2,1,0:T(8,128)(2,1)} %copy-done, bf16[1024,128]{1,0:T(8,128)(2,1)} %shard_map.145.m_ref, ...), custom_call_target="tpu_custom_call" | custom-call | flops 402653184 | bytes 2097152 | tf_op jit(solution)/shard_map/pallas_call | solution.py:390
  198.6 5.0 %collective-permute-done.31.refs_2_ = bf16[512,640]{1,0:T(8,128)(2,1)S(1)} collective-permute-done((bf16[512,640]{1,0:T(8,128)(2,1)}, bf16[512,640]{1,0:T(8,128)(2,1)S(1)}, u32[]{:S(2)}, u32[]{:S(2)}) %collective-permute-start.31) | collective-permute-done | bytes 655392 | tf_op jit(solution)/shard_map/ppermute | solution.py:37
  206.3 10.6 %collective-permute-done.24.refs_1_ = bf16[512,640]{1,0:T(8,128)(2,1)S(1)} collective-permute-done((bf16[512,640]{1,0:T(8,128)(2,1)}, bf16[512,640]{1,0:T(8,128)(2,1)S(1)}, u32[]{:S(2)}, u32[]{:S(2)}) %collective-permute-start.24) | collective-permute-done | bytes 655392 | tf_op jit(solution)/shard_map/ppermute | solution.py:37
  217.6 13.4 %collective-permute-done.30.refs_1_ = bf16[512,640]{1,0:T(8,128)(2,1)} collective-permute-done((bf16[512,640]{1,0:T(8,128)(2,1)S(1)}, bf16[512,640]{1,0:T(8,128)(2,1)}, u32[]{:S(2)}, u32[]{:S(2)}) %collective-permute-start.30) | collective-permute-done | bytes 655392 | tf_op jit(solution)/shard_map/ppermute | solution.py:37
  231.0 10.6 %shard_map.150 = (bf16[512,640]{1,0:T(8,128)(2,1)}, bf16[512,640]{1,0:T(8,128)(2,1)}, bf16[512,640]{1,0:T(8,128)(2,1)}, f32[512,640]{1,0:T(8,128)}) custom-call(s32[8]{0:T(128)} %stack.178.index_ref, bf16[512,640]{1,0:T(8,128)(2,1)} %shard_map.149.refs_0_, bf16[512,640]{1,0:T(8,128)(2,1)} %collective-permute-done.30.refs_1_, bf16[512,640]{1,0:T(8,128)(2,1)} %copy-done.23, ...), custom_call_target="tpu_custom_call" | custom-call | flops 4294967296 | bytes 10485760 | tf_op jit(solution)/shard_map/pallas_call | solution.py:447
  244.9 10.5 %shard_map.148 = (bf16[512,640]{1,0:T(8,128)(2,1)}, bf16[512,640]{1,0:T(8,128)(2,1)}, bf16[512,640]{1,0:T(8,128)(2,1)}, f32[512,640]{1,0:T(8,128)}) custom-call(s32[8]{0:T(128)} %stack.178.index_ref, bf16[512,640]{1,0:T(8,128)(2,1)} %shard_map.146.refs_0_, bf16[512,640]{1,0:T(8,128)(2,1)} %copy-done.22, bf16[512,640]{1,0:T(8,128)(2,1)} %copy-done.24, ...), custom_call_target="tpu_custom_call" | custom-call | flops 4294967296 | bytes 10485760 | tf_op jit(solution)/shard_map/pallas_call | solution.py:447
  260.9 13.6 %collective-permute-done.28 = bf16[512,640]{1,0:T(8,128)(2,1)S(1)} collective-permute-done((bf16[512,640]{1,0:T(8,128)(2,1)}, bf16[512,640]{1,0:T(8,128)(2,1)S(1)}, u32[]{:S(2)}, u32[]{:S(2)}) %collective-permute-start.28) | collective-permute-done | bytes 655392 | tf_op jit(solution)/shard_map/ppermute | solution.py:37
  274.7 6.9 %collective-permute-done.35.refs_5_ = bf16[512,640]{1,0:T(8,128)(2,1)S(1)} collective-permute-done((bf16[512,640]{1,0:T(8,128)(2,1)S(1)}, bf16[512,640]{1,0:T(8,128)(2,1)S(1)}, u32[]{:S(2)}, u32[]{:S(2)}) %collective-permute-start.35) | collective-permute-done | bytes 655392 | tf_op jit(solution)/shard_map/ppermute | solution.py:37
  281.6 7.0 %collective-permute-done.29.refs_2_ = bf16[512,640]{1,0:T(8,128)(2,1)S(1)} collective-permute-done((bf16[512,640]{1,0:T(8,128)(2,1)S(1)}, bf16[512,640]{1,0:T(8,128)(2,1)S(1)}, u32[]{:S(2)}, u32[]{:S(2)}) %collective-permute-start.29) | collective-permute-done | bytes 655392 | tf_op jit(solution)/shard_map/ppermute | solution.py:37
  289.5 6.2 %shard_map.151 = f32[1024,512]{1,0:T(8,128)} custom-call(s32[5,8]{1,0:T(8,128)} %stack.169.meta_ref, f32[512,640]{1,0:T(8,128)} %get-tuple-element.61.refs_0_, bf16[512,640]{1,0:T(8,128)(2,1)} %copy-done.29, bf16[512,640]{1,0:T(8,128)(2,1)} %copy-done.31, f32[512,640]{1,0:T(8,128)} %get-tuple-element.65.refs_3_, bf16[512,640]{1,0:T(8,128)(2,1)} %copy-done.30, ...), custom_call_target="tpu_custom_call" | custom-call | flops 67108864 | bytes 7340032 | tf_op jit(solution)/shard_map/pallas_call | solution.py:522
  (158 shorter events, 71.1 us)
Async XLA Ops:
  15.2 49.2 %all-to-all-start = ((bf16[8,256,512]{2,1,0:T(8,128)(2,1)}), bf16[8,256,512]{2,1,0:T(8,128)(2,1)S(1)}, u32[]{:S(2)}, u32[]{:S(2)}) async-start(bf16[8,256,512]{2,1,0:T(8,128)(2,1)} %get-tuple-element.55), calls=%async_computation | async-start | bytes 4194304 | tf_op jit(solution)/shard_map/all_to_all | solution.py:575
  21.1 210.0 %all-gather.3.cloned.1.call-start = ((), (), s32[]{:S(2)}) async-start(), calls=%async_computation.4 | async-start | bytes 9437184 | tf_op jit(solution)/shard_map/all_gather | solution.py:586
  21.1 15.6 %collective-permute-start = (bf16[1024,256]{1,0:T(8,128)(2,1)S(1)}, bf16[1024,256]{1,0:T(8,128)(2,1)S(1)}, u32[]{:S(2)}, u32[]{:S(2)}) collective-permute-start(bf16[1024,256]{1,0:T(8,128)(2,1)S(1)} %copy-done.11), channel_id=1, source_target_pairs={{0,1},{1,2},{2,3},{3,0},{4,5},{5,6},{6,7},{7,4},{8,9},{9,10},{10,1... | collective-permute-start | bytes 1572872 | tf_op jit(solution)/shard_map/ppermute | solution.py:37
  22.7 15.6 %collective-permute-start.1 = (bf16[1024,256]{1,0:T(8,128)(2,1)S(1)}, bf16[1024,256]{1,0:T(8,128)(2,1)S(1)}, u32[]{:S(2)}, u32[]{:S(2)}) collective-permute-start(bf16[1024,256]{1,0:T(8,128)(2,1)S(1)} %copy-done.11), channel_id=1, source_target_pairs={{0,3},{1,0},{2,1},{3,2},{4,7},{5,4},{6,5},{7,6},{8,11},{9,8},{10,9... | collective-permute-start | bytes 1572872 | tf_op jit(solution)/shard_map/ppermute | solution.py:37
  24.4 15.6 %collective-permute-start.4 = (bf16[1024,256]{1,0:T(8,128)(2,1)S(1)}, bf16[1024,256]{1,0:T(8,128)(2,1)S(1)}, u32[]{:S(2)}, u32[]{:S(2)}) collective-permute-start(bf16[1024,256]{1,0:T(8,128)(2,1)S(1)} %copy-done.12), channel_id=1, source_target_pairs={{0,4},{4,8},{8,12},{12,0},{1,5},{5,9},{9,13},{13,1},{2,6},{6,10},{... | collective-permute-start | bytes 1572872 | tf_op jit(solution)/shard_map/ppermute | solution.py:37
  26.0 17.0 %collective-permute-start.5 = (bf16[1024,256]{1,0:T(8,128)(2,1)S(1)}, bf16[1024,256]{1,0:T(8,128)(2,1)S(1)}, u32[]{:S(2)}, u32[]{:S(2)}) collective-permute-start(bf16[1024,256]{1,0:T(8,128)(2,1)S(1)} %copy-done.12), channel_id=1, source_target_pairs={{0,12},{4,0},{8,4},{12,8},{1,13},{5,1},{9,5},{13,9},{2,14},{6,2},{... | collective-permute-start | bytes 1572872 | tf_op jit(solution)/shard_map/ppermute | solution.py:37
  27.7 19.7 %collective-permute-start.10 = (bf16[512,256]{1,0:T(8,128)(2,1)}, bf16[512,256]{1,0:T(8,128)(2,1)S(1)}, u32[]{:S(2)}, u32[]{:S(2)}) collective-permute-start(bf16[512,256]{1,0:T(8,128)(2,1)} %get-tuple-element.41), channel_id=1, source_target_pairs={{0,8},{4,12},{8,0},{12,4},{1,9},{5,13},{9,1},{13,5},{2,10},{6,14},... | collective-permute-start | bytes 786440 | tf_op jit(solution)/shard_map/ppermute | solution.py:37
  68.1 31.7 %collective-permute-start.11 = (bf16[1024,512]{1,0:T(8,128)(2,1)S(1)}, bf16[1024,512]{1,0:T(8,128)(2,1)}, u32[]{:S(2)}, u32[]{:S(2)}) collective-permute-start(bf16[1024,512]{1,0:T(8,128)(2,1)S(1)} %copy-done.2), channel_id=1, source_target_pairs={{0,4},{4,8},{8,12},{12,0},{1,5},{5,9},{9,13},{13,1},{2,6},{6,10},{... | collective-permute-start | bytes 3145736 | tf_op jit(solution)/shard_map/ppermute | solution.py:37
  68.4 32.9 %collective-permute-start.13 = (bf16[1024,512]{1,0:T(8,128)(2,1)}, bf16[1024,512]{1,0:T(8,128)(2,1)}, u32[]{:S(2)}, u32[]{:S(2)}) collective-permute-start(bf16[1024,512]{1,0:T(8,128)(2,1)} %get-tuple-element.43.refs_1_), channel_id=1, source_target_pairs={{0,12},{4,0},{8,4},{12,8},{1,13},{5,1},{9,5},{13,9},{2,14},{6,2},{... | collective-permute-start | bytes 3145736 | tf_op jit(solution)/shard_map/ppermute | solution.py:37
  73.1 45.7 %collective-permute-start.15 = (bf16[1024,512]{1,0:T(8,128)(2,1)}, bf16[1024,512]{1,0:T(8,128)(2,1)}, u32[]{:S(2)}, u32[]{:S(2)}) collective-permute-start(bf16[1024,512]{1,0:T(8,128)(2,1)} %get-tuple-element.44.refs_2_), channel_id=1, source_target_pairs={{0,1},{1,2},{2,3},{3,0},{4,5},{5,6},{6,7},{7,4},{8,9},{9,10},{10,1... | collective-permute-start | bytes 3145736 | tf_op jit(solution)/shard_map/ppermute | solution.py:37
  73.3 48.5 %collective-permute-start.17 = (bf16[1024,512]{1,0:T(8,128)(2,1)}, bf16[1024,512]{1,0:T(8,128)(2,1)}, u32[]{:S(2)}, u32[]{:S(2)}) collective-permute-start(bf16[1024,512]{1,0:T(8,128)(2,1)} %get-tuple-element.45.refs_3_), channel_id=1, source_target_pairs={{0,3},{1,0},{2,1},{3,2},{4,7},{5,4},{6,5},{7,6},{8,11},{9,8},{10,9... | collective-permute-start | bytes 3145736 | tf_op jit(solution)/shard_map/ppermute | solution.py:37
  81.4 30.7 %all-to-all-start.1 = ((f32[16,64,192]{2,1,0:T(8,128)}), f32[16,64,192]{2,1,0:T(8,128)S(1)}, u32[]{:S(2)}, u32[]{:S(2)}) async-start(f32[16,64,192]{2,1,0:T(8,128)} %bitcast.79), calls=%async_computation.1 | async-start | bytes 2097152 | tf_op jit(solution)/shard_map/all_to_all | solution.py:230
  98.0 34.7 %collective-permute-start.19 = (bf16[1024,512]{1,0:T(8,128)(2,1)}, bf16[1024,512]{1,0:T(8,128)(2,1)S(1)}, u32[]{:S(2)}, u32[]{:S(2)}) collective-permute-start(bf16[1024,512]{1,0:T(8,128)(2,1)} %get-tuple-element.47), channel_id=1, source_target_pairs={{0,4},{4,8},{8,12},{12,0},{1,5},{5,9},{9,13},{13,1},{2,6},{6,10},{... | collective-permute-start | bytes 3145736 | tf_op jit(solution)/shard_map/ppermute | solution.py:37
  99.8 34.1 %collective-permute-start.20 = (bf16[1024,512]{1,0:T(8,128)(2,1)}, bf16[1024,512]{1,0:T(8,128)(2,1)}, u32[]{:S(2)}, u32[]{:S(2)}) collective-permute-start(bf16[1024,512]{1,0:T(8,128)(2,1)} %get-tuple-element.48), channel_id=1, source_target_pairs={{0,12},{4,0},{8,4},{12,8},{1,13},{5,1},{9,5},{13,9},{2,14},{6,2},{... | collective-permute-start | bytes 3145736 | tf_op jit(solution)/shard_map/ppermute | solution.py:37
  101.3 34.6 %collective-permute-start.21 = (bf16[1024,512]{1,0:T(8,128)(2,1)}, bf16[1024,512]{1,0:T(8,128)(2,1)}, u32[]{:S(2)}, u32[]{:S(2)}) collective-permute-start(bf16[1024,512]{1,0:T(8,128)(2,1)} %get-tuple-element.49), channel_id=1, source_target_pairs={{0,1},{1,2},{2,3},{3,0},{4,5},{5,6},{6,7},{7,4},{8,9},{9,10},{10,1... | collective-permute-start | bytes 3145736 | tf_op jit(solution)/shard_map/ppermute | solution.py:37
  115.2 22.4 %all-to-all-start.2 = ((bf16[16,64,192]{2,1,0:T(8,128)(2,1)}), bf16[16,64,192]{2,1,0:T(8,128)(2,1)S(1)}, u32[]{:S(2)}, u32[]{:S(2)}) async-start(bf16[16,64,192]{2,1,0:T(8,128)(2,1)} %get-tuple-element.57), calls=%async_computation.2 | async-start | bytes 1048576 | tf_op jit(solution)/shard_map/all_to_all | solution.py:637
  118.8 33.9 %collective-permute-start.22 = (bf16[1024,512]{1,0:T(8,128)(2,1)}, bf16[1024,512]{1,0:T(8,128)(2,1)}, u32[]{:S(2)}, u32[]{:S(2)}) collective-permute-start(bf16[1024,512]{1,0:T(8,128)(2,1)} %get-tuple-element.50), channel_id=1, source_target_pairs={{0,3},{1,0},{2,1},{3,2},{4,7},{5,4},{6,5},{7,6},{8,11},{9,8},{10,9... | collective-permute-start | bytes 3145736 | tf_op jit(solution)/shard_map/ppermute | solution.py:37
  121.9 39.4 %collective-permute-start.12 = (bf16[1024,512]{1,0:T(8,128)(2,1)}, bf16[1024,512]{1,0:T(8,128)(2,1)S(1)}, u32[]{:S(2)}, u32[]{:S(2)}) collective-permute-start(bf16[1024,512]{1,0:T(8,128)(2,1)} %collective-permute-done.11.refs_0_), channel_id=1, source_target_pairs={{0,4},{4,8},{8,12},{12,0},{1,5},{5,9},{9,13},{13,1},{2,6},{6,10},{... | collective-permute-start | bytes 3145736 | tf_op jit(solution)/shard_map/ppermute | solution.py:37
  132.7 28.6 %collective-permute-start.14 = (bf16[1024,512]{1,0:T(8,128)(2,1)}, bf16[1024,512]{1,0:T(8,128)(2,1)}, u32[]{:S(2)}, u32[]{:S(2)}) collective-permute-start(bf16[1024,512]{1,0:T(8,128)(2,1)} %collective-permute-done.13.refs_1_), channel_id=1, source_target_pairs={{0,12},{4,0},{8,4},{12,8},{1,13},{5,1},{9,5},{13,9},{2,14},{6,2},{... | collective-permute-start | bytes 3145736 | tf_op jit(solution)/shard_map/ppermute | solution.py:37
  134.0 27.4 %collective-permute-start.16 = (bf16[1024,512]{1,0:T(8,128)(2,1)}, bf16[1024,512]{1,0:T(8,128)(2,1)}, u32[]{:S(2)}, u32[]{:S(2)}) collective-permute-start(bf16[1024,512]{1,0:T(8,128)(2,1)} %collective-permute-done.15.refs_2_), channel_id=1, source_target_pairs={{0,1},{1,2},{2,3},{3,0},{4,5},{5,6},{6,7},{7,4},{8,9},{9,10},{10,1... | collective-permute-start | bytes 3145736 | tf_op jit(solution)/shard_map/ppermute | solution.py:37
  135.9 30.1 %collective-permute-start.18 = (bf16[1024,512]{1,0:T(8,128)(2,1)}, bf16[1024,512]{1,0:T(8,128)(2,1)}, u32[]{:S(2)}, u32[]{:S(2)}) collective-permute-start(bf16[1024,512]{1,0:T(8,128)(2,1)} %collective-permute-done.17.refs_3_), channel_id=1, source_target_pairs={{0,3},{1,0},{2,1},{3,2},{4,7},{5,4},{6,5},{7,6},{8,11},{9,8},{10,9... | collective-permute-start | bytes 3145736 | tf_op jit(solution)/shard_map/ppermute | solution.py:37
  137.6 28.3 %all-to-all-start.3 = ((bf16[8,64,1152]{2,1,0:T(8,128)(2,1)}), bf16[8,64,1152]{2,1,0:T(8,128)(2,1)S(1)}, u32[]{:S(2)}, u32[]{:S(2)}) async-start(bf16[8,64,1152]{2,1,0:T(8,128)(2,1)} %get-tuple-element.58), calls=%async_computation.3 | async-start | bytes 2359296 | tf_op jit(solution)/shard_map/all_to_all | solution.py:613
  197.8 19.1 %collective-permute-start.24 = (bf16[512,640]{1,0:T(8,128)(2,1)}, bf16[512,640]{1,0:T(8,128)(2,1)S(1)}, u32[]{:S(2)}, u32[]{:S(2)}) collective-permute-start(bf16[512,640]{1,0:T(8,128)(2,1)} %shard_map.146.refs_0_), channel_id=1, source_target_pairs={{0,4},{4,8},{8,12},{12,0},{1,5},{5,9},{9,13},{13,1},{2,6},{6,10},{... | collective-permute-start | bytes 1966088 | tf_op jit(solution)/shard_map/ppermute | solution.py:37
  197.8 33.2 %collective-permute-start.30 = (bf16[512,640]{1,0:T(8,128)(2,1)S(1)}, bf16[512,640]{1,0:T(8,128)(2,1)}, u32[]{:S(2)}, u32[]{:S(2)}) collective-permute-start(bf16[512,640]{1,0:T(8,128)(2,1)S(1)} %copy-done.10), channel_id=1, source_target_pairs={{0,4},{4,8},{8,12},{12,0},{1,5},{5,9},{9,13},{13,1},{2,6},{6,10},{... | collective-permute-start | bytes 1966088 | tf_op jit(solution)/shard_map/ppermute | solution.py:37
  203.6 27.4 %collective-permute-start.32 = (bf16[512,640]{1,0:T(8,128)(2,1)S(1)}, bf16[512,640]{1,0:T(8,128)(2,1)}, u32[]{:S(2)}, u32[]{:S(2)}) collective-permute-start(bf16[512,640]{1,0:T(8,128)(2,1)S(1)} %collective-permute-done.31.refs_2_), channel_id=1, source_target_pairs={{0,12},{4,0},{8,4},{12,8},{1,13},{5,1},{9,5},{13,9},{2,14},{6,2},{... | collective-permute-start | bytes 1966088 | tf_op jit(solution)/shard_map/ppermute | solution.py:37
  206.3 36.9 %collective-permute-start.25 = (bf16[512,640]{1,0:T(8,128)(2,1)}, bf16[512,640]{1,0:T(8,128)(2,1)S(1)}, u32[]{:S(2)}, u32[]{:S(2)}) collective-permute-start(bf16[512,640]{1,0:T(8,128)(2,1)} %shard_map.146.refs_0_), channel_id=1, source_target_pairs={{0,12},{4,0},{8,4},{12,8},{1,13},{5,1},{9,5},{13,9},{2,14},{6,2},{... | collective-permute-start | bytes 1966088 | tf_op jit(solution)/shard_map/ppermute | solution.py:37
  216.9 26.3 %collective-permute-start.26 = (bf16[512,640]{1,0:T(8,128)(2,1)S(1)}, bf16[512,640]{1,0:T(8,128)(2,1)S(1)}, u32[]{:S(2)}, u32[]{:S(2)}) collective-permute-start(bf16[512,640]{1,0:T(8,128)(2,1)S(1)} %collective-permute-done.24.refs_1_), channel_id=1, source_target_pairs={{0,4},{4,8},{8,12},{12,0},{1,5},{5,9},{9,13},{13,1},{2,6},{6,10},{... | collective-permute-start | bytes 1966088 | tf_op jit(solution)/shard_map/ppermute | solution.py:37
  241.6 17.8 %collective-permute-start.33 = (bf16[512,640]{1,0:T(8,128)(2,1)}, bf16[512,640]{1,0:T(8,128)(2,1)S(1)}, u32[]{:S(2)}, u32[]{:S(2)}) collective-permute-start(bf16[512,640]{1,0:T(8,128)(2,1)} %get-tuple-element.67), channel_id=1, source_target_pairs={{0,3},{1,0},{2,1},{3,2},{4,7},{5,4},{6,5},{7,6},{8,11},{9,8},{10,9... | collective-permute-start | bytes 1966088 | tf_op jit(solution)/shard_map/ppermute | solution.py:37
  255.4 19.1 %collective-permute-start.28 = (bf16[512,640]{1,0:T(8,128)(2,1)}, bf16[512,640]{1,0:T(8,128)(2,1)S(1)}, u32[]{:S(2)}, u32[]{:S(2)}) collective-permute-start(bf16[512,640]{1,0:T(8,128)(2,1)} %get-tuple-element.64), channel_id=1, source_target_pairs={{0,1},{1,2},{2,3},{3,0},{4,5},{5,6},{6,7},{7,4},{8,9},{9,10},{10,1... | collective-permute-start | bytes 1966088 | tf_op jit(solution)/shard_map/ppermute | solution.py:37
  256.2 25.4 %collective-permute-start.35 = (bf16[512,640]{1,0:T(8,128)(2,1)S(1)}, bf16[512,640]{1,0:T(8,128)(2,1)S(1)}, u32[]{:S(2)}, u32[]{:S(2)}) collective-permute-start(bf16[512,640]{1,0:T(8,128)(2,1)S(1)} %copy-done.34), channel_id=1, source_target_pairs={{0,1},{1,2},{2,3},{3,0},{4,5},{5,6},{6,7},{7,4},{8,9},{9,10},{10,1... | collective-permute-start | bytes 1966088 | tf_op jit(solution)/shard_map/ppermute | solution.py:37
  256.8 24.8 %collective-permute-start.27 = (bf16[512,640]{1,0:T(8,128)(2,1)}, bf16[512,640]{1,0:T(8,128)(2,1)S(1)}, u32[]{:S(2)}, u32[]{:S(2)}) collective-permute-start(bf16[512,640]{1,0:T(8,128)(2,1)} %get-tuple-element.62), channel_id=1, source_target_pairs={{0,3},{1,0},{2,1},{3,2},{4,7},{5,4},{6,5},{7,6},{8,11},{9,8},{10,9... | collective-permute-start | bytes 1966088 | tf_op jit(solution)/shard_map/ppermute | solution.py:37
  259.6 22.1 %collective-permute-start.34 = (bf16[512,640]{1,0:T(8,128)(2,1)S(1)}, bf16[512,640]{1,0:T(8,128)(2,1)S(1)}, u32[]{:S(2)}, u32[]{:S(2)}) collective-permute-start(bf16[512,640]{1,0:T(8,128)(2,1)S(1)} %add.296), channel_id=1, source_target_pairs={{0,3},{1,0},{2,1},{3,2},{4,7},{5,4},{6,5},{7,6},{8,11},{9,8},{10,9... | collective-permute-start | bytes 1966088 | tf_op jit(solution)/shard_map/ppermute | solution.py:37
  (44 other events, 418.4 us)
Sparse Core Ops, SparseCore 0:
  68.2 49.6 all-gather.2

commit v11 on v10

--- a/solution.py
+++ b/solution.py
@@ -45,12 +45,11 @@
     return block, behind, ahead, far_low, far_high
 
 
-def gather_onward(low, high, axis):
-    return shift(low, axis, 1), shift(high, axis, -1)
-
-
-def gather_next(low, high, axis):
-    return shift(high, axis, 1), shift(low, axis, -1)
+def ring_gather_rows(block, axis):
+    half = block.shape[0] // 2
+    behind = shift(block, axis, 1)
+    ahead = shift(block, axis, -1)
+    return block, behind, ahead, (shift(behind[:half], axis, 1), shift(ahead[half:], axis, -1))
 
 
 def ring_gather_whole(block, axis, step):
@@ -233,25 +232,36 @@
 
 
 def project(index, total, blocks, weights, tile, last=None, after=(), rows=256):
-    tokens = blocks[0].shape[0]
-    counts = [b.shape[1] // rows for b in blocks]
+    split = isinstance(blocks[0], tuple)
+    columns = [b[0] if split else b for b in blocks]
+    tokens = columns[0].shape[0] * (2 if split else 1)
+    counts = [b.shape[1] // rows for b in columns]
     pieces = sum(counts)
+    inputs = [h for b in blocks for h in b] if split else list(blocks)
     kinds = len(weights)
     first = total is None
     tail, tail_operands, tail_specs, dtype = last or (None, [], [], f32)
 
     def body(index_ref, meta_ref, *refs):
-        x_refs = refs[: len(blocks)]
-        w_refs = refs[len(blocks) : len(blocks) + kinds * pieces]
-        rest = refs[len(blocks) + kinds * pieces :]
+        x_refs = refs[: len(inputs)]
+        w_refs = refs[len(inputs) : len(inputs) + kinds * pieces]
+        rest = refs[len(inputs) + kinds * pieces :]
+        if split:
+            top = pl.program_id(0) == 0
+            xs = [
+                jnp.where(top, x_refs[2 * k][...], x_refs[2 * k + 1][...])
+                for k in range(len(blocks))
+            ]
+        else:
+            xs = [ref[...] for ref in x_refs]
         outs = rest[len(rest) - kinds :]
         for kind in range(kinds):
             mine = w_refs[kind * pieces : (kind + 1) * pieces]
             acc = None if first else rest[kind][...]
             at = 0
-            for x_ref, n in zip(x_refs, counts):
+            for x, n in zip(xs, counts):
                 w = jnp.concatenate([r[...] for r in mine[at : at + n]], axis=0)
-                add = jnp.dot(x_ref[...], w, preferred_element_type=f32)
+                add = jnp.dot(x, w, preferred_element_type=f32)
                 acc = add if acc is None else acc + add
                 at += n
             if tail is not None:
@@ -263,8 +273,11 @@
 
     widths = [w.shape[1] for w in weights]
     row_specs = [pl.BlockSpec((tile, w), lambda i, p, m: (i, 0)) for w in widths]
-    in_specs = [pl.BlockSpec((tile, b.shape[1]), lambda i, p, m: (i, 0)) for b in blocks]
-    operands = list(blocks)
+    def row_block(b):
+        return pl.BlockSpec((tile, b.shape[1]), lambda i, p, m: (0 if split else i, 0))
+
+    in_specs = [row_block(b) for b in inputs]
+    operands = list(inputs)
     for w in weights:
         in_specs += [weight(k, w.shape[1]) for k in range(pieces)]
         operands += [w] * pieces
@@ -412,7 +425,7 @@
     )(meta, q, shrunk, up, down, mine, other, cosine, sine)
 
 
-def output_partial(shards, pieces, weights):
+def output_partial(shards, pieces, weights, after):
     tokens = pieces[0].shape[0]
     count, (depth, width) = len(shards) // 2, weights.shape[1:]
     unit = depth // SIDE
@@ -421,7 +434,7 @@
 
     def body(index_ref, *refs):
         x_refs, (w_low, w_high) = refs[:SIDE], refs[SIDE : SIDE + 2]
-        outs, x_all = refs[SIDE + 2 : -1], refs[-1]
+        outs, x_all = refs[-1 - count : -1], refs[-1]
         step = pl.program_id(0)
 
         @pl.when(step == 0)
@@ -452,7 +465,8 @@
             grid=(count,),
             in_specs=[pl.BlockSpec(p.shape, lambda j, d: (0, 0)) for p in pieces]
             + [pl.BlockSpec((1, depth, width), lambda j, d: (d[2 * j], 0, 0))]
-            + [pl.BlockSpec((1, depth, width), lambda j, d: (d[2 * j + 1], 0, 0))],
+            + [pl.BlockSpec((1, depth, width), lambda j, d: (d[2 * j + 1], 0, 0))]
+            + passive(after),
             out_specs=[pl.BlockSpec((tokens, whole), lambda j, d: (0, 0))] * count,
             scratch_shapes=[pltpu.VMEM((tokens, depth), bf16)],
         ),
@@ -460,19 +474,31 @@
         cost_estimate=cost(
             4 * tokens * depth * count * width, 2 * depth * (tokens + 2 * count * width)
         ),
-    )(jnp.stack(shards).astype(i32), *pieces, weights, weights)
-
-
-def output_ring(pieces, weights, axis, step):
+    )(jnp.stack(shards).astype(i32), *pieces, weights, weights, *after)
+
+
+def handed_on(block, after):
+    return pl.pallas_call(
+        lambda *refs: None,
+        out_shape=jax.ShapeDtypeStruct(block.shape, block.dtype),
+        in_specs=passive([block, *after]),
+        out_specs=pl.BlockSpec(memory_space=pl.ANY),
+        input_output_aliases={0: 0},
+        compiler_params=params(),
+        cost_estimate=cost(0, 0),
+    )(block, *after)
+
+
+def output_ring(pieces, weights, axis, step, after):
     me, behind, ahead, far = ring_order(lax.axis_index(axis))
     shards = [2 * place + side for place in (far, ahead, behind, me) for side in range(2)]
-    to_far, to_ahead, to_behind, mine = output_partial(shards, pieces, weights)
+    to_far, to_ahead, to_behind, mine = output_partial(shards, pieces, weights, after)
     passing = shift(to_far, axis, step)
     if step == 1:
         to_ahead = to_ahead + passing
     else:
         to_behind = to_behind + passing
-    return mine, shift(to_behind, axis, -1), shift(to_ahead, axis, 1)
+    return (mine, shift(to_behind, axis, -1), shift(to_ahead, axis, 1)), to_far
 
 
 def finish(meta, parts, up, rank, wide):
@@ -578,11 +604,10 @@
     first_b = ring_gather(x_b, "y", x_b.shape[1] // 2)
 
     got = [sent[0], shift(sent[2], "y", 1), shift(sent[1], "y", -1), shift(sent[3], "y", 2)]
-    halves = [first_a[:2], first_a[2:], first_b[:2], first_b[2:]]
-    low_a, high_a, low_b, high_b = join(halves, got[1:])
-    far_a = gather_onward(low_a, high_a, "y")
-    far_b = gather_onward(low_b, high_b, "x")
-    wo_mine = stack_rows(got, [down, low_a])
+    flat_a, flat_b = join([first_a, first_b], got[1:])
+    a = ring_gather_rows(flat_a, "y")
+    b = ring_gather_rows(flat_b, "x")
+    wo_mine = stack_rows(got, [down, flat_a])
     wo_all = lax.all_gather(wo_mine, ADAPTER_AXES, axis=0)
 
     def rows_a(k, cols):
@@ -595,48 +620,27 @@
         return jnp.stack(rows).astype(i32)
 
     every = range(SIDE)
-    low, high = (0, 1), (2, 3)
     total = project(
-        (index_of(rows_a(0, every) + rows_b(0, every)), meta),
-        None,
-        [low_a, high_a, low_b, high_b],
+        (index_of(rows_a(0, every) + rows_b(0, every)), meta), None, [a[0], b[0]], [wq, wkv], 512
+    )
+
+    pieces = scatter_rows(rank_partial(meta, x, down, 3 * rank, [flat_a]))
+    copies, up_out = share_sum(pieces, up_out, [total[1]])
+    up = lax.all_to_all(up_out, ADAPTER_AXES, 0, 0, tiled=True)
+
+    total = project(
+        (
+            index_of(rows_a(1, every) + rows_a(2, every) + rows_b(1, every) + rows_b(2, every)),
+            meta,
+        ),
+        total,
+        [*a[1:3], *b[1:3]],
         [wq, wkv],
         512,
     )
-
-    again = join(halves, [total[1]])
-    next_a = gather_next(again[0], again[1], "y")
-    next_b = gather_next(again[2], again[3], "x")
-
-    pieces = scatter_rows(rank_partial(meta, x, down, 3 * rank, [low_a]))
-    copies, up_out = share_sum(pieces, up_out, [total[1]])
-    up = lax.all_to_all(up_out, ADAPTER_AXES, 0, 0, tiled=True)
-
-    a_low, a_high = shift(far_a[0], "y", 1), shift(far_a[1], "y", -1)
-    b_low, b_high = shift(far_b[0], "x", 1), shift(far_b[1], "x", -1)
-    total = project(
-        (
-            index_of(rows_a(1, low) + rows_a(2, high) + rows_b(1, low) + rows_b(2, high)),
-            meta,
-        ),
-        total,
-        [*far_a, *far_b],
-        [wq, wkv],
-        512,
-    )
-    total = project(
-        (
-            index_of(rows_a(1, high) + rows_a(2, low) + rows_b(1, high) + rows_b(2, low)),
-            meta,
-        ),
-        total,
-        [*next_a, *next_b],
-        [wq, wkv],
-        512,
-    )
     shrunk = lax.all_to_all(copies, TENSOR_AXES, 0, 0, tiled=True).reshape(tokens, 3 * rank)
     final = (index_of(rows_a(3, every) + rows_b(3, every)), meta)
-    far = [a_low, a_high, b_low, b_high]
+    far = [a[3], b[3]]
     tail = key_value_tail(shrunk, up, cosine, sine, wide, wkv.shape[1], 512)
     (mine,) = project(final, total[1:], far, [wkv], 512, tail)
     other = lax.ppermute(mine, "x", [(i, i ^ 1) for i in range(SIDE)])
@@ -650,7 +654,12 @@
             meta, q, shrunk, up, down, mine, other, cosine, sine, cut * each, each
         )
         step = 1 - 2 * cut
-        parts.append(output_ring(ring_gather_whole(attended, "y", step), wo_all, "x", step))
+        if cut > 0:
+            attended = handed_on(attended, near)
+        gathered = ring_gather_whole(attended, "y", step)
+        near = gathered[1:3]
+        terms, away = output_ring(gathered, wo_all, "x", step, [away] if cut > 0 else [])
+        parts.append(terms)
     return finish(meta, parts, up, rank, wide)
 
 

time: 307 us -> 319 us (1.039)
  waiting for transfers between devices: 101 us -> 117 us
  local copies, waits for them, and re-layouts: 11.5 us -> 20 us
  Pallas kernels: 105 us -> 97.3 us
  starting transfers between devices: 69.6 us -> 66.2 us
    all_to_all x1, waiting for transfers between devices: 9.03 us -> 35.7 us  [scatter_rows(): lax.all_to_all(partial.reshape(ways, rows // ways, rank), TENSOR_AXES, 0,...]
    ppermute x35 -> x31, waiting for transfers between devices: 91.4 us -> 78.4 us  [shift(): lax.ppermute(block, axis, [(i, (i + step) % SIDE) for i in range(SIDE)])]
    slice x0 -> x4, local copies, waits for them, and re-layouts: none -> 8.03 us  [the longest x2 4.57 us: ring_gather_rows(): ahead[half:]]
    pallas_call x2 -> x1, Pallas kernels: 9.53 us -> 4.88 us  [join(): pl.pallas_call(body, out_shape=tuple((jax.ShapeDtypeStruct((tokens, w), b...]
    ppermute x35 -> x31, starting transfers between devices: 50.5 us -> 46.5 us  [shift(): lax.ppermute(block, axis, [(i, (i + step) % SIDE) for i in range(SIDE)])]
    pallas_call x5 -> x4, Pallas kernels: 37.9 us -> 34.3 us  [project(): pl.pallas_call(body, out_shape=tuple((jax.ShapeDtypeStruct((tokens, w), d...]
    unnamed x70 -> x66, local copies, waits for them, and re-layouts: 7.34 us -> 8.55 us
  transfers between devices with their start and end apart: 41 -> 37, of which waited for: 16 -> 15; matrix products, arithmetic and copies ran while one was open for 2% -> 4% of each run, Pallas kernels for 29% -> 22%
where the time goes in v11:
time: 319 us; the launch traced here: 317 us
  waiting for transfers between devices  117 us (37%)
  Pallas kernels  97.3 us (31%)
  starting transfers between devices  66.2 us (21%)
  local copies, waits for them, and re-layouts  20 us (6%)
  between operations  13.9 us (4%)
    ppermute x31, waiting for transfers between devices, shift(): lax.ppermute(block, axis, [(i, (i + step) % SIDE) for i in range(SIDE)])  78.4 us
    ppermute x31, starting transfers between devices, shift(): lax.ppermute(block, axis, [(i, (i + step) % SIDE) for i in range(SIDE)])  46.5 us
    all_to_all x1, waiting for transfers between devices, scatter_rows(): lax.all_to_all(partial.reshape(ways, rows // ways, rank), TENSOR_AXES, 0,...  35.7 us
    pallas_call x4, Pallas kernels, project(): pl.pallas_call(body, out_shape=tuple((jax.ShapeDtypeStruct((tokens, w), d...  34.3 us
    pallas_call x2, Pallas kernels, output_partial(): pl.pallas_call(body, out_shape=tuple((jax.ShapeDtypeStruct((tokens, whole...  21.2 us
    pallas_call x2, Pallas kernels, attention(): pl.pallas_call(body, out_shape=jax.ShapeDtypeStruct((count * BLOCK, wide...  13.2 us
    unnamed x66, local copies, waits for them, and re-layouts  8.55 us
    pallas_call x1, Pallas kernels, pick_local(): pl.pallas_call(body, out_shape=tuple((jax.ShapeDtypeStruct(s, bf16) for s...  7.97 us
  transfers between devices with their start and end apart: 37, of which 15 were waited for; matrix products, arithmetic and copies ran while one was open for 4% of the time, Pallas kernels for 22%

profile of v11, /device:TPU:0, one launch (start us, length us, event | category | flops | bytes accessed | tf_op | source)
XLA Modules:
  0.0 317.1 jit_solution(11733312209709376199)
XLA Ops:
  7.9 8.0 %shard_map.136 = (bf16[8,256,512]{2,1,0:T(8,128)(2,1)}, bf16[8,64,1152]{2,1,0:T(8,128)(2,1)}, bf16[1024,256]{1,0:T(8,128)(2,1)}, bf16[1024,256]{1,0:T(8,128)(2,1...) custom-call(s32[12]{0:T(128)} %pad_add_fusion.pick_ref, ...), custom_call_target="tpu_custom_call" | custom-call | bytes 6553600 | tf_op jit(solution)/shard_map/pallas_call | solution.py:95
  15.9 5.0 %all-to-all-start = ((bf16[8,256,512]{2,1,0:T(8,128)(2,1)}), bf16[8,256,512]{2,1,0:T(8,128)(2,1)S(1)}, u32[]{:S(2)}, u32[]{:S(2)}) async-start(bf16[8,256,512]{2,1,0:T(8,128)(2,1)} %get-tuple-element.39), calls=%async_computation | async-start | bytes 4194304 | tf_op jit(solution)/shard_map/all_to_all | solution.py:601
  29.4 7.0 %collective-permute-done.refs_1_ = bf16[1024,256]{1,0:T(8,128)(2,1)S(1)} collective-permute-done((bf16[1024,256]{1,0:T(8,128)(2,1)S(1)}, bf16[1024,256]{1,0:T(8,128)(2,1)S(1)}, u32[]{:S(2)}, u32[]{:S(2)}) %collective-permute-start) | collective-permute-done | bytes 524320 | tf_op jit(solution)/shard_map/ppermute | solution.py:37
  43.4 4.0 %collective-permute-done.10.refs_12_.refs_3_ = bf16[512,256]{1,0:T(8,128)(2,1)S(1)} collective-permute-done((bf16[512,256]{1,0:T(8,128)(2,1)}, bf16[512,256]{1,0:T(8,128)(2,1)S(1)}, u32[]{:S(2)}, u32[]{:S(2)}) %collective-permute-start.10) | collective-permute-done | bytes 262176 | tf_op jit(solution)/shard_map/ppermute | solution.py:37
  48.8 2.9 collective-permute-done.8.refs_10_.refs_1_
  53.6 3.2 collective-permute-done.6.refs_8_
  59.6 4.9 %shard_map.137 = (bf16[1024,1024]{1,0:T(8,128)(2,1)}, bf16[1024,1024]{1,0:T(8,128)(2,1)}) custom-call(bf16[1024,256]{1,0:T(8,128)(2,1)} %get-tuple-element.29.refs_0_, bf16[1024,256]{1,0:T(8,128)(2,1)} %copy-done.7, bf16[1024,256]{1,0:T(8,128)(2,1)} %copy-done.8, bf16[1024,128]{1,0:T(8,128)(2,1)} %copy-done.26, bf16[1024,128]{1,0:T(8,128)(2,1)} %copy-done.27, ...), custom_call_target="tpu_custom_call" | custom-call | bytes 8388608 | tf_op jit(solution)/shard_map/pallas_call | solution.py:187
  68.4 3.0 collective-permute-start.13
  71.7 3.0 collective-permute-start.17
  75.8 5.1 %shard_map.141 = f32[1024,192]{1,0:T(8,128)} custom-call(s32[5,8]{1,0:T(8,128)} %stack.166.meta_ref, bf16[1024,512]{1,0:T(8,128)(2,1)} %x_ref.3, bf16[8,256,512]{2,1,0:T(8,128)(2,1)} %copy-done, bf16[8,256,512]{2,1,0:T(8,128)(2,1)} %copy-done, bf16[1024,1024]{1,0:T(8,128)(2,1)} %get-tuple-element.34.refs_0_.rest_2_.refs_5_), custom_call_target="tpu_custom_call" | custom-call | flops 201326592 | bytes 2621440 | tf_op jit(solution)/shard_map/pallas_call | solution.py:155
  80.8 4.3 %all-to-all-start.1 = ((f32[16,64,192]{2,1,0:T(8,128)}), f32[16,64,192]{2,1,0:T(8,128)}, u32[]{:S(2)}, u32[]{:S(2)}) async-start(f32[16,64,192]{2,1,0:T(8,128)} %bitcast.79), calls=%async_computation.1 | async-start | bytes 2097152 | tf_op jit(solution)/shard_map/all_to_all | solution.py:229
  85.9 7.9 %shard_map.138 = (f32[1024,512]{1,0:T(8,128)}, f32[1024,128]{1,0:T(8,128)}) custom-call(s32[8]{0:T(128)} %stack.215.index_ref, s32[5,8]{1,0:T(8,128)} %stack.166.meta_ref, bf16[1024,1024]{1,0:T(8,128)(2,1)} %get-tuple-element.34.refs_0_.rest_2_.refs_5_, bf16[1024,1024]{1,0:T(8,128)(2,1)} %get-tuple-element.35.refs_1_, bf16[8192,512]{1,0:T(8,128)(2,1)} %refs_11_.6, ...), custom_call_target="tpu_custom_call" | custom-call | flops 2684354560 | bytes 12058624 | tf_op jit(solution)/shard_map/pallas_call | solution.py:292
  93.8 35.7 %all-to-all-done.1.p_ref = f32[16,64,192]{2,1,0:T(8,128)} async-done(((f32[16,64,192]{2,1,0:T(8,128)}), f32[16,64,192]{2,1,0:T(8,128)}, u32[]{:S(2)}, u32[]{:S(2)}) %all-to-all-start.1) | async-done | bytes 786464 | tf_op jit(solution)/shard_map/all_to_all | solution.py:229
  131.7 6.0 %all-to-all-start.2 = ((bf16[16,64,192]{2,1,0:T(8,128)(2,1)}), bf16[16,64,192]{2,1,0:T(8,128)(2,1)S(1)}, u32[]{:S(2)}, u32[]{:S(2)}) async-start(bf16[16,64,192]{2,1,0:T(8,128)(2,1)} %get-tuple-element.41), calls=%async_computation.2 | async-start | bytes 1048576 | tf_op jit(solution)/shard_map/all_to_all | solution.py:641
  152.2 3.7 %all-to-all-start.3 = ((bf16[8,64,1152]{2,1,0:T(8,128)(2,1)}), bf16[8,64,1152]{2,1,0:T(8,128)(2,1)S(1)}, u32[]{:S(2)}, u32[]{:S(2)}) async-start(bf16[8,64,1152]{2,1,0:T(8,128)(2,1)} %get-tuple-element.42), calls=%async_computation.3 | async-start | bytes 2359296 | tf_op jit(solution)/shard_map/all_to_all | solution.py:629
  157.2 13.2 %shard_map.139 = (f32[1024,512]{1,0:T(8,128)}, f32[1024,128]{1,0:T(8,128)}) custom-call(s32[16]{0:T(128)} %stack.206.index_ref, s32[5,8]{1,0:T(8,128)} %stack.166.meta_ref, bf16[1024,1024]{1,0:T(8,128)(2,1)} %copy-done.3, bf16[1024,1024]{1,0:T(8,128)(2,1)} %collective-permute-done.13.refs_1_, ...), custom_call_target="tpu_custom_call", output_to_operand_aliasing={{0}: (38, {}), {1}: (39, {})} | custom-call | flops 5368709120 | bytes 18874368 | tf_op jit(solution)/shard_map/pallas_call | solution.py:292
  174.4 5.8 %shard_map.143.m_ref = bf16[1024,128]{1,0:T(8,128)(2,1)} custom-call(s32[8]{0:T(128)} %stack.184.index_ref, s32[5,8]{1,0:T(8,128)} %stack.166.meta_ref, bf16[512,1024]{1,0:T(8,128)(2,1)} %collective-permute-done.12.refs_0_, bf16[512,1024]{1,0:T(8,128)(2,1)} %collective-permute-done.14.refs_1_, bf16[512,1024]{1,0:T(8,128)(2,1)} %copy-done.4, ...), custom_call_target="tpu_custom_call" | custom-call | flops 536870912 | bytes 5767168 | tf_op jit(solution)/shard_map/pallas_call | solution.py:292
  181.0 7.4 %shard_map.140.q_ref = f32[1024,512]{1,0:T(8,128)} custom-call(s32[8]{0:T(128)} %stack.184.index_ref, s32[5,8]{1,0:T(8,128)} %stack.166.meta_ref, bf16[512,1024]{1,0:T(8,128)(2,1)} %collective-permute-done.12.refs_0_, bf16[512,1024]{1,0:T(8,128)(2,1)} %collective-permute-done.14.refs_1_, ...), custom_call_target="tpu_custom_call", output_to_operand_aliasing={{}: (14, {})} | custom-call | flops 2147483648 | bytes 10485760 | tf_op jit(solution)/shard_map/pallas_call | solution.py:292
  189.1 6.6 %shard_map.144.refs_0_ = bf16[512,640]{1,0:T(8,128)(2,1)} custom-call(s32[5,8]{1,0:T(8,128)} %stack.166.meta_ref, f32[1024,512]{1,0:T(8,128)} %shard_map.140.q_ref, bf16[1024,192]{1,0:T(8,128)(2,1)} %bitcast.77, bf16[8,64,1152]{2,1,0:T(8,128)(2,1)} %copy-done.1, bf16[8,256,512]{2,1,0:T(8,128)(2,1)} %copy-done, bf16[1024,128]{1,0:T(8,128)(2,1)} %shard_map.143.m_ref, ...), custom_call_target="tpu_custom_call" | custom-call | flops 402653184 | bytes 2097152 | tf_op jit(solution)/shard_map/pallas_call | solution.py:403
  196.3 2.6 collective-permute-start.21
  198.9 6.6 %shard_map.147.refs_0_ = bf16[512,640]{1,0:T(8,128)(2,1)} custom-call(s32[5,8]{1,0:T(8,128)} %stack.166.meta_ref, f32[1024,512]{1,0:T(8,128)} %shard_map.140.q_ref, bf16[1024,192]{1,0:T(8,128)(2,1)} %bitcast.78, bf16[8,64,1152]{2,1,0:T(8,128)(2,1)} %copy-done.1, bf16[8,256,512]{2,1,0:T(8,128)(2,1)} %copy-done, bf16[1024,128]{1,0:T(8,128)(2,1)} %shard_map.143.m_ref, ...), custom_call_target="tpu_custom_call" | custom-call | flops 402653184 | bytes 2097152 | tf_op jit(solution)/shard_map/pallas_call | solution.py:403
  205.5 7.5 %collective-permute-done.20.refs_1_ = bf16[512,640]{1,0:T(8,128)(2,1)S(1)} collective-permute-done((bf16[512,640]{1,0:T(8,128)(2,1)}, bf16[512,640]{1,0:T(8,128)(2,1)S(1)}, u32[]{:S(2)}, u32[]{:S(2)}) %collective-permute-start.20) | collective-permute-done | bytes 655392 | tf_op jit(solution)/shard_map/ppermute | solution.py:37
  216.9 13.1 %collective-permute-done.27.refs_2_ = bf16[512,640]{1,0:T(8,128)(2,1)S(1)} collective-permute-done((bf16[512,640]{1,0:T(8,128)(2,1)}, bf16[512,640]{1,0:T(8,128)(2,1)S(1)}, u32[]{:S(2)}, u32[]{:S(2)}) %collective-permute-start.27) | collective-permute-done | bytes 655392 | tf_op jit(solution)/shard_map/ppermute | solution.py:37
  230.0 3.0 collective-permute-start.28
  236.8 10.5 %shard_map.146 = (bf16[512,640]{1,0:T(8,128)(2,1)}, bf16[512,640]{1,0:T(8,128)(2,1)}, bf16[512,640]{1,0:T(8,128)(2,1)}, f32[512,640]{1,0:T(8,128)}) custom-call(s32[8]{0:T(128)} %stack.175.index_ref, bf16[512,640]{1,0:T(8,128)(2,1)} %shard_map.144.refs_0_, bf16[512,640]{1,0:T(8,128)(2,1)} %copy-done.5, bf16[512,640]{1,0:T(8,128)(2,1)} %copy-done.6, ...), custom_call_target="tpu_custom_call" | custom-call | flops 4294967296 | bytes 10485760 | tf_op jit(solution)/shard_map/pallas_call | solution.py:460
  248.4 10.7 %shard_map.149 = (bf16[512,640]{1,0:T(8,128)(2,1)}, bf16[512,640]{1,0:T(8,128)(2,1)}, bf16[512,640]{1,0:T(8,128)(2,1)}, f32[512,640]{1,0:T(8,128)}) custom-call(s32[8]{0:T(128)} %stack.175.index_ref, bf16[512,640]{1,0:T(8,128)(2,1)} %shard_map.148.refs_0_, bf16[512,640]{1,0:T(8,128)(2,1)} %copy-done.16, bf16[512,640]{1,0:T(8,128)(2,1)} %copy-done.15, ...), custom_call_target="tpu_custom_call" | custom-call | flops 4294967296 | bytes 10485760 | tf_op jit(solution)/shard_map/pallas_call | solution.py:460
  264.5 12.5 %collective-permute-done.29 = bf16[512,640]{1,0:T(8,128)(2,1)S(1)} collective-permute-done((bf16[512,640]{1,0:T(8,128)(2,1)}, bf16[512,640]{1,0:T(8,128)(2,1)S(1)}, u32[]{:S(2)}, u32[]{:S(2)}) %collective-permute-start.29) | collective-permute-done | bytes 655392 | tf_op jit(solution)/shard_map/ppermute | solution.py:37
  278.3 3.3 %collective-permute-start.30 = (bf16[512,640]{1,0:T(8,128)(2,1)S(1)}, bf16[512,640]{1,0:T(8,128)(2,1)S(1)}, u32[]{:S(2)}, u32[]{:S(2)}) collective-permute-start(bf16[512,640]{1,0:T(8,128)(2,1)S(1)} %add.296), channel_id=1, source_target_pairs={{0,3},{1,0},{2,1},{3,2},{4,7},{5,4},{6,5},{7,6},{8,11},{9,8},{10,9... | collective-permute-start | bytes 1966088 | tf_op jit(solution)/shard_map/ppermute | solution.py:37
  281.9 12.3 %collective-permute-done.31.refs_5_ = bf16[512,640]{1,0:T(8,128)(2,1)S(1)} collective-permute-done((bf16[512,640]{1,0:T(8,128)(2,1)}, bf16[512,640]{1,0:T(8,128)(2,1)S(1)}, u32[]{:S(2)}, u32[]{:S(2)}) %collective-permute-start.31) | collective-permute-done | bytes 655392 | tf_op jit(solution)/shard_map/ppermute | solution.py:37
  294.1 6.3 %collective-permute-done.30.refs_4_ = bf16[512,640]{1,0:T(8,128)(2,1)S(1)} collective-permute-done((bf16[512,640]{1,0:T(8,128)(2,1)S(1)}, bf16[512,640]{1,0:T(8,128)(2,1)S(1)}, u32[]{:S(2)}, u32[]{:S(2)}) %collective-permute-start.30) | collective-permute-done | bytes 655392 | tf_op jit(solution)/shard_map/ppermute | solution.py:37
  300.5 2.8 collective-permute-done.25.refs_2_
  304.1 6.2 %shard_map.150 = f32[1024,512]{1,0:T(8,128)} custom-call(s32[5,8]{1,0:T(8,128)} %stack.166.meta_ref, f32[512,640]{1,0:T(8,128)} %get-tuple-element.45.refs_0_, bf16[512,640]{1,0:T(8,128)(2,1)} %copy-done.22, bf16[512,640]{1,0:T(8,128)(2,1)} %copy-done.24, f32[512,640]{1,0:T(8,128)} %get-tuple-element.49.refs_3_, bf16[512,640]{1,0:T(8,128)(2,1)} %copy-done.23, ...), custom_call_target="tpu_custom_call" | custom-call | flops 67108864 | bytes 7340032 | tf_op jit(solution)/shard_map/pallas_call | solution.py:548
  (148 shorter events, 68.9 us)
Async XLA Ops:
  15.9 48.6 %all-to-all-start = ((bf16[8,256,512]{2,1,0:T(8,128)(2,1)}), bf16[8,256,512]{2,1,0:T(8,128)(2,1)S(1)}, u32[]{:S(2)}, u32[]{:S(2)}) async-start(bf16[8,256,512]{2,1,0:T(8,128)(2,1)} %get-tuple-element.39), calls=%async_computation | async-start | bytes 4194304 | tf_op jit(solution)/shard_map/all_to_all | solution.py:601
  20.9 215.1 %all-gather.3.cloned.1.call-start = ((), (), s32[]{:S(2)}) async-start(), calls=%async_computation.4 | async-start | bytes 9437184 | tf_op jit(solution)/shard_map/all_gather | solution.py:611
  20.9 15.6 %collective-permute-start = (bf16[1024,256]{1,0:T(8,128)(2,1)S(1)}, bf16[1024,256]{1,0:T(8,128)(2,1)S(1)}, u32[]{:S(2)}, u32[]{:S(2)}) collective-permute-start(bf16[1024,256]{1,0:T(8,128)(2,1)S(1)} %copy-done.25), channel_id=1, source_target_pairs={{0,1},{1,2},{2,3},{3,0},{4,5},{5,6},{6,7},{7,4},{8,9},{9,10},{10,1... | collective-permute-start | bytes 1572872 | tf_op jit(solution)/shard_map/ppermute | solution.py:37
  22.5 15.6 %collective-permute-start.1 = (bf16[1024,256]{1,0:T(8,128)(2,1)S(1)}, bf16[1024,256]{1,0:T(8,128)(2,1)S(1)}, u32[]{:S(2)}, u32[]{:S(2)}) collective-permute-start(bf16[1024,256]{1,0:T(8,128)(2,1)S(1)} %copy-done.25), channel_id=1, source_target_pairs={{0,3},{1,0},{2,1},{3,2},{4,7},{5,4},{6,5},{7,6},{8,11},{9,8},{10,9... | collective-permute-start | bytes 1572872 | tf_op jit(solution)/shard_map/ppermute | solution.py:37
  24.2 15.6 %collective-permute-start.4 = (bf16[1024,256]{1,0:T(8,128)(2,1)}, bf16[1024,256]{1,0:T(8,128)(2,1)S(1)}, u32[]{:S(2)}, u32[]{:S(2)}) collective-permute-start(bf16[1024,256]{1,0:T(8,128)(2,1)} %get-tuple-element.30.refs_5_), channel_id=1, source_target_pairs={{0,4},{4,8},{8,12},{12,0},{1,5},{5,9},{9,13},{13,1},{2,6},{6,10},{... | collective-permute-start | bytes 1572872 | tf_op jit(solution)/shard_map/ppermute | solution.py:37
  25.8 17.6 %collective-permute-start.5 = (bf16[1024,256]{1,0:T(8,128)(2,1)}, bf16[1024,256]{1,0:T(8,128)(2,1)S(1)}, u32[]{:S(2)}, u32[]{:S(2)}) collective-permute-start(bf16[1024,256]{1,0:T(8,128)(2,1)} %get-tuple-element.30.refs_5_), channel_id=1, source_target_pairs={{0,12},{4,0},{8,4},{12,8},{1,13},{5,1},{9,5},{13,9},{2,14},{6,2},{... | collective-permute-start | bytes 1572872 | tf_op jit(solution)/shard_map/ppermute | solution.py:37
  27.5 19.9 %collective-permute-start.10 = (bf16[512,256]{1,0:T(8,128)(2,1)}, bf16[512,256]{1,0:T(8,128)(2,1)S(1)}, u32[]{:S(2)}, u32[]{:S(2)}) collective-permute-start(bf16[512,256]{1,0:T(8,128)(2,1)} %get-tuple-element.33), channel_id=1, source_target_pairs={{0,8},{4,12},{8,0},{12,4},{1,9},{5,13},{9,1},{13,5},{2,10},{6,14},... | collective-permute-start | bytes 786440 | tf_op jit(solution)/shard_map/ppermute | solution.py:37
  36.5 15.3 %collective-permute-start.8 = (bf16[512,256]{1,0:T(8,128)(2,1)}, bf16[512,256]{1,0:T(8,128)(2,1)S(1)}, u32[]{:S(2)}, u32[]{:S(2)}) collective-permute-start(bf16[512,256]{1,0:T(8,128)(2,1)} %get-tuple-element.31), channel_id=1, source_target_pairs={{0,4},{4,8},{8,12},{12,0},{1,5},{5,9},{9,13},{13,1},{2,6},{6,10},{... | collective-permute-start | bytes 786440 | tf_op jit(solution)/shard_map/ppermute | solution.py:37
  38.1 15.4 %collective-permute-start.9 = (bf16[512,256]{1,0:T(8,128)(2,1)}, bf16[512,256]{1,0:T(8,128)(2,1)S(1)}, u32[]{:S(2)}, u32[]{:S(2)}) collective-permute-start(bf16[512,256]{1,0:T(8,128)(2,1)} %get-tuple-element.32), channel_id=1, source_target_pairs={{0,12},{4,0},{8,4},{12,8},{1,13},{5,1},{9,5},{13,9},{2,14},{6,2},{... | collective-permute-start | bytes 786440 | tf_op jit(solution)/shard_map/ppermute | solution.py:37
  68.2 69.5 %collective-permute-start.11 = (bf16[1024,1024]{1,0:T(8,128)(2,1)}, bf16[1024,1024]{1,0:T(8,128)(2,1)S(1)}, u32[]{:S(2)}, u32[]{:S(2)}) collective-permute-start(bf16[1024,1024]{1,0:T(8,128)(2,1)} %get-tuple-element.34.refs_0_.rest_2_.refs_5_), channel_id=1, source_target_pairs={{0,4},{4,8},{8,12},{12,0},{1,5},{5,9},{9,13},{13,1},{2,6},{6,10},{... | collective-permute-start | bytes 6291464 | tf_op jit(solution)/shard_map/ppermute | solution.py:37
  68.4 72.3 %collective-permute-start.13 = (bf16[1024,1024]{1,0:T(8,128)(2,1)}, bf16[1024,1024]{1,0:T(8,128)(2,1)}, u32[]{:S(2)}, u32[]{:S(2)}) collective-permute-start(bf16[1024,1024]{1,0:T(8,128)(2,1)} %get-tuple-element.34.refs_0_.rest_2_.refs_5_), channel_id=1, source_target_pairs={{0,12},{4,0},{8,4},{12,8},{1,13},{5,1},{9,5},{13,9},{2,14},{6,2},{... | collective-permute-start | bytes 6291464 | tf_op jit(solution)/shard_map/ppermute | solution.py:37
  71.5 72.9 %collective-permute-start.15 = (bf16[1024,1024]{1,0:T(8,128)(2,1)}, bf16[1024,1024]{1,0:T(8,128)(2,1)}, u32[]{:S(2)}, u32[]{:S(2)}) collective-permute-start(bf16[1024,1024]{1,0:T(8,128)(2,1)} %get-tuple-element.35.refs_1_), channel_id=1, source_target_pairs={{0,1},{1,2},{2,3},{3,0},{4,5},{5,6},{6,7},{7,4},{8,9},{9,10},{10,1... | collective-permute-start | bytes 6291464 | tf_op jit(solution)/shard_map/ppermute | solution.py:37
  71.7 76.8 %collective-permute-start.17 = (bf16[1024,1024]{1,0:T(8,128)(2,1)}, bf16[1024,1024]{1,0:T(8,128)(2,1)}, u32[]{:S(2)}, u32[]{:S(2)}) collective-permute-start(bf16[1024,1024]{1,0:T(8,128)(2,1)} %get-tuple-element.35.refs_1_), channel_id=1, source_target_pairs={{0,3},{1,0},{2,1},{3,2},{4,7},{5,4},{6,5},{7,6},{8,11},{9,8},{10,9... | collective-permute-start | bytes 6291464 | tf_op jit(solution)/shard_map/ppermute | solution.py:37
  80.8 48.8 %all-to-all-start.1 = ((f32[16,64,192]{2,1,0:T(8,128)}), f32[16,64,192]{2,1,0:T(8,128)}, u32[]{:S(2)}, u32[]{:S(2)}) async-start(f32[16,64,192]{2,1,0:T(8,128)} %bitcast.79), calls=%async_computation.1 | async-start | bytes 2097152 | tf_op jit(solution)/shard_map/all_to_all | solution.py:229
  131.7 20.5 %all-to-all-start.2 = ((bf16[16,64,192]{2,1,0:T(8,128)(2,1)}), bf16[16,64,192]{2,1,0:T(8,128)(2,1)S(1)}, u32[]{:S(2)}, u32[]{:S(2)}) async-start(bf16[16,64,192]{2,1,0:T(8,128)(2,1)} %get-tuple-element.41), calls=%async_computation.2 | async-start | bytes 1048576 | tf_op jit(solution)/shard_map/all_to_all | solution.py:641
  138.8 34.3 %collective-permute-start.12 = (bf16[512,1024]{1,0:T(8,128)(2,1)}, bf16[512,1024]{1,0:T(8,128)(2,1)}, u32[]{:S(2)}, u32[]{:S(2)}) collective-permute-start(bf16[512,1024]{1,0:T(8,128)(2,1)} %slice.36), channel_id=1, source_target_pairs={{0,4},{4,8},{8,12},{12,0},{1,5},{5,9},{9,13},{13,1},{2,6},{6,10},{... | collective-permute-start | bytes 3145736 | tf_op jit(solution)/shard_map/ppermute | solution.py:37
  143.0 30.0 %collective-permute-start.14 = (bf16[512,1024]{1,0:T(8,128)(2,1)}, bf16[512,1024]{1,0:T(8,128)(2,1)}, u32[]{:S(2)}, u32[]{:S(2)}) collective-permute-start(bf16[512,1024]{1,0:T(8,128)(2,1)} %slice.37), channel_id=1, source_target_pairs={{0,12},{4,0},{8,4},{12,8},{1,13},{5,1},{9,5},{13,9},{2,14},{6,2},{... | collective-permute-start | bytes 3145736 | tf_op jit(solution)/shard_map/ppermute | solution.py:37
  146.7 26.4 %collective-permute-start.16 = (bf16[512,1024]{1,0:T(8,128)(2,1)}, bf16[512,1024]{1,0:T(8,128)(2,1)S(1)}, u32[]{:S(2)}, u32[]{:S(2)}) collective-permute-start(bf16[512,1024]{1,0:T(8,128)(2,1)} %slice.38), channel_id=1, source_target_pairs={{0,1},{1,2},{2,3},{3,0},{4,5},{5,6},{6,7},{7,4},{8,9},{9,10},{10,1... | collective-permute-start | bytes 3145736 | tf_op jit(solution)/shard_map/ppermute | solution.py:37
  150.9 22.2 %collective-permute-start.18 = (bf16[512,1024]{1,0:T(8,128)(2,1)}, bf16[512,1024]{1,0:T(8,128)(2,1)}, u32[]{:S(2)}, u32[]{:S(2)}) collective-permute-start(bf16[512,1024]{1,0:T(8,128)(2,1)} %slice.39), channel_id=1, source_target_pairs={{0,3},{1,0},{2,1},{3,2},{4,7},{5,4},{6,5},{7,6},{8,11},{9,8},{10,9... | collective-permute-start | bytes 3145736 | tf_op jit(solution)/shard_map/ppermute | solution.py:37
  152.2 20.9 %all-to-all-start.3 = ((bf16[8,64,1152]{2,1,0:T(8,128)(2,1)}), bf16[8,64,1152]{2,1,0:T(8,128)(2,1)S(1)}, u32[]{:S(2)}, u32[]{:S(2)}) async-start(bf16[8,64,1152]{2,1,0:T(8,128)(2,1)} %get-tuple-element.42), calls=%async_computation.3 | async-start | bytes 2359296 | tf_op jit(solution)/shard_map/all_to_all | solution.py:629
  195.7 17.4 %collective-permute-start.20 = (bf16[512,640]{1,0:T(8,128)(2,1)}, bf16[512,640]{1,0:T(8,128)(2,1)S(1)}, u32[]{:S(2)}, u32[]{:S(2)}) collective-permute-start(bf16[512,640]{1,0:T(8,128)(2,1)} %shard_map.144.refs_0_), channel_id=1, source_target_pairs={{0,4},{4,8},{8,12},{12,0},{1,5},{5,9},{9,13},{13,1},{2,6},{6,10},{... | collective-permute-start | bytes 1966088 | tf_op jit(solution)/shard_map/ppermute | solution.py:37
  196.3 16.8 %collective-permute-start.21 = (bf16[512,640]{1,0:T(8,128)(2,1)}, bf16[512,640]{1,0:T(8,128)(2,1)S(1)}, u32[]{:S(2)}, u32[]{:S(2)}) collective-permute-start(bf16[512,640]{1,0:T(8,128)(2,1)} %shard_map.144.refs_0_), channel_id=1, source_target_pairs={{0,12},{4,0},{8,4},{12,8},{1,13},{5,1},{9,5},{13,9},{2,14},{6,2},{... | collective-permute-start | bytes 1966088 | tf_op jit(solution)/shard_map/ppermute | solution.py:37
  214.7 15.3 %collective-permute-start.27 = (bf16[512,640]{1,0:T(8,128)(2,1)}, bf16[512,640]{1,0:T(8,128)(2,1)S(1)}, u32[]{:S(2)}, u32[]{:S(2)}) collective-permute-start(bf16[512,640]{1,0:T(8,128)(2,1)} %shard_map.148.refs_0_), channel_id=1, source_target_pairs={{0,12},{4,0},{8,4},{12,8},{1,13},{5,1},{9,5},{13,9},{2,14},{6,2},{... | collective-permute-start | bytes 1966088 | tf_op jit(solution)/shard_map/ppermute | solution.py:37
  216.9 19.1 %collective-permute-start.22 = (bf16[512,640]{1,0:T(8,128)(2,1)}, bf16[512,640]{1,0:T(8,128)(2,1)S(1)}, u32[]{:S(2)}, u32[]{:S(2)}) collective-permute-start(bf16[512,640]{1,0:T(8,128)(2,1)} %copy-done.5), channel_id=1, source_target_pairs={{0,4},{4,8},{8,12},{12,0},{1,5},{5,9},{9,13},{13,1},{2,6},{6,10},{... | collective-permute-start | bytes 1966088 | tf_op jit(solution)/shard_map/ppermute | solution.py:37
  216.9 30.5 %collective-permute-start.26 = (bf16[512,640]{1,0:T(8,128)(2,1)}, bf16[512,640]{1,0:T(8,128)(2,1)S(1)}, u32[]{:S(2)}, u32[]{:S(2)}) collective-permute-start(bf16[512,640]{1,0:T(8,128)(2,1)} %shard_map.148.refs_0_), channel_id=1, source_target_pairs={{0,4},{4,8},{8,12},{12,0},{1,5},{5,9},{9,13},{13,1},{2,6},{6,10},{... | collective-permute-start | bytes 1966088 | tf_op jit(solution)/shard_map/ppermute | solution.py:37
  230.0 17.4 %collective-permute-start.28 = (bf16[512,640]{1,0:T(8,128)(2,1)S(1)}, bf16[512,640]{1,0:T(8,128)(2,1)S(1)}, u32[]{:S(2)}, u32[]{:S(2)}) collective-permute-start(bf16[512,640]{1,0:T(8,128)(2,1)S(1)} %collective-permute-done.27.refs_2_), channel_id=1, source_target_pairs={{0,12},{4,0},{8,4},{12,8},{1,13},{5,1},{9,5},{13,9},{2,14},{6,2},{... | collective-permute-start | bytes 1966088 | tf_op jit(solution)/shard_map/ppermute | solution.py:37
  259.1 17.9 %collective-permute-start.29 = (bf16[512,640]{1,0:T(8,128)(2,1)}, bf16[512,640]{1,0:T(8,128)(2,1)S(1)}, u32[]{:S(2)}, u32[]{:S(2)}) collective-permute-start(bf16[512,640]{1,0:T(8,128)(2,1)} %get-tuple-element.51), channel_id=1, source_target_pairs={{0,3},{1,0},{2,1},{3,2},{4,7},{5,4},{6,5},{7,6},{8,11},{9,8},{10,9... | collective-permute-start | bytes 1966088 | tf_op jit(solution)/shard_map/ppermute | solution.py:37
  261.2 20.4 %collective-permute-start.24 = (bf16[512,640]{1,0:T(8,128)(2,1)S(1)}, bf16[512,640]{1,0:T(8,128)(2,1)S(1)}, u32[]{:S(2)}, u32[]{:S(2)}) collective-permute-start(bf16[512,640]{1,0:T(8,128)(2,1)S(1)} %copy-done.18), channel_id=1, source_target_pairs={{0,1},{1,2},{2,3},{3,0},{4,5},{5,6},{6,7},{7,4},{8,9},{9,10},{10,1... | collective-permute-start | bytes 1966088 | tf_op jit(solution)/shard_map/ppermute | solution.py:37
  261.2 32.9 %collective-permute-start.31 = (bf16[512,640]{1,0:T(8,128)(2,1)}, bf16[512,640]{1,0:T(8,128)(2,1)S(1)}, u32[]{:S(2)}, u32[]{:S(2)}) collective-permute-start(bf16[512,640]{1,0:T(8,128)(2,1)} %get-tuple-element.52), channel_id=1, source_target_pairs={{0,1},{1,2},{2,3},{3,0},{4,5},{5,6},{6,7},{7,4},{8,9},{9,10},{10,1... | collective-permute-start | bytes 1966088 | tf_op jit(solution)/shard_map/ppermute | solution.py:37
  262.5 31.7 %collective-permute-start.23 = (bf16[512,640]{1,0:T(8,128)(2,1)S(1)}, bf16[512,640]{1,0:T(8,128)(2,1)S(1)}, u32[]{:S(2)}, u32[]{:S(2)}) collective-permute-start(bf16[512,640]{1,0:T(8,128)(2,1)S(1)} %copy-done.32), channel_id=1, source_target_pairs={{0,3},{1,0},{2,1},{3,2},{4,7},{5,4},{6,5},{7,6},{8,11},{9,8},{10,9... | collective-permute-start | bytes 1966088 | tf_op jit(solution)/shard_map/ppermute | solution.py:37
  278.3 22.2 %collective-permute-start.30 = (bf16[512,640]{1,0:T(8,128)(2,1)S(1)}, bf16[512,640]{1,0:T(8,128)(2,1)S(1)}, u32[]{:S(2)}, u32[]{:S(2)}) collective-permute-start(bf16[512,640]{1,0:T(8,128)(2,1)S(1)} %add.296), channel_id=1, source_target_pairs={{0,3},{1,0},{2,1},{3,2},{4,7},{5,4},{6,5},{7,6},{8,11},{9,8},{10,9... | collective-permute-start | bytes 1966088 | tf_op jit(solution)/shard_map/ppermute | solution.py:37
  281.8 21.5 %collective-permute-start.25 = (bf16[512,640]{1,0:T(8,128)(2,1)S(1)}, bf16[512,640]{1,0:T(8,128)(2,1)S(1)}, u32[]{:S(2)}, u32[]{:S(2)}) collective-permute-start(bf16[512,640]{1,0:T(8,128)(2,1)S(1)} %add.295), channel_id=1, source_target_pairs={{0,1},{1,2},{2,3},{3,0},{4,5},{5,6},{6,7},{7,4},{8,9},{9,10},{10,1... | collective-permute-start | bytes 1966088 | tf_op jit(solution)/shard_map/ppermute | solution.py:37
  (38 other events, 307.4 us)
Sparse Core Ops, SparseCore 0:
  68.3 49.7 all-gather.2

commit v12 on v10

--- a/solution.py
+++ b/solution.py
@@ -51,12 +51,6 @@
 
 def gather_next(low, high, axis):
     return shift(high, axis, 1), shift(low, axis, -1)
-
-
-def ring_gather_whole(block, axis, step):
-    behind = shift(block, axis, 1)
-    ahead = shift(block, axis, -1)
-    return block, behind, ahead, shift(behind if step == 1 else ahead, axis, step)
 
 
 def ring_order(index):
@@ -417,20 +411,22 @@
     count, (depth, width) = len(shards) // 2, weights.shape[1:]
     unit = depth // SIDE
     whole = 2 * width + HEAD
+    cut = pieces[3].shape[1]
     low, high = slice(0, width), slice(width + HEAD, whole)
 
     def body(index_ref, *refs):
-        x_refs, (w_low, w_high) = refs[:SIDE], refs[SIDE : SIDE + 2]
-        outs, x_all = refs[SIDE + 2 : -1], refs[-1]
+        x_refs, (w_low, w_high) = refs[: SIDE + 1], refs[SIDE + 1 : SIDE + 3]
+        outs, x_all = refs[SIDE + 3 : -1], refs[-1]
         step = pl.program_id(0)
 
         @pl.when(step == 0)
         def _():
-            for k, ref in enumerate(x_refs):
-                x_all[:, k * unit : (k + 1) * unit] = ref[:, :unit]
-            rank = x_refs[0][:, unit:].astype(f32)
-            for ref in x_refs[1:]:
-                rank = rank + ref[:, unit:].astype(f32)
+            rank = jnp.zeros((tokens, HEAD), f32)
+            for ref, begin in zip(x_refs, (0, unit, 2 * unit, 3 * unit, 3 * unit + cut)):
+                held = min(ref.shape[1], depth - begin, unit)
+                x_all[:, begin : begin + held] = ref[:, :held]
+                if held < ref.shape[1]:
+                    rank = rank + ref[:, held:].astype(f32)
             for out in outs:
                 out[:, width : width + HEAD] = rank.astype(out.dtype)
 
@@ -650,7 +646,8 @@
             meta, q, shrunk, up, down, mine, other, cosine, sine, cut * each, each
         )
         step = 1 - 2 * cut
-        parts.append(output_ring(ring_gather_whole(attended, "y", step), wo_all, "x", step))
+        gathered = ring_gather(attended, "y", wide // 2)
+        parts.append(output_ring(gathered, wo_all, "x", step))
     return finish(meta, parts, up, rank, wide)
 
 

time: 307 us -> 304 us (level)
  waiting for transfers between devices: 101 us -> 92.8 us
  starting transfers between devices: 69.6 us -> 75.8 us
    ppermute x35 -> x37, waiting for transfers between devices: 91.4 us -> 83.6 us  [shift(): lax.ppermute(block, axis, [(i, (i + step) % SIDE) for i in range(SIDE)])]
    ppermute x35 -> x37, starting transfers between devices: 50.5 us -> 56.7 us  [shift(): lax.ppermute(block, axis, [(i, (i + step) % SIDE) for i in range(SIDE)])]
    unnamed x70 -> x68, local copies, waits for them, and re-layouts: 7.34 us -> 5.66 us
  transfers between devices with their start and end apart: 41 -> 43, of which waited for: 16 -> 17; matrix products, arithmetic and copies ran while one was open for 2% -> 2% of each run, Pallas kernels for 29% -> 30%
where the time goes in v12:
time: 304 us; the launch traced here: 301 us
  Pallas kernels  106 us (35%)
  waiting for transfers between devices  92.8 us (31%)
  starting transfers between devices  75.8 us (25%)
  between operations  13.8 us (5%)
  local copies, waits for them, and re-layouts  11.5 us (4%)
    ppermute x37, waiting for transfers between devices, shift(): lax.ppermute(block, axis, [(i, (i + step) % SIDE) for i in range(SIDE)])  83.6 us
    ppermute x37, starting transfers between devices, shift(): lax.ppermute(block, axis, [(i, (i + step) % SIDE) for i in range(SIDE)])  56.7 us
    pallas_call x5, Pallas kernels, project(): pl.pallas_call(body, out_shape=tuple((jax.ShapeDtypeStruct((tokens, w), d...  37.8 us
    pallas_call x2, Pallas kernels, output_partial(): pl.pallas_call(body, out_shape=tuple((jax.ShapeDtypeStruct((tokens, whole...  21.2 us
    pallas_call x2, Pallas kernels, attention(): pl.pallas_call(body, out_shape=jax.ShapeDtypeStruct((count * BLOCK, wide...  13.2 us
    pallas_call x2, Pallas kernels, join(): pl.pallas_call(body, out_shape=tuple((jax.ShapeDtypeStruct((tokens, w), b...  9.54 us
    all_to_all x1, waiting for transfers between devices, scatter_rows(): lax.all_to_all(partial.reshape(ways, rows // ways, rank), TENSOR_AXES, 0,...  8.89 us
    pallas_call x1, Pallas kernels, pick_local(): pl.pallas_call(body, out_shape=tuple((jax.ShapeDtypeStruct(s, bf16) for s...  7.79 us
  transfers between devices with their start and end apart: 43, of which 17 were waited for; matrix products, arithmetic and copies ran while one was open for 2% of the time, Pallas kernels for 30%

profile of v12, /device:TPU:0, one launch (start us, length us, event | category | flops | bytes accessed | tf_op | source)
XLA Modules:
  0.0 301.5 jit_solution(2493459427773745306)
XLA Ops:
  8.0 7.8 %shard_map.136 = (bf16[8,256,512]{2,1,0:T(8,128)(2,1)}, bf16[8,64,1152]{2,1,0:T(8,128)(2,1)}, bf16[1024,256]{1,0:T(8,128)(2,1)}, bf16[1024,256]{1,0:T(8,128)(2,1...) custom-call(s32[12]{0:T(128)} %pad_add_fusion.pick_ref, ...), custom_call_target="tpu_custom_call" | custom-call | bytes 6553600 | tf_op jit(solution)/shard_map/pallas_call | solution.py:90
  15.8 5.7 %all-to-all-start = ((bf16[8,256,512]{2,1,0:T(8,128)(2,1)}), bf16[8,256,512]{2,1,0:T(8,128)(2,1)S(1)}, u32[]{:S(2)}, u32[]{:S(2)}) async-start(bf16[8,256,512]{2,1,0:T(8,128)(2,1)} %get-tuple-element.55), calls=%async_computation | async-start | bytes 4194304 | tf_op jit(solution)/shard_map/all_to_all | solution.py:571
  30.1 7.0 %collective-permute-done.refs_1_ = bf16[1024,256]{1,0:T(8,128)(2,1)S(1)} collective-permute-done((bf16[1024,256]{1,0:T(8,128)(2,1)S(1)}, bf16[1024,256]{1,0:T(8,128)(2,1)S(1)}, u32[]{:S(2)}, u32[]{:S(2)}) %collective-permute-start) | collective-permute-done | bytes 524320 | tf_op jit(solution)/shard_map/ppermute | solution.py:37
  44.0 3.8 %collective-permute-done.10.refs_12_.refs_3_ = bf16[512,256]{1,0:T(8,128)(2,1)S(1)} collective-permute-done((bf16[512,256]{1,0:T(8,128)(2,1)}, bf16[512,256]{1,0:T(8,128)(2,1)S(1)}, u32[]{:S(2)}, u32[]{:S(2)}) %collective-permute-start.10) | collective-permute-done | bytes 262176 | tf_op jit(solution)/shard_map/ppermute | solution.py:37
  49.3 3.0 %collective-permute-done.8.refs_10_.refs_1_ = bf16[512,256]{1,0:T(8,128)(2,1)S(1)} collective-permute-done((bf16[512,256]{1,0:T(8,128)(2,1)}, bf16[512,256]{1,0:T(8,128)(2,1)S(1)}, u32[]{:S(2)}, u32[]{:S(2)}) %collective-permute-start.8) | collective-permute-done | bytes 262176 | tf_op jit(solution)/shard_map/ppermute | solution.py:37
  54.0 3.3 %collective-permute-done.6.refs_8_ = bf16[1024,128]{1,0:T(8,128)(2,1)S(1)} collective-permute-done((bf16[1024,128]{1,0:T(8,128)(2,1)S(1)}, bf16[1024,128]{1,0:T(8,128)(2,1)S(1)}, u32[]{:S(2)}, u32[]{:S(2)}) %collective-permute-start.6) | collective-permute-done | bytes 262176 | tf_op jit(solution)/shard_map/ppermute | solution.py:37
  60.1 4.8 %shard_map.137 = (bf16[1024,512]{1,0:T(8,128)(2,1)}, bf16[1024,512]{1,0:T(8,128)(2,1)}, bf16[1024,512]{1,0:T(8,128)(2,1)}, bf16[1024,512]{1,0:T(8,128)(2,1)}) custom-call(bf16[1024,256]{1,0:T(8,128)(2,1)} %get-tuple-element.37.refs_0_, bf16[1024,256]{1,0:T(8,128)(2,1)} %copy-done.6, bf16[1024,256]{1,0:T(8,128)(2,1)} %copy-done.7, ...), custom_call_target="tpu_custom_call" | custom-call | bytes 8388608 | tf_op jit(solution)/shard_map/pallas_call | solution.py:182
  76.8 5.3 %shard_map.143 = f32[1024,192]{1,0:T(8,128)} custom-call(s32[5,8]{1,0:T(8,128)} %stack.169.meta_ref, bf16[1024,512]{1,0:T(8,128)(2,1)} %x_ref.3, bf16[8,256,512]{2,1,0:T(8,128)(2,1)} %copy-done, bf16[8,256,512]{2,1,0:T(8,128)(2,1)} %copy-done, bf16[1024,512]{1,0:T(8,128)(2,1)} %get-tuple-element.42.refs_0_.rest_2_.refs_5_), custom_call_target="tpu_custom_call" | custom-call | flops 201326592 | bytes 2621440 | tf_op jit(solution)/shard_map/pallas_call | solution.py:150
  82.1 3.7 %all-to-all-start.1 = ((f32[16,64,192]{2,1,0:T(8,128)}), f32[16,64,192]{2,1,0:T(8,128)S(1)}, u32[]{:S(2)}, u32[]{:S(2)}) async-start(f32[16,64,192]{2,1,0:T(8,128)} %bitcast.79), calls=%async_computation.1 | async-start | bytes 2097152 | tf_op jit(solution)/shard_map/all_to_all | solution.py:224
  85.8 8.1 %shard_map.138 = (f32[1024,512]{1,0:T(8,128)}, f32[1024,128]{1,0:T(8,128)}) custom-call(s32[8]{0:T(128)} %stack.210.index_ref, s32[5,8]{1,0:T(8,128)} %stack.169.meta_ref, bf16[1024,512]{1,0:T(8,128)(2,1)} %get-tuple-element.42.refs_0_.rest_2_.refs_5_, bf16[1024,512]{1,0:T(8,128)(2,1)} %get-tuple-element.43.refs_1_, ...), custom_call_target="tpu_custom_call" | custom-call | flops 2684354560 | bytes 12058624 | tf_op jit(solution)/shard_map/pallas_call | solution.py:273
  93.9 4.8 %shard_map.139 = (bf16[1024,512]{1,0:T(8,128)(2,1)}, bf16[1024,512]{1,0:T(8,128)(2,1)}, bf16[1024,512]{1,0:T(8,128)(2,1)}, bf16[1024,512]{1,0:T(8,128)(2,1)}) custom-call(bf16[1024,256]{1,0:T(8,128)(2,1)} %get-tuple-element.37.refs_0_, bf16[1024,256]{1,0:T(8,128)(2,1)} %copy-done.6, bf16[1024,256]{1,0:T(8,128)(2,1)} %copy-done.7, ...), custom_call_target="tpu_custom_call" | custom-call | bytes 8388608 | tf_op jit(solution)/shard_map/pallas_call | solution.py:182
  103.7 8.9 %all-to-all-done.1.p_ref = f32[16,64,192]{2,1,0:T(8,128)S(1)} async-done(((f32[16,64,192]{2,1,0:T(8,128)}), f32[16,64,192]{2,1,0:T(8,128)S(1)}, u32[]{:S(2)}, u32[]{:S(2)}) %all-to-all-start.1) | async-done | bytes 786464 | tf_op jit(solution)/shard_map/all_to_all | solution.py:224
  115.7 3.6 %all-to-all-start.2 = ((bf16[16,64,192]{2,1,0:T(8,128)(2,1)}), bf16[16,64,192]{2,1,0:T(8,128)(2,1)S(1)}, u32[]{:S(2)}, u32[]{:S(2)}) async-start(bf16[16,64,192]{2,1,0:T(8,128)(2,1)} %get-tuple-element.57), calls=%async_computation.2 | async-start | bytes 1048576 | tf_op jit(solution)/shard_map/all_to_all | solution.py:633
  119.3 3.1 %collective-permute-start.22 = (bf16[1024,512]{1,0:T(8,128)(2,1)}, bf16[1024,512]{1,0:T(8,128)(2,1)}, u32[]{:S(2)}, u32[]{:S(2)}) collective-permute-start(bf16[1024,512]{1,0:T(8,128)(2,1)} %get-tuple-element.50), channel_id=1, source_target_pairs={{0,3},{1,0},{2,1},{3,2},{4,7},{5,4},{6,5},{7,6},{8,11},{9,8},{10,9... | collective-permute-start | bytes 3145736 | tf_op jit(solution)/shard_map/ppermute | solution.py:37
  123.9 9.4 %collective-permute-done.19.refs_0_ = bf16[1024,512]{1,0:T(8,128)(2,1)S(1)} collective-permute-done((bf16[1024,512]{1,0:T(8,128)(2,1)}, bf16[1024,512]{1,0:T(8,128)(2,1)S(1)}, u32[]{:S(2)}, u32[]{:S(2)}) %collective-permute-start.19) | collective-permute-done | bytes 1048608 | tf_op jit(solution)/shard_map/ppermute | solution.py:37
  138.2 4.7 %all-to-all-start.3 = ((bf16[8,64,1152]{2,1,0:T(8,128)(2,1)}), bf16[8,64,1152]{2,1,0:T(8,128)(2,1)S(1)}, u32[]{:S(2)}, u32[]{:S(2)}) async-start(bf16[8,64,1152]{2,1,0:T(8,128)(2,1)} %get-tuple-element.58), calls=%async_computation.3 | async-start | bytes 2359296 | tf_op jit(solution)/shard_map/all_to_all | solution.py:609
  144.9 8.6 %shard_map.140 = (f32[1024,512]{1,0:T(8,128)}, f32[1024,128]{1,0:T(8,128)}) custom-call(s32[8]{0:T(128)} %stack.219.index_ref, s32[5,8]{1,0:T(8,128)} %stack.169.meta_ref, bf16[1024,512]{1,0:T(8,128)(2,1)} %collective-permute-done.11.refs_0_, bf16[1024,512]{1,0:T(8,128)(2,1)} %collective-permute-done.13.refs_1_, ...), custom_call_target="tpu_custom_call", output_to_operand_aliasing={{0}: (22, {}), {1}: (23, {})} | custom-call | flops 2684354560 | bytes 12058624 | tf_op jit(solution)/shard_map/pallas_call | solution.py:273
  153.5 8.6 %shard_map.141 = (f32[1024,512]{1,0:T(8,128)}, f32[1024,128]{1,0:T(8,128)}) custom-call(s32[8]{0:T(128)} %stack.201.index_ref, s32[5,8]{1,0:T(8,128)} %stack.169.meta_ref, bf16[1024,512]{1,0:T(8,128)(2,1)} %copy-done.16, bf16[1024,512]{1,0:T(8,128)(2,1)} %collective-permute-done.20.refs_1_, ...), custom_call_target="tpu_custom_call", output_to_operand_aliasing={{0}: (22, {}), {1}: (23, {})} | custom-call | flops 2684354560 | bytes 12058624 | tf_op jit(solution)/shard_map/pallas_call | solution.py:273
  162.1 4.4 %collective-permute-done.18.refs_3_ = bf16[1024,512]{1,0:T(8,128)(2,1)} collective-permute-done((bf16[1024,512]{1,0:T(8,128)(2,1)}, bf16[1024,512]{1,0:T(8,128)(2,1)}, u32[]{:S(2)}, u32[]{:S(2)}) %collective-permute-start.18) | collective-permute-done | bytes 1048608 | tf_op jit(solution)/shard_map/ppermute | solution.py:37
  167.6 5.5 %shard_map.145.m_ref = bf16[1024,128]{1,0:T(8,128)(2,1)} custom-call(s32[8]{0:T(128)} %stack.187.index_ref, s32[5,8]{1,0:T(8,128)} %stack.169.meta_ref, bf16[1024,512]{1,0:T(8,128)(2,1)} %copy-done.4, bf16[1024,512]{1,0:T(8,128)(2,1)} %collective-permute-done.14.refs_1_, bf16[1024,512]{1,0:T(8,128)(2,1)} %collective-permute-done.16.refs_2_, ...), custom_call_target="tpu_custom_call" | custom-call | flops 536870912 | bytes 5767168 | tf_op jit(solution)/shard_map/pallas_call | solution.py:273
  174.6 7.1 %shard_map.142.q_ref = f32[1024,512]{1,0:T(8,128)} custom-call(s32[8]{0:T(128)} %stack.187.index_ref, s32[5,8]{1,0:T(8,128)} %stack.169.meta_ref, bf16[1024,512]{1,0:T(8,128)(2,1)} %copy-done.4, bf16[1024,512]{1,0:T(8,128)(2,1)} %collective-permute-done.14.refs_1_, ...), custom_call_target="tpu_custom_call", output_to_operand_aliasing={{}: (14, {})} | custom-call | flops 2147483648 | bytes 10485760 | tf_op jit(solution)/shard_map/pallas_call | solution.py:273
  182.4 6.6 %shard_map.149.refs_0_ = bf16[512,640]{1,0:T(8,128)(2,1)} custom-call(s32[5,8]{1,0:T(8,128)} %stack.169.meta_ref, f32[1024,512]{1,0:T(8,128)} %shard_map.142.q_ref, bf16[1024,192]{1,0:T(8,128)(2,1)} %bitcast.77, bf16[8,64,1152]{2,1,0:T(8,128)(2,1)} %copy-done.1, bf16[8,256,512]{2,1,0:T(8,128)(2,1)} %copy-done, bf16[1024,128]{1,0:T(8,128)(2,1)} %shard_map.145.m_ref, ...), custom_call_target="tpu_custom_call" | custom-call | flops 402653184 | bytes 2097152 | tf_op jit(solution)/shard_map/pallas_call | solution.py:384
  191.7 6.6 %shard_map.146.refs_0_ = bf16[512,640]{1,0:T(8,128)(2,1)} custom-call(s32[5,8]{1,0:T(8,128)} %stack.169.meta_ref, f32[1024,512]{1,0:T(8,128)} %shard_map.142.q_ref, bf16[1024,192]{1,0:T(8,128)(2,1)} %bitcast.78, bf16[8,64,1152]{2,1,0:T(8,128)(2,1)} %copy-done.1, bf16[8,256,512]{2,1,0:T(8,128)(2,1)} %copy-done, bf16[1024,128]{1,0:T(8,128)(2,1)} %shard_map.145.m_ref, ...), custom_call_target="tpu_custom_call" | custom-call | flops 402653184 | bytes 2097152 | tf_op jit(solution)/shard_map/pallas_call | solution.py:384
  198.3 3.2 %collective-permute-start.25 = (bf16[512,640]{1,0:T(8,128)(2,1)}, bf16[512,640]{1,0:T(8,128)(2,1)S(1)}, u32[]{:S(2)}, u32[]{:S(2)}) collective-permute-start(bf16[512,640]{1,0:T(8,128)(2,1)} %shard_map.146.refs_0_), channel_id=1, source_target_pairs={{0,12},{4,0},{8,4},{12,8},{1,13},{5,1},{9,5},{13,9},{2,14},{6,2},{... | collective-permute-start | bytes 1966088 | tf_op jit(solution)/shard_map/ppermute | solution.py:37
  201.5 4.8 %collective-permute-done.32.refs_2_ = bf16[512,640]{1,0:T(8,128)(2,1)S(1)} collective-permute-done((bf16[512,640]{1,0:T(8,128)(2,1)}, bf16[512,640]{1,0:T(8,128)(2,1)S(1)}, u32[]{:S(2)}, u32[]{:S(2)}) %collective-permute-start.32) | collective-permute-done | bytes 655392 | tf_op jit(solution)/shard_map/ppermute | solution.py:37
  210.5 9.8 %collective-permute-done.25.refs_2_ = bf16[512,640]{1,0:T(8,128)(2,1)S(1)} collective-permute-done((bf16[512,640]{1,0:T(8,128)(2,1)}, bf16[512,640]{1,0:T(8,128)(2,1)S(1)}, u32[]{:S(2)}, u32[]{:S(2)}) %collective-permute-start.25) | collective-permute-done | bytes 655392 | tf_op jit(solution)/shard_map/ppermute | solution.py:37
  227.7 10.6 %shard_map.150 = (bf16[512,640]{1,0:T(8,128)(2,1)}, bf16[512,640]{1,0:T(8,128)(2,1)}, bf16[512,640]{1,0:T(8,128)(2,1)}, f32[512,640]{1,0:T(8,128)}) custom-call(s32[8]{0:T(128)} %stack.178.index_ref, bf16[512,640]{1,0:T(8,128)(2,1)} %shard_map.149.refs_0_, bf16[512,640]{1,0:T(8,128)(2,1)} %copy-done.15, bf16[512,640]{1,0:T(8,128)(2,1)} %copy-done.13, ...), custom_call_target="tpu_custom_call" | custom-call | flops 4294967296 | bytes 10485760 | tf_op jit(solution)/shard_map/pallas_call | solution.py:443
  240.8 10.6 %shard_map.148 = (bf16[512,640]{1,0:T(8,128)(2,1)}, bf16[512,640]{1,0:T(8,128)(2,1)}, bf16[512,640]{1,0:T(8,128)(2,1)}, f32[512,640]{1,0:T(8,128)}) custom-call(s32[8]{0:T(128)} %stack.178.index_ref, bf16[512,640]{1,0:T(8,128)(2,1)} %shard_map.146.refs_0_, bf16[512,640]{1,0:T(8,128)(2,1)} %copy-done.14, bf16[512,640]{1,0:T(8,128)(2,1)} %copy-done.12, ...), custom_call_target="tpu_custom_call" | custom-call | flops 4294967296 | bytes 10485760 | tf_op jit(solution)/shard_map/pallas_call | solution.py:443
  256.9 13.6 %collective-permute-done.29 = bf16[512,640]{1,0:T(8,128)(2,1)S(1)} collective-permute-done((bf16[512,640]{1,0:T(8,128)(2,1)}, bf16[512,640]{1,0:T(8,128)(2,1)S(1)}, u32[]{:S(2)}, u32[]{:S(2)}) %collective-permute-start.29) | collective-permute-done | bytes 655392 | tf_op jit(solution)/shard_map/ppermute | solution.py:37
  270.8 9.9 %collective-permute-done.37.refs_5_ = bf16[512,640]{1,0:T(8,128)(2,1)S(1)} collective-permute-done((bf16[512,640]{1,0:T(8,128)(2,1)S(1)}, bf16[512,640]{1,0:T(8,128)(2,1)S(1)}, u32[]{:S(2)}, u32[]{:S(2)}) %collective-permute-start.37) | collective-permute-done | bytes 655392 | tf_op jit(solution)/shard_map/ppermute | solution.py:37
  280.6 7.0 %collective-permute-done.30.refs_2_ = bf16[512,640]{1,0:T(8,128)(2,1)S(1)} collective-permute-done((bf16[512,640]{1,0:T(8,128)(2,1)S(1)}, bf16[512,640]{1,0:T(8,128)(2,1)S(1)}, u32[]{:S(2)}, u32[]{:S(2)}) %collective-permute-start.30) | collective-permute-done | bytes 655392 | tf_op jit(solution)/shard_map/ppermute | solution.py:37
  288.5 6.2 %shard_map.151 = f32[1024,512]{1,0:T(8,128)} custom-call(s32[5,8]{1,0:T(8,128)} %stack.169.meta_ref, f32[512,640]{1,0:T(8,128)} %get-tuple-element.61.refs_0_, bf16[512,640]{1,0:T(8,128)(2,1)} %copy-done.28, bf16[512,640]{1,0:T(8,128)(2,1)} %copy-done.30, f32[512,640]{1,0:T(8,128)} %get-tuple-element.65.refs_3_, bf16[512,640]{1,0:T(8,128)(2,1)} %copy-done.29, ...), custom_call_target="tpu_custom_call" | custom-call | flops 67108864 | bytes 7340032 | tf_op jit(solution)/shard_map/pallas_call | solution.py:518
  (164 shorter events, 77.7 us)
Async XLA Ops:
  15.8 49.1 %all-to-all-start = ((bf16[8,256,512]{2,1,0:T(8,128)(2,1)}), bf16[8,256,512]{2,1,0:T(8,128)(2,1)S(1)}, u32[]{:S(2)}, u32[]{:S(2)}) async-start(bf16[8,256,512]{2,1,0:T(8,128)(2,1)} %get-tuple-element.55), calls=%async_computation | async-start | bytes 4194304 | tf_op jit(solution)/shard_map/all_to_all | solution.py:571
  21.5 206.2 %all-gather.3.cloned.1.call-start = ((), (), s32[]{:S(2)}) async-start(), calls=%async_computation.4 | async-start | bytes 9437184 | tf_op jit(solution)/shard_map/all_gather | solution.py:582
  26.4 17.0 %collective-permute-start.5 = (bf16[1024,256]{1,0:T(8,128)(2,1)S(1)}, bf16[1024,256]{1,0:T(8,128)(2,1)S(1)}, u32[]{:S(2)}, u32[]{:S(2)}) collective-permute-start(bf16[1024,256]{1,0:T(8,128)(2,1)S(1)} %copy-done.11), channel_id=1, source_target_pairs={{0,12},{4,0},{8,4},{12,8},{1,13},{5,1},{9,5},{13,9},{2,14},{6,2},{... | collective-permute-start | bytes 1572872 | tf_op jit(solution)/shard_map/ppermute | solution.py:37
  28.1 19.7 %collective-permute-start.10 = (bf16[512,256]{1,0:T(8,128)(2,1)}, bf16[512,256]{1,0:T(8,128)(2,1)S(1)}, u32[]{:S(2)}, u32[]{:S(2)}) collective-permute-start(bf16[512,256]{1,0:T(8,128)(2,1)} %get-tuple-element.41), channel_id=1, source_target_pairs={{0,8},{4,12},{8,0},{12,4},{1,9},{5,13},{9,1},{13,5},{2,10},{6,14},... | collective-permute-start | bytes 786440 | tf_op jit(solution)/shard_map/ppermute | solution.py:37
  68.6 31.9 %collective-permute-start.11 = (bf16[1024,512]{1,0:T(8,128)(2,1)S(1)}, bf16[1024,512]{1,0:T(8,128)(2,1)}, u32[]{:S(2)}, u32[]{:S(2)}) collective-permute-start(bf16[1024,512]{1,0:T(8,128)(2,1)S(1)} %copy-done.2), channel_id=1, source_target_pairs={{0,4},{4,8},{8,12},{12,0},{1,5},{5,9},{9,13},{13,1},{2,6},{6,10},{... | collective-permute-start | bytes 3145736 | tf_op jit(solution)/shard_map/ppermute | solution.py:37
  68.8 33.1 %collective-permute-start.13 = (bf16[1024,512]{1,0:T(8,128)(2,1)}, bf16[1024,512]{1,0:T(8,128)(2,1)}, u32[]{:S(2)}, u32[]{:S(2)}) collective-permute-start(bf16[1024,512]{1,0:T(8,128)(2,1)} %get-tuple-element.43.refs_1_), channel_id=1, source_target_pairs={{0,12},{4,0},{8,4},{12,8},{1,13},{5,1},{9,5},{13,9},{2,14},{6,2},{... | collective-permute-start | bytes 3145736 | tf_op jit(solution)/shard_map/ppermute | solution.py:37
  73.6 45.7 %collective-permute-start.15 = (bf16[1024,512]{1,0:T(8,128)(2,1)}, bf16[1024,512]{1,0:T(8,128)(2,1)}, u32[]{:S(2)}, u32[]{:S(2)}) collective-permute-start(bf16[1024,512]{1,0:T(8,128)(2,1)} %get-tuple-element.44.refs_2_), channel_id=1, source_target_pairs={{0,1},{1,2},{2,3},{3,0},{4,5},{5,6},{6,7},{7,4},{8,9},{9,10},{10,1... | collective-permute-start | bytes 3145736 | tf_op jit(solution)/shard_map/ppermute | solution.py:37
  73.9 48.5 %collective-permute-start.17 = (bf16[1024,512]{1,0:T(8,128)(2,1)}, bf16[1024,512]{1,0:T(8,128)(2,1)}, u32[]{:S(2)}, u32[]{:S(2)}) collective-permute-start(bf16[1024,512]{1,0:T(8,128)(2,1)} %get-tuple-element.45.refs_3_), channel_id=1, source_target_pairs={{0,3},{1,0},{2,1},{3,2},{4,7},{5,4},{6,5},{7,6},{8,11},{9,8},{10,9... | collective-permute-start | bytes 3145736 | tf_op jit(solution)/shard_map/ppermute | solution.py:37
  82.1 30.5 %all-to-all-start.1 = ((f32[16,64,192]{2,1,0:T(8,128)}), f32[16,64,192]{2,1,0:T(8,128)S(1)}, u32[]{:S(2)}, u32[]{:S(2)}) async-start(f32[16,64,192]{2,1,0:T(8,128)} %bitcast.79), calls=%async_computation.1 | async-start | bytes 2097152 | tf_op jit(solution)/shard_map/all_to_all | solution.py:224
  98.6 34.7 %collective-permute-start.19 = (bf16[1024,512]{1,0:T(8,128)(2,1)}, bf16[1024,512]{1,0:T(8,128)(2,1)S(1)}, u32[]{:S(2)}, u32[]{:S(2)}) collective-permute-start(bf16[1024,512]{1,0:T(8,128)(2,1)} %get-tuple-element.47), channel_id=1, source_target_pairs={{0,4},{4,8},{8,12},{12,0},{1,5},{5,9},{9,13},{13,1},{2,6},{6,10},{... | collective-permute-start | bytes 3145736 | tf_op jit(solution)/shard_map/ppermute | solution.py:37
  100.5 34.1 %collective-permute-start.20 = (bf16[1024,512]{1,0:T(8,128)(2,1)}, bf16[1024,512]{1,0:T(8,128)(2,1)}, u32[]{:S(2)}, u32[]{:S(2)}) collective-permute-start(bf16[1024,512]{1,0:T(8,128)(2,1)} %get-tuple-element.48), channel_id=1, source_target_pairs={{0,12},{4,0},{8,4},{12,8},{1,13},{5,1},{9,5},{13,9},{2,14},{6,2},{... | collective-permute-start | bytes 3145736 | tf_op jit(solution)/shard_map/ppermute | solution.py:37
  102.0 34.5 %collective-permute-start.21 = (bf16[1024,512]{1,0:T(8,128)(2,1)}, bf16[1024,512]{1,0:T(8,128)(2,1)}, u32[]{:S(2)}, u32[]{:S(2)}) collective-permute-start(bf16[1024,512]{1,0:T(8,128)(2,1)} %get-tuple-element.49), channel_id=1, source_target_pairs={{0,1},{1,2},{2,3},{3,0},{4,5},{5,6},{6,7},{7,4},{8,9},{9,10},{10,1... | collective-permute-start | bytes 3145736 | tf_op jit(solution)/shard_map/ppermute | solution.py:37
  115.7 22.4 %all-to-all-start.2 = ((bf16[16,64,192]{2,1,0:T(8,128)(2,1)}), bf16[16,64,192]{2,1,0:T(8,128)(2,1)S(1)}, u32[]{:S(2)}, u32[]{:S(2)}) async-start(bf16[16,64,192]{2,1,0:T(8,128)(2,1)} %get-tuple-element.57), calls=%async_computation.2 | async-start | bytes 1048576 | tf_op jit(solution)/shard_map/all_to_all | solution.py:633
  119.3 34.1 %collective-permute-start.22 = (bf16[1024,512]{1,0:T(8,128)(2,1)}, bf16[1024,512]{1,0:T(8,128)(2,1)}, u32[]{:S(2)}, u32[]{:S(2)}) collective-permute-start(bf16[1024,512]{1,0:T(8,128)(2,1)} %get-tuple-element.50), channel_id=1, source_target_pairs={{0,3},{1,0},{2,1},{3,2},{4,7},{5,4},{6,5},{7,6},{8,11},{9,8},{10,9... | collective-permute-start | bytes 3145736 | tf_op jit(solution)/shard_map/ppermute | solution.py:37
  122.4 39.7 %collective-permute-start.12 = (bf16[1024,512]{1,0:T(8,128)(2,1)}, bf16[1024,512]{1,0:T(8,128)(2,1)S(1)}, u32[]{:S(2)}, u32[]{:S(2)}) collective-permute-start(bf16[1024,512]{1,0:T(8,128)(2,1)} %collective-permute-done.11.refs_0_), channel_id=1, source_target_pairs={{0,4},{4,8},{8,12},{12,0},{1,5},{5,9},{9,13},{13,1},{2,6},{6,10},{... | collective-permute-start | bytes 3145736 | tf_op jit(solution)/shard_map/ppermute | solution.py:37
  133.3 28.8 %collective-permute-start.14 = (bf16[1024,512]{1,0:T(8,128)(2,1)}, bf16[1024,512]{1,0:T(8,128)(2,1)}, u32[]{:S(2)}, u32[]{:S(2)}) collective-permute-start(bf16[1024,512]{1,0:T(8,128)(2,1)} %collective-permute-done.13.refs_1_), channel_id=1, source_target_pairs={{0,12},{4,0},{8,4},{12,8},{1,13},{5,1},{9,5},{13,9},{2,14},{6,2},{... | collective-permute-start | bytes 3145736 | tf_op jit(solution)/shard_map/ppermute | solution.py:37
  134.6 27.5 %collective-permute-start.16 = (bf16[1024,512]{1,0:T(8,128)(2,1)}, bf16[1024,512]{1,0:T(8,128)(2,1)}, u32[]{:S(2)}, u32[]{:S(2)}) collective-permute-start(bf16[1024,512]{1,0:T(8,128)(2,1)} %collective-permute-done.15.refs_2_), channel_id=1, source_target_pairs={{0,1},{1,2},{2,3},{3,0},{4,5},{5,6},{6,7},{7,4},{8,9},{9,10},{10,1... | collective-permute-start | bytes 3145736 | tf_op jit(solution)/shard_map/ppermute | solution.py:37
  136.5 30.1 %collective-permute-start.18 = (bf16[1024,512]{1,0:T(8,128)(2,1)}, bf16[1024,512]{1,0:T(8,128)(2,1)}, u32[]{:S(2)}, u32[]{:S(2)}) collective-permute-start(bf16[1024,512]{1,0:T(8,128)(2,1)} %collective-permute-done.17.refs_3_), channel_id=1, source_target_pairs={{0,3},{1,0},{2,1},{3,2},{4,7},{5,4},{6,5},{7,6},{8,11},{9,8},{10,9... | collective-permute-start | bytes 3145736 | tf_op jit(solution)/shard_map/ppermute | solution.py:37
  138.2 28.4 %all-to-all-start.3 = ((bf16[8,64,1152]{2,1,0:T(8,128)(2,1)}), bf16[8,64,1152]{2,1,0:T(8,128)(2,1)S(1)}, u32[]{:S(2)}, u32[]{:S(2)}) async-start(bf16[8,64,1152]{2,1,0:T(8,128)(2,1)} %get-tuple-element.58), calls=%async_computation.3 | async-start | bytes 2359296 | tf_op jit(solution)/shard_map/all_to_all | solution.py:609
  189.0 17.3 %collective-permute-start.32 = (bf16[512,640]{1,0:T(8,128)(2,1)}, bf16[512,640]{1,0:T(8,128)(2,1)S(1)}, u32[]{:S(2)}, u32[]{:S(2)}) collective-permute-start(bf16[512,640]{1,0:T(8,128)(2,1)} %shard_map.149.refs_0_), channel_id=1, source_target_pairs={{0,12},{4,0},{8,4},{12,8},{1,13},{5,1},{9,5},{13,9},{2,14},{6,2},{... | collective-permute-start | bytes 1966088 | tf_op jit(solution)/shard_map/ppermute | solution.py:37
  191.7 17.4 %collective-permute-start.31 = (bf16[512,640]{1,0:T(8,128)(2,1)}, bf16[512,640]{1,0:T(8,128)(2,1)S(1)}, u32[]{:S(2)}, u32[]{:S(2)}) collective-permute-start(bf16[512,640]{1,0:T(8,128)(2,1)} %shard_map.149.refs_0_), channel_id=1, source_target_pairs={{0,4},{4,8},{8,12},{12,0},{1,5},{5,9},{9,13},{13,1},{2,6},{6,10},{... | collective-permute-start | bytes 1966088 | tf_op jit(solution)/shard_map/ppermute | solution.py:37
  198.3 22.1 %collective-permute-start.25 = (bf16[512,640]{1,0:T(8,128)(2,1)}, bf16[512,640]{1,0:T(8,128)(2,1)S(1)}, u32[]{:S(2)}, u32[]{:S(2)}) collective-permute-start(bf16[512,640]{1,0:T(8,128)(2,1)} %shard_map.146.refs_0_), channel_id=1, source_target_pairs={{0,12},{4,0},{8,4},{12,8},{1,13},{5,1},{9,5},{13,9},{2,14},{6,2},{... | collective-permute-start | bytes 1966088 | tf_op jit(solution)/shard_map/ppermute | solution.py:37
  201.5 21.6 %collective-permute-start.24 = (bf16[512,640]{1,0:T(8,128)(2,1)}, bf16[512,640]{1,0:T(8,128)(2,1)S(1)}, u32[]{:S(2)}, u32[]{:S(2)}) collective-permute-start(bf16[512,640]{1,0:T(8,128)(2,1)} %shard_map.146.refs_0_), channel_id=1, source_target_pairs={{0,4},{4,8},{8,12},{12,0},{1,5},{5,9},{9,13},{13,1},{2,6},{6,10},{... | collective-permute-start | bytes 1966088 | tf_op jit(solution)/shard_map/ppermute | solution.py:37
  206.4 21.3 %collective-permute-start.34 = (bf16[512,384]{1,0:T(8,128)(2,1)S(1)}, bf16[512,384]{1,0:T(8,128)(2,1)}, u32[]{:S(2)}, u32[]{:S(2)}) collective-permute-start(bf16[512,384]{1,0:T(8,128)(2,1)S(1)} %slice.39), channel_id=1, source_target_pairs={{0,12},{4,0},{8,4},{12,8},{1,13},{5,1},{9,5},{13,9},{2,14},{6,2},{... | collective-permute-start | bytes 1179656 | tf_op jit(solution)/shard_map/ppermute | solution.py:37
  209.9 16.7 %collective-permute-start.33 = (bf16[512,256]{1,0:T(8,128)(2,1)}, bf16[512,256]{1,0:T(8,128)(2,1)}, u32[]{:S(2)}, u32[]{:S(2)}) collective-permute-start(bf16[512,256]{1,0:T(8,128)(2,1)} %slice.38), channel_id=1, source_target_pairs={{0,4},{4,8},{8,12},{12,0},{1,5},{5,9},{9,13},{13,1},{2,6},{6,10},{... | collective-permute-start | bytes 786440 | tf_op jit(solution)/shard_map/ppermute | solution.py:37
  220.4 20.4 %collective-permute-start.27 = (bf16[512,384]{1,0:T(8,128)(2,1)S(1)}, bf16[512,384]{1,0:T(8,128)(2,1)}, u32[]{:S(2)}, u32[]{:S(2)}) collective-permute-start(bf16[512,384]{1,0:T(8,128)(2,1)S(1)} %slice.37), channel_id=1, source_target_pairs={{0,12},{4,0},{8,4},{12,8},{1,13},{5,1},{9,5},{13,9},{2,14},{6,2},{... | collective-permute-start | bytes 1179656 | tf_op jit(solution)/shard_map/ppermute | solution.py:37
  223.9 16.9 %collective-permute-start.26 = (bf16[512,256]{1,0:T(8,128)(2,1)}, bf16[512,256]{1,0:T(8,128)(2,1)}, u32[]{:S(2)}, u32[]{:S(2)}) collective-permute-start(bf16[512,256]{1,0:T(8,128)(2,1)} %slice.36), channel_id=1, source_target_pairs={{0,4},{4,8},{8,12},{12,0},{1,5},{5,9},{9,13},{13,1},{2,6},{6,10},{... | collective-permute-start | bytes 786440 | tf_op jit(solution)/shard_map/ppermute | solution.py:37
  251.4 19.1 %collective-permute-start.29 = (bf16[512,640]{1,0:T(8,128)(2,1)}, bf16[512,640]{1,0:T(8,128)(2,1)S(1)}, u32[]{:S(2)}, u32[]{:S(2)}) collective-permute-start(bf16[512,640]{1,0:T(8,128)(2,1)} %get-tuple-element.64), channel_id=1, source_target_pairs={{0,1},{1,2},{2,3},{3,0},{4,5},{5,6},{6,7},{7,4},{8,9},{9,10},{10,1... | collective-permute-start | bytes 1966088 | tf_op jit(solution)/shard_map/ppermute | solution.py:37
  251.4 29.2 %collective-permute-start.37 = (bf16[512,640]{1,0:T(8,128)(2,1)S(1)}, bf16[512,640]{1,0:T(8,128)(2,1)S(1)}, u32[]{:S(2)}, u32[]{:S(2)}) collective-permute-start(bf16[512,640]{1,0:T(8,128)(2,1)S(1)} %copy-done.33), channel_id=1, source_target_pairs={{0,1},{1,2},{2,3},{3,0},{4,5},{5,6},{6,7},{7,4},{8,9},{9,10},{10,1... | collective-permute-start | bytes 1966088 | tf_op jit(solution)/shard_map/ppermute | solution.py:37
  253.0 27.7 %collective-permute-start.28 = (bf16[512,640]{1,0:T(8,128)(2,1)}, bf16[512,640]{1,0:T(8,128)(2,1)S(1)}, u32[]{:S(2)}, u32[]{:S(2)}) collective-permute-start(bf16[512,640]{1,0:T(8,128)(2,1)} %get-tuple-element.62), channel_id=1, source_target_pairs={{0,3},{1,0},{2,1},{3,2},{4,7},{5,4},{6,5},{7,6},{8,11},{9,8},{10,9... | collective-permute-start | bytes 1966088 | tf_op jit(solution)/shard_map/ppermute | solution.py:37
  254.9 25.7 %collective-permute-start.36 = (bf16[512,640]{1,0:T(8,128)(2,1)S(1)}, bf16[512,640]{1,0:T(8,128)(2,1)S(1)}, u32[]{:S(2)}, u32[]{:S(2)}) collective-permute-start(bf16[512,640]{1,0:T(8,128)(2,1)S(1)} %add.296), channel_id=1, source_target_pairs={{0,3},{1,0},{2,1},{3,2},{4,7},{5,4},{6,5},{7,6},{8,11},{9,8},{10,9... | collective-permute-start | bytes 1966088 | tf_op jit(solution)/shard_map/ppermute | solution.py:37
  270.7 17.0 %collective-permute-start.30 = (bf16[512,640]{1,0:T(8,128)(2,1)S(1)}, bf16[512,640]{1,0:T(8,128)(2,1)S(1)}, u32[]{:S(2)}, u32[]{:S(2)}) collective-permute-start(bf16[512,640]{1,0:T(8,128)(2,1)S(1)} %add.295), channel_id=1, source_target_pairs={{0,1},{1,2},{2,3},{3,0},{4,5},{5,6},{6,7},{7,4},{8,9},{9,10},{10,1... | collective-permute-start | bytes 1966088 | tf_op jit(solution)/shard_map/ppermute | solution.py:37
  (45 other events, 459.2 us)
Sparse Core Ops, SparseCore 0:
  68.7 49.6 all-gather.2

commit v13 on v12

--- a/solution.py
+++ b/solution.py
@@ -459,16 +459,36 @@
     )(jnp.stack(shards).astype(i32), *pieces, weights, weights)
 
 
+def add_blocks(a, b, after):
+    rows, width = a.shape
+    tile = rows // 2
+
+    def body(a_ref, b_ref, *refs):
+        refs[-1][...] = (a_ref[...].astype(f32) + b_ref[...].astype(f32)).astype(bf16)
+
+    spec = pl.BlockSpec((tile, width), lambda i: (i, 0))
+    return pl.pallas_call(
+        body,
+        out_shape=jax.ShapeDtypeStruct(a.shape, bf16),
+        grid=(2,),
+        in_specs=[spec, spec] + passive(after),
+        out_specs=spec,
+        compiler_params=params(),
+        cost_estimate=cost(rows * width, 6 * rows * width),
+    )(a, b, *after)
+
+
 def output_ring(pieces, weights, axis, step):
     me, behind, ahead, far = ring_order(lax.axis_index(axis))
     shards = [2 * place + side for place in (far, ahead, behind, me) for side in range(2)]
     to_far, to_ahead, to_behind, mine = output_partial(shards, pieces, weights)
     passing = shift(to_far, axis, step)
     if step == 1:
-        to_ahead = to_ahead + passing
-    else:
-        to_behind = to_behind + passing
-    return mine, shift(to_behind, axis, -1), shift(to_ahead, axis, 1)
+        to_ahead = add_blocks(to_ahead, passing, [])
+        return mine, shift(to_behind, axis, -1), shift(to_ahead, axis, 1)
+    from_behind = shift(to_ahead, axis, 1)
+    to_behind = add_blocks(to_behind, passing, [from_behind])
+    return mine, shift(to_behind, axis, -1), from_behind
 
 
 def finish(meta, parts, up, rank, wide):

time: 304 us -> 297 us (0.977)
  waiting for transfers between devices: 92.8 us -> 83.9 us
    ppermute x37, waiting for transfers between devices: 83.6 us -> 74.4 us  [shift(): lax.ppermute(block, axis, [(i, (i + step) % SIDE) for i in range(SIDE)])]
    pallas_call x0 -> x2, Pallas kernels: none -> 4.15 us  [add_blocks(): pl.pallas_call(body, out_shape=jax.ShapeDtypeStruct(a.shape, bf16), grid=...]
    unnamed x68 -> x66, local copies, waits for them, and re-layouts: 5.66 us -> 7.31 us
  transfers between devices with their start and end apart: 43 -> 43, of which waited for: 17 -> 19; matrix products, arithmetic and copies ran while one was open for 2% -> 2% of each run, Pallas kernels for 30% -> 32%
where the time goes in v13:
time: 297 us; the launch traced here: 294 us
  Pallas kernels  109 us (37%)
  waiting for transfers between devices  83.9 us (28%)
  starting transfers between devices  73.1 us (25%)
  between operations  13.8 us (5%)
  local copies, waits for them, and re-layouts  13 us (4%)
    ppermute x37, waiting for transfers between devices, shift(): lax.ppermute(block, axis, [(i, (i + step) % SIDE) for i in range(SIDE)])  74.4 us
    ppermute x37, starting transfers between devices, shift(): lax.ppermute(block, axis, [(i, (i + step) % SIDE) for i in range(SIDE)])  53.9 us
    pallas_call x5, Pallas kernels, project(): pl.pallas_call(body, out_shape=tuple((jax.ShapeDtypeStruct((tokens, w), d...  37.9 us
    pallas_call x2, Pallas kernels, output_partial(): pl.pallas_call(body, out_shape=tuple((jax.ShapeDtypeStruct((tokens, whole...  21.2 us
    pallas_call x2, Pallas kernels, attention(): pl.pallas_call(body, out_shape=jax.ShapeDtypeStruct((count * BLOCK, wide...  13.2 us
    pallas_call x2, Pallas kernels, join(): pl.pallas_call(body, out_shape=tuple((jax.ShapeDtypeStruct((tokens, w), b...  9.53 us
    all_to_all x1, waiting for transfers between devices, scatter_rows(): lax.all_to_all(partial.reshape(ways, rows // ways, rank), TENSOR_AXES, 0,...  9.02 us
    pallas_call x1, Pallas kernels, pick_local(): pl.pallas_call(body, out_shape=tuple((jax.ShapeDtypeStruct(s, bf16) for s...  7.33 us
  transfers between devices with their start and end apart: 43, of which 19 were waited for; matrix products, arithmetic and copies ran while one was open for 2% of the time, Pallas kernels for 32%

profile of v13, /device:TPU:0, one launch (start us, length us, event | category | flops | bytes accessed | tf_op | source)
XLA Modules:
  0.0 294.4 jit_solution(4311920246137606029)
XLA Ops:
  7.9 7.3 %shard_map.136 = (bf16[8,256,512]{2,1,0:T(8,128)(2,1)}, bf16[8,64,1152]{2,1,0:T(8,128)(2,1)}, bf16[1024,256]{1,0:T(8,128)(2,1)}, bf16[1024,256]{1,0:T(8,128)(2,1...) custom-call(s32[12]{0:T(128)} %pad_add_fusion.pick_ref, ...), custom_call_target="tpu_custom_call" | custom-call | bytes 6553600 | tf_op jit(solution)/shard_map/pallas_call | solution.py:90
  15.3 5.9 %all-to-all-start = ((bf16[8,256,512]{2,1,0:T(8,128)(2,1)}), bf16[8,256,512]{2,1,0:T(8,128)(2,1)S(1)}, u32[]{:S(2)}, u32[]{:S(2)}) async-start(bf16[8,256,512]{2,1,0:T(8,128)(2,1)} %get-tuple-element.55), calls=%async_computation | async-start | bytes 4194304 | tf_op jit(solution)/shard_map/all_to_all | solution.py:591
  29.7 7.0 %collective-permute-done.refs_1_ = bf16[1024,256]{1,0:T(8,128)(2,1)S(1)} collective-permute-done((bf16[1024,256]{1,0:T(8,128)(2,1)S(1)}, bf16[1024,256]{1,0:T(8,128)(2,1)S(1)}, u32[]{:S(2)}, u32[]{:S(2)}) %collective-permute-start) | collective-permute-done | bytes 524320 | tf_op jit(solution)/shard_map/ppermute | solution.py:37
  43.6 3.8 %collective-permute-done.10.refs_12_.refs_3_ = bf16[512,256]{1,0:T(8,128)(2,1)S(1)} collective-permute-done((bf16[512,256]{1,0:T(8,128)(2,1)}, bf16[512,256]{1,0:T(8,128)(2,1)S(1)}, u32[]{:S(2)}, u32[]{:S(2)}) %collective-permute-start.10) | collective-permute-done | bytes 262176 | tf_op jit(solution)/shard_map/ppermute | solution.py:37
  53.7 3.3 %collective-permute-done.6.refs_8_ = bf16[1024,128]{1,0:T(8,128)(2,1)S(1)} collective-permute-done((bf16[1024,128]{1,0:T(8,128)(2,1)S(1)}, bf16[1024,128]{1,0:T(8,128)(2,1)S(1)}, u32[]{:S(2)}, u32[]{:S(2)}) %collective-permute-start.6) | collective-permute-done | bytes 262176 | tf_op jit(solution)/shard_map/ppermute | solution.py:37
  59.8 4.7 %shard_map.137 = (bf16[1024,512]{1,0:T(8,128)(2,1)}, bf16[1024,512]{1,0:T(8,128)(2,1)}, bf16[1024,512]{1,0:T(8,128)(2,1)}, bf16[1024,512]{1,0:T(8,128)(2,1)}) custom-call(bf16[1024,256]{1,0:T(8,128)(2,1)} %get-tuple-element.37.refs_0_, bf16[1024,256]{1,0:T(8,128)(2,1)} %copy-done.6, bf16[1024,256]{1,0:T(8,128)(2,1)} %copy-done.7, ...), custom_call_target="tpu_custom_call" | custom-call | bytes 8388608 | tf_op jit(solution)/shard_map/pallas_call | solution.py:182
  76.4 5.1 %shard_map.143 = f32[1024,192]{1,0:T(8,128)} custom-call(s32[5,8]{1,0:T(8,128)} %stack.169.meta_ref, bf16[1024,512]{1,0:T(8,128)(2,1)} %x_ref.3, bf16[8,256,512]{2,1,0:T(8,128)(2,1)} %copy-done, bf16[8,256,512]{2,1,0:T(8,128)(2,1)} %copy-done, bf16[1024,512]{1,0:T(8,128)(2,1)} %get-tuple-element.42.refs_0_.rest_2_.refs_5_), custom_call_target="tpu_custom_call" | custom-call | flops 201326592 | bytes 2621440 | tf_op jit(solution)/shard_map/pallas_call | solution.py:150
  81.5 3.7 %all-to-all-start.1 = ((f32[16,64,192]{2,1,0:T(8,128)}), f32[16,64,192]{2,1,0:T(8,128)S(1)}, u32[]{:S(2)}, u32[]{:S(2)}) async-start(f32[16,64,192]{2,1,0:T(8,128)} %bitcast.79), calls=%async_computation.1 | async-start | bytes 2097152 | tf_op jit(solution)/shard_map/all_to_all | solution.py:224
  85.2 8.1 %shard_map.138 = (f32[1024,512]{1,0:T(8,128)}, f32[1024,128]{1,0:T(8,128)}) custom-call(s32[8]{0:T(128)} %stack.210.index_ref, s32[5,8]{1,0:T(8,128)} %stack.169.meta_ref, bf16[1024,512]{1,0:T(8,128)(2,1)} %get-tuple-element.42.refs_0_.rest_2_.refs_5_, bf16[1024,512]{1,0:T(8,128)(2,1)} %get-tuple-element.43.refs_1_, ...), custom_call_target="tpu_custom_call" | custom-call | flops 2684354560 | bytes 12058624 | tf_op jit(solution)/shard_map/pallas_call | solution.py:273
  93.3 4.8 %shard_map.139 = (bf16[1024,512]{1,0:T(8,128)(2,1)}, bf16[1024,512]{1,0:T(8,128)(2,1)}, bf16[1024,512]{1,0:T(8,128)(2,1)}, bf16[1024,512]{1,0:T(8,128)(2,1)}) custom-call(bf16[1024,256]{1,0:T(8,128)(2,1)} %get-tuple-element.37.refs_0_, bf16[1024,256]{1,0:T(8,128)(2,1)} %copy-done.6, bf16[1024,256]{1,0:T(8,128)(2,1)} %copy-done.7, ...), custom_call_target="tpu_custom_call" | custom-call | bytes 8388608 | tf_op jit(solution)/shard_map/pallas_call | solution.py:182
  103.2 9.0 %all-to-all-done.1.p_ref = f32[16,64,192]{2,1,0:T(8,128)S(1)} async-done(((f32[16,64,192]{2,1,0:T(8,128)}), f32[16,64,192]{2,1,0:T(8,128)S(1)}, u32[]{:S(2)}, u32[]{:S(2)}) %all-to-all-start.1) | async-done | bytes 786464 | tf_op jit(solution)/shard_map/all_to_all | solution.py:224
  115.3 3.6 %all-to-all-start.2 = ((bf16[16,64,192]{2,1,0:T(8,128)(2,1)}), bf16[16,64,192]{2,1,0:T(8,128)(2,1)S(1)}, u32[]{:S(2)}, u32[]{:S(2)}) async-start(bf16[16,64,192]{2,1,0:T(8,128)(2,1)} %get-tuple-element.57), calls=%async_computation.2 | async-start | bytes 1048576 | tf_op jit(solution)/shard_map/all_to_all | solution.py:653
  118.9 3.1 %collective-permute-start.22 = (bf16[1024,512]{1,0:T(8,128)(2,1)}, bf16[1024,512]{1,0:T(8,128)(2,1)}, u32[]{:S(2)}, u32[]{:S(2)}) collective-permute-start(bf16[1024,512]{1,0:T(8,128)(2,1)} %get-tuple-element.50), channel_id=1, source_target_pairs={{0,3},{1,0},{2,1},{3,2},{4,7},{5,4},{6,5},{7,6},{8,11},{9,8},{10,9... | collective-permute-start | bytes 3145736 | tf_op jit(solution)/shard_map/ppermute | solution.py:37
  123.5 9.4 %collective-permute-done.19.refs_0_ = bf16[1024,512]{1,0:T(8,128)(2,1)S(1)} collective-permute-done((bf16[1024,512]{1,0:T(8,128)(2,1)}, bf16[1024,512]{1,0:T(8,128)(2,1)S(1)}, u32[]{:S(2)}, u32[]{:S(2)}) %collective-permute-start.19) | collective-permute-done | bytes 1048608 | tf_op jit(solution)/shard_map/ppermute | solution.py:37
  137.7 4.5 %all-to-all-start.3 = ((bf16[8,64,1152]{2,1,0:T(8,128)(2,1)}), bf16[8,64,1152]{2,1,0:T(8,128)(2,1)S(1)}, u32[]{:S(2)}, u32[]{:S(2)}) async-start(bf16[8,64,1152]{2,1,0:T(8,128)(2,1)} %get-tuple-element.58), calls=%async_computation.3 | async-start | bytes 2359296 | tf_op jit(solution)/shard_map/all_to_all | solution.py:629
  144.3 8.6 %shard_map.140 = (f32[1024,512]{1,0:T(8,128)}, f32[1024,128]{1,0:T(8,128)}) custom-call(s32[8]{0:T(128)} %stack.219.index_ref, s32[5,8]{1,0:T(8,128)} %stack.169.meta_ref, bf16[1024,512]{1,0:T(8,128)(2,1)} %collective-permute-done.11.refs_0_, bf16[1024,512]{1,0:T(8,128)(2,1)} %collective-permute-done.13.refs_1_, ...), custom_call_target="tpu_custom_call", output_to_operand_aliasing={{0}: (22, {}), {1}: (23, {})} | custom-call | flops 2684354560 | bytes 12058624 | tf_op jit(solution)/shard_map/pallas_call | solution.py:273
  152.9 8.6 %shard_map.141 = (f32[1024,512]{1,0:T(8,128)}, f32[1024,128]{1,0:T(8,128)}) custom-call(s32[8]{0:T(128)} %stack.201.index_ref, s32[5,8]{1,0:T(8,128)} %stack.169.meta_ref, bf16[1024,512]{1,0:T(8,128)(2,1)} %copy-done.17, bf16[1024,512]{1,0:T(8,128)(2,1)} %collective-permute-done.20.refs_1_, ...), custom_call_target="tpu_custom_call", output_to_operand_aliasing={{0}: (22, {}), {1}: (23, {})} | custom-call | flops 2684354560 | bytes 12058624 | tf_op jit(solution)/shard_map/pallas_call | solution.py:273
  161.5 4.6 %collective-permute-done.18.refs_3_ = bf16[1024,512]{1,0:T(8,128)(2,1)} collective-permute-done((bf16[1024,512]{1,0:T(8,128)(2,1)}, bf16[1024,512]{1,0:T(8,128)(2,1)}, u32[]{:S(2)}, u32[]{:S(2)}) %collective-permute-start.18) | collective-permute-done | bytes 1048608 | tf_op jit(solution)/shard_map/ppermute | solution.py:37
  167.2 5.5 %shard_map.145.m_ref = bf16[1024,128]{1,0:T(8,128)(2,1)} custom-call(s32[8]{0:T(128)} %stack.187.index_ref, s32[5,8]{1,0:T(8,128)} %stack.169.meta_ref, bf16[1024,512]{1,0:T(8,128)(2,1)} %copy-done.4, bf16[1024,512]{1,0:T(8,128)(2,1)} %collective-permute-done.14.refs_1_, bf16[1024,512]{1,0:T(8,128)(2,1)} %collective-permute-done.16.refs_2_, ...), custom_call_target="tpu_custom_call" | custom-call | flops 536870912 | bytes 5767168 | tf_op jit(solution)/shard_map/pallas_call | solution.py:273
  174.1 7.1 %shard_map.142.q_ref = f32[1024,512]{1,0:T(8,128)} custom-call(s32[8]{0:T(128)} %stack.187.index_ref, s32[5,8]{1,0:T(8,128)} %stack.169.meta_ref, bf16[1024,512]{1,0:T(8,128)(2,1)} %copy-done.4, bf16[1024,512]{1,0:T(8,128)(2,1)} %collective-permute-done.14.refs_1_, ...), custom_call_target="tpu_custom_call", output_to_operand_aliasing={{}: (14, {})} | custom-call | flops 2147483648 | bytes 10485760 | tf_op jit(solution)/shard_map/pallas_call | solution.py:273
  181.9 6.6 %shard_map.150.refs_0_ = bf16[512,640]{1,0:T(8,128)(2,1)} custom-call(s32[5,8]{1,0:T(8,128)} %stack.169.meta_ref, f32[1024,512]{1,0:T(8,128)} %shard_map.142.q_ref, bf16[1024,192]{1,0:T(8,128)(2,1)} %bitcast.77, bf16[8,64,1152]{2,1,0:T(8,128)(2,1)} %copy-done.1, bf16[8,256,512]{2,1,0:T(8,128)(2,1)} %copy-done, bf16[1024,128]{1,0:T(8,128)(2,1)} %shard_map.145.m_ref, ...), custom_call_target="tpu_custom_call" | custom-call | flops 402653184 | bytes 2097152 | tf_op jit(solution)/shard_map/pallas_call | solution.py:384
  191.2 6.6 %shard_map.146.refs_0_ = bf16[512,640]{1,0:T(8,128)(2,1)} custom-call(s32[5,8]{1,0:T(8,128)} %stack.169.meta_ref, f32[1024,512]{1,0:T(8,128)} %shard_map.142.q_ref, bf16[1024,192]{1,0:T(8,128)(2,1)} %bitcast.78, bf16[8,64,1152]{2,1,0:T(8,128)(2,1)} %copy-done.1, bf16[8,256,512]{2,1,0:T(8,128)(2,1)} %copy-done, bf16[1024,128]{1,0:T(8,128)(2,1)} %shard_map.145.m_ref, ...), custom_call_target="tpu_custom_call" | custom-call | flops 402653184 | bytes 2097152 | tf_op jit(solution)/shard_map/pallas_call | solution.py:384
  197.8 3.2 %collective-permute-start.25 = (bf16[512,640]{1,0:T(8,128)(2,1)}, bf16[512,640]{1,0:T(8,128)(2,1)S(1)}, u32[]{:S(2)}, u32[]{:S(2)}) collective-permute-start(bf16[512,640]{1,0:T(8,128)(2,1)} %shard_map.146.refs_0_), channel_id=1, source_target_pairs={{0,12},{4,0},{8,4},{12,8},{1,13},{5,1},{9,5},{13,9},{2,14},{6,2},{... | collective-permute-start | bytes 1966088 | tf_op jit(solution)/shard_map/ppermute | solution.py:37
  201.0 4.7 %collective-permute-done.32.refs_2_ = bf16[512,640]{1,0:T(8,128)(2,1)S(1)} collective-permute-done((bf16[512,640]{1,0:T(8,128)(2,1)}, bf16[512,640]{1,0:T(8,128)(2,1)S(1)}, u32[]{:S(2)}, u32[]{:S(2)}) %collective-permute-start.32) | collective-permute-done | bytes 655392 | tf_op jit(solution)/shard_map/ppermute | solution.py:37
  209.8 9.9 %collective-permute-done.25.refs_2_ = bf16[512,640]{1,0:T(8,128)(2,1)S(1)} collective-permute-done((bf16[512,640]{1,0:T(8,128)(2,1)}, bf16[512,640]{1,0:T(8,128)(2,1)S(1)}, u32[]{:S(2)}, u32[]{:S(2)}) %collective-permute-start.25) | collective-permute-done | bytes 655392 | tf_op jit(solution)/shard_map/ppermute | solution.py:37
  227.0 10.6 %shard_map.151 = (bf16[512,640]{1,0:T(8,128)(2,1)}, bf16[512,640]{1,0:T(8,128)(2,1)}, bf16[512,640]{1,0:T(8,128)(2,1)}, f32[512,640]{1,0:T(8,128)}) custom-call(s32[8]{0:T(128)} %stack.178.index_ref, bf16[512,640]{1,0:T(8,128)(2,1)} %shard_map.150.refs_0_, bf16[512,640]{1,0:T(8,128)(2,1)} %copy-done.16, bf16[512,640]{1,0:T(8,128)(2,1)} %copy-done.14, ...), custom_call_target="tpu_custom_call" | custom-call | flops 4294967296 | bytes 10485760 | tf_op jit(solution)/shard_map/pallas_call | solution.py:443
  239.7 10.6 %shard_map.148 = (bf16[512,640]{1,0:T(8,128)(2,1)}, bf16[512,640]{1,0:T(8,128)(2,1)}, bf16[512,640]{1,0:T(8,128)(2,1)}, f32[512,640]{1,0:T(8,128)}) custom-call(s32[8]{0:T(128)} %stack.178.index_ref, bf16[512,640]{1,0:T(8,128)(2,1)} %shard_map.146.refs_0_, bf16[512,640]{1,0:T(8,128)(2,1)} %copy-done.15, bf16[512,640]{1,0:T(8,128)(2,1)} %copy-done.13, ...), custom_call_target="tpu_custom_call" | custom-call | flops 4294967296 | bytes 10485760 | tf_op jit(solution)/shard_map/pallas_call | solution.py:443
  253.6 4.1 %collective-permute-done.36.refs_0_.refs_5_ = bf16[512,640]{1,0:T(8,128)(2,1)S(1)} collective-permute-done((bf16[512,640]{1,0:T(8,128)(2,1)}, bf16[512,640]{1,0:T(8,128)(2,1)S(1)}, u32[]{:S(2)}, u32[]{:S(2)}) %collective-permute-start.36) | collective-permute-done | bytes 655392 | tf_op jit(solution)/shard_map/ppermute | solution.py:37
  260.6 5.0 %collective-permute-done.29.b_ref = bf16[512,640]{1,0:T(8,128)(2,1)S(1)} collective-permute-done((bf16[512,640]{1,0:T(8,128)(2,1)}, bf16[512,640]{1,0:T(8,128)(2,1)S(1)}, u32[]{:S(2)}, u32[]{:S(2)}) %collective-permute-start.29) | collective-permute-done | bytes 655392 | tf_op jit(solution)/shard_map/ppermute | solution.py:37
  269.6 7.0 %collective-permute-done.37.refs_4_ = bf16[512,640]{1,0:T(8,128)(2,1)S(1)} collective-permute-done((bf16[512,640]{1,0:T(8,128)(2,1)}, bf16[512,640]{1,0:T(8,128)(2,1)S(1)}, u32[]{:S(2)}, u32[]{:S(2)}) %collective-permute-start.37) | collective-permute-done | bytes 655392 | tf_op jit(solution)/shard_map/ppermute | solution.py:37
  276.6 4.0 %collective-permute-done.30.refs_2_ = bf16[512,640]{1,0:T(8,128)(2,1)S(1)} collective-permute-done((bf16[512,640]{1,0:T(8,128)(2,1)}, bf16[512,640]{1,0:T(8,128)(2,1)S(1)}, u32[]{:S(2)}, u32[]{:S(2)}) %collective-permute-start.30) | collective-permute-done | bytes 655392 | tf_op jit(solution)/shard_map/ppermute | solution.py:37
  281.4 6.2 %shard_map.153 = f32[1024,512]{1,0:T(8,128)} custom-call(s32[5,8]{1,0:T(8,128)} %stack.169.meta_ref, f32[512,640]{1,0:T(8,128)} %get-tuple-element.61.refs_0_, bf16[512,640]{1,0:T(8,128)(2,1)} %copy-done.28, bf16[512,640]{1,0:T(8,128)(2,1)} %copy-done.30, f32[512,640]{1,0:T(8,128)} %get-tuple-element.65.refs_3_, bf16[512,640]{1,0:T(8,128)(2,1)} %copy-done.29, ...), custom_call_target="tpu_custom_call" | custom-call | flops 67108864 | bytes 7340032 | tf_op jit(solution)/shard_map/pallas_call | solution.py:538
  (162 shorter events, 84.4 us)
Async XLA Ops:
  15.3 49.3 %all-to-all-start = ((bf16[8,256,512]{2,1,0:T(8,128)(2,1)}), bf16[8,256,512]{2,1,0:T(8,128)(2,1)S(1)}, u32[]{:S(2)}, u32[]{:S(2)}) async-start(bf16[8,256,512]{2,1,0:T(8,128)(2,1)} %get-tuple-element.55), calls=%async_computation | async-start | bytes 4194304 | tf_op jit(solution)/shard_map/all_to_all | solution.py:591
  21.2 205.8 %all-gather.3.cloned.1.call-start = ((), (), s32[]{:S(2)}) async-start(), calls=%async_computation.4 | async-start | bytes 9437184 | tf_op jit(solution)/shard_map/all_gather | solution.py:602
  24.5 15.6 %collective-permute-start.4 = (bf16[1024,256]{1,0:T(8,128)(2,1)S(1)}, bf16[1024,256]{1,0:T(8,128)(2,1)S(1)}, u32[]{:S(2)}, u32[]{:S(2)}) collective-permute-start(bf16[1024,256]{1,0:T(8,128)(2,1)S(1)} %copy-done.12), channel_id=1, source_target_pairs={{0,4},{4,8},{8,12},{12,0},{1,5},{5,9},{9,13},{13,1},{2,6},{6,10},{... | collective-permute-start | bytes 1572872 | tf_op jit(solution)/shard_map/ppermute | solution.py:37
  26.1 17.0 %collective-permute-start.5 = (bf16[1024,256]{1,0:T(8,128)(2,1)S(1)}, bf16[1024,256]{1,0:T(8,128)(2,1)S(1)}, u32[]{:S(2)}, u32[]{:S(2)}) collective-permute-start(bf16[1024,256]{1,0:T(8,128)(2,1)S(1)} %copy-done.12), channel_id=1, source_target_pairs={{0,12},{4,0},{8,4},{12,8},{1,13},{5,1},{9,5},{13,9},{2,14},{6,2},{... | collective-permute-start | bytes 1572872 | tf_op jit(solution)/shard_map/ppermute | solution.py:37
  27.8 19.7 %collective-permute-start.10 = (bf16[512,256]{1,0:T(8,128)(2,1)}, bf16[512,256]{1,0:T(8,128)(2,1)S(1)}, u32[]{:S(2)}, u32[]{:S(2)}) collective-permute-start(bf16[512,256]{1,0:T(8,128)(2,1)} %get-tuple-element.41), channel_id=1, source_target_pairs={{0,8},{4,12},{8,0},{12,4},{1,9},{5,13},{9,1},{13,5},{2,10},{6,14},... | collective-permute-start | bytes 786440 | tf_op jit(solution)/shard_map/ppermute | solution.py:37
  68.2 31.7 %collective-permute-start.11 = (bf16[1024,512]{1,0:T(8,128)(2,1)S(1)}, bf16[1024,512]{1,0:T(8,128)(2,1)}, u32[]{:S(2)}, u32[]{:S(2)}) collective-permute-start(bf16[1024,512]{1,0:T(8,128)(2,1)S(1)} %copy-done.2), channel_id=1, source_target_pairs={{0,4},{4,8},{8,12},{12,0},{1,5},{5,9},{9,13},{13,1},{2,6},{6,10},{... | collective-permute-start | bytes 3145736 | tf_op jit(solution)/shard_map/ppermute | solution.py:37
  68.5 32.9 %collective-permute-start.13 = (bf16[1024,512]{1,0:T(8,128)(2,1)}, bf16[1024,512]{1,0:T(8,128)(2,1)}, u32[]{:S(2)}, u32[]{:S(2)}) collective-permute-start(bf16[1024,512]{1,0:T(8,128)(2,1)} %get-tuple-element.43.refs_1_), channel_id=1, source_target_pairs={{0,12},{4,0},{8,4},{12,8},{1,13},{5,1},{9,5},{13,9},{2,14},{6,2},{... | collective-permute-start | bytes 3145736 | tf_op jit(solution)/shard_map/ppermute | solution.py:37
  73.2 45.7 %collective-permute-start.15 = (bf16[1024,512]{1,0:T(8,128)(2,1)}, bf16[1024,512]{1,0:T(8,128)(2,1)}, u32[]{:S(2)}, u32[]{:S(2)}) collective-permute-start(bf16[1024,512]{1,0:T(8,128)(2,1)} %get-tuple-element.44.refs_2_), channel_id=1, source_target_pairs={{0,1},{1,2},{2,3},{3,0},{4,5},{5,6},{6,7},{7,4},{8,9},{9,10},{10,1... | collective-permute-start | bytes 3145736 | tf_op jit(solution)/shard_map/ppermute | solution.py:37
  73.4 48.5 %collective-permute-start.17 = (bf16[1024,512]{1,0:T(8,128)(2,1)}, bf16[1024,512]{1,0:T(8,128)(2,1)}, u32[]{:S(2)}, u32[]{:S(2)}) collective-permute-start(bf16[1024,512]{1,0:T(8,128)(2,1)} %get-tuple-element.45.refs_3_), channel_id=1, source_target_pairs={{0,3},{1,0},{2,1},{3,2},{4,7},{5,4},{6,5},{7,6},{8,11},{9,8},{10,9... | collective-permute-start | bytes 3145736 | tf_op jit(solution)/shard_map/ppermute | solution.py:37
  81.5 30.7 %all-to-all-start.1 = ((f32[16,64,192]{2,1,0:T(8,128)}), f32[16,64,192]{2,1,0:T(8,128)S(1)}, u32[]{:S(2)}, u32[]{:S(2)}) async-start(f32[16,64,192]{2,1,0:T(8,128)} %bitcast.79), calls=%async_computation.1 | async-start | bytes 2097152 | tf_op jit(solution)/shard_map/all_to_all | solution.py:224
  98.1 34.7 %collective-permute-start.19 = (bf16[1024,512]{1,0:T(8,128)(2,1)}, bf16[1024,512]{1,0:T(8,128)(2,1)S(1)}, u32[]{:S(2)}, u32[]{:S(2)}) collective-permute-start(bf16[1024,512]{1,0:T(8,128)(2,1)} %get-tuple-element.47), channel_id=1, source_target_pairs={{0,4},{4,8},{8,12},{12,0},{1,5},{5,9},{9,13},{13,1},{2,6},{6,10},{... | collective-permute-start | bytes 3145736 | tf_op jit(solution)/shard_map/ppermute | solution.py:37
  99.9 34.1 %collective-permute-start.20 = (bf16[1024,512]{1,0:T(8,128)(2,1)}, bf16[1024,512]{1,0:T(8,128)(2,1)}, u32[]{:S(2)}, u32[]{:S(2)}) collective-permute-start(bf16[1024,512]{1,0:T(8,128)(2,1)} %get-tuple-element.48), channel_id=1, source_target_pairs={{0,12},{4,0},{8,4},{12,8},{1,13},{5,1},{9,5},{13,9},{2,14},{6,2},{... | collective-permute-start | bytes 3145736 | tf_op jit(solution)/shard_map/ppermute | solution.py:37
  101.4 34.6 %collective-permute-start.21 = (bf16[1024,512]{1,0:T(8,128)(2,1)}, bf16[1024,512]{1,0:T(8,128)(2,1)}, u32[]{:S(2)}, u32[]{:S(2)}) collective-permute-start(bf16[1024,512]{1,0:T(8,128)(2,1)} %get-tuple-element.49), channel_id=1, source_target_pairs={{0,1},{1,2},{2,3},{3,0},{4,5},{5,6},{6,7},{7,4},{8,9},{9,10},{10,1... | collective-permute-start | bytes 3145736 | tf_op jit(solution)/shard_map/ppermute | solution.py:37
  115.3 22.4 %all-to-all-start.2 = ((bf16[16,64,192]{2,1,0:T(8,128)(2,1)}), bf16[16,64,192]{2,1,0:T(8,128)(2,1)S(1)}, u32[]{:S(2)}, u32[]{:S(2)}) async-start(bf16[16,64,192]{2,1,0:T(8,128)(2,1)} %get-tuple-element.57), calls=%async_computation.2 | async-start | bytes 1048576 | tf_op jit(solution)/shard_map/all_to_all | solution.py:653
  118.9 34.0 %collective-permute-start.22 = (bf16[1024,512]{1,0:T(8,128)(2,1)}, bf16[1024,512]{1,0:T(8,128)(2,1)}, u32[]{:S(2)}, u32[]{:S(2)}) collective-permute-start(bf16[1024,512]{1,0:T(8,128)(2,1)} %get-tuple-element.50), channel_id=1, source_target_pairs={{0,3},{1,0},{2,1},{3,2},{4,7},{5,4},{6,5},{7,6},{8,11},{9,8},{10,9... | collective-permute-start | bytes 3145736 | tf_op jit(solution)/shard_map/ppermute | solution.py:37
  122.0 39.5 %collective-permute-start.12 = (bf16[1024,512]{1,0:T(8,128)(2,1)}, bf16[1024,512]{1,0:T(8,128)(2,1)S(1)}, u32[]{:S(2)}, u32[]{:S(2)}) collective-permute-start(bf16[1024,512]{1,0:T(8,128)(2,1)} %collective-permute-done.11.refs_0_), channel_id=1, source_target_pairs={{0,4},{4,8},{8,12},{12,0},{1,5},{5,9},{9,13},{13,1},{2,6},{6,10},{... | collective-permute-start | bytes 3145736 | tf_op jit(solution)/shard_map/ppermute | solution.py:37
  132.8 28.7 %collective-permute-start.14 = (bf16[1024,512]{1,0:T(8,128)(2,1)}, bf16[1024,512]{1,0:T(8,128)(2,1)}, u32[]{:S(2)}, u32[]{:S(2)}) collective-permute-start(bf16[1024,512]{1,0:T(8,128)(2,1)} %collective-permute-done.13.refs_1_), channel_id=1, source_target_pairs={{0,12},{4,0},{8,4},{12,8},{1,13},{5,1},{9,5},{13,9},{2,14},{6,2},{... | collective-permute-start | bytes 3145736 | tf_op jit(solution)/shard_map/ppermute | solution.py:37
  134.1 27.4 %collective-permute-start.16 = (bf16[1024,512]{1,0:T(8,128)(2,1)}, bf16[1024,512]{1,0:T(8,128)(2,1)}, u32[]{:S(2)}, u32[]{:S(2)}) collective-permute-start(bf16[1024,512]{1,0:T(8,128)(2,1)} %collective-permute-done.15.refs_2_), channel_id=1, source_target_pairs={{0,1},{1,2},{2,3},{3,0},{4,5},{5,6},{6,7},{7,4},{8,9},{9,10},{10,1... | collective-permute-start | bytes 3145736 | tf_op jit(solution)/shard_map/ppermute | solution.py:37
  136.0 30.1 %collective-permute-start.18 = (bf16[1024,512]{1,0:T(8,128)(2,1)}, bf16[1024,512]{1,0:T(8,128)(2,1)}, u32[]{:S(2)}, u32[]{:S(2)}) collective-permute-start(bf16[1024,512]{1,0:T(8,128)(2,1)} %collective-permute-done.17.refs_3_), channel_id=1, source_target_pairs={{0,3},{1,0},{2,1},{3,2},{4,7},{5,4},{6,5},{7,6},{8,11},{9,8},{10,9... | collective-permute-start | bytes 3145736 | tf_op jit(solution)/shard_map/ppermute | solution.py:37
  137.7 28.3 %all-to-all-start.3 = ((bf16[8,64,1152]{2,1,0:T(8,128)(2,1)}), bf16[8,64,1152]{2,1,0:T(8,128)(2,1)S(1)}, u32[]{:S(2)}, u32[]{:S(2)}) async-start(bf16[8,64,1152]{2,1,0:T(8,128)(2,1)} %get-tuple-element.58), calls=%async_computation.3 | async-start | bytes 2359296 | tf_op jit(solution)/shard_map/all_to_all | solution.py:629
  188.5 17.2 %collective-permute-start.32 = (bf16[512,640]{1,0:T(8,128)(2,1)}, bf16[512,640]{1,0:T(8,128)(2,1)S(1)}, u32[]{:S(2)}, u32[]{:S(2)}) collective-permute-start(bf16[512,640]{1,0:T(8,128)(2,1)} %shard_map.150.refs_0_), channel_id=1, source_target_pairs={{0,12},{4,0},{8,4},{12,8},{1,13},{5,1},{9,5},{13,9},{2,14},{6,2},{... | collective-permute-start | bytes 1966088 | tf_op jit(solution)/shard_map/ppermute | solution.py:37
  191.2 17.2 %collective-permute-start.31 = (bf16[512,640]{1,0:T(8,128)(2,1)}, bf16[512,640]{1,0:T(8,128)(2,1)S(1)}, u32[]{:S(2)}, u32[]{:S(2)}) collective-permute-start(bf16[512,640]{1,0:T(8,128)(2,1)} %shard_map.150.refs_0_), channel_id=1, source_target_pairs={{0,4},{4,8},{8,12},{12,0},{1,5},{5,9},{9,13},{13,1},{2,6},{6,10},{... | collective-permute-start | bytes 1966088 | tf_op jit(solution)/shard_map/ppermute | solution.py:37
  197.8 21.9 %collective-permute-start.25 = (bf16[512,640]{1,0:T(8,128)(2,1)}, bf16[512,640]{1,0:T(8,128)(2,1)S(1)}, u32[]{:S(2)}, u32[]{:S(2)}) collective-permute-start(bf16[512,640]{1,0:T(8,128)(2,1)} %shard_map.146.refs_0_), channel_id=1, source_target_pairs={{0,12},{4,0},{8,4},{12,8},{1,13},{5,1},{9,5},{13,9},{2,14},{6,2},{... | collective-permute-start | bytes 1966088 | tf_op jit(solution)/shard_map/ppermute | solution.py:37
  201.0 21.4 %collective-permute-start.24 = (bf16[512,640]{1,0:T(8,128)(2,1)}, bf16[512,640]{1,0:T(8,128)(2,1)S(1)}, u32[]{:S(2)}, u32[]{:S(2)}) collective-permute-start(bf16[512,640]{1,0:T(8,128)(2,1)} %shard_map.146.refs_0_), channel_id=1, source_target_pairs={{0,4},{4,8},{8,12},{12,0},{1,5},{5,9},{9,13},{13,1},{2,6},{6,10},{... | collective-permute-start | bytes 1966088 | tf_op jit(solution)/shard_map/ppermute | solution.py:37
  205.7 21.3 %collective-permute-start.34 = (bf16[512,384]{1,0:T(8,128)(2,1)S(1)}, bf16[512,384]{1,0:T(8,128)(2,1)}, u32[]{:S(2)}, u32[]{:S(2)}) collective-permute-start(bf16[512,384]{1,0:T(8,128)(2,1)S(1)} %slice.39), channel_id=1, source_target_pairs={{0,12},{4,0},{8,4},{12,8},{1,13},{5,1},{9,5},{13,9},{2,14},{6,2},{... | collective-permute-start | bytes 1179656 | tf_op jit(solution)/shard_map/ppermute | solution.py:37
  209.2 16.7 %collective-permute-start.33 = (bf16[512,256]{1,0:T(8,128)(2,1)}, bf16[512,256]{1,0:T(8,128)(2,1)}, u32[]{:S(2)}, u32[]{:S(2)}) collective-permute-start(bf16[512,256]{1,0:T(8,128)(2,1)} %slice.38), channel_id=1, source_target_pairs={{0,4},{4,8},{8,12},{12,0},{1,5},{5,9},{9,13},{13,1},{2,6},{6,10},{... | collective-permute-start | bytes 786440 | tf_op jit(solution)/shard_map/ppermute | solution.py:37
  219.8 19.9 %collective-permute-start.27 = (bf16[512,384]{1,0:T(8,128)(2,1)S(1)}, bf16[512,384]{1,0:T(8,128)(2,1)}, u32[]{:S(2)}, u32[]{:S(2)}) collective-permute-start(bf16[512,384]{1,0:T(8,128)(2,1)S(1)} %slice.37), channel_id=1, source_target_pairs={{0,12},{4,0},{8,4},{12,8},{1,13},{5,1},{9,5},{13,9},{2,14},{6,2},{... | collective-permute-start | bytes 1179656 | tf_op jit(solution)/shard_map/ppermute | solution.py:37
  223.2 16.5 %collective-permute-start.26 = (bf16[512,256]{1,0:T(8,128)(2,1)}, bf16[512,256]{1,0:T(8,128)(2,1)}, u32[]{:S(2)}, u32[]{:S(2)}) collective-permute-start(bf16[512,256]{1,0:T(8,128)(2,1)} %slice.36), channel_id=1, source_target_pairs={{0,4},{4,8},{8,12},{12,0},{1,5},{5,9},{9,13},{13,1},{2,6},{6,10},{... | collective-permute-start | bytes 786440 | tf_op jit(solution)/shard_map/ppermute | solution.py:37
  237.6 15.9 %collective-permute-start.35 = (bf16[512,640]{1,0:T(8,128)(2,1)}, bf16[512,640]{1,0:T(8,128)(2,1)S(1)}, u32[]{:S(2)}, u32[]{:S(2)}) collective-permute-start(bf16[512,640]{1,0:T(8,128)(2,1)} %get-tuple-element.67), channel_id=1, source_target_pairs={{0,3},{1,0},{2,1},{3,2},{4,7},{5,4},{6,5},{7,6},{8,11},{9,8},{10,9... | collective-permute-start | bytes 1966088 | tf_op jit(solution)/shard_map/ppermute | solution.py:37
  239.6 18.1 %collective-permute-start.36 = (bf16[512,640]{1,0:T(8,128)(2,1)}, bf16[512,640]{1,0:T(8,128)(2,1)S(1)}, u32[]{:S(2)}, u32[]{:S(2)}) collective-permute-start(bf16[512,640]{1,0:T(8,128)(2,1)} %get-tuple-element.68), channel_id=1, source_target_pairs={{0,1},{1,2},{2,3},{3,0},{4,5},{5,6},{6,7},{7,4},{8,9},{9,10},{10,1... | collective-permute-start | bytes 1966088 | tf_op jit(solution)/shard_map/ppermute | solution.py:37
  252.1 17.5 %collective-permute-start.28 = (bf16[512,640]{1,0:T(8,128)(2,1)}, bf16[512,640]{1,0:T(8,128)(2,1)S(1)}, u32[]{:S(2)}, u32[]{:S(2)}) collective-permute-start(bf16[512,640]{1,0:T(8,128)(2,1)} %get-tuple-element.62), channel_id=1, source_target_pairs={{0,3},{1,0},{2,1},{3,2},{4,7},{5,4},{6,5},{7,6},{8,11},{9,8},{10,9... | collective-permute-start | bytes 1966088 | tf_op jit(solution)/shard_map/ppermute | solution.py:37
  260.6 16.0 %collective-permute-start.37 = (bf16[512,640]{1,0:T(8,128)(2,1)}, bf16[512,640]{1,0:T(8,128)(2,1)S(1)}, u32[]{:S(2)}, u32[]{:S(2)}) collective-permute-start(bf16[512,640]{1,0:T(8,128)(2,1)} %shard_map.152), channel_id=1, source_target_pairs={{0,3},{1,0},{2,1},{3,2},{4,7},{5,4},{6,5},{7,6},{8,11},{9,8},{10,9... | collective-permute-start | bytes 1966088 | tf_op jit(solution)/shard_map/ppermute | solution.py:37
  (44 other events, 405.9 us)
Sparse Core Ops, SparseCore 0:
  68.3 49.6 all-gather.2

commit v14 on v13

--- a/solution.py
+++ b/solution.py
@@ -370,7 +370,7 @@
         for h in range(heads):
             at = slice(h * HEAD, (h + 1) * HEAD)
             weights = jnp.where(allowed, jnp.exp(scores[at, :] * scale), 0.0)
-            weights = weights * (1.0 / jnp.sum(weights, axis=1, keepdims=True))
+            weights = weights / jnp.sum(weights, axis=1, keepdims=True)
             mixed = jnp.dot(weights.astype(bf16), values, preferred_element_type=f32)
             att[:, at] = mixed.astype(bf16)
         head = lax.dot_general(

time: 297 us -> 297 us (level)
  no operation moved by 1% of the time
where the time goes in v14:
time: 297 us; the launch traced here: 295 us
  Pallas kernels  109 us (37%)
  waiting for transfers between devices  83.9 us (28%)
  starting transfers between devices  73.1 us (25%)
  between operations  13.8 us (5%)
  local copies, waits for them, and re-layouts  13 us (4%)
    ppermute x37, waiting for transfers between devices, shift(): lax.ppermute(block, axis, [(i, (i + step) % SIDE) for i in range(SIDE)])  74.5 us
    ppermute x37, starting transfers between devices, shift(): lax.ppermute(block, axis, [(i, (i + step) % SIDE) for i in range(SIDE)])  53.8 us
    pallas_call x5, Pallas kernels, project(): pl.pallas_call(body, out_shape=tuple((jax.ShapeDtypeStruct((tokens, w), d...  37.8 us
    pallas_call x2, Pallas kernels, output_partial(): pl.pallas_call(body, out_shape=tuple((jax.ShapeDtypeStruct((tokens, whole...  21.2 us
    pallas_call x2, Pallas kernels, attention(): pl.pallas_call(body, out_shape=jax.ShapeDtypeStruct((count * BLOCK, wide...  13.2 us
    pallas_call x2, Pallas kernels, join(): pl.pallas_call(body, out_shape=tuple((jax.ShapeDtypeStruct((tokens, w), b...  9.53 us
    all_to_all x1, waiting for transfers between devices, scatter_rows(): lax.all_to_all(partial.reshape(ways, rows // ways, rank), TENSOR_AXES, 0,...  8.98 us
    pallas_call x1, Pallas kernels, pick_local(): pl.pallas_call(body, out_shape=tuple((jax.ShapeDtypeStruct(s, bf16) for s...  7.5 us
  transfers between devices with their start and end apart: 43, of which 19 were waited for; matrix products, arithmetic and copies ran while one was open for 2% of the time, Pallas kernels for 32%

profile of v14, /device:TPU:0, one launch (start us, length us, event | category | flops | bytes accessed | tf_op | source)
XLA Modules:
  0.0 294.6 jit_solution(4311920246137606029)
XLA Ops:
  7.9 7.5 %shard_map.136 = (bf16[8,256,512]{2,1,0:T(8,128)(2,1)}, bf16[8,64,1152]{2,1,0:T(8,128)(2,1)}, bf16[1024,256]{1,0:T(8,128)(2,1)}, bf16[1024,256]{1,0:T(8,128)(2,1...) custom-call(s32[12]{0:T(128)} %pad_add_fusion.pick_ref, ...), custom_call_target="tpu_custom_call" | custom-call | bytes 6553600 | tf_op jit(solution)/shard_map/pallas_call | solution.py:90
  15.4 5.9 %all-to-all-start = ((bf16[8,256,512]{2,1,0:T(8,128)(2,1)}), bf16[8,256,512]{2,1,0:T(8,128)(2,1)S(1)}, u32[]{:S(2)}, u32[]{:S(2)}) async-start(bf16[8,256,512]{2,1,0:T(8,128)(2,1)} %get-tuple-element.55), calls=%async_computation | async-start | bytes 4194304 | tf_op jit(solution)/shard_map/all_to_all | solution.py:591
  29.9 7.0 %collective-permute-done.refs_1_ = bf16[1024,256]{1,0:T(8,128)(2,1)S(1)} collective-permute-done((bf16[1024,256]{1,0:T(8,128)(2,1)S(1)}, bf16[1024,256]{1,0:T(8,128)(2,1)S(1)}, u32[]{:S(2)}, u32[]{:S(2)}) %collective-permute-start) | collective-permute-done | bytes 524320 | tf_op jit(solution)/shard_map/ppermute | solution.py:37
  43.8 3.8 %collective-permute-done.10.refs_12_.refs_3_ = bf16[512,256]{1,0:T(8,128)(2,1)S(1)} collective-permute-done((bf16[512,256]{1,0:T(8,128)(2,1)}, bf16[512,256]{1,0:T(8,128)(2,1)S(1)}, u32[]{:S(2)}, u32[]{:S(2)}) %collective-permute-start.10) | collective-permute-done | bytes 262176 | tf_op jit(solution)/shard_map/ppermute | solution.py:37
  53.9 3.3 %collective-permute-done.6.refs_8_ = bf16[1024,128]{1,0:T(8,128)(2,1)S(1)} collective-permute-done((bf16[1024,128]{1,0:T(8,128)(2,1)S(1)}, bf16[1024,128]{1,0:T(8,128)(2,1)S(1)}, u32[]{:S(2)}, u32[]{:S(2)}) %collective-permute-start.6) | collective-permute-done | bytes 262176 | tf_op jit(solution)/shard_map/ppermute | solution.py:37
  60.0 4.7 %shard_map.137 = (bf16[1024,512]{1,0:T(8,128)(2,1)}, bf16[1024,512]{1,0:T(8,128)(2,1)}, bf16[1024,512]{1,0:T(8,128)(2,1)}, bf16[1024,512]{1,0:T(8,128)(2,1)}) custom-call(bf16[1024,256]{1,0:T(8,128)(2,1)} %get-tuple-element.37.refs_0_, bf16[1024,256]{1,0:T(8,128)(2,1)} %copy-done.6, bf16[1024,256]{1,0:T(8,128)(2,1)} %copy-done.7, ...), custom_call_target="tpu_custom_call" | custom-call | bytes 8388608 | tf_op jit(solution)/shard_map/pallas_call | solution.py:182
  76.6 5.2 %shard_map.143 = f32[1024,192]{1,0:T(8,128)} custom-call(s32[5,8]{1,0:T(8,128)} %stack.169.meta_ref, bf16[1024,512]{1,0:T(8,128)(2,1)} %x_ref.3, bf16[8,256,512]{2,1,0:T(8,128)(2,1)} %copy-done, bf16[8,256,512]{2,1,0:T(8,128)(2,1)} %copy-done, bf16[1024,512]{1,0:T(8,128)(2,1)} %get-tuple-element.42.refs_0_.rest_2_.refs_5_), custom_call_target="tpu_custom_call" | custom-call | flops 201326592 | bytes 2621440 | tf_op jit(solution)/shard_map/pallas_call | solution.py:150
  81.8 3.7 %all-to-all-start.1 = ((f32[16,64,192]{2,1,0:T(8,128)}), f32[16,64,192]{2,1,0:T(8,128)S(1)}, u32[]{:S(2)}, u32[]{:S(2)}) async-start(f32[16,64,192]{2,1,0:T(8,128)} %bitcast.79), calls=%async_computation.1 | async-start | bytes 2097152 | tf_op jit(solution)/shard_map/all_to_all | solution.py:224
  85.4 8.1 %shard_map.138 = (f32[1024,512]{1,0:T(8,128)}, f32[1024,128]{1,0:T(8,128)}) custom-call(s32[8]{0:T(128)} %stack.210.index_ref, s32[5,8]{1,0:T(8,128)} %stack.169.meta_ref, bf16[1024,512]{1,0:T(8,128)(2,1)} %get-tuple-element.42.refs_0_.rest_2_.refs_5_, bf16[1024,512]{1,0:T(8,128)(2,1)} %get-tuple-element.43.refs_1_, ...), custom_call_target="tpu_custom_call" | custom-call | flops 2684354560 | bytes 12058624 | tf_op jit(solution)/shard_map/pallas_call | solution.py:273
  93.5 4.8 %shard_map.139 = (bf16[1024,512]{1,0:T(8,128)(2,1)}, bf16[1024,512]{1,0:T(8,128)(2,1)}, bf16[1024,512]{1,0:T(8,128)(2,1)}, bf16[1024,512]{1,0:T(8,128)(2,1)}) custom-call(bf16[1024,256]{1,0:T(8,128)(2,1)} %get-tuple-element.37.refs_0_, bf16[1024,256]{1,0:T(8,128)(2,1)} %copy-done.6, bf16[1024,256]{1,0:T(8,128)(2,1)} %copy-done.7, ...), custom_call_target="tpu_custom_call" | custom-call | bytes 8388608 | tf_op jit(solution)/shard_map/pallas_call | solution.py:182
  103.4 9.0 %all-to-all-done.1.p_ref = f32[16,64,192]{2,1,0:T(8,128)S(1)} async-done(((f32[16,64,192]{2,1,0:T(8,128)}), f32[16,64,192]{2,1,0:T(8,128)S(1)}, u32[]{:S(2)}, u32[]{:S(2)}) %all-to-all-start.1) | async-done | bytes 786464 | tf_op jit(solution)/shard_map/all_to_all | solution.py:224
  115.5 3.6 %all-to-all-start.2 = ((bf16[16,64,192]{2,1,0:T(8,128)(2,1)}), bf16[16,64,192]{2,1,0:T(8,128)(2,1)S(1)}, u32[]{:S(2)}, u32[]{:S(2)}) async-start(bf16[16,64,192]{2,1,0:T(8,128)(2,1)} %get-tuple-element.57), calls=%async_computation.2 | async-start | bytes 1048576 | tf_op jit(solution)/shard_map/all_to_all | solution.py:653
  119.1 3.1 %collective-permute-start.22 = (bf16[1024,512]{1,0:T(8,128)(2,1)}, bf16[1024,512]{1,0:T(8,128)(2,1)}, u32[]{:S(2)}, u32[]{:S(2)}) collective-permute-start(bf16[1024,512]{1,0:T(8,128)(2,1)} %get-tuple-element.50), channel_id=1, source_target_pairs={{0,3},{1,0},{2,1},{3,2},{4,7},{5,4},{6,5},{7,6},{8,11},{9,8},{10,9... | collective-permute-start | bytes 3145736 | tf_op jit(solution)/shard_map/ppermute | solution.py:37
  123.7 9.4 %collective-permute-done.19.refs_0_ = bf16[1024,512]{1,0:T(8,128)(2,1)S(1)} collective-permute-done((bf16[1024,512]{1,0:T(8,128)(2,1)}, bf16[1024,512]{1,0:T(8,128)(2,1)S(1)}, u32[]{:S(2)}, u32[]{:S(2)}) %collective-permute-start.19) | collective-permute-done | bytes 1048608 | tf_op jit(solution)/shard_map/ppermute | solution.py:37
  137.9 4.6 %all-to-all-start.3 = ((bf16[8,64,1152]{2,1,0:T(8,128)(2,1)}), bf16[8,64,1152]{2,1,0:T(8,128)(2,1)S(1)}, u32[]{:S(2)}, u32[]{:S(2)}) async-start(bf16[8,64,1152]{2,1,0:T(8,128)(2,1)} %get-tuple-element.58), calls=%async_computation.3 | async-start | bytes 2359296 | tf_op jit(solution)/shard_map/all_to_all | solution.py:629
  144.5 8.6 %shard_map.140 = (f32[1024,512]{1,0:T(8,128)}, f32[1024,128]{1,0:T(8,128)}) custom-call(s32[8]{0:T(128)} %stack.219.index_ref, s32[5,8]{1,0:T(8,128)} %stack.169.meta_ref, bf16[1024,512]{1,0:T(8,128)(2,1)} %collective-permute-done.11.refs_0_, bf16[1024,512]{1,0:T(8,128)(2,1)} %collective-permute-done.13.refs_1_, ...), custom_call_target="tpu_custom_call", output_to_operand_aliasing={{0}: (22, {}), {1}: (23, {})} | custom-call | flops 2684354560 | bytes 12058624 | tf_op jit(solution)/shard_map/pallas_call | solution.py:273
  153.1 8.6 %shard_map.141 = (f32[1024,512]{1,0:T(8,128)}, f32[1024,128]{1,0:T(8,128)}) custom-call(s32[8]{0:T(128)} %stack.201.index_ref, s32[5,8]{1,0:T(8,128)} %stack.169.meta_ref, bf16[1024,512]{1,0:T(8,128)(2,1)} %copy-done.17, bf16[1024,512]{1,0:T(8,128)(2,1)} %collective-permute-done.20.refs_1_, ...), custom_call_target="tpu_custom_call", output_to_operand_aliasing={{0}: (22, {}), {1}: (23, {})} | custom-call | flops 2684354560 | bytes 12058624 | tf_op jit(solution)/shard_map/pallas_call | solution.py:273
  161.7 4.6 %collective-permute-done.18.refs_3_ = bf16[1024,512]{1,0:T(8,128)(2,1)} collective-permute-done((bf16[1024,512]{1,0:T(8,128)(2,1)}, bf16[1024,512]{1,0:T(8,128)(2,1)}, u32[]{:S(2)}, u32[]{:S(2)}) %collective-permute-start.18) | collective-permute-done | bytes 1048608 | tf_op jit(solution)/shard_map/ppermute | solution.py:37
  167.3 5.5 %shard_map.145.m_ref = bf16[1024,128]{1,0:T(8,128)(2,1)} custom-call(s32[8]{0:T(128)} %stack.187.index_ref, s32[5,8]{1,0:T(8,128)} %stack.169.meta_ref, bf16[1024,512]{1,0:T(8,128)(2,1)} %copy-done.4, bf16[1024,512]{1,0:T(8,128)(2,1)} %collective-permute-done.14.refs_1_, bf16[1024,512]{1,0:T(8,128)(2,1)} %collective-permute-done.16.refs_2_, ...), custom_call_target="tpu_custom_call" | custom-call | flops 536870912 | bytes 5767168 | tf_op jit(solution)/shard_map/pallas_call | solution.py:273
  174.3 7.1 %shard_map.142.q_ref = f32[1024,512]{1,0:T(8,128)} custom-call(s32[8]{0:T(128)} %stack.187.index_ref, s32[5,8]{1,0:T(8,128)} %stack.169.meta_ref, bf16[1024,512]{1,0:T(8,128)(2,1)} %copy-done.4, bf16[1024,512]{1,0:T(8,128)(2,1)} %collective-permute-done.14.refs_1_, ...), custom_call_target="tpu_custom_call", output_to_operand_aliasing={{}: (14, {})} | custom-call | flops 2147483648 | bytes 10485760 | tf_op jit(solution)/shard_map/pallas_call | solution.py:273
  182.1 6.6 %shard_map.150.refs_0_ = bf16[512,640]{1,0:T(8,128)(2,1)} custom-call(s32[5,8]{1,0:T(8,128)} %stack.169.meta_ref, f32[1024,512]{1,0:T(8,128)} %shard_map.142.q_ref, bf16[1024,192]{1,0:T(8,128)(2,1)} %bitcast.77, bf16[8,64,1152]{2,1,0:T(8,128)(2,1)} %copy-done.1, bf16[8,256,512]{2,1,0:T(8,128)(2,1)} %copy-done, bf16[1024,128]{1,0:T(8,128)(2,1)} %shard_map.145.m_ref, ...), custom_call_target="tpu_custom_call" | custom-call | flops 402653184 | bytes 2097152 | tf_op jit(solution)/shard_map/pallas_call | solution.py:384
  191.4 6.6 %shard_map.146.refs_0_ = bf16[512,640]{1,0:T(8,128)(2,1)} custom-call(s32[5,8]{1,0:T(8,128)} %stack.169.meta_ref, f32[1024,512]{1,0:T(8,128)} %shard_map.142.q_ref, bf16[1024,192]{1,0:T(8,128)(2,1)} %bitcast.78, bf16[8,64,1152]{2,1,0:T(8,128)(2,1)} %copy-done.1, bf16[8,256,512]{2,1,0:T(8,128)(2,1)} %copy-done, bf16[1024,128]{1,0:T(8,128)(2,1)} %shard_map.145.m_ref, ...), custom_call_target="tpu_custom_call" | custom-call | flops 402653184 | bytes 2097152 | tf_op jit(solution)/shard_map/pallas_call | solution.py:384
  198.0 3.2 %collective-permute-start.25 = (bf16[512,640]{1,0:T(8,128)(2,1)}, bf16[512,640]{1,0:T(8,128)(2,1)S(1)}, u32[]{:S(2)}, u32[]{:S(2)}) collective-permute-start(bf16[512,640]{1,0:T(8,128)(2,1)} %shard_map.146.refs_0_), channel_id=1, source_target_pairs={{0,12},{4,0},{8,4},{12,8},{1,13},{5,1},{9,5},{13,9},{2,14},{6,2},{... | collective-permute-start | bytes 1966088 | tf_op jit(solution)/shard_map/ppermute | solution.py:37
  201.2 4.7 %collective-permute-done.32.refs_2_ = bf16[512,640]{1,0:T(8,128)(2,1)S(1)} collective-permute-done((bf16[512,640]{1,0:T(8,128)(2,1)}, bf16[512,640]{1,0:T(8,128)(2,1)S(1)}, u32[]{:S(2)}, u32[]{:S(2)}) %collective-permute-start.32) | collective-permute-done | bytes 655392 | tf_op jit(solution)/shard_map/ppermute | solution.py:37
  210.0 10.0 %collective-permute-done.25.refs_2_ = bf16[512,640]{1,0:T(8,128)(2,1)S(1)} collective-permute-done((bf16[512,640]{1,0:T(8,128)(2,1)}, bf16[512,640]{1,0:T(8,128)(2,1)S(1)}, u32[]{:S(2)}, u32[]{:S(2)}) %collective-permute-start.25) | collective-permute-done | bytes 655392 | tf_op jit(solution)/shard_map/ppermute | solution.py:37
  227.3 10.6 %shard_map.151 = (bf16[512,640]{1,0:T(8,128)(2,1)}, bf16[512,640]{1,0:T(8,128)(2,1)}, bf16[512,640]{1,0:T(8,128)(2,1)}, f32[512,640]{1,0:T(8,128)}) custom-call(s32[8]{0:T(128)} %stack.178.index_ref, bf16[512,640]{1,0:T(8,128)(2,1)} %shard_map.150.refs_0_, bf16[512,640]{1,0:T(8,128)(2,1)} %copy-done.16, bf16[512,640]{1,0:T(8,128)(2,1)} %copy-done.14, ...), custom_call_target="tpu_custom_call" | custom-call | flops 4294967296 | bytes 10485760 | tf_op jit(solution)/shard_map/pallas_call | solution.py:443
  240.0 10.6 %shard_map.148 = (bf16[512,640]{1,0:T(8,128)(2,1)}, bf16[512,640]{1,0:T(8,128)(2,1)}, bf16[512,640]{1,0:T(8,128)(2,1)}, f32[512,640]{1,0:T(8,128)}) custom-call(s32[8]{0:T(128)} %stack.178.index_ref, bf16[512,640]{1,0:T(8,128)(2,1)} %shard_map.146.refs_0_, bf16[512,640]{1,0:T(8,128)(2,1)} %copy-done.15, bf16[512,640]{1,0:T(8,128)(2,1)} %copy-done.13, ...), custom_call_target="tpu_custom_call" | custom-call | flops 4294967296 | bytes 10485760 | tf_op jit(solution)/shard_map/pallas_call | solution.py:443
  253.8 4.1 %collective-permute-done.36.refs_0_.refs_5_ = bf16[512,640]{1,0:T(8,128)(2,1)S(1)} collective-permute-done((bf16[512,640]{1,0:T(8,128)(2,1)}, bf16[512,640]{1,0:T(8,128)(2,1)S(1)}, u32[]{:S(2)}, u32[]{:S(2)}) %collective-permute-start.36) | collective-permute-done | bytes 655392 | tf_op jit(solution)/shard_map/ppermute | solution.py:37
  260.8 5.0 %collective-permute-done.29.b_ref = bf16[512,640]{1,0:T(8,128)(2,1)S(1)} collective-permute-done((bf16[512,640]{1,0:T(8,128)(2,1)}, bf16[512,640]{1,0:T(8,128)(2,1)S(1)}, u32[]{:S(2)}, u32[]{:S(2)}) %collective-permute-start.29) | collective-permute-done | bytes 655392 | tf_op jit(solution)/shard_map/ppermute | solution.py:37
  269.8 7.0 %collective-permute-done.37.refs_4_ = bf16[512,640]{1,0:T(8,128)(2,1)S(1)} collective-permute-done((bf16[512,640]{1,0:T(8,128)(2,1)}, bf16[512,640]{1,0:T(8,128)(2,1)S(1)}, u32[]{:S(2)}, u32[]{:S(2)}) %collective-permute-start.37) | collective-permute-done | bytes 655392 | tf_op jit(solution)/shard_map/ppermute | solution.py:37
  276.8 4.0 %collective-permute-done.30.refs_2_ = bf16[512,640]{1,0:T(8,128)(2,1)S(1)} collective-permute-done((bf16[512,640]{1,0:T(8,128)(2,1)}, bf16[512,640]{1,0:T(8,128)(2,1)S(1)}, u32[]{:S(2)}, u32[]{:S(2)}) %collective-permute-start.30) | collective-permute-done | bytes 655392 | tf_op jit(solution)/shard_map/ppermute | solution.py:37
  281.6 6.2 %shard_map.153 = f32[1024,512]{1,0:T(8,128)} custom-call(s32[5,8]{1,0:T(8,128)} %stack.169.meta_ref, f32[512,640]{1,0:T(8,128)} %get-tuple-element.61.refs_0_, bf16[512,640]{1,0:T(8,128)(2,1)} %copy-done.28, bf16[512,640]{1,0:T(8,128)(2,1)} %copy-done.30, f32[512,640]{1,0:T(8,128)} %get-tuple-element.65.refs_3_, bf16[512,640]{1,0:T(8,128)(2,1)} %copy-done.29, ...), custom_call_target="tpu_custom_call" | custom-call | flops 67108864 | bytes 7340032 | tf_op jit(solution)/shard_map/pallas_call | solution.py:538
  (162 shorter events, 84.4 us)
Async XLA Ops:
  15.4 49.3 %all-to-all-start = ((bf16[8,256,512]{2,1,0:T(8,128)(2,1)}), bf16[8,256,512]{2,1,0:T(8,128)(2,1)S(1)}, u32[]{:S(2)}, u32[]{:S(2)}) async-start(bf16[8,256,512]{2,1,0:T(8,128)(2,1)} %get-tuple-element.55), calls=%async_computation | async-start | bytes 4194304 | tf_op jit(solution)/shard_map/all_to_all | solution.py:591
  21.4 205.9 %all-gather.3.cloned.1.call-start = ((), (), s32[]{:S(2)}) async-start(), calls=%async_computation.4 | async-start | bytes 9437184 | tf_op jit(solution)/shard_map/all_gather | solution.py:602
  24.7 15.6 %collective-permute-start.4 = (bf16[1024,256]{1,0:T(8,128)(2,1)S(1)}, bf16[1024,256]{1,0:T(8,128)(2,1)S(1)}, u32[]{:S(2)}, u32[]{:S(2)}) collective-permute-start(bf16[1024,256]{1,0:T(8,128)(2,1)S(1)} %copy-done.12), channel_id=1, source_target_pairs={{0,4},{4,8},{8,12},{12,0},{1,5},{5,9},{9,13},{13,1},{2,6},{6,10},{... | collective-permute-start | bytes 1572872 | tf_op jit(solution)/shard_map/ppermute | solution.py:37
  26.3 17.0 %collective-permute-start.5 = (bf16[1024,256]{1,0:T(8,128)(2,1)S(1)}, bf16[1024,256]{1,0:T(8,128)(2,1)S(1)}, u32[]{:S(2)}, u32[]{:S(2)}) collective-permute-start(bf16[1024,256]{1,0:T(8,128)(2,1)S(1)} %copy-done.12), channel_id=1, source_target_pairs={{0,12},{4,0},{8,4},{12,8},{1,13},{5,1},{9,5},{13,9},{2,14},{6,2},{... | collective-permute-start | bytes 1572872 | tf_op jit(solution)/shard_map/ppermute | solution.py:37
  28.0 19.7 %collective-permute-start.10 = (bf16[512,256]{1,0:T(8,128)(2,1)}, bf16[512,256]{1,0:T(8,128)(2,1)S(1)}, u32[]{:S(2)}, u32[]{:S(2)}) collective-permute-start(bf16[512,256]{1,0:T(8,128)(2,1)} %get-tuple-element.41), channel_id=1, source_target_pairs={{0,8},{4,12},{8,0},{12,4},{1,9},{5,13},{9,1},{13,5},{2,10},{6,14},... | collective-permute-start | bytes 786440 | tf_op jit(solution)/shard_map/ppermute | solution.py:37
  68.4 31.8 %collective-permute-start.11 = (bf16[1024,512]{1,0:T(8,128)(2,1)S(1)}, bf16[1024,512]{1,0:T(8,128)(2,1)}, u32[]{:S(2)}, u32[]{:S(2)}) collective-permute-start(bf16[1024,512]{1,0:T(8,128)(2,1)S(1)} %copy-done.2), channel_id=1, source_target_pairs={{0,4},{4,8},{8,12},{12,0},{1,5},{5,9},{9,13},{13,1},{2,6},{6,10},{... | collective-permute-start | bytes 3145736 | tf_op jit(solution)/shard_map/ppermute | solution.py:37
  68.7 33.0 %collective-permute-start.13 = (bf16[1024,512]{1,0:T(8,128)(2,1)}, bf16[1024,512]{1,0:T(8,128)(2,1)}, u32[]{:S(2)}, u32[]{:S(2)}) collective-permute-start(bf16[1024,512]{1,0:T(8,128)(2,1)} %get-tuple-element.43.refs_1_), channel_id=1, source_target_pairs={{0,12},{4,0},{8,4},{12,8},{1,13},{5,1},{9,5},{13,9},{2,14},{6,2},{... | collective-permute-start | bytes 3145736 | tf_op jit(solution)/shard_map/ppermute | solution.py:37
  73.4 45.7 %collective-permute-start.15 = (bf16[1024,512]{1,0:T(8,128)(2,1)}, bf16[1024,512]{1,0:T(8,128)(2,1)}, u32[]{:S(2)}, u32[]{:S(2)}) collective-permute-start(bf16[1024,512]{1,0:T(8,128)(2,1)} %get-tuple-element.44.refs_2_), channel_id=1, source_target_pairs={{0,1},{1,2},{2,3},{3,0},{4,5},{5,6},{6,7},{7,4},{8,9},{9,10},{10,1... | collective-permute-start | bytes 3145736 | tf_op jit(solution)/shard_map/ppermute | solution.py:37
  73.6 48.5 %collective-permute-start.17 = (bf16[1024,512]{1,0:T(8,128)(2,1)}, bf16[1024,512]{1,0:T(8,128)(2,1)}, u32[]{:S(2)}, u32[]{:S(2)}) collective-permute-start(bf16[1024,512]{1,0:T(8,128)(2,1)} %get-tuple-element.45.refs_3_), channel_id=1, source_target_pairs={{0,3},{1,0},{2,1},{3,2},{4,7},{5,4},{6,5},{7,6},{8,11},{9,8},{10,9... | collective-permute-start | bytes 3145736 | tf_op jit(solution)/shard_map/ppermute | solution.py:37
  81.8 30.6 %all-to-all-start.1 = ((f32[16,64,192]{2,1,0:T(8,128)}), f32[16,64,192]{2,1,0:T(8,128)S(1)}, u32[]{:S(2)}, u32[]{:S(2)}) async-start(f32[16,64,192]{2,1,0:T(8,128)} %bitcast.79), calls=%async_computation.1 | async-start | bytes 2097152 | tf_op jit(solution)/shard_map/all_to_all | solution.py:224
  98.3 34.7 %collective-permute-start.19 = (bf16[1024,512]{1,0:T(8,128)(2,1)}, bf16[1024,512]{1,0:T(8,128)(2,1)S(1)}, u32[]{:S(2)}, u32[]{:S(2)}) collective-permute-start(bf16[1024,512]{1,0:T(8,128)(2,1)} %get-tuple-element.47), channel_id=1, source_target_pairs={{0,4},{4,8},{8,12},{12,0},{1,5},{5,9},{9,13},{13,1},{2,6},{6,10},{... | collective-permute-start | bytes 3145736 | tf_op jit(solution)/shard_map/ppermute | solution.py:37
  100.2 34.1 %collective-permute-start.20 = (bf16[1024,512]{1,0:T(8,128)(2,1)}, bf16[1024,512]{1,0:T(8,128)(2,1)}, u32[]{:S(2)}, u32[]{:S(2)}) collective-permute-start(bf16[1024,512]{1,0:T(8,128)(2,1)} %get-tuple-element.48), channel_id=1, source_target_pairs={{0,12},{4,0},{8,4},{12,8},{1,13},{5,1},{9,5},{13,9},{2,14},{6,2},{... | collective-permute-start | bytes 3145736 | tf_op jit(solution)/shard_map/ppermute | solution.py:37
  101.6 34.6 %collective-permute-start.21 = (bf16[1024,512]{1,0:T(8,128)(2,1)}, bf16[1024,512]{1,0:T(8,128)(2,1)}, u32[]{:S(2)}, u32[]{:S(2)}) collective-permute-start(bf16[1024,512]{1,0:T(8,128)(2,1)} %get-tuple-element.49), channel_id=1, source_target_pairs={{0,1},{1,2},{2,3},{3,0},{4,5},{5,6},{6,7},{7,4},{8,9},{9,10},{10,1... | collective-permute-start | bytes 3145736 | tf_op jit(solution)/shard_map/ppermute | solution.py:37
  115.5 22.4 %all-to-all-start.2 = ((bf16[16,64,192]{2,1,0:T(8,128)(2,1)}), bf16[16,64,192]{2,1,0:T(8,128)(2,1)S(1)}, u32[]{:S(2)}, u32[]{:S(2)}) async-start(bf16[16,64,192]{2,1,0:T(8,128)(2,1)} %get-tuple-element.57), calls=%async_computation.2 | async-start | bytes 1048576 | tf_op jit(solution)/shard_map/all_to_all | solution.py:653
  119.1 34.0 %collective-permute-start.22 = (bf16[1024,512]{1,0:T(8,128)(2,1)}, bf16[1024,512]{1,0:T(8,128)(2,1)}, u32[]{:S(2)}, u32[]{:S(2)}) collective-permute-start(bf16[1024,512]{1,0:T(8,128)(2,1)} %get-tuple-element.50), channel_id=1, source_target_pairs={{0,3},{1,0},{2,1},{3,2},{4,7},{5,4},{6,5},{7,6},{8,11},{9,8},{10,9... | collective-permute-start | bytes 3145736 | tf_op jit(solution)/shard_map/ppermute | solution.py:37
  122.2 39.5 %collective-permute-start.12 = (bf16[1024,512]{1,0:T(8,128)(2,1)}, bf16[1024,512]{1,0:T(8,128)(2,1)S(1)}, u32[]{:S(2)}, u32[]{:S(2)}) collective-permute-start(bf16[1024,512]{1,0:T(8,128)(2,1)} %collective-permute-done.11.refs_0_), channel_id=1, source_target_pairs={{0,4},{4,8},{8,12},{12,0},{1,5},{5,9},{9,13},{13,1},{2,6},{6,10},{... | collective-permute-start | bytes 3145736 | tf_op jit(solution)/shard_map/ppermute | solution.py:37
  133.0 28.7 %collective-permute-start.14 = (bf16[1024,512]{1,0:T(8,128)(2,1)}, bf16[1024,512]{1,0:T(8,128)(2,1)}, u32[]{:S(2)}, u32[]{:S(2)}) collective-permute-start(bf16[1024,512]{1,0:T(8,128)(2,1)} %collective-permute-done.13.refs_1_), channel_id=1, source_target_pairs={{0,12},{4,0},{8,4},{12,8},{1,13},{5,1},{9,5},{13,9},{2,14},{6,2},{... | collective-permute-start | bytes 3145736 | tf_op jit(solution)/shard_map/ppermute | solution.py:37
  134.3 27.4 %collective-permute-start.16 = (bf16[1024,512]{1,0:T(8,128)(2,1)}, bf16[1024,512]{1,0:T(8,128)(2,1)}, u32[]{:S(2)}, u32[]{:S(2)}) collective-permute-start(bf16[1024,512]{1,0:T(8,128)(2,1)} %collective-permute-done.15.refs_2_), channel_id=1, source_target_pairs={{0,1},{1,2},{2,3},{3,0},{4,5},{5,6},{6,7},{7,4},{8,9},{9,10},{10,1... | collective-permute-start | bytes 3145736 | tf_op jit(solution)/shard_map/ppermute | solution.py:37
  136.2 30.1 %collective-permute-start.18 = (bf16[1024,512]{1,0:T(8,128)(2,1)}, bf16[1024,512]{1,0:T(8,128)(2,1)}, u32[]{:S(2)}, u32[]{:S(2)}) collective-permute-start(bf16[1024,512]{1,0:T(8,128)(2,1)} %collective-permute-done.17.refs_3_), channel_id=1, source_target_pairs={{0,3},{1,0},{2,1},{3,2},{4,7},{5,4},{6,5},{7,6},{8,11},{9,8},{10,9... | collective-permute-start | bytes 3145736 | tf_op jit(solution)/shard_map/ppermute | solution.py:37
  137.9 28.3 %all-to-all-start.3 = ((bf16[8,64,1152]{2,1,0:T(8,128)(2,1)}), bf16[8,64,1152]{2,1,0:T(8,128)(2,1)S(1)}, u32[]{:S(2)}, u32[]{:S(2)}) async-start(bf16[8,64,1152]{2,1,0:T(8,128)(2,1)} %get-tuple-element.58), calls=%async_computation.3 | async-start | bytes 2359296 | tf_op jit(solution)/shard_map/all_to_all | solution.py:629
  188.7 17.2 %collective-permute-start.32 = (bf16[512,640]{1,0:T(8,128)(2,1)}, bf16[512,640]{1,0:T(8,128)(2,1)S(1)}, u32[]{:S(2)}, u32[]{:S(2)}) collective-permute-start(bf16[512,640]{1,0:T(8,128)(2,1)} %shard_map.150.refs_0_), channel_id=1, source_target_pairs={{0,12},{4,0},{8,4},{12,8},{1,13},{5,1},{9,5},{13,9},{2,14},{6,2},{... | collective-permute-start | bytes 1966088 | tf_op jit(solution)/shard_map/ppermute | solution.py:37
  191.4 17.2 %collective-permute-start.31 = (bf16[512,640]{1,0:T(8,128)(2,1)}, bf16[512,640]{1,0:T(8,128)(2,1)S(1)}, u32[]{:S(2)}, u32[]{:S(2)}) collective-permute-start(bf16[512,640]{1,0:T(8,128)(2,1)} %shard_map.150.refs_0_), channel_id=1, source_target_pairs={{0,4},{4,8},{8,12},{12,0},{1,5},{5,9},{9,13},{13,1},{2,6},{6,10},{... | collective-permute-start | bytes 1966088 | tf_op jit(solution)/shard_map/ppermute | solution.py:37
  198.0 22.0 %collective-permute-start.25 = (bf16[512,640]{1,0:T(8,128)(2,1)}, bf16[512,640]{1,0:T(8,128)(2,1)S(1)}, u32[]{:S(2)}, u32[]{:S(2)}) collective-permute-start(bf16[512,640]{1,0:T(8,128)(2,1)} %shard_map.146.refs_0_), channel_id=1, source_target_pairs={{0,12},{4,0},{8,4},{12,8},{1,13},{5,1},{9,5},{13,9},{2,14},{6,2},{... | collective-permute-start | bytes 1966088 | tf_op jit(solution)/shard_map/ppermute | solution.py:37
  201.2 21.4 %collective-permute-start.24 = (bf16[512,640]{1,0:T(8,128)(2,1)}, bf16[512,640]{1,0:T(8,128)(2,1)S(1)}, u32[]{:S(2)}, u32[]{:S(2)}) collective-permute-start(bf16[512,640]{1,0:T(8,128)(2,1)} %shard_map.146.refs_0_), channel_id=1, source_target_pairs={{0,4},{4,8},{8,12},{12,0},{1,5},{5,9},{9,13},{13,1},{2,6},{6,10},{... | collective-permute-start | bytes 1966088 | tf_op jit(solution)/shard_map/ppermute | solution.py:37
  206.0 21.2 %collective-permute-start.34 = (bf16[512,384]{1,0:T(8,128)(2,1)S(1)}, bf16[512,384]{1,0:T(8,128)(2,1)}, u32[]{:S(2)}, u32[]{:S(2)}) collective-permute-start(bf16[512,384]{1,0:T(8,128)(2,1)S(1)} %slice.39), channel_id=1, source_target_pairs={{0,12},{4,0},{8,4},{12,8},{1,13},{5,1},{9,5},{13,9},{2,14},{6,2},{... | collective-permute-start | bytes 1179656 | tf_op jit(solution)/shard_map/ppermute | solution.py:37
  209.4 16.7 %collective-permute-start.33 = (bf16[512,256]{1,0:T(8,128)(2,1)}, bf16[512,256]{1,0:T(8,128)(2,1)}, u32[]{:S(2)}, u32[]{:S(2)}) collective-permute-start(bf16[512,256]{1,0:T(8,128)(2,1)} %slice.38), channel_id=1, source_target_pairs={{0,4},{4,8},{8,12},{12,0},{1,5},{5,9},{9,13},{13,1},{2,6},{6,10},{... | collective-permute-start | bytes 786440 | tf_op jit(solution)/shard_map/ppermute | solution.py:37
  220.1 19.9 %collective-permute-start.27 = (bf16[512,384]{1,0:T(8,128)(2,1)S(1)}, bf16[512,384]{1,0:T(8,128)(2,1)}, u32[]{:S(2)}, u32[]{:S(2)}) collective-permute-start(bf16[512,384]{1,0:T(8,128)(2,1)S(1)} %slice.37), channel_id=1, source_target_pairs={{0,12},{4,0},{8,4},{12,8},{1,13},{5,1},{9,5},{13,9},{2,14},{6,2},{... | collective-permute-start | bytes 1179656 | tf_op jit(solution)/shard_map/ppermute | solution.py:37
  223.4 16.5 %collective-permute-start.26 = (bf16[512,256]{1,0:T(8,128)(2,1)}, bf16[512,256]{1,0:T(8,128)(2,1)}, u32[]{:S(2)}, u32[]{:S(2)}) collective-permute-start(bf16[512,256]{1,0:T(8,128)(2,1)} %slice.36), channel_id=1, source_target_pairs={{0,4},{4,8},{8,12},{12,0},{1,5},{5,9},{9,13},{13,1},{2,6},{6,10},{... | collective-permute-start | bytes 786440 | tf_op jit(solution)/shard_map/ppermute | solution.py:37
  237.9 15.9 %collective-permute-start.35 = (bf16[512,640]{1,0:T(8,128)(2,1)}, bf16[512,640]{1,0:T(8,128)(2,1)S(1)}, u32[]{:S(2)}, u32[]{:S(2)}) collective-permute-start(bf16[512,640]{1,0:T(8,128)(2,1)} %get-tuple-element.67), channel_id=1, source_target_pairs={{0,3},{1,0},{2,1},{3,2},{4,7},{5,4},{6,5},{7,6},{8,11},{9,8},{10,9... | collective-permute-start | bytes 1966088 | tf_op jit(solution)/shard_map/ppermute | solution.py:37
  239.8 18.1 %collective-permute-start.36 = (bf16[512,640]{1,0:T(8,128)(2,1)}, bf16[512,640]{1,0:T(8,128)(2,1)S(1)}, u32[]{:S(2)}, u32[]{:S(2)}) collective-permute-start(bf16[512,640]{1,0:T(8,128)(2,1)} %get-tuple-element.68), channel_id=1, source_target_pairs={{0,1},{1,2},{2,3},{3,0},{4,5},{5,6},{6,7},{7,4},{8,9},{9,10},{10,1... | collective-permute-start | bytes 1966088 | tf_op jit(solution)/shard_map/ppermute | solution.py:37
  252.3 17.5 %collective-permute-start.28 = (bf16[512,640]{1,0:T(8,128)(2,1)}, bf16[512,640]{1,0:T(8,128)(2,1)S(1)}, u32[]{:S(2)}, u32[]{:S(2)}) collective-permute-start(bf16[512,640]{1,0:T(8,128)(2,1)} %get-tuple-element.62), channel_id=1, source_target_pairs={{0,3},{1,0},{2,1},{3,2},{4,7},{5,4},{6,5},{7,6},{8,11},{9,8},{10,9... | collective-permute-start | bytes 1966088 | tf_op jit(solution)/shard_map/ppermute | solution.py:37
  260.8 16.0 %collective-permute-start.37 = (bf16[512,640]{1,0:T(8,128)(2,1)}, bf16[512,640]{1,0:T(8,128)(2,1)S(1)}, u32[]{:S(2)}, u32[]{:S(2)}) collective-permute-start(bf16[512,640]{1,0:T(8,128)(2,1)} %shard_map.152), channel_id=1, source_target_pairs={{0,3},{1,0},{2,1},{3,2},{4,7},{5,4},{6,5},{7,6},{8,11},{9,8},{10,9... | collective-permute-start | bytes 1966088 | tf_op jit(solution)/shard_map/ppermute | solution.py:37
  (44 other events, 405.8 us)
Sparse Core Ops, SparseCore 0:
  68.5 49.6 all-gather.2
